TPU v7x, 32 devices: a whole 2x2x4 slice. The times are simulated.
32 devices in a mesh: blk: 8 (over z, x), uly: 4 (over y, core).
Axes of the slice: x: 2, y: 2, z: 4, core: 2. Of those that a mesh axis runs over, the one named last changes fastest.
Arguments:
- tokens: bfloat16 [4096, 2048], P(('blk', 'uly')), may hold values from -6 to 6
- segments: int32 [4096], replicated, may hold values from 0 to 66, as said below
- cotangent: bfloat16 [4096, 2048], P(('blk', 'uly')), may hold values from -6 to 6
- attn_gain: float32 [2048], P('blk'), may hold values from 0.5 to 1.5
- w_query: float32 [2048, 2048], P('blk', 'uly'), may hold values from -0.125 to 0.125
- w_key: float32 [2048, 2048], P('blk', 'uly'), may hold values from -0.125 to 0.125
- w_value: float32 [2048, 2048], P('blk', 'uly'), may hold values from -0.125 to 0.125
- w_output: float32 [2048, 2048], P('blk', 'uly'), may hold values from -0.5 to 0.5
- mlp_gain: float32 [2048], P('blk'), may hold values from 0.5 to 1.5
- w_gate: float32 [2048, 8192], P('blk', 'uly'), may hold values from -0.125 to 0.125
- w_up: float32 [2048, 8192], P('blk', 'uly'), may hold values from -0.125 to 0.125
- w_down: float32 [2048, 8192], P('blk', 'uly'), may hold values from -0.0625 to 0.0625
Outputs:
- output: float32 [4096, 2048], P(('blk', 'uly'))
- grad_tokens: float32 [4096, 2048], P(('blk', 'uly'))
- grad_attn_gain: float32 [2048], P('blk')
- grad_query: float32 [2048, 2048], P('blk', 'uly')
- grad_key: float32 [2048, 2048], P('blk', 'uly')
- grad_value: float32 [2048, 2048], P('blk', 'uly')
- grad_output: float32 [2048, 2048], P('blk', 'uly')
- grad_mlp_gain: float32 [2048], P('blk')
- grad_gate: float32 [2048, 8192], P('blk', 'uly')
- grad_up: float32 [2048, 8192], P('blk', 'uly')
- grad_down: float32 [2048, 8192], P('blk', 'uly')
Inputs may be any that keep to these rules, and one draw needn't show every extreme that they name: `segments`: document numbers start at 0, never fall and rise by at most one from a token to the next; one document starts within the first 512 tokens and ends within the last 512; there are exactly 3 + 2 * (32) documents.
All inputs are finite; a program needn't handle non-finite values.
Results may differ from a plain program's by a relative error of at most 0.023.
Values may be sent and summed in bfloat16 or wider, within the bound.
No kernel may reach another device: no remote copies, remote signals or barrier semaphores. Data moves between devices by JAX's collectives and lax.ppermute only.
A program may use at most 384 MiB of HBM per device.

v0:
```python
import math

import jax
import jax.numpy as jnp
from jax import lax
from jax.sharding import PartitionSpec as P

H = 32
HD = 64


theta_base = 130000.0
epsilon = 1e-05


def doc_positions(segments):
    count = segments.shape[0]
    index = jnp.arange(count, dtype=jnp.int32)
    first = jnp.concatenate([jnp.ones((1,), bool), segments[1:] != segments[:-1]])
    start = lax.cummax(jnp.where(first, index, 0), axis=0)
    return index - start


def rotary_tables(positions):
    half = HD // 2
    freqs = theta_base ** (-(jnp.arange(half, dtype=jnp.float32) * 2.0) / HD)
    angles = positions.astype(jnp.float32)[:, None] * freqs[None, :]
    return (jnp.cos(angles)[:, None, :], jnp.sin(angles)[:, None, :])


def rotate(value, cosine, sine):
    half = HD // 2
    first, second = (value[..., :half], value[..., half:])
    return jnp.concatenate(
        [first * cosine - second * sine, second * cosine + first * sine], axis=-1
    )


def rotate_back(value, cosine, sine):
    half = HD // 2
    first, second = (value[..., :half], value[..., half:])
    return jnp.concatenate(
        [first * cosine + second * sine, second * cosine - first * sine], axis=-1
    )


def contract_rows(left, right):
    return lax.dot_general(
        left, right, (((0,), (0,)), ((), ())), preferred_element_type=jnp.float32
    )


def contract_cols(left, right):
    return lax.dot_general(
        left, right, (((1,), (1,)), ((), ())), preferred_element_type=jnp.float32
    )


def rms_scale(value):
    return lax.rsqrt(jnp.mean(value * value, axis=-1, keepdims=True) + epsilon)


def on_device(
    tokens,
    segments,
    cotangent,
    attn_gain,
    w_query,
    w_key,
    w_value,
    w_output,
    mlp_gain,
    w_gate,
    w_up,
    w_down,
):
    n_uly = lax.axis_size("uly")
    tok = tokens.shape[0]
    rows_group = tok * n_uly
    seq = segments.shape[0]
    heads_local = H // n_uly
    feats = heads_local * HD
    scale = 1.0 / math.sqrt(HD)
    blk_idx = lax.axis_index("blk")
    own_start = lax.axis_index("uly") * tok
    q_first = blk_idx * rows_group
    positions = doc_positions(segments)
    q_segs = lax.dynamic_slice_in_dim(segments, q_first, rows_group, 0)
    q_pos = lax.dynamic_slice_in_dim(positions, q_first, rows_group, 0)
    q_index = q_first + jnp.arange(rows_group, dtype=jnp.int32)
    q_last = q_first + rows_group - 1
    cosine, sine = rotary_tables(q_pos)
    bf = jnp.bfloat16
    attn_params = (
        lax.all_gather(attn_gain.astype(bf), "blk", axis=0, tiled=True),
        lax.all_gather(w_query.astype(bf), "blk", axis=0, tiled=True),
        lax.all_gather(w_key.astype(bf), "blk", axis=0, tiled=True),
        lax.all_gather(w_value.astype(bf), "blk", axis=0, tiled=True),
        lax.all_gather(w_output.astype(bf), "blk", axis=0, tiled=True),
    )
    rows_all, cot_all = (
        lax.all_gather(tokens, "uly", axis=0, tiled=True),
        lax.all_gather(cotangent, "uly", axis=0, tiled=True),
    )
    gain1 = attn_params[0].astype(jnp.float32)
    x = rows_all.astype(jnp.float32)
    r1 = rms_scale(x)
    normed = (x * r1 * gain1).astype(bf)
    query = jnp.dot(normed, attn_params[1], preferred_element_type=jnp.float32).astype(bf)
    key = jnp.dot(normed, attn_params[2], preferred_element_type=jnp.float32).astype(bf)
    v_group = jnp.dot(normed, attn_params[3], preferred_element_type=jnp.float32).astype(bf)
    q_rot = rotate(
        query.astype(jnp.float32).reshape(rows_group, heads_local, HD), cosine, sine
    ).astype(bf)
    k_rot = rotate(
        key.astype(jnp.float32).reshape(rows_group, heads_local, HD), cosine, sine
    ).astype(bf)
    k_flat = k_rot.reshape(rows_group, feats)

    def block_mask(k_seg, k_start, width):
        k_idx = k_start + jnp.arange(width, dtype=jnp.int32)
        return (q_segs[:, None] == k_seg[None, :]) & (k_idx[None, :] <= q_index[:, None])

    start_state = (
        jnp.full((heads_local, rows_group), -1e30, jnp.float32),
        jnp.zeros((heads_local, rows_group), jnp.float32),
        jnp.zeros((heads_local, rows_group, HD), jnp.float32),
    )
    carry = start_state
    key_piece = lax.all_gather(k_flat, "blk", axis=0, tiled=True)
    value_piece = lax.all_gather(v_group, "blk", axis=0, tiled=True)
    nrows = key_piece.shape[0]
    fold_width = math.gcd(nrows, 512)

    def one_block(state, step):
        k_start = step * fold_width
        k_head = lax.dynamic_slice_in_dim(key_piece, step * fold_width, fold_width, 0).reshape(
            fold_width, heads_local, HD
        )
        v_head = lax.dynamic_slice_in_dim(value_piece, step * fold_width, fold_width, 0).reshape(
            fold_width, heads_local, HD
        )
        k_seg = lax.dynamic_slice_in_dim(segments, k_start, fold_width, 0)
        live = (k_start <= q_last) & (k_seg[fold_width - 1] >= q_segs[0])

        def attend(current):
            best, total, accum = current
            scores = (
                jnp.einsum("qhd,khd->hqk", q_rot, k_head, preferred_element_type=jnp.float32)
                * scale
            )
            allowed = block_mask(k_seg, k_start, fold_width)[None]
            masked = jnp.where(allowed, scores, -1e30)
            best_new = jnp.maximum(best, jnp.max(masked, axis=-1))
            probs = jnp.where(allowed, jnp.exp(masked - best_new[..., None]), 0.0)
            factor = jnp.exp(best - best_new)
            total = total * factor + jnp.sum(probs, axis=-1)
            accum = accum * factor[..., None] + jnp.einsum(
                "hqk,khd->hqd", probs.astype(bf), v_head, preferred_element_type=jnp.float32
            )
            return (best_new, total, accum)

        return (lax.cond(live, attend, lambda current: current, state), None)

    carry, unused = lax.scan(one_block, carry, jnp.arange(nrows // fold_width, dtype=jnp.int32))
    best, total, accum = carry
    lse = best + jnp.log(total)
    o_group = (
        jnp.transpose(accum / total[..., None], (1, 0, 2)).reshape(rows_group, feats).astype(bf)
    )
    attn_out = lax.psum(contract_cols(o_group, attn_params[4]).astype(jnp.bfloat16), "uly").astype(
        jnp.float32
    )
    x1 = x + attn_out
    mlp_params = (
        lax.all_gather(mlp_gain.astype(bf), "blk", axis=0, tiled=True),
        lax.all_gather(w_gate.astype(bf), "blk", axis=0, tiled=True),
        lax.all_gather(w_up.astype(bf), "blk", axis=0, tiled=True),
        lax.all_gather(w_down.astype(bf), "blk", axis=0, tiled=True),
    )
    gain2 = mlp_params[0].astype(jnp.float32)
    r2 = rms_scale(x1)
    normed2 = (x1 * r2 * gain2).astype(bf)
    gate = jnp.dot(normed2, mlp_params[1], preferred_element_type=jnp.float32)
    up = jnp.dot(normed2, mlp_params[2], preferred_element_type=jnp.float32)
    sigma = jax.nn.sigmoid(gate)
    silu_gate = gate * sigma
    act = (silu_gate * up).astype(bf)
    mlp_own = lax.psum_scatter(
        contract_cols(act, mlp_params[3]).astype(jnp.bfloat16),
        "uly",
        scatter_dimension=0,
        tiled=True,
    ).astype(jnp.float32)
    output = lax.dynamic_slice_in_dim(x1, own_start, tok, 0) + mlp_own
    grad_out = cot_all.astype(jnp.float32)
    d_act = jnp.dot(cot_all, mlp_params[3], preferred_element_type=jnp.float32)
    d_gate = (d_act * up * (sigma * (1.0 + gate * (1.0 - sigma)))).astype(bf)
    d_up = (d_act * silu_gate).astype(bf)
    d_norm2 = lax.psum(
        (contract_cols(d_gate, mlp_params[1]) + contract_cols(d_up, mlp_params[2])).astype(
            jnp.bfloat16
        ),
        "uly",
    ).astype(jnp.float32)
    mlp_grads = lax.psum_scatter(
        jnp.concatenate(
            [
                contract_rows(normed2, d_gate),
                contract_rows(normed2, d_up),
                contract_rows(cot_all, act),
            ],
            axis=1,
        ).astype(jnp.bfloat16),
        "blk",
        scatter_dimension=0,
        tiled=True,
    ).astype(jnp.float32)
    ff_local = w_gate.shape[1]
    gain2_term = jnp.sum(d_norm2 * x1 * r2, axis=0)
    z_two = gain2 * d_norm2
    dx1 = grad_out + r2 * z_two - x1 * r2 * r2 * r2 * jnp.mean(z_two * x1, axis=-1, keepdims=True)
    d_attn = dx1.astype(bf)
    d_o_group = jnp.dot(d_attn, attn_params[4], preferred_element_type=jnp.float32).astype(bf)
    do_head = d_o_group.reshape(rows_group, heads_local, HD)
    delta = jnp.transpose(
        jnp.sum(
            (d_o_group.astype(jnp.float32) * o_group.astype(jnp.float32)).reshape(
                rows_group, heads_local, HD
            ),
            axis=-1,
        )
    )
    keys_all, values_all = (
        lax.all_gather(k_flat, "blk", axis=0, tiled=True),
        lax.all_gather(v_group, "blk", axis=0, tiled=True),
    )
    width = math.gcd(seq, 512)

    def score_grads(k_head, v_head, k_seg, k_start):
        scores = (
            jnp.einsum("qhd,khd->hqk", q_rot, k_head, preferred_element_type=jnp.float32) * scale
        )
        allowed = block_mask(k_seg, k_start, width)[None]
        probs = jnp.exp(jnp.where(allowed, scores - lse[..., None], -1e30))
        d_prob = jnp.einsum("qhd,khd->hqk", do_head, v_head, preferred_element_type=jnp.float32)
        d_score = (probs * (d_prob - delta[..., None])).astype(bf)
        return (probs, d_score)

    def key_block(step):
        k_start = step * width
        k_head = lax.dynamic_slice_in_dim(keys_all, k_start, width, 0).reshape(
            width, heads_local, HD
        )
        v_head = lax.dynamic_slice_in_dim(values_all, k_start, width, 0).reshape(
            width, heads_local, HD
        )
        k_seg = lax.dynamic_slice_in_dim(segments, k_start, width, 0)
        live = (k_start <= q_last) & (k_seg[width - 1] >= q_segs[0])
        return (k_start, k_head, v_head, k_seg, live)

    def back_block(dq_acc, step):
        k_start, k_head, v_head, k_seg, live = key_block(step)

        def work(acc):
            probs, d_score = score_grads(k_head, v_head, k_seg, k_start)
            acc = acc + jnp.einsum(
                "hqk,khd->hqd", d_score, k_head, preferred_element_type=jnp.float32
            )
            d_key = jnp.einsum("hqk,qhd->khd", d_score, q_rot, preferred_element_type=jnp.float32)
            d_value = jnp.einsum(
                "hqk,qhd->khd", probs.astype(bf), do_head, preferred_element_type=jnp.float32
            )
            return (
                acc,
                jnp.concatenate(
                    [d_key.reshape(width, feats), d_value.reshape(width, feats)], axis=1
                ),
            )

        def skip(acc):
            return (acc, jnp.zeros((width, 2 * feats), jnp.float32))

        return lax.cond(live, work, skip, dq_acc)

    dq_acc, key_terms = lax.scan(
        back_block,
        jnp.zeros((heads_local, rows_group, HD), jnp.float32),
        jnp.arange(seq // width, dtype=jnp.int32),
    )
    key_sums = lax.psum_scatter(
        key_terms.reshape(seq, 2 * feats).astype(jnp.bfloat16),
        "blk",
        scatter_dimension=0,
        tiled=True,
    ).astype(jnp.float32)
    dk_sum = key_sums[:, :feats].reshape(rows_group, heads_local, HD)
    dv_sum = key_sums[:, feats:]
    d_query = (
        rotate_back(jnp.transpose(dq_acc, (1, 0, 2)) * scale, cosine, sine)
        .reshape(rows_group, feats)
        .astype(bf)
    )
    d_key = rotate_back(dk_sum * scale, cosine, sine).reshape(rows_group, feats).astype(bf)
    d_value = dv_sum.astype(bf)
    d_norm1_part = (
        contract_cols(d_query, attn_params[1])
        + contract_cols(d_key, attn_params[2])
        + contract_cols(d_value, attn_params[3])
    )
    d_norm1 = lax.psum(d_norm1_part.astype(jnp.bfloat16), "uly").astype(jnp.float32)
    gain1_term = jnp.sum(d_norm1 * x * r1, axis=0)
    z_one = gain1 * d_norm1
    grad_rows = dx1 + r1 * z_one - x * r1 * r1 * r1 * jnp.mean(z_one * x, axis=-1, keepdims=True)
    grad_input = lax.dynamic_slice_in_dim(grad_rows, own_start, tok, 0)
    attn_sums = (
        lax.psum_scatter(
            gain1_term.astype(jnp.bfloat16), "blk", scatter_dimension=0, tiled=True
        ).astype(jnp.float32),
        lax.psum_scatter(
            gain2_term.astype(jnp.bfloat16), "blk", scatter_dimension=0, tiled=True
        ).astype(jnp.float32),
        lax.psum_scatter(
            contract_rows(normed, d_query).astype(jnp.bfloat16),
            "blk",
            scatter_dimension=0,
            tiled=True,
        ).astype(jnp.float32),
        lax.psum_scatter(
            contract_rows(normed, d_key).astype(jnp.bfloat16),
            "blk",
            scatter_dimension=0,
            tiled=True,
        ).astype(jnp.float32),
        lax.psum_scatter(
            contract_rows(normed, d_value).astype(jnp.bfloat16),
            "blk",
            scatter_dimension=0,
            tiled=True,
        ).astype(jnp.float32),
        lax.psum_scatter(
            contract_rows(d_attn, o_group).astype(jnp.bfloat16),
            "blk",
            scatter_dimension=0,
            tiled=True,
        ).astype(jnp.float32),
    )
    return (
        output,
        grad_input,
        attn_sums[0],
        attn_sums[2],
        attn_sums[3],
        attn_sums[4],
        attn_sums[5],
        attn_sums[1],
        mlp_grads[:, :ff_local],
        mlp_grads[:, ff_local : 2 * ff_local],
        mlp_grads[:, 2 * ff_local :],
    )


def solution(mesh):
    placed = (
        P(("blk", "uly"), None),
        P(),
        P(("blk", "uly"), None),
        P("blk"),
        P("blk", "uly"),
        P("blk", "uly"),
        P("blk", "uly"),
        P("blk", "uly"),
        P("blk"),
        P("blk", "uly"),
        P("blk", "uly"),
        P("blk", "uly"),
    )
    return jax.shard_map(
        on_device,
        mesh=mesh,
        in_specs=placed,
        out_specs=(
            P(("blk", "uly"), None),
            P(("blk", "uly"), None),
            P("blk"),
            P("blk", "uly"),
            P("blk", "uly"),
            P("blk", "uly"),
            P("blk", "uly"),
            P("blk"),
            P("blk", "uly"),
            P("blk", "uly"),
            P("blk", "uly"),
        ),
        check_vma=False,
    )
```

profile of v0, /device:TPU:0, one launch (start us, length us, event | category | flops | bytes accessed | tf_op | source)
XLA Modules:
  0.0 2100.3 jit_solution(6630326677172605802)
XLA Ops:
  14.2 22.2 %all-gather = bf16[8,1,256]{2,1,0:T(2,128)(2,1)S(1)} all-gather(bf16[1,1,256]{2,1,0:T(2,128)(2,1)S(1)} %reshape.321), channel_id=1, replica_groups=mesh['blk'=8,'uly'=4] {'blk'}, dimensions={0}, use_global_device_ids=true | all-gather | bytes 4608 | tf_op jit(solution)/shard_map/all_gather | solution.py:95
  38.6 48.3 %all-gather.22.cloned.1.call-done = bf16[2048,512]{1,0:T(8,128)(2,1)} async-done(((bf16[256,512]{1,0:T(8,128)(2,1)}), bf16[2048,512]{1,0:T(8,128)(2,1)}) %all-gather.22.cloned.1.call-update) | async-done | bytes 2097168 | tf_op jit(solution)/shard_map/all_gather | solution.py:98
  92.7 44.8 %all-gather.20.cloned.1.call-done = bf16[2048,512]{1,0:T(8,128)(2,1)} async-done(((bf16[256,512]{1,0:T(8,128)(2,1)}), bf16[2048,512]{1,0:T(8,128)(2,1)}) %all-gather.20.cloned.1.call-update) | async-done | bytes 2097168 | tf_op jit(solution)/shard_map/all_gather | solution.py:96
  141.6 46.3 %all-gather.16.cloned.1.call-done = bf16[2048,512]{1,0:T(8,128)(2,1)} async-done(((bf16[256,512]{1,0:T(8,128)(2,1)}), bf16[2048,512]{1,0:T(8,128)(2,1)}) %all-gather.16.cloned.1.call-update) | async-done | bytes 2097168 | tf_op jit(solution)/shard_map/all_gather | solution.py:97
  194.5 67.8 %all-gather.24.cloned.1.call-done = bf16[4096,512]{1,0:T(8,128)(2,1)} async-done(((bf16[512,512]{1,0:T(8,128)(2,1)}), bf16[4096,512]{1,0:T(8,128)(2,1)}) %all-gather.24.cloned.1.call-update) | async-done | bytes 4194320 | tf_op jit(solution)/shard_map/all_gather | solution.py:131
  268.7 69.4 %all-gather.18.cloned.1.call-done = bf16[4096,512]{0,1:T(8,128)(2,1)} async-done(((bf16[512,512]{0,1:T(8,128)(2,1)}), bf16[4096,512]{0,1:T(8,128)(2,1)}) %all-gather.18.cloned.1.call-update) | async-done | bytes 4194320 | tf_op jit(solution)/shard_map/all_gather | solution.py:130
  339.2 39.2 %while.31 = (s32[]{:T(128)}, f32[8,512]{1,0:T(8,128)S(1)}, f32[8,512]{1,0:T(8,128)S(1)}, f32[8,512,64]{1,2,0:T(8,128)}, s32[8]{0:T(128)S(1)}, /*index=5*/s32[]{:...) while((s32[]{:T(128)}, f32[8,512]{1,0:T(8,128)S(1)}, ...), condition=%wide.region_8.9_spmd.clone, body=%wide.region_3.8_spmd.clone.sunk | while | flops 565453824 | bytes 40653280 | solution.py:165
  343.0 9.0 conditional.6
  401.8 72.4 %all-gather.1 = bf16[8,1,256]{2,1,0:T(2,128)(2,1)S(1)} all-gather(bf16[1,1,256]{2,1,0:T(2,128)(2,1)S(1)} %reshape.323), channel_id=1, replica_groups=mesh['blk'=8,'uly'=4] {'blk'}, dimensions={0}, use_global_device_ids=true | all-gather | bytes 4608 | tf_op jit(solution)/shard_map/all_gather | solution.py:176
  474.3 22.4 %all-reduce.7.cloned.1.call-done = bf16[512,2048]{1,0:T(8,128)(2,1)} async-done(((bf16[512,2048]{1,0:T(8,128)(2,1)}), bf16[512,2048]{1,0:T(8,128)(2,1)}) %all-reduce.7.cloned.1.call-update) | async-done | bytes 2097168 | tf_op jit(solution)/shard_map/psum | solution.py:171
  501.6 123.1 %all-gather.28.cloned.1.call-done = bf16[2048,2048]{1,0:T(8,128)(2,1)} async-done(((bf16[256,2048]{1,0:T(8,128)(2,1)}), bf16[2048,2048]{1,0:T(8,128)(2,1)}) %all-gather.28.cloned.1.call-update) | async-done | bytes 8388624 | tf_op jit(solution)/shard_map/all_gather | solution.py:177
  624.7 10.6 fusion.47
  635.3 115.3 %all-gather.30.cloned.1.call-done = bf16[2048,2048]{1,0:T(8,128)(2,1)} async-done(((bf16[256,2048]{1,0:T(8,128)(2,1)}), bf16[2048,2048]{1,0:T(8,128)(2,1)}) %all-gather.30.cloned.1.call-update) | async-done | bytes 8388624 | tf_op jit(solution)/shard_map/all_gather | solution.py:178
  750.6 10.5 fusion.48
  761.1 12.0 all-gather.34.cloned.1.call-done
  773.0 127.7 %all-gather.32.cloned.1.call-done = bf16[2048,2048]{1,0:T(8,128)(2,1)} async-done(((bf16[256,2048]{1,0:T(8,128)(2,1)}), bf16[2048,2048]{1,0:T(8,128)(2,1)}) %all-gather.32.cloned.1.call-update) | async-done | bytes 8388624 | tf_op jit(solution)/shard_map/all_gather | solution.py:179
  900.8 14.7 multiply_convert_fusion
  930.8 49.7 %all-reduce.9.cloned.1.call-done = bf16[512,2048]{1,0:T(8,128)(2,1)} async-done(((bf16[512,2048]{1,0:T(8,128)(2,1)}), bf16[512,2048]{1,0:T(8,128)(2,1)}) %all-reduce.9.cloned.1.call-update) | async-done | bytes 2097168 | tf_op jit(solution)/shard_map/psum | solution.py:200
  992.1 57.7 %while.32 = (s32[]{:T(128)}, f32[8,512,64]{1,2,0:T(8,128)}, bf16[8,512,1024]{2,1,0:T(8,128)(2,1)}, s32[8]{0:T(128)S(1)}, s32[]{:T(128)}, /*index=5*/s32[4096]{0:...) while((s32[]{:T(128)}, f32[8,512,64]{1,2,0:T(8,128)}, ...), condition=%wide.region_18.19_spmd.clone, body=%wide.region_15.18_spmd.clone.sunk | while | flops 1366295552 | bytes 53809564 | solution.py:286
  995.7 15.0 conditional.7
  1051.4 9.1 convolution_convert_fusion.6
  1066.8 236.3 %reduce-scatter.10.cloned.1.call-done = bf16[512,1024]{1,0:T(8,128)(2,1)} async-done(((bf16[4096,1024]{1,0:T(8,128)(2,1)}), bf16[512,1024]{1,0:T(8,128)(2,1)}) %reduce-scatter.10.cloned.1.call-update) | async-done | bytes 1048592 | tf_op jit(solution)/shard_map/reduce_scatter | solution.py:291
  1318.5 10.1 convolution_convert_fusion
  1331.4 10.2 convolution_convert_fusion.1
  1348.5 18.2 pad_maximum_fusion
  1371.1 36.1 %reduce-scatter.18.cloned.1.call-done = bf16[256,512]{1,0:T(8,128)(2,1)} async-done(((bf16[2048,512]{1,0:T(8,128)(2,1)}), bf16[256,512]{1,0:T(8,128)(2,1)}) %reduce-scatter.18.cloned.1.call-update) | async-done | bytes 262160 | tf_op jit(solution)/shard_map/reduce_scatter | solution.py:341
  1409.0 50.9 %all-reduce.11.cloned.1.call-done = bf16[512,2048]{1,0:T(8,128)(2,1)} async-done(((bf16[512,2048]{1,0:T(8,128)(2,1)}), bf16[512,2048]{1,0:T(8,128)(2,1)}) %all-reduce.11.cloned.1.call-update) | async-done | bytes 2097168 | tf_op jit(solution)/shard_map/psum | solution.py:311
  1466.3 22.0 %all-reduce.2 = (bf16[2048]{0:T(1024)(128)(2,1)S(1)}, bf16[2048]{0:T(1024)(128)(2,1)S(1)}) all-reduce(bf16[2048]{0:T(1024)(128)(2,1)S(1)} %get-tuple-element.568, bf16[2048]{0:T(1024)(128)(2,1)S(1)} %copy-done.23), channel_id=4, replica_groups=mesh['blk'=8,'uly'=4] {'blk'}, use_global_device_ids=true, to_apply=%region_23.24.clone | all-reduce | flops 4096 | bytes 16384
  1492.8 38.8 %reduce-scatter.12.cloned.1.call-done = bf16[256,512]{1,0:T(8,128)(2,1)} async-done(((bf16[2048,512]{1,0:T(8,128)(2,1)}), bf16[256,512]{1,0:T(8,128)(2,1)}) %reduce-scatter.12.cloned.1.call-update) | async-done | bytes 262160 | tf_op jit(solution)/shard_map/reduce_scatter | solution.py:323
  1533.4 69.0 %reduce-scatter.14.cloned.1.call-done = bf16[256,512]{1,0:T(8,128)(2,1)} async-done(((bf16[2048,512]{1,0:T(8,128)(2,1)}), bf16[256,512]{1,0:T(8,128)(2,1)}) %reduce-scatter.14.cloned.1.call-update) | async-done | bytes 262160 | tf_op jit(solution)/shard_map/reduce_scatter | solution.py:329
  1604.2 69.3 %reduce-scatter.16.cloned.1.call-done = bf16[256,512]{1,0:T(8,128)(2,1)} async-done(((bf16[2048,512]{1,0:T(8,128)(2,1)}), bf16[256,512]{1,0:T(8,128)(2,1)}) %reduce-scatter.16.cloned.1.call-update) | async-done | bytes 262160 | tf_op jit(solution)/shard_map/reduce_scatter | solution.py:335
  1675.2 406.1 %reduce-scatter.20.cloned.1.call-done = bf16[256,6144]{0,1:T(8,128)(2,1)} async-done(((bf16[2048,6144]{0,1:T(8,128)(2,1)}), bf16[256,6144]{0,1:T(8,128)(2,1)}) %reduce-scatter.20.cloned.1.call-update) | async-done | bytes 3145744 | tf_op jit(solution)/shard_map/reduce_scatter | solution.py:206
  (330 shorter events, 220.6 us)
Async XLA Ops:
  7.2 29.3 %all-gather.14.cloned.1.call-start = ((), (), s32[]{:S(2)}) async-start(), calls=%async_computation.7 | async-start | bytes 2621440 | tf_op jit(solution)/shard_map/all_gather | solution.py:102
  7.9 79.0 %all-gather.22.cloned.1.call-start = ((), (), s32[]{:S(2)}) async-start(), calls=%async_computation.11 | async-start | bytes 2359296 | tf_op jit(solution)/shard_map/all_gather | solution.py:98
  9.8 127.7 %all-gather.20.cloned.1.call-start = ((), (), s32[]{:S(2)}) async-start(), calls=%async_computation.10 | async-start | bytes 2359296 | tf_op jit(solution)/shard_map/all_gather | solution.py:96
  11.6 176.2 %all-gather.16.cloned.1.call-start = ((), (), s32[]{:S(2)}) async-start(), calls=%async_computation.8 | async-start | bytes 2359296 | tf_op jit(solution)/shard_map/all_gather | solution.py:97
  13.5 248.9 %all-gather.24.cloned.1.call-start = ((), (), s32[]{:S(2)}) async-start(), calls=%async_computation.12 | async-start | bytes 4718592 | tf_op jit(solution)/shard_map/all_gather | solution.py:131
  36.4 151.4 %copy-start.21 = (f32[8,1,256]{2,1,0:T(1,128)}, f32[8,1,256]{2,1,0:T(1,128)S(1)}, u32[]{:S(2)}) copy-start(f32[8,1,256]{2,1,0:T(1,128)S(1)} %convert_element_type.251) | copy-start | bytes 24580
  38.6 149.3 %copy-start.24 = (f32[512]{0:T(512)}, f32[512]{0:T(512)S(1)}, u32[]{:S(2)}) copy-start(f32[512]{0:T(512)S(1)} %add_rsqrt_fusion.1) | copy-start | bytes 6148
  86.9 50.6 %copy-start = (bf16[512,2048]{1,0:T(8,128)(2,1)S(1)}, bf16[512,2048]{1,0:T(8,128)(2,1)}, u32[]{:S(2)}) copy-start(bf16[512,2048]{1,0:T(8,128)(2,1)} %all-gather.14.cloned.1.call-done) | copy-start | bytes 6291460
  91.4 246.7 %all-gather.18.cloned.1.call-start = ((), (), s32[]{:S(2)}) async-start(), calls=%async_computation.9 | async-start | bytes 4718592 | tf_op jit(solution)/shard_map/all_gather | solution.py:130
  92.6 98.4 %copy-start.16 = (f32[512,32]{0,1:T(8,128)}, f32[512,32]{0,1:T(8,128)S(1)}, u32[]{:S(2)}) copy-start(f32[512,32]{0,1:T(8,128)S(1)} %get-tuple-element.658) | copy-start | bytes 196612
  92.7 98.4 %copy-start.18 = (f32[512,32]{0,1:T(8,128)}, f32[512,32]{0,1:T(8,128)S(1)}, u32[]{:S(2)}) copy-start(f32[512,32]{0,1:T(8,128)S(1)} %get-tuple-element.659) | copy-start | bytes 196612
  192.3 196.1 %all-gather.26.cloned.1.call-start = ((), (), s32[]{:S(2)}) async-start(), calls=%async_computation.13 | async-start | bytes 2359296 | tf_op jit(solution)/shard_map/all_gather | solution.py:99
  194.1 302.6 %all-reduce.7.cloned.1.call-start = ((), (), s32[]{:S(2)}) async-start(), calls=%async_computation.14 | async-start | bytes 4194304 | tf_op jit(solution)/shard_map/psum | solution.py:171
  392.6 232.0 %all-gather.28.cloned.1.call-start = ((), (), s32[]{:S(2)}) async-start(), calls=%async_computation.15 | async-start | bytes 9437184 | tf_op jit(solution)/shard_map/all_gather | solution.py:177
  395.4 355.1 %all-gather.30.cloned.1.call-start = ((), (), s32[]{:S(2)}) async-start(), calls=%async_computation.16 | async-start | bytes 9437184 | tf_op jit(solution)/shard_map/all_gather | solution.py:178
  398.2 374.8 %all-gather.34.cloned.1.call-start = ((), (), s32[]{:S(2)}) async-start(), calls=%async_computation.19 | async-start | bytes 2621440 | tf_op jit(solution)/shard_map/all_gather | solution.py:103
  399.0 501.8 %all-gather.32.cloned.1.call-start = ((), (), s32[]{:S(2)}) async-start(), calls=%async_computation.17 | async-start | bytes 9437184 | tf_op jit(solution)/shard_map/all_gather | solution.py:179
  401.8 578.7 %all-reduce.9.cloned.1.call-start = ((), (), s32[]{:S(2)}) async-start(), calls=%async_computation.20 | async-start | bytes 4194304 | tf_op jit(solution)/shard_map/psum | solution.py:200
  930.8 372.4 %reduce-scatter.10.cloned.1.call-start = ((), (), s32[]{:S(2)}) async-start(), calls=%async_computation.21 | async-start | bytes 9437184 | tf_op jit(solution)/shard_map/reduce_scatter | solution.py:291
  1049.8 318.8 %reduce-scatter.8.cloned.1.call-start = ((), (), s32[]{:S(2)}) async-start(), calls=%async_computation.18 | async-start | bytes 2621440 | tf_op jit(solution)/shard_map/reduce_scatter | solution.py:189
  1060.5 346.7 %reduce-scatter.18.cloned.1.call-start = ((), (), s32[]{:S(2)}) async-start(), calls=%async_computation.26 | async-start | bytes 2359296 | tf_op jit(solution)/shard_map/reduce_scatter | solution.py:341
  1065.4 239.2 %copy-start.17 = (f32[512,32]{0,1:T(8,128)S(1)}, f32[512,32]{0,1:T(8,128)}, u32[]{:S(2)}) copy-start(f32[512,32]{0,1:T(8,128)} %copy-done.16) | copy-start | bytes 196612
  1065.4 239.3 %copy-start.19 = (f32[512,32]{0,1:T(8,128)S(1)}, f32[512,32]{0,1:T(8,128)}, u32[]{:S(2)}) copy-start(f32[512,32]{0,1:T(8,128)} %copy-done.18) | copy-start | bytes 196612
  1065.4 394.5 %all-reduce.11.cloned.1.call-start = ((), (), s32[]{:S(2)}) async-start(), calls=%async_computation.22 | async-start | bytes 4194304 | tf_op jit(solution)/shard_map/psum | solution.py:311
  1312.4 219.2 %reduce-scatter.12.cloned.1.call-start = ((), (), s32[]{:S(2)}) async-start(), calls=%async_computation.23 | async-start | bytes 2359296 | tf_op jit(solution)/shard_map/reduce_scatter | solution.py:323
  1315.3 287.0 %reduce-scatter.14.cloned.1.call-start = ((), (), s32[]{:S(2)}) async-start(), calls=%async_computation.24 | async-start | bytes 2359296 | tf_op jit(solution)/shard_map/reduce_scatter | solution.py:329
  1318.2 10.3 copy-start.15
  1318.2 355.2 %reduce-scatter.16.cloned.1.call-start = ((), (), s32[]{:S(2)}) async-start(), calls=%async_computation.25 | async-start | bytes 2359296 | tf_op jit(solution)/shard_map/reduce_scatter | solution.py:335
  1331.3 750.0 %reduce-scatter.20.cloned.1.call-start = ((), (), s32[]{:S(2)}) async-start(), calls=%async_computation.27 | async-start | bytes 28311552 | tf_op jit(solution)/shard_map/reduce_scatter | solution.py:206
  1331.4 10.2 copy-start.11
  1331.4 10.2 copy-start.32
  1409.0 57.3 %copy-start.23 = (bf16[2048]{0:T(1024)(128)(2,1)S(1)}, bf16[2048]{0:T(1024)(128)(2,1)}, u32[]{:S(2)}) copy-start(bf16[2048]{0:T(1024)(128)(2,1)} %get-tuple-element.566) | copy-start | bytes 12292
  (22 other events, 73.1 us)
Sparse Core Ops, SparseCore 0:
  9.6 25.2 all-gather.13
  37.6 49.2 all-gather.21
  89.6 47.8 all-gather.19
  140.0 47.7 all-gather.15
  190.4 71.8 all-gather.23
  264.8 73.2 all-gather.17
  340.8 47.5 all-gather.25
  392.8 103.8 all-reduce.6
  499.6 124.9 all-gather.27
  627.4 123.1 all-gather.29
  752.2 20.7 all-gather.33
  775.8 124.9 all-gather.31
  930.9 49.5 all-reduce.8
  1049.9 253.1 reduce-scatter.9
  1305.6 30.4 reduce-scatter.7
  1339.5 67.6 reduce-scatter.17
  1409.4 50.4 all-reduce.10
  1463.7 67.8 reduce-scatter.11
  1535.5 66.7 reduce-scatter.13
  1606.7 66.6 reduce-scatter.15
  1677.8 403.4 reduce-scatter.19
where the time goes:
time: 2110 us; the launch traced here: 2100 us
  waiting for transfers between devices  1640 us (78%)
  matrix products  139 us (7%)
  blocking collectives  117 us (6%)
  other arithmetic  80.2 us (4%)
  local copies, waits for them, and re-layouts  71.9 us (3%)
  loops' own time  31.6 us (1%)
    reduce_scatter x1, waiting for transfers between devices, on_device(): lax.psum_scatter(jnp.concatenate([contract_rows(normed2, d_gate), contrac...  406 us
    reduce_scatter x1, waiting for transfers between devices, on_device(): lax.psum_scatter(key_terms.reshape(seq, 2 * feats).astype(jnp.bfloat16),...  236 us
    all_gather x1, waiting for transfers between devices, on_device(): lax.all_gather(w_down.astype(bf), 'blk', axis=0, tiled=True)  128 us
    all_gather x1, waiting for transfers between devices, on_device(): lax.all_gather(w_gate.astype(bf), 'blk', axis=0, tiled=True)  123 us
    all_gather x1, waiting for transfers between devices, on_device(): lax.all_gather(w_up.astype(bf), 'blk', axis=0, tiled=True)  115 us
    all_gather x1, blocking collectives, on_device(): lax.all_gather(mlp_gain.astype(bf), 'blk', axis=0, tiled=True)  72.4 us
    all_gather x1, waiting for transfers between devices, on_device(): key_piece = lax.all_gather(k_flat, 'blk', axis=0, tiled=True)  69.4 us
    reduce_scatter x1, waiting for transfers between devices, on_device(): lax.psum_scatter(contract_rows(normed, d_value).astype(jnp.bfloat16), 'bl...  69.3 us
  transfers between devices with their start and end apart: 21, of which 19 were waited for; matrix products, arithmetic and copies ran while one was open for 9% of the time, Pallas kernels for 0%

commit v1 on v0

v1 whole, which is shorter than its diff:
```python
import functools
import math

import jax
import jax.numpy as jnp
from jax import lax
from jax.experimental import pallas as pl
from jax.experimental.pallas import tpu as pltpu
from jax.sharding import PartitionSpec as P

H = 32
HD = 64
LANES = 128

theta_base = 130000.0
epsilon = 1e-05
bf = jnp.bfloat16
f32 = jnp.float32
NEG = -1e30


def dot_t(left, right):
    return lax.dot_general(left, right, (((1,), (1,)), ((), ())), preferred_element_type=f32)


def dot_n(left, right):
    return jnp.dot(left, right, preferred_element_type=f32)


def dot_c(left, right):
    return lax.dot_general(left, right, (((0,), (0,)), ((), ())), preferred_element_type=f32)


def rms_scale(value):
    return lax.rsqrt(jnp.mean(value * value, axis=-1, keepdims=True) + epsilon)


def gather(value, axis):
    return lax.all_gather(value, axis, axis=0, tiled=True)


def scatter(value, axis):
    return lax.psum_scatter(value, axis, scatter_dimension=0, tiled=True)


def swap(value, axis):
    return lax.all_to_all(value, axis, 0, 0, tiled=True)


def allowed_block(segk_ref, seg_q, pos_q, chunk, width):
    seg_k = segk_ref[pl.ds(pl.multiple_of(chunk * width, width), width), :]
    pos_k = chunk * width + lax.broadcasted_iota(jnp.int32, (width, 1), 0)
    return (seg_k == seg_q) & (pos_k <= pos_q)


def head_lanes(rows, head):
    lane = lax.broadcasted_iota(jnp.int32, (rows, LANES), 1)
    return (lane < HD) if head == 0 else (lane >= HD)


def attend_kernel(tile, segk_ref, segq_ref, posq_ref, q_ref, k_ref, v_ref, o_ref, lse_ref, vt_ref):
    nu, nb, tok, _ = k_ref.shape
    width = nu * tok
    rows = tile * tok
    j = pl.program_id(1)

    @pl.when(j == 0)
    def _():
        for c in range(nb):
            vt_ref[c] = v_ref[:, c].reshape(width, LANES).T

    seg_q, pos_q = segq_ref[0], posq_ref[0]
    q = q_ref[...] * jnp.asarray(1.0 / math.sqrt(HD), bf)
    q_heads = [jnp.where(head_lanes(rows, h), q, jnp.zeros_like(q)) for h in range(2)]

    def step(chunk, state):
        k = k_ref[:, chunk].reshape(width, LANES)
        v_t = vt_ref[chunk]
        ok = allowed_block(segk_ref, seg_q, pos_q, chunk, width)
        new = []
        for h in range(2):
            best, total, acc = state[h]
            s = jnp.where(ok, dot_t(k, q_heads[h]), NEG)
            best_new = jnp.maximum(best, jnp.max(s, axis=0, keepdims=True))
            p = jnp.exp(s - best_new)
            factor = jnp.exp(best - best_new)
            total = total * factor + jnp.sum(p, axis=0, keepdims=True)
            acc = acc * factor + dot_n(v_t[h * HD : (h + 1) * HD], p.astype(bf))
            new.append((best_new, total, acc))
        return tuple(new)

    start = (
        jnp.full((1, rows), NEG, f32),
        jnp.zeros((1, rows), f32),
        jnp.zeros((HD, rows), f32),
    )
    state = lax.fori_loop(0, (j + 1) * tile, step, (start, start))
    o_t = jnp.concatenate([acc / total for _, total, acc in state], axis=0)
    o_ref[...] = o_t.T.astype(bf)
    lse_ref[0, 0] = jnp.concatenate([best + jnp.log(total) for best, total, _ in state], axis=0)


def attend(segments, seg_q, pos_q, q, k, v, tile):
    nu, nb, tok, feats = k.shape
    rows = tile * tok
    nq = nb // tile
    pairs = feats // LANES
    row_spec = pl.BlockSpec((1, 1, rows), lambda p, j: (j, 0, 0))
    kv_spec = pl.BlockSpec((nu, nb, tok, LANES), lambda p, j: (0, 0, 0, p))
    q_spec = pl.BlockSpec((rows, LANES), lambda p, j: (j, p))
    return pl.pallas_call(
        functools.partial(attend_kernel, tile),
        grid=(pairs, nq),
        in_specs=[
            pl.BlockSpec((nu * nb * tok, 1), lambda p, j: (0, 0)),
            row_spec,
            row_spec,
            q_spec,
            kv_spec,
            kv_spec,
        ],
        out_specs=[q_spec, pl.BlockSpec((1, 1, 2, rows), lambda p, j: (p, j, 0, 0))],
        out_shape=[
            jax.ShapeDtypeStruct((nb * tok, feats), bf),
            jax.ShapeDtypeStruct((pairs, nq, 2, rows), f32),
        ],
        scratch_shapes=[pltpu.VMEM((nb, LANES, nu * tok), bf)],
        compiler_params=pltpu.CompilerParams(vmem_limit_bytes=48 * 2**20),
        name="attend",
    )(segments, seg_q, pos_q, q, k, v)


def attend_back_kernel(
    tile,
    segk_ref,
    segq_ref,
    posq_ref,
    cos_ref,
    sin_ref,
    q_ref,
    do_ref,
    o_ref,
    lse_ref,
    k_ref,
    v_ref,
    dq_ref,
    dkv_ref,
    acc_ref,
    delta_ref,
):
    nu, _, tok, _ = k_ref.shape
    nq = segq_ref.shape[0]
    width = nu * tok
    rows = tile * tok
    chunk = pl.program_id(1)
    scale = jnp.asarray(1.0 / math.sqrt(HD), bf)

    @pl.when(chunk == 0)
    def _():
        acc_ref[...] = jnp.zeros_like(acc_ref)
        lane = lax.broadcasted_iota(jnp.int32, (8, LANES), 1)
        row = lax.broadcasted_iota(jnp.int32, (8, LANES), 0)
        pick = jnp.where(lane // HD == row, 1.0, 0.0).astype(f32)
        for j in range(nq):
            part = do_ref[pl.ds(j * rows, rows), :].astype(f32) * o_ref[
                pl.ds(j * rows, rows), :
            ].astype(f32)
            delta_ref[j] = lax.dot_general(
                pick,
                part,
                (((1,), (1,)), ((), ())),
                preferred_element_type=f32,
                precision=lax.Precision.HIGHEST,
            )

    k = k_ref[:, 0].reshape(width, LANES)
    v = v_ref[:, 0].reshape(width, LANES)

    def step(j, state):
        dk, dv = state
        at = pl.ds(pl.multiple_of(j * rows, rows), rows)
        q = q_ref[at, :] * scale
        do = do_ref[at, :]
        ok = allowed_block(segk_ref, segq_ref[j], posq_ref[j], chunk, width)
        parts = []
        for h in range(2):
            mine = head_lanes(rows, h)
            q_h = jnp.where(mine, q, jnp.zeros_like(q))
            do_h = jnp.where(mine, do, jnp.zeros_like(do))
            p = jnp.exp(jnp.where(ok, dot_t(k, q_h) - lse_ref[0, j, h : h + 1], NEG))
            ds = (p * (dot_t(v, do_h) - delta_ref[j, h : h + 1])).astype(bf)
            dv = dv + dot_n(p.astype(bf), do_h)
            dk = dk + dot_n(ds, q_h)
            parts.append(dot_c(ds, k))
        acc_ref[at, :] = acc_ref[at, :] + jnp.where(head_lanes(rows, 0), parts[0], parts[1])
        return dk, dv

    zero = jnp.zeros((width, LANES), f32)
    dk, dv = lax.fori_loop(chunk // tile, nq, step, (zero, zero))
    dkv_ref[:, 0, 0] = dk.astype(bf).reshape(nu, tok, LANES)
    dkv_ref[:, 1, 0] = dv.astype(bf).reshape(nu, tok, LANES)

    @pl.when(chunk == pl.num_programs(1) - 1)
    def _():
        dq = acc_ref[...] * (1.0 / math.sqrt(HD))
        lane = lax.broadcasted_iota(jnp.int32, dq.shape, 1)
        other = jnp.where(
            lane % HD < HD // 2,
            pltpu.roll(dq, LANES - HD // 2, 1),
            pltpu.roll(dq, HD // 2, 1),
        )
        dq_ref[...] = (dq * cos_ref[...] - other * sin_ref[...]).astype(bf)


def attend_back(segments, seg_q, pos_q, cosine, sine, q, do, o, lse, k, v, tile):
    nu, nb, tok, feats = k.shape
    rows = tile * tok
    nq = nb // tile
    pairs = feats // LANES
    whole_rows = pl.BlockSpec((nq, 1, rows), lambda p, c: (0, 0, 0))
    table = pl.BlockSpec((nb * tok, LANES), lambda p, c: (0, 0))
    q_spec = pl.BlockSpec((nb * tok, LANES), lambda p, c: (0, p))
    kv_spec = pl.BlockSpec((nu, 1, tok, LANES), lambda p, c: (0, c, 0, p))
    return pl.pallas_call(
        functools.partial(attend_back_kernel, tile),
        grid=(pairs, nb),
        in_specs=[
            pl.BlockSpec((nu * nb * tok, 1), lambda p, c: (0, 0)),
            whole_rows,
            whole_rows,
            table,
            table,
            q_spec,
            q_spec,
            q_spec,
            pl.BlockSpec((1, nq, 2, rows), lambda p, c: (p, 0, 0, 0)),
            kv_spec,
            kv_spec,
        ],
        out_specs=[
            q_spec,
            pl.BlockSpec((nu, 2, 1, tok, LANES), lambda p, c: (0, 0, c, 0, p)),
        ],
        out_shape=[
            jax.ShapeDtypeStruct((nb * tok, feats), bf),
            jax.ShapeDtypeStruct((nu, 2, nb, tok, feats), bf),
        ],
        scratch_shapes=[pltpu.VMEM((nb * tok, LANES), f32), pltpu.VMEM((nq, 8, rows), f32)],
        compiler_params=pltpu.CompilerParams(vmem_limit_bytes=48 * 2**20),
        name="attend_back",
    )(segments, seg_q, pos_q, cosine, sine, q, do, o, lse, k, v)


def to_group(parts, strided):
    n, feats_u, rows = parts.shape
    nb, nu = lax.axis_size("blk"), lax.axis_size("uly")
    group = feats_u * nu // nb
    if strided:
        piece = feats_u // nb
        sent = jnp.transpose(parts.reshape(n, nb, piece, rows), (1, 0, 2, 3))
        got = gather(swap(sent, "blk")[None], "uly")
        return jnp.transpose(got, (2, 0, 3, 1, 4)).reshape(n, group, nb * rows)
    full = gather(parts[None], "uly")
    sent = jnp.transpose(full, (0, 2, 1, 3)).reshape(nb, group, n, rows)
    return jnp.transpose(swap(sent, "blk"), (2, 1, 0, 3)).reshape(n, group, nb * rows)


def from_group(grads, strided):
    n, group, all_rows = grads.shape
    nb, nu = lax.axis_size("blk"), lax.axis_size("uly")
    rows = all_rows // nb
    feats_u = group * nb // nu
    if strided:
        piece = group // nu
        mine = scatter(
            jnp.transpose(grads.reshape(n, nu, piece, nb, rows), (1, 3, 0, 2, 4)), "uly"
        )
        got = swap(mine[0], "blk")
        return jnp.transpose(got, (1, 0, 2, 3)).reshape(n, feats_u, rows)
    got = swap(jnp.transpose(grads.reshape(n, group, nb, rows), (2, 1, 0, 3)), "blk")
    mine = scatter(got.reshape(nu, feats_u, n, rows), "uly")
    return jnp.transpose(mine[0], (1, 0, 2))


def on_device(
    tokens,
    segments,
    cotangent,
    attn_gain,
    w_query,
    w_key,
    w_value,
    w_output,
    mlp_gain,
    w_gate,
    w_up,
    w_down,
):
    nb, nu = lax.axis_size("blk"), lax.axis_size("uly")
    b, u = lax.axis_index("blk"), lax.axis_index("uly")
    tok, dim = tokens.shape
    seq = segments.shape[0]
    rows = w_query.shape[0]
    feats_u = w_query.shape[1]
    heads_u = feats_u // HD
    strided = heads_u % nb == 0
    group = feats_u * nu // nb
    padded = -(-group // LANES) * LANES
    count = nb * tok
    tile = 2 if nb % 2 == 0 else 1
    both = ("blk", "uly")

    x_all = gather(tokens, "blk")
    flipped = [jnp.transpose(w.astype(bf)) for w in (w_query, w_key, w_value, w_output)]
    w_qkv = to_group(jnp.stack(flipped[:3]), strided).reshape(3 * group, dim)
    gains = gather(jnp.stack([attn_gain, mlp_gain]).astype(bf)[None], "blk")
    gain1, gain2 = [
        jnp.transpose(gains, (1, 0, 2)).reshape(2, dim)[i].astype(f32) for i in range(2)
    ]
    w_out = gather(flipped[3][None], both).reshape(nb, nu, feats_u, rows)
    if strided:
        piece = feats_u // nb
        w_out = jnp.transpose(
            w_out.reshape(nb, nu, nb, piece, rows), (2, 1, 3, 0, 4)
        ).reshape(dim, dim)
    else:
        w_out = jnp.transpose(w_out, (1, 2, 0, 3)).reshape(dim, dim)
    cot_all = gather(cotangent, "blk")
    ff_u = w_gate.shape[1]
    ff_piece = ff_u // nb
    hidden = ff_piece * nu
    w_ff = jnp.stack([w.astype(bf) for w in (w_gate, w_up, w_down)])
    w_ff = jnp.transpose(w_ff.reshape(3, rows, nb, ff_piece), (2, 0, 1, 3))
    w_ff = gather(swap(w_ff, "blk")[None], "uly")
    w_ff = jnp.transpose(w_ff, (2, 1, 3, 0, 4)).reshape(3, dim, hidden)

    seg_mine = lax.dynamic_index_in_dim(segments.reshape(nb, nu, tok), u, 1, False).reshape(count)
    index = (
        jnp.arange(nb, dtype=jnp.int32)[:, None] * (nu * tok)
        + u * tok
        + jnp.arange(tok, dtype=jnp.int32)[None, :]
    ).reshape(count)
    first = jnp.sum((segments[None, :] < seg_mine[:, None]).astype(jnp.int32), axis=1)
    lane = jnp.arange(LANES, dtype=jnp.int32)
    freq = theta_base ** (-((lane % (HD // 2)).astype(f32) * 2.0) / HD)
    angles = (index - first).astype(f32)[:, None] * freq[None, :]
    cosine = jnp.cos(angles)
    sine = jnp.sin(angles) * jnp.where(lane % HD < HD // 2, -1.0, 1.0)[None, :]
    feat = jnp.arange(padded, dtype=jnp.int32)
    partner = jnp.where(feat % HD < HD // 2, feat + HD // 2, feat - HD // 2)
    turn = (feat[:, None] == partner[None, :]).astype(bf)
    cos_wide = jnp.tile(cosine, (1, padded // LANES))
    sin_wide = jnp.tile(sine, (1, padded // LANES))
    seg_col = segments[:, None]
    seg_rows = seg_mine.reshape(nb // tile, 1, tile * tok)
    pos_rows = index.reshape(nb // tile, 1, tile * tok)

    x = x_all.astype(f32)
    r1 = rms_scale(x)
    normed = (x * r1 * gain1).astype(bf)
    qkv = dot_t(normed, w_qkv).astype(bf)

    def part(i):
        return jnp.pad(qkv[:, i * group : (i + 1) * group], ((0, 0), (0, padded - group)))

    def rotate(value):
        return (value.astype(f32) * cos_wide + dot_n(value, turn) * sin_wide).astype(bf)

    q_rot, k_rot = rotate(part(0)), rotate(part(1))
    keys = gather(k_rot.reshape(1, nb, tok, padded), "uly")
    values = gather(part(2).reshape(1, nb, tok, padded), "uly")
    o, lse = attend(seg_col, seg_rows, pos_rows, q_rot, keys, values, tile)
    o_all = gather(o[:, :group][None], "blk")
    o_wide = jnp.transpose(o_all, (1, 0, 2)).reshape(count, dim)
    x1 = x + dot_n(o_wide, w_out)

    r2 = rms_scale(x1)
    normed2 = (x1 * r2 * gain2).astype(bf)
    gate = dot_n(normed2, w_ff[0])
    up = dot_n(normed2, w_ff[1])
    sigma = jax.nn.sigmoid(gate)
    silu_gate = gate * sigma
    act = (silu_gate * up).astype(bf)
    d_act = dot_n(cot_all, w_ff[2])
    d_gate = (d_act * up * (sigma * (1.0 + gate * (1.0 - sigma)))).astype(bf)
    d_up = (d_act * silu_gate).astype(bf)
    d_norm2 = scatter(
        (dot_t(d_gate, w_ff[0]) + dot_t(d_up, w_ff[1])).astype(bf), "blk"
    ).astype(f32)
    mlp_out = scatter(dot_t(act, w_ff[2]).astype(bf), "blk").astype(f32)
    x1_own = lax.dynamic_slice_in_dim(x1, b * tok, tok, 0)
    output = x1_own + mlp_out

    ff_grads = jnp.stack([dot_c(normed2, d_gate), dot_c(normed2, d_up), dot_c(cot_all, act)])
    ff_grads = jnp.transpose(
        ff_grads.astype(bf).reshape(3, nb, rows, nu, ff_piece), (3, 1, 0, 2, 4)
    )
    ff_grads = swap(scatter(ff_grads, "uly")[0], "blk")
    ff_grads = jnp.transpose(ff_grads, (1, 2, 0, 3)).reshape(3, rows, ff_u).astype(f32)

    r2_own = rms_scale(x1_own)
    gain2_part = jnp.sum(d_norm2 * x1_own * r2_own, axis=0)
    z_two = gain2 * d_norm2
    dx1 = (
        cotangent.astype(f32)
        + r2_own * z_two
        - x1_own * r2_own * r2_own * r2_own * jnp.mean(z_two * x1_own, axis=-1, keepdims=True)
    )
    d_attn = dx1.astype(bf)
    d_o = dot_t(d_attn, w_out).astype(bf)
    d_o = swap(jnp.transpose(d_o.reshape(tok, nb, group), (1, 0, 2)), "blk").reshape(count, group)
    d_o = jnp.pad(d_o, ((0, 0), (0, padded - group)))
    d_attn_all = gather(d_attn, "blk")
    dq, dkv = attend_back(
        seg_col, seg_rows, pos_rows, cosine, sine, q_rot, d_o, o, lse, keys, values, tile
    )
    dkv = scatter(dkv, "uly")[0]
    dk = dkv[0].reshape(count, padded)
    dv = dkv[1].reshape(count, padded)
    dk = (dk.astype(f32) * cos_wide - dot_n(dk, turn) * sin_wide).astype(bf)
    dqkv = jnp.concatenate([dq[:, :group], dk[:, :group], dv[:, :group]], axis=1)
    d_norm1_part = dot_n(dqkv, w_qkv)
    gain1_part = jnp.sum(d_norm1_part * x * r1, axis=0)
    d_norm1 = scatter(d_norm1_part.astype(bf), "blk").astype(f32)
    x_own = tokens.astype(f32)
    r1_own = rms_scale(x_own)
    z_one = gain1 * d_norm1
    grad_tokens = (
        dx1
        + r1_own * z_one
        - x_own * r1_own * r1_own * r1_own * jnp.mean(z_one * x_own, axis=-1, keepdims=True)
    )
    attn_grads = jnp.concatenate(
        [
            dot_c(dqkv, normed).astype(bf).reshape(3, group, dim),
            dot_c(o[:, :group], d_attn_all).astype(bf)[None],
        ]
    )
    attn_grads = jnp.transpose(from_group(attn_grads, strided), (0, 2, 1)).astype(f32)
    gain_sums = lax.psum(jnp.stack([gain1_part, gain2_part]), both)
    gain_own = lax.dynamic_slice_in_dim(gain_sums, b * rows, rows, 1)
    return (
        output,
        grad_tokens,
        gain_own[0],
        attn_grads[0],
        attn_grads[1],
        attn_grads[2],
        attn_grads[3],
        gain_own[1],
        ff_grads[0],
        ff_grads[1],
        ff_grads[2],
    )


def solution(mesh):
    tokens_split = P(("blk", "uly"), None)
    weights = P("blk", "uly")
    return jax.shard_map(
        on_device,
        mesh=mesh,
        in_specs=(
            tokens_split,
            P(),
            tokens_split,
            P("blk"),
            weights,
            weights,
            weights,
            weights,
            P("blk"),
            weights,
            weights,
            weights,
        ),
        out_specs=(
            tokens_split,
            tokens_split,
            P("blk"),
            weights,
            weights,
            weights,
            weights,
            P("blk"),
            weights,
            weights,
            weights,
        ),
        check_vma=False,
    )
```

time: 2110 us -> 1260 us (0.60)
  waiting for transfers between devices: 1640 us -> 462 us
  blocking collectives: 117 us -> 322 us
  local copies, waits for them, and re-layouts: 71.9 us -> 200 us
  Pallas kernels: 0 us -> 91.6 us
  other arithmetic: 80.2 us -> 32.4 us
  loops' own time: 31.6 us -> 0 us
  matrix products: 139 us -> 114 us
    reduce_scatter x7 -> x6, waiting for transfers between devices: 855 us -> 301 us  [scatter(): return lax.psum_scatter(value, axis, scatter_dimension=0, tiled=True)]
    all_gather x11 -> x9, waiting for transfers between devices: 663 us -> 160 us  [gather(): return lax.all_gather(value, axis, axis=0, tiled=True)]
    all_to_all x0 -> x3, blocking collectives: none -> 179 us  [swap(): return lax.all_to_all(value, axis, 0, 0, tiled=True)]
    psum x0 -> x1, blocking collectives: none -> 124 us  [on_device(): gain_sums = lax.psum(jnp.stack([gain1_part, gain2_part]), both)]
    psum x3 -> x0, waiting for transfers between devices: 123 us -> none  [the longest x1 50.9 us: on_device(): lax.psum(d_norm1_part.astype(jnp.bfloat16), 'uly').astype(jnp.float32)]
    pallas_call x0 -> x2, Pallas kernels: none -> 91.6 us  [the longest x1 49.2 us: attend_back(): pl.pallas_call(functools.partial(attend_back_kernel, tile), grid=(pairs,...]
    all_gather x2 -> x1, blocking collectives: 94.7 us -> 18.6 us  [gather(): return lax.all_gather(value, axis, axis=0, tiled=True)]
    unnamed x69 -> x100, local copies, waits for them, and re-layouts: 18.6 us -> 87.8 us
  transfers between devices with their start and end apart: 21 -> 17, of which waited for: 19 -> 11; matrix products, arithmetic and copies ran while one was open for 9% -> 21% of each run, Pallas kernels for 0% -> 7%
where the time goes in v1:
time: 1260 us; the launch traced here: 1250 us
  waiting for transfers between devices  462 us (37%)
  blocking collectives  322 us (26%)
  local copies, waits for them, and re-layouts  200 us (16%)
  matrix products  114 us (9%)
  Pallas kernels  91.6 us (7%)
  other arithmetic  32.4 us (3%)
  between operations  15 us (1%)
    reduce_scatter x6, waiting for transfers between devices, scatter(): return lax.psum_scatter(value, axis, scatter_dimension=0, tiled=True)  301 us
    all_to_all x3, blocking collectives, swap(): return lax.all_to_all(value, axis, 0, 0, tiled=True)  179 us
    all_gather x9, waiting for transfers between devices, gather(): return lax.all_gather(value, axis, axis=0, tiled=True)  160 us
    psum x1, blocking collectives, on_device(): gain_sums = lax.psum(jnp.stack([gain1_part, gain2_part]), both)  124 us
    unnamed x100, local copies, waits for them, and re-layouts  87.8 us
    dot_general x8, matrix products, dot_n(): return jnp.dot(left, right, preferred_element_type=f32)  52.8 us
    pallas_call x1, Pallas kernels, attend_back(): pl.pallas_call(functools.partial(attend_back_kernel, tile), grid=(pairs,...  49.2 us
    pallas_call x1, Pallas kernels, attend(): pl.pallas_call(functools.partial(attend_kernel, tile), grid=(pairs, nq),...  42.4 us
  transfers between devices with their start and end apart: 17, of which 11 were waited for; matrix products, arithmetic and copies ran while one was open for 21% of the time, Pallas kernels for 7%

profile of v1, /device:TPU:0, one launch (start us, length us, event | category | flops | bytes accessed | tf_op | source)
XLA Modules:
  0.0 1249.3 jit_solution(11595978792690644778)
XLA Ops:
  11.0 27.3 %all_to_all.25 = bf16[8,3,64,256]{3,2,1,0:T(8,128)(2,1)} all-to-all(bf16[8,3,64,256]{3,2,1,0:T(8,128)(2,1)S(1)} %copy.193), channel_id=1, replica_groups=mesh['blk'=8,'uly'=4] {'blk'}, dimensions={0} | all-to-all | bytes 1572864 | tf_op jit(solution)/shard_map/all_to_all | solution.py:47
  39.2 18.6 %all_gather.31 = bf16[8,2,256]{2,1,0:T(2,128)(2,1)S(1)} all-gather(bf16[1,2,256]{2,1,0:T(2,128)(2,1)S(1)} %pad_maximum_fusion.4), channel_id=1, replica_groups=mesh['blk'=8,'uly'=4] {'blk'}, dimensions={0}, use_global_device_ids=true | all-gather | bytes 9216 | tf_op jit(solution)/shard_map/all_gather | solution.py:39
  72.7 68.9 %all-gather.14.cloned.1.call-done = bf16[1024,2048]{1,0:T(8,128)(2,1)} async-done(((bf16[128,2048]{1,0:T(8,128)(2,1)}), bf16[1024,2048]{1,0:T(8,128)(2,1)}) %all-gather.14.cloned.1.call-update) | async-done | bytes 4194320 | tf_op jit(solution)/shard_map/all_gather | solution.py:39
  158.9 15.0 %all-gather.16.cloned.1.call-done.k_ref = bf16[4,8,128,256]{3,2,1,0:T(8,128)(2,1)} async-done(((bf16[1,8,128,256]{3,2,1,0:T(8,128)(2,1)}), bf16[4,8,128,256]{3,2,1,0:T(8,128)(2,1)}) %all-gather.16.cloned.1.call-update) | async-done | bytes 2097168 | tf_op jit(solution)/shard_map/all_gather | solution.py:39
  174.0 24.6 %all-gather.18.cloned.1.call-done.v_ref = bf16[4,8,128,256]{3,2,1,0:T(8,128)(2,1)} async-done(((bf16[1,8,128,256]{3,2,1,0:T(8,128)(2,1)}), bf16[4,8,128,256]{3,2,1,0:T(8,128)(2,1)}) %all-gather.18.cloned.1.call-update) | async-done | bytes 2097168 | tf_op jit(solution)/shard_map/all_gather | solution.py:39
  201.2 42.4 %attend.1 = (bf16[1024,256]{1,0:T(8,128)(2,1)S(1)}, f32[2,4,2,256]{3,2,1,0:T(2,128)S(1)}) custom-call(s32[4096,1]{1,0:T(8,128)S(1)} %copy.195.segk_ref, s32[4,1,256]{2,1,0:T(1,128)S(1)} %bitcast.172, s32[4,1,256]{2,1,0:T(1,128)S(1)} %broadcast_add_fusion.posq_ref, bf16[1024,256]{1,0:T(8,128)(2,1)S(1)} %copy-done.1, bf16[4,8,128,256]{3,2,1,0:T(8,128)(2,1)S(1)} %copy-done, ...), custom_call_target="tpu_custom_call" | custom-call | tf_op jit(solution)/shard_map/attend/pallas_call | solution.py:111
  255.1 119.8 %all_to_all.26 = bf16[8,3,256,256]{2,3,1,0:T(8,128)(2,1)} all-to-all(bf16[8,3,256,256]{2,3,1,0:T(8,128)(2,1)S(1)} %copy.202), channel_id=1, replica_groups=mesh['blk'=8,'uly'=4] {'blk'}, dimensions={0} | all-to-all | bytes 6291456 | tf_op jit(solution)/shard_map/all_to_all | solution.py:47
  380.3 15.4 %copy.198 = bf16[8,4,64,8,256]{4,3,2,1,0:T(8,128)(2,1)} copy(bf16[8,4,64,8,256]{4,2,0,1,3:T(8,128)(2,1)} %bitcast.190) | data formatting | bytes 16777216 | tf_op jit(solution)/shard_map/transpose | solution.py:323
  395.8 19.7 %copy.233 = bf16[256,8,8,256]{3,1,2,0:T(8,128)(2,1)} copy(bf16[256,8,8,256]{3,2,1,0:T(8,128)(2,1)} %bitcast.176) | data formatting | bytes 16777216
  421.9 14.5 %multiply_reduce_fusion = (f32[1024]{0:T(1024)S(1)}, f32[1024,2048]{1,0:T(8,128)S(1)}) fusion(bf16[1024,2048]{0,1:T(8,128)(2,1)} %bitcast.202, bf16[2048,2048]{1,0:T(8,128)(2,1)} %bitcast.174, bf16[1024,2048]{1,0:T(8,128)(2,1)} %all-gather.14.cloned.1.call-done), kind=kOutput, calls=%fused_computation.13 | convolution fusion | flops 8598322176 | bytes 25169920 | tf_op jit(solution)/shard_map/dot_general | solution.py:27
  442.4 34.0 %all-gather.30.cloned.1.call-done = bf16[32,3,256,256]{3,2,1,0:T(8,128)(2,1)} async-done(((bf16[8,3,256,256]{3,2,1,0:T(8,128)(2,1)}), bf16[32,3,256,256]{3,2,1,0:T(8,128)(2,1)}) %all-gather.30.cloned.1.call-update) | async-done | bytes 12582928 | tf_op jit(solution)/shard_map/all_gather | solution.py:39
  476.4 9.1 fusion.46
  485.5 8.0 copy.204
  499.2 7.9 copy.205
  512.8 7.9 copy.206
  539.3 12.7 %all-gather.20.cloned.1.call-done = bf16[1024,2048]{1,0:T(8,128)(2,1)} async-done(((bf16[128,2048]{1,0:T(8,128)(2,1)}), bf16[1024,2048]{1,0:T(8,128)(2,1)}) %all-gather.20.cloned.1.call-update) | async-done | bytes 4194320 | tf_op jit(solution)/shard_map/all_gather | solution.py:39
  552.0 13.3 %fusion.7 = (bf16[1024,1024]{1,0:T(8,128)(2,1)S(1)}, bf16[1024,1024]{1,0:T(8,128)(2,1)S(1)}, bf16[1024,1024]{1,0:T(8,128)(2,1)}) fusion(f32[1024,1024]{1,0:T(8,128)} %fusion.50, f32[1024,1024]{1,0:T(8,128)} %fusion.51, bf16[2048,1024]{0,1:T(8,128)(2,1)} %bitcast.195, bf16[1024,2048]{1,0:T(8,128)(2,1)} %all-gather.20.cloned.1.call-done), kind=kOutput, calls=%fused_computation.20 | convolution fusion | flops 4310695936 | bytes 23068672 | tf_op jit(solution)/shard_map/dot_general | solution.py:27
  577.4 85.0 %reduce-scatter.9.cloned.1.call-done = bf16[128,2048]{1,0:T(8,128)(2,1)} async-done(((bf16[1024,2048]{1,0:T(8,128)(2,1)}), bf16[128,2048]{1,0:T(8,128)(2,1)}) %reduce-scatter.9.cloned.1.call-update) | async-done | bytes 524304 | tf_op jit(solution)/shard_map/reduce_scatter | solution.py:43
  673.7 32.4 %all_to_all.27 = bf16[8,128,256]{2,1,0:T(8,128)(2,1)S(1)} all-to-all(bf16[8,128,256]{2,1,0:T(8,128)(2,1)S(1)} %bitcast.215), channel_id=1, replica_groups=mesh['blk'=8,'uly'=4] {'blk'}, dimensions={0} | all-to-all | bytes 1048576 | tf_op jit(solution)/shard_map/all_to_all | solution.py:47
  706.1 49.2 %attend_back.1 = (bf16[1024,256]{1,0:T(8,128)(2,1)S(1)}, bf16[4,2,8,128,256]{4,3,2,1,0:T(8,128)(2,1)}) custom-call(s32[4096,1]{1,0:T(8,128)S(1)} %copy.195.segk_ref, s32[4,1,256]{2,1,0:T(1,128)S(1)} %bitcast.173, s32[4,1,256]{2,1,0:T(1,128)S(1)} %broadcast_add_fusion.posq_ref, f32[1024,128]{1,0:T(8,128)S(1)} %get-tuple-element.112.cos_ref, ...), custom_call_target="tpu_custom_call" | custom-call | tf_op jit(solution)/shard_map/attend_back/pallas_call | solution.py:224
  762.1 36.9 %reduce-scatter.11.cloned.1.call-done = bf16[1,2,8,128,256]{4,3,2,1,0:T(8,128)(2,1)} async-done(((bf16[4,2,8,128,256]{4,3,2,1,0:T(8,128)(2,1)}), bf16[1,2,8,128,256]{4,3,2,1,0:T(8,128)(2,1)}) %reduce-scatter.11.cloned.1.call-update) | async-done | bytes 1048592 | tf_op jit(solution)/shard_map/reduce_scatter | solution.py:43
  812.5 7.0 convolution_convert_fusion
  822.9 7.7 copy.216
  830.6 8.4 convolution_convert_fusion.1
  839.0 7.9 stack.69
  858.2 7.9 stack.68
  877.5 7.8 fusion.4
  887.6 9.1 convolution_convert_fusion.3
  902.2 73.8 %reduce-scatter.17.cloned.1.call-done = bf16[1,8,3,256,256]{4,3,2,1,0:T(8,128)(2,1)} async-done(((bf16[4,8,3,256,256]{4,3,2,1,0:T(8,128)(2,1)}), bf16[1,8,3,256,256]{4,3,2,1,0:T(8,128)(2,1)}) %reduce-scatter.17.cloned.1.call-update) | async-done | bytes 3145744 | tf_op jit(solution)/shard_map/reduce_scatter | solution.py:43
  982.6 123.8 %psum.7 = f32[2,2048]{1,0:T(2,128)S(1)} all-reduce(f32[2,2048]{1,0:T(2,128)S(1)} %pad_maximum_fusion.3), channel_id=1, replica_groups=mesh['blk'=8,'uly'=4] {'blk','uly'}, use_global_device_ids=true, to_apply=%region_13.14 | all-reduce | flops 4096 | bytes 32768 | tf_op jit(solution)/shard_map/psum | solution.py:440
  1107.0 15.5 %reduce-scatter.13.cloned.1.call-done = bf16[128,2048]{1,0:T(8,128)(2,1)} async-done(((bf16[1024,2048]{1,0:T(8,128)(2,1)}), bf16[128,2048]{1,0:T(8,128)(2,1)}) %reduce-scatter.13.cloned.1.call-update) | async-done | bytes 524304 | tf_op jit(solution)/shard_map/reduce_scatter | solution.py:43
  1124.0 89.6 %reduce-scatter.7.cloned.1.call-done = bf16[128,2048]{1,0:T(8,128)(2,1)} async-done(((bf16[1024,2048]{1,0:T(8,128)(2,1)}), bf16[128,2048]{1,0:T(8,128)(2,1)}) %reduce-scatter.7.cloned.1.call-update) | async-done | bytes 524304 | tf_op jit(solution)/shard_map/reduce_scatter | solution.py:43
  (208 shorter events, 213.0 us)
Async XLA Ops:
  7.2 58.9 %all-gather.24.cloned.1.call-start = ((), (), s32[]{:S(2)}) async-start(), calls=%async_computation.22 | async-start | bytes 3932160 | tf_op jit(solution)/shard_map/all_gather | solution.py:39
  7.2 31.9 %copy-start.31 = (f32[256]{0:T(256)S(1)}, f32[256]{0:T(256)}, u32[]{:S(2)}) copy-start(f32[256]{0:T(256)} %param.20) | copy-start | bytes 3076
  7.2 31.9 %copy-start.32 = (f32[256]{0:T(256)S(1)}, f32[256]{0:T(256)}, u32[]{:S(2)}) copy-start(f32[256]{0:T(256)} %param.15) | copy-start | bytes 3076
  7.2 50.6 %copy-start.30 = (s32[4096]{0:T(1024)S(1)}, s32[4096]{0:T(1024)}, u32[]{:S(2)}) copy-start(s32[4096]{0:T(1024)} %param.13) | copy-start | bytes 49156
  38.3 103.3 %all-gather.14.cloned.1.call-start = ((), (), s32[]{:S(2)}) async-start(), calls=%async_computation.11 | async-start | bytes 4718592 | tf_op jit(solution)/shard_map/all_gather | solution.py:39
  39.1 134.9 %all-gather.16.cloned.1.call-start = ((), (), s32[]{:S(2)}) async-start(), calls=%async_computation.12 | async-start | bytes 2621440 | tf_op jit(solution)/shard_map/all_gather | solution.py:39
  153.0 45.6 %all-gather.18.cloned.1.call-start = ((), (), s32[]{:S(2)}) async-start(), calls=%async_computation.13 | async-start | bytes 2621440 | tf_op jit(solution)/shard_map/all_gather | solution.py:39
  153.9 226.5 %all-gather.28.cloned.1.call-start = ((), (), s32[]{:S(2)}) async-start(), calls=%async_computation.24 | async-start | bytes 8650752 | tf_op jit(solution)/shard_map/all_gather | solution.py:39
  154.8 260.7 %all-gather.26.cloned.1.call-start = ((), (), s32[]{:S(2)}) async-start(), calls=%async_computation.23 | async-start | bytes 4718592 | tf_op jit(solution)/shard_map/all_gather | solution.py:39
  244.5 232.0 %all-gather.30.cloned.1.call-start = ((), (), s32[]{:S(2)}) async-start(), calls=%async_computation.25 | async-start | bytes 15728640 | tf_op jit(solution)/shard_map/all_gather | solution.py:39
  379.5 172.5 %all-gather.20.cloned.1.call-start = ((), (), s32[]{:S(2)}) async-start(), calls=%async_computation.15 | async-start | bytes 4718592 | tf_op jit(solution)/shard_map/all_gather | solution.py:39
  380.3 282.1 %reduce-scatter.9.cloned.1.call-start = ((), (), s32[]{:S(2)}) async-start(), calls=%async_computation.16 | async-start | bytes 4718592 | tf_op jit(solution)/shard_map/reduce_scatter | solution.py:43
  520.7 6.0 copy-start.15
  520.7 6.0 copy-start.21
  526.7 6.5 copy-start.23
  552.0 13.3 %copy-start.22 = (bf16[128,8,8,256]{3,1,2,0:T(8,128)(2,1)S(1)}, bf16[128,8,8,256]{3,1,2,0:T(8,128)(2,1)}, u32[]{:S(2)}) copy-start(bf16[128,8,8,256]{3,1,2,0:T(8,128)(2,1)} %copy.234) | copy-start | bytes 12582916
  575.9 180.2 %all-gather.22.cloned.1.call-start = ((), (), s32[]{:S(2)}) async-start(), calls=%async_computation.19 | async-start | bytes 4718592 | tf_op jit(solution)/shard_map/all_gather | solution.py:39
  666.9 132.1 %reduce-scatter.11.cloned.1.call-start = ((), (), s32[]{:S(2)}) async-start(), calls=%async_computation.17 | async-start | bytes 5242880 | tf_op jit(solution)/shard_map/reduce_scatter | solution.py:43
  667.1 39.0 %copy-start.2 = (bf16[1024,256]{1,0:T(8,128)(2,1)S(1)}, bf16[1024,256]{1,0:T(8,128)(2,1)}, u32[]{:S(2)}) copy-start(bf16[1024,256]{1,0:T(8,128)(2,1)} %fusion.12.q_ref) | copy-start | bytes 1572868
  667.1 39.0 %copy-start.4 = (bf16[1024,256]{1,0:T(8,128)(2,1)S(1)}, bf16[1024,256]{1,0:T(8,128)(2,1)}, u32[]{:S(2)}) copy-start(bf16[1024,256]{1,0:T(8,128)(2,1)} %copy-done.3) | copy-start | bytes 1572868
  756.1 140.6 %reduce-scatter.15.cloned.1.call-start = ((), (), s32[]{:S(2)}) async-start(), calls=%async_computation.20 | async-start | bytes 5242880 | tf_op jit(solution)/shard_map/reduce_scatter | solution.py:43
  760.6 39.9 %copy-start.10 = (f32[1024,2,128]{2,1,0:T(2,128)S(1)}, f32[1024,2,128]{2,1,0:T(2,128)}, u32[]{:S(2)}) copy-start(f32[1024,2,128]{2,1,0:T(2,128)} %copy-done.9) | copy-start | bytes 3145732
  760.6 39.9 %copy-start.12 = (f32[1024,2,128]{2,1,0:T(2,128)S(1)}, f32[1024,2,128]{2,1,0:T(2,128)}, u32[]{:S(2)}) copy-start(f32[1024,2,128]{2,1,0:T(2,128)} %copy-done.11) | copy-start | bytes 3145732
  760.9 39.9 %copy-start.7 = (bf16[1024,256]{1,0:T(8,128)(2,1)S(1)}, bf16[1024,256]{1,0:T(8,128)(2,1)}, u32[]{:S(2)}) copy-start(bf16[1024,256]{1,0:T(8,128)(2,1)} %copy-done.6) | copy-start | bytes 1572868
  800.8 5.4 copy-start.28
  810.9 165.2 %reduce-scatter.17.cloned.1.call-start = ((), (), s32[]{:S(2)}) async-start(), calls=%async_computation.21 | async-start | bytes 15728640 | tf_op jit(solution)/shard_map/reduce_scatter | solution.py:43
  822.9 7.7 copy-start.36
  846.9 5.1 copy-start.38
  876.5 246.0 %reduce-scatter.13.cloned.1.call-start = ((), (), s32[]{:S(2)}) async-start(), calls=%async_computation.18 | async-start | bytes 4718592 | tf_op jit(solution)/shard_map/reduce_scatter | solution.py:43
  885.3 328.3 %reduce-scatter.7.cloned.1.call-start = ((), (), s32[]{:S(2)}) async-start(), calls=%async_computation.14 | async-start | bytes 4718592 | tf_op jit(solution)/shard_map/reduce_scatter | solution.py:43
  896.8 79.3 %all-to-all-start.3 = ((bf16[8,4,64,256]{3,2,1,0:T(8,128)(2,1)}), bf16[8,4,64,256]{3,2,1,0:T(8,128)(2,1)S(1)}, u32[]{:S(2)}, u32[]{:S(2)}) async-start(bf16[8,4,64,256]{3,2,1,0:T(8,128)(2,1)} %bitcast.219), calls=%async_computation.8 | async-start | bytes 2097152 | tf_op jit(solution)/shard_map/all_to_all | solution.py:47
  977.0 250.4 %all-to-all-start.4 = ((bf16[8,3,256,256]{3,2,1,0:T(8,128)(2,1)}), bf16[8,3,256,256]{3,2,1,0:T(8,128)(2,1)S(1)}, u32[]{:S(2)}, u32[]{:S(2)}) async-start(bf16[8,3,256,256]{3,2,1,0:T(8,128)(2,1)} %bitcast.210), calls=%async_computation.10 | async-start | bytes 6291456 | tf_op jit(solution)/shard_map/all_to_all | solution.py:47
  (24 other events, 62.1 us)
Sparse Core Ops, SparseCore 0:
  38.4 27.5 all-gather.23
  68.2 73.3 all-gather.13
  153.1 20.8 all-gather.15
  176.0 22.5 all-gather.17
  201.9 94.5 all-gather.27
  299.0 94.6 all-gather.25
  395.2 81.1 all-gather.29
  478.6 73.3 all-gather.19
  576.1 86.3 reduce-scatter.8
  667.0 84.3 all-gather.21
  756.2 42.7 reduce-scatter.10
  811.0 44.4 reduce-scatter.14
  876.6 99.4 reduce-scatter.16
  980.0 142.4 reduce-scatter.12
  1126.0 87.6 reduce-scatter.6

commit v2 on v1

v2 whole, which is shorter than its diff:
```python
import functools
import math

import jax
import jax.numpy as jnp
from jax import lax
from jax.experimental import pallas as pl
from jax.experimental.pallas import tpu as pltpu
from jax.sharding import PartitionSpec as P

H = 32
HD = 64
LANES = 128
PAD = 16

theta_base = 130000.0
epsilon = 1e-05
bf = jnp.bfloat16
f32 = jnp.float32
NEG = -1e30


def dot_t(left, right):
    return lax.dot_general(left, right, (((1,), (1,)), ((), ())), preferred_element_type=f32)


def dot_n(left, right):
    return jnp.dot(left, right, preferred_element_type=f32)


def dot_c(left, right):
    return lax.dot_general(left, right, (((0,), (0,)), ((), ())), preferred_element_type=f32)


def rms_scale(value):
    return lax.rsqrt(jnp.mean(value * value, axis=-1, keepdims=True) + epsilon)


def params(mib=56):
    return pltpu.CompilerParams(vmem_limit_bytes=mib * 2**20)


def cost(micros):
    return pl.CostEstimate(flops=int(micros * 0.25 * 1.1e9), bytes_accessed=0, transcendentals=0)


def full(shape):
    return pl.BlockSpec(shape, lambda *grid: (0,) * len(shape))


def after(value, *others):
    return lax.optimization_barrier((value, *others))[0]


def hop(value, axis, slow, fast):
    size = lax.axis_size(axis)
    ring = size // 2
    pairs = [(i, ((i // 2 + slow) % ring) * 2 + (i % 2 ^ fast)) for i in range(size)]
    return lax.ppermute(value, axis, pairs)


def near(axis, slow, fast):
    ring = lax.axis_size(axis) // 2
    i = lax.axis_index(axis)
    return ((i // 2 + slow + ring) % ring) * 2 + (i % 2 ^ fast)


def place(out, piece, at):
    return lax.dynamic_update_slice_in_dim(out, piece[None], at, 0)


def pick(parts, at):
    return lax.dynamic_index_in_dim(parts, at, 0, False)


def together(*plans):
    results = [None] * len(plans)
    sent = {i: None for i in range(len(plans))}
    while sent:
        waiting = {}
        for i, value in sent.items():
            try:
                waiting[i] = list(plans[i].send(value))
            except StopIteration as end:
                results[i] = end.value
        flat = [v for values in waiting.values() for v in values]
        if flat:
            flat = list(lax.optimization_barrier(tuple(flat)))
        sent = {}
        for i, values in waiting.items():
            sent[i] = [flat.pop(0) for _ in values]
    return results


def chain(first, *rest):
    value = yield from first
    for plan in rest:
        value = yield from plan(value)
    return value


def gather_plan(value, axis):
    size = lax.axis_size(axis)
    ring = size // 2
    out = jnp.zeros((size, *value.shape), value.dtype)
    fresh = {0: value}
    crossed = {}
    for s in range(1, ring // 2 + 2):
        for at, piece in fresh.items():
            out = place(out, piece, near(axis, at, 0))
            crossed[at] = hop(piece, axis, 0, 1)
        arriving = {}
        if s <= ring // 2:
            arriving[-s] = hop(fresh[1 - s], axis, 1, 0)
        if s <= (ring - 1) // 2:
            arriving[s] = hop(fresh[s - 1], axis, -1, 0)
        if arriving:
            fresh = dict(zip(arriving, (yield list(arriving.values()))))
    landed = dict(zip(crossed, (yield list(crossed.values()))))
    for at, piece in landed.items():
        out = place(out, piece, near(axis, at, 1))
    return out


def scatter_plan(parts, axis):
    ring = lax.axis_size(axis) // 2
    far, back = ring // 2, (ring - 1) // 2
    order = []
    for s in range(far, 0, -1):
        order.append((s, 1))
        if s <= back:
            order.append((s, -1))
    crossing = {
        s * way: hop(pick(parts, near(axis, s * way, 1)), axis, 0, 1) for s, way in order
    }
    crossing[0] = hop(pick(parts, near(axis, 0, 1)), axis, 0, 1)
    carried = {1: None, -1: None}
    for s, way in order:
        wait = [crossing[s * way]] + ([] if carried[way] is None else [carried[way]])
        total = pick(parts, near(axis, s * way, 0)).astype(f32)
        for piece in (yield wait):
            total = total + piece.astype(f32)
        carried[way] = hop(total.astype(bf), axis, way, 0)
    total = pick(parts, near(axis, 0, 0)).astype(f32)
    for piece in (yield [crossing[0]] + [v for v in carried.values() if v is not None]):
        total = total + piece.astype(f32)
    return total


def swap_plan(parts, axis):
    ring = lax.axis_size(axis) // 2
    fast = lax.axis_index(axis) % 2
    slow = lax.axis_index(axis) // 2
    columns = jnp.swapaxes(parts.reshape(ring, 2, *parts.shape[1:]), 0, 1)
    kept = pick(columns, fast)
    (given,) = yield [hop(pick(columns, 1 - fast), axis, 0, 1)]
    pairs = jnp.stack([jnp.where(fast == 0, kept, given), jnp.where(fast == 0, given, kept)], 1)
    out = place(jnp.zeros_like(pairs), pick(pairs, slow), slow)
    arrived = yield [hop(pick(pairs, (slow + s) % ring), axis, s, 0) for s in range(1, ring)]
    for s, piece in enumerate(arrived, 1):
        out = place(out, piece, (slow - s + ring) % ring)
    return out.reshape(parts.shape)


def exchange(part, axis):
    got, places = [], []
    for slow in range(lax.axis_size(axis) // 2):
        for fast in range(2):
            piece = part(near(axis, slow, fast))
            got.append(hop(piece, axis, slow, fast) if slow or fast else piece)
            places.append(near(axis, -slow, fast))
    return got, places


def gather_near_plan(value, axis, spare=0):
    ring = lax.axis_size(axis) // 2
    crossed = [hop(value, axis, 0, 1)]
    got = [hop(value, axis, s, 0) for s in range(1, ring)]
    for _ in range(spare):
        yield []
    got = yield got
    crossed += [hop(piece, axis, 0, 1) for piece in got]
    crossed = yield crossed
    return [value, *got, *crossed]


def scatter_near_plan(parts, axis):
    ring = lax.axis_size(axis) // 2
    crossed = yield [hop(part, axis, 0, 1) for part in parts[ring:]]
    sums = [mine.astype(f32) + piece.astype(f32) for mine, piece in zip(parts, crossed)]
    total = sums[0]
    for piece in (yield [hop(sums[s].astype(bf), axis, -s, 0) for s in range(1, ring)]):
        total = total + piece.astype(f32)
    return total.astype(bf)


def gather(value, axis):
    return lax.all_gather(value, axis, axis=0, tiled=True)


def scatter(value, axis):
    return lax.psum_scatter(value, axis, scatter_dimension=0, tiled=True)


def turned(value):
    width = value.shape[1]
    lane = lax.broadcasted_iota(jnp.int32, value.shape, 1)
    return jnp.where(
        lane % HD < HD // 2,
        pltpu.roll(value, width - HD // 2, 1),
        pltpu.roll(value, HD // 2, 1),
    )


def wide(table, width):
    return jnp.concatenate([table] * (width // LANES), axis=1)


def weight_block(w_ref, block, part, piece):
    w = w_ref[:, block, part * piece : (part + 1) * piece, :]
    return w.reshape(w.shape[0] * piece, w.shape[2])


def project_kernel(piece, x_ref, w_ref, cos_ref, sin_ref, q_ref, kv_ref, normed_ref):
    blocks, width = w_ref.shape[1], w_ref.shape[3]
    x = x_ref[...].astype(f32)
    r1 = rms_scale(x)
    total = [0.0, 0.0, 0.0]
    for block in range(blocks):
        at = slice(block * width, (block + 1) * width)
        gain = w_ref[0, block, 3 * piece : 3 * piece + PAD, :][0:1].astype(f32)
        normed = (x[:, at] * r1 * gain).astype(bf)
        normed_ref[:, at] = normed
        for part in range(3):
            total[part] = total[part] + dot_t(normed, weight_block(w_ref, block, part, piece))
    feats = total[0].shape[1]
    cosine, sine = wide(cos_ref[...], feats), wide(sin_ref[...], feats)

    def rotate(value):
        value = value.astype(bf).astype(f32)
        return (value * cosine + turned(value) * sine).astype(bf)

    q_ref[...] = rotate(total[0])
    kv_ref[0] = rotate(total[1])
    kv_ref[1] = total[2].astype(bf)


def project(x_all, w, cosine, sine, piece, rows):
    count, dim = x_all.shape
    feats = w.shape[0] * piece
    tiled = lambda n: pl.BlockSpec((rows, n), lambda i: (i, 0))
    return pl.pallas_call(
        functools.partial(project_kernel, piece),
        grid=(count // rows,),
        in_specs=[tiled(dim), full(w.shape), tiled(LANES), tiled(LANES)],
        out_specs=[
            tiled(feats),
            pl.BlockSpec((2, rows, feats), lambda i: (0, i, 0)),
            tiled(dim),
        ],
        out_shape=[
            jax.ShapeDtypeStruct((count, feats), bf),
            jax.ShapeDtypeStruct((2, count, feats), bf),
            jax.ShapeDtypeStruct((count, dim), bf),
        ],
        compiler_params=params(),
        cost_estimate=cost(count * 0.009),
        name="project",
    )(x_all, w, cosine, sine)


def flip_kernel(piece, q_ref, k_ref, v_ref, o_ref, ga_ref, gm_ref, sent_ref, out_ref):
    size = sent_ref.shape[0]
    for i, ref in enumerate((q_ref, k_ref, v_ref)):
        sent_ref[:, i * piece : (i + 1) * piece, :] = (
            ref[...].T.astype(bf).reshape(size, piece, ref.shape[0])
        )
    row = lax.broadcasted_iota(jnp.int32, (PAD, q_ref.shape[0]), 0)
    gains = jnp.where(row == 0, ga_ref[...], gm_ref[...]).astype(bf)
    for j in range(size):
        sent_ref[j, 3 * piece :, :] = gains
    out_ref[...] = o_ref[...].T.astype(bf)


def flip(w_query, w_key, w_value, w_output, attn_gain, mlp_gain, size):
    rows, feats = w_query.shape
    piece = feats // size
    return pl.pallas_call(
        functools.partial(flip_kernel, piece),
        out_shape=[
            jax.ShapeDtypeStruct((size, 3 * piece + PAD, rows), bf),
            jax.ShapeDtypeStruct((feats, rows), bf),
        ],
        compiler_params=params(),
        cost_estimate=cost(5),
        name="flip",
    )(w_query, w_key, w_value, w_output, attn_gain[None], mlp_gain[None])


def allowed_block(segk_ref, seg_q, pos_q, chunk, width):
    seg_k = segk_ref[pl.ds(pl.multiple_of(chunk * width, width), width), :]
    pos_k = chunk * width + lax.broadcasted_iota(jnp.int32, (width, 1), 0)
    return (seg_k == seg_q) & (pos_k <= pos_q)


def head_lanes(rows, head):
    lane = lax.broadcasted_iota(jnp.int32, (rows, LANES), 1)
    return (lane < HD) if head == 0 else (lane >= HD)


def attend_kernel(tile, segk_ref, segq_ref, posq_ref, q_ref, kv_ref, o_ref, lse_ref, vt_ref):
    nu, _, nb, tok, _ = kv_ref.shape
    width = nu * tok
    rows = tile * tok
    j = pl.program_id(1)

    @pl.when(j == 0)
    def _():
        for c in range(nb):
            vt_ref[c] = kv_ref[:, 1, c].reshape(width, LANES).T

    seg_q, pos_q = segq_ref[0], posq_ref[0]
    q = q_ref[...] * jnp.asarray(1.0 / math.sqrt(HD), bf)
    q_heads = [jnp.where(head_lanes(rows, h), q, jnp.zeros_like(q)) for h in range(2)]

    def step(chunk, state):
        k = kv_ref[:, 0, chunk].reshape(width, LANES)
        v_t = vt_ref[chunk]
        ok = allowed_block(segk_ref, seg_q, pos_q, chunk, width)
        new = []
        for h in range(2):
            best, total, acc = state[h]
            s = jnp.where(ok, dot_t(k, q_heads[h]), NEG)
            best_new = jnp.maximum(best, jnp.max(s, axis=0, keepdims=True))
            p = jnp.exp(s - best_new)
            factor = jnp.exp(best - best_new)
            total = total * factor + jnp.sum(p, axis=0, keepdims=True)
            acc = acc * factor + dot_n(v_t[h * HD : (h + 1) * HD], p.astype(bf))
            new.append((best_new, total, acc))
        return tuple(new)

    start = (
        jnp.full((1, rows), NEG, f32),
        jnp.zeros((1, rows), f32),
        jnp.zeros((HD, rows), f32),
    )
    state = lax.fori_loop(0, (j + 1) * tile, step, (start, start))
    o_t = jnp.concatenate([acc / total for _, total, acc in state], axis=0)
    o_ref[...] = o_t.T.astype(bf)
    lse_ref[0, 0] = jnp.concatenate([best + jnp.log(total) for best, total, _ in state], axis=0)


def attend(segments, seg_q, pos_q, q, kv, tile):
    nu, _, nb, tok, feats = kv.shape
    rows = tile * tok
    nq = nb // tile
    pairs = feats // LANES
    row_spec = pl.BlockSpec((1, 1, rows), lambda p, j: (j, 0, 0))
    q_spec = pl.BlockSpec((rows, LANES), lambda p, j: (j, p))
    return pl.pallas_call(
        functools.partial(attend_kernel, tile),
        grid=(pairs, nq),
        in_specs=[
            full(segments.shape),
            row_spec,
            row_spec,
            q_spec,
            pl.BlockSpec((nu, 2, nb, tok, LANES), lambda p, j: (0, 0, 0, 0, p)),
        ],
        out_specs=[q_spec, pl.BlockSpec((1, 1, 2, rows), lambda p, j: (p, j, 0, 0))],
        out_shape=[
            jax.ShapeDtypeStruct((nb * tok, feats), bf),
            jax.ShapeDtypeStruct((pairs, nq, 2, rows), f32),
        ],
        scratch_shapes=[pltpu.VMEM((nb, LANES, nu * tok), bf)],
        compiler_params=params(),
        cost_estimate=cost(44 * nb * tok * nb / 8192),
        name="attend",
    )(segments, seg_q, pos_q, q, kv)


def attend_back_kernel(
    tile,
    segk_ref,
    segq_ref,
    posq_ref,
    cos_ref,
    sin_ref,
    q_ref,
    do_ref,
    o_ref,
    lse_ref,
    kv_ref,
    dq_ref,
    dkv_ref,
    acc_ref,
    delta_ref,
):
    nu, _, _, tok, _ = kv_ref.shape
    nq = segq_ref.shape[0]
    width = nu * tok
    rows = tile * tok
    chunk = pl.program_id(1)
    scale = jnp.asarray(1.0 / math.sqrt(HD), bf)

    @pl.when(chunk == 0)
    def _():
        acc_ref[...] = jnp.zeros_like(acc_ref)
        lane = lax.broadcasted_iota(jnp.int32, (8, LANES), 1)
        row = lax.broadcasted_iota(jnp.int32, (8, LANES), 0)
        mine = jnp.where(lane // HD == row, 1.0, 0.0).astype(f32)
        for j in range(nq):
            part = do_ref[pl.ds(j * rows, rows), :].astype(f32) * o_ref[
                pl.ds(j * rows, rows), :
            ].astype(f32)
            delta_ref[j] = lax.dot_general(
                mine,
                part,
                (((1,), (1,)), ((), ())),
                preferred_element_type=f32,
                precision=lax.Precision.HIGHEST,
            )

    k = kv_ref[:, 0, 0].reshape(width, LANES)
    v = kv_ref[:, 1, 0].reshape(width, LANES)

    def step(j, state):
        dk, dv = state
        at = pl.ds(pl.multiple_of(j * rows, rows), rows)
        q = q_ref[at, :] * scale
        do = do_ref[at, :]
        ok = allowed_block(segk_ref, segq_ref[j], posq_ref[j], chunk, width)
        parts = []
        for h in range(2):
            mine = head_lanes(rows, h)
            q_h = jnp.where(mine, q, jnp.zeros_like(q))
            do_h = jnp.where(mine, do, jnp.zeros_like(do))
            p = jnp.exp(jnp.where(ok, dot_t(k, q_h) - lse_ref[0, j, h : h + 1], NEG))
            ds = (p * (dot_t(v, do_h) - delta_ref[j, h : h + 1])).astype(bf)
            dv = dv + dot_n(p.astype(bf), do_h)
            dk = dk + dot_n(ds, q_h)
            parts.append(dot_c(ds, k))
        acc_ref[at, :] = acc_ref[at, :] + jnp.where(head_lanes(rows, 0), parts[0], parts[1])
        return dk, dv

    zero = jnp.zeros((width, LANES), f32)
    dk, dv = lax.fori_loop(chunk // tile, nq, step, (zero, zero))
    dkv_ref[:, 0, 0] = dk.astype(bf).reshape(nu, tok, LANES)
    dkv_ref[:, 1, 0] = dv.astype(bf).reshape(nu, tok, LANES)

    @pl.when(chunk == pl.num_programs(1) - 1)
    def _():
        dq = acc_ref[...] * (1.0 / math.sqrt(HD))
        dq_ref[...] = (dq * cos_ref[...] - turned(dq) * sin_ref[...]).astype(bf)


def attend_back(segments, seg_q, pos_q, cosine, sine, q, do, o, lse, kv, tile):
    nu, _, nb, tok, feats = kv.shape
    rows = tile * tok
    nq = nb // tile
    pairs = feats // LANES
    whole_rows = full((nq, 1, rows))
    table = full((nb * tok, LANES))
    q_spec = pl.BlockSpec((nb * tok, LANES), lambda p, c: (0, p))
    kv_spec = pl.BlockSpec((nu, 2, 1, tok, LANES), lambda p, c: (0, 0, c, 0, p))
    return pl.pallas_call(
        functools.partial(attend_back_kernel, tile),
        grid=(pairs, nb),
        in_specs=[
            full(segments.shape),
            whole_rows,
            whole_rows,
            table,
            table,
            q_spec,
            q_spec,
            q_spec,
            pl.BlockSpec((1, nq, 2, rows), lambda p, c: (p, 0, 0, 0)),
            kv_spec,
        ],
        out_specs=[q_spec, kv_spec],
        out_shape=[
            jax.ShapeDtypeStruct((nb * tok, feats), bf),
            jax.ShapeDtypeStruct((nu, 2, nb, tok, feats), bf),
        ],
        scratch_shapes=[pltpu.VMEM((nb * tok, LANES), f32), pltpu.VMEM((nq, 8, rows), f32)],
        compiler_params=params(),
        cost_estimate=cost(50 * nb * tok * nb / 8192),
        name="attend_back",
    )(segments, seg_q, pos_q, cosine, sine, q, do, o, lse, kv)


def output_kernel(x_ref, o_ref, w_ref, gain_ref, x1_ref, normed_ref):
    blocks, pieces, groups, piece, width = w_ref.shape
    square = 0.0
    for block in range(blocks):
        at = slice(block * width, (block + 1) * width)
        total = x_ref[:, at].astype(f32)
        for g in range(groups):
            total = total + dot_n(o_ref[g], w_ref[block, :, g].reshape(pieces * piece, width))
        x1_ref[:, at] = total
        square = square + jnp.sum(total * total, axis=1, keepdims=True)
    r2 = lax.rsqrt(square * (1.0 / (blocks * width)) + epsilon)
    normed_ref[...] = (x1_ref[...] * r2 * gain_ref[...]).astype(bf)


def output_project(x_all, o_all, w_out, gain, rows):
    count, dim = x_all.shape
    groups, _, feats = o_all.shape
    tiled = pl.BlockSpec((rows, dim), lambda i: (i, 0))
    return pl.pallas_call(
        output_kernel,
        grid=(count // rows,),
        in_specs=[
            tiled,
            pl.BlockSpec((groups, rows, feats), lambda i: (0, i, 0)),
            full(w_out.shape),
            full(gain.shape),
        ],
        out_specs=[tiled, tiled],
        out_shape=[
            jax.ShapeDtypeStruct((count, dim), f32),
            jax.ShapeDtypeStruct((count, dim), bf),
        ],
        compiler_params=params(),
        cost_estimate=cost(count * 0.015),
        name="output_project",
    )(x_all, o_all, w_out, gain)


def output_back_kernel(d_ref, w_ref, out_ref):
    blocks, pieces, _, piece, width = w_ref.shape
    total = 0.0
    for block in range(blocks):
        at = slice(block * width, (block + 1) * width)
        total = total + dot_t(d_ref[:, at], w_ref[block, :, 0].reshape(pieces * piece, width))
    out_ref[0] = total.astype(bf)


def output_back(d_attn, w_out):
    tok, dim = d_attn.shape
    blocks, pieces, groups, piece, width = w_out.shape
    return pl.pallas_call(
        output_back_kernel,
        grid=(groups,),
        in_specs=[
            full(d_attn.shape),
            pl.BlockSpec((blocks, pieces, 1, piece, width), lambda g: (0, 0, g, 0, 0)),
        ],
        out_specs=pl.BlockSpec((1, tok, pieces * piece), lambda g: (g, 0, 0)),
        out_shape=jax.ShapeDtypeStruct((groups, tok, pieces * piece), bf),
        compiler_params=params(),
        cost_estimate=cost(8),
        name="output_back",
    )(d_attn, w_out)


def project_back_kernel(
    piece, x_ref, w_ref, cos_ref, sin_ref, dq_ref, dkv_ref, dk_ref, dn_ref, gain_ref
):
    blocks, width = w_ref.shape[1], w_ref.shape[3]
    feats = dq_ref.shape[1]
    cosine, sine = wide(cos_ref[...], feats), wide(sin_ref[...], feats)
    dk = dkv_ref[0].astype(f32)
    dk = (dk * cosine - turned(dk) * sine).astype(bf)
    dk_ref[...] = dk
    x = x_ref[...].astype(f32)
    r1 = rms_scale(x)
    parts = (dq_ref[...], dk, dkv_ref[1])

    @pl.when(pl.program_id(0) == 0)
    def _():
        gain_ref[...] = jnp.zeros_like(gain_ref)

    for block in range(blocks):
        at = slice(block * width, (block + 1) * width)
        total = 0.0
        for part in range(3):
            total = total + dot_n(parts[part], weight_block(w_ref, block, part, piece))
        dn_ref[:, at] = total.astype(bf)
        gain_ref[:, at] = gain_ref[:, at] + jnp.sum(total * (x[:, at] * r1), axis=0, keepdims=True)


def project_back(x_all, w, cosine, sine, dq, dkv, piece, rows):
    count, dim = x_all.shape
    feats = dq.shape[1]
    tiled = lambda n: pl.BlockSpec((rows, n), lambda i: (i, 0))
    return pl.pallas_call(
        functools.partial(project_back_kernel, piece),
        grid=(count // rows,),
        in_specs=[
            tiled(dim),
            full(w.shape),
            tiled(LANES),
            tiled(LANES),
            tiled(feats),
            pl.BlockSpec((2, rows, feats), lambda i: (0, i, 0)),
        ],
        out_specs=[tiled(feats), tiled(dim), full((1, dim))],
        out_shape=[
            jax.ShapeDtypeStruct((count, feats), bf),
            jax.ShapeDtypeStruct((count, dim), bf),
            jax.ShapeDtypeStruct((1, dim), f32),
        ],
        compiler_params=params(),
        cost_estimate=cost(count * 0.01),
        name="project_back",
    )(x_all, w, cosine, sine, dq, dkv)


def projection_grads_kernel(pieces, n, *refs):
    lefts, (right_ref, gain_ref, out_ref, turned_ref) = refs[:n], refs[n:]

    @pl.when(pl.program_id(0) == 0)
    def _():
        for i in range(n):
            turned_ref[i] = lefts[i][...].T

    feats = turned_ref.shape[1]
    piece = feats // pieces
    right = right_ref[...]
    width = right.shape[1]
    for i in range(n):
        grad = dot_n(turned_ref[i], right).astype(bf)
        out_ref[:, 0, i * piece : (i + 1) * piece, :] = grad.reshape(pieces, piece, width)
    gain = gain_ref[...].astype(bf)
    for u in range(pieces):
        out_ref[u, 0, n * piece :, :] = gain


def projection_grads(lefts, right, gain, pieces, width):
    n = len(lefts)
    count, feats = lefts[0].shape
    dim = right.shape[1]
    rows = n * (feats // pieces) + PAD
    return pl.pallas_call(
        functools.partial(projection_grads_kernel, pieces, n),
        grid=(dim // width,),
        in_specs=[full((count, feats))] * n
        + [
            pl.BlockSpec((count, width), lambda i: (0, i)),
            pl.BlockSpec((PAD, width), lambda i: (0, i)),
        ],
        out_specs=pl.BlockSpec((pieces, 1, rows, width), lambda i: (0, i, 0, 0)),
        out_shape=jax.ShapeDtypeStruct((pieces, dim // width, rows, width), bf),
        scratch_shapes=[pltpu.VMEM((n, feats, count), bf)],
        compiler_params=params(),
        cost_estimate=cost(2.5 * n),
        name="projection_grads",
    )(*lefts, right, gain)


def output_grads_kernel(o_ref, d_ref, out_ref):
    pieces, _, piece, width = out_ref.shape
    grad = dot_n(o_ref[0].T, d_ref[...])
    out_ref[:, 0] = grad.astype(bf).reshape(pieces, piece, width)


def output_grads(o_all, d_columns, pieces):
    groups, count, feats = o_all.shape
    width = d_columns.shape[1]
    shape = (pieces, groups, feats // pieces, width)
    return pl.pallas_call(
        output_grads_kernel,
        grid=(groups,),
        in_specs=[
            pl.BlockSpec((1, count, feats), lambda g: (g, 0, 0)),
            full(d_columns.shape),
        ],
        out_specs=pl.BlockSpec((pieces, 1, *shape[2:]), lambda g: (0, g, 0, 0)),
        out_shape=jax.ShapeDtypeStruct(shape, bf),
        compiler_params=params(),
        cost_estimate=cost(6),
        name="output_grads",
    )(o_all, d_columns)


def prepare_kernel(wg_ref, wu_ref, wd_ref, out_ref):
    for i, ref in enumerate((wg_ref, wu_ref, wd_ref)):
        out_ref[0, i] = ref[...].astype(bf)


def prepare(w_gate, w_up, w_down, size):
    rows, columns = w_gate.shape
    width = columns // size
    if width % LANES:
        stacked = jnp.stack([w.astype(bf) for w in (w_gate, w_up, w_down)])
        return jnp.transpose(stacked.reshape(3, rows, size, width), (2, 0, 1, 3))
    spec = pl.BlockSpec((rows, width), lambda i: (0, i))
    return pl.pallas_call(
        prepare_kernel,
        grid=(size,),
        in_specs=[spec] * 3,
        out_specs=pl.BlockSpec((1, 3, rows, width), lambda i: (i, 0, 0, 0)),
        out_shape=jax.ShapeDtypeStruct((size, 3, rows, width), bf),
        compiler_params=params(),
        cost_estimate=cost(4),
        name="prepare",
    )(w_gate, w_up, w_down)


def assemble_kernel(n, at_ref, *refs):
    rows = refs[0].shape[1]
    for k in range(n):
        at = pl.ds(pl.multiple_of(at_ref[k] * rows, rows), rows)
        refs[n][:, at, :] = refs[k][...]


def assemble(parts, places):
    n = len(parts)
    _, rows, width = parts[0].shape
    return pl.pallas_call(
        functools.partial(assemble_kernel, n),
        grid_spec=pltpu.PrefetchScalarGridSpec(
            num_scalar_prefetch=1,
            grid=(1,),
            in_specs=[full(parts[0].shape)] * n,
            out_specs=full((3, n * rows, width)),
        ),
        out_shape=jax.ShapeDtypeStruct((3, n * rows, width), bf),
        compiler_params=params(),
        cost_estimate=cost(4),
        name="assemble",
    )(jnp.stack(places).astype(jnp.int32), *parts)


def finish_kernel(n, at_ref, *refs):
    width = refs[0].shape[2]
    for k in range(n):
        at = pl.ds(pl.multiple_of(at_ref[k] * width, width), width)
        for i in range(3):
            refs[n + i][:, at] = refs[k][i].astype(f32)


def finish(parts, places):
    n = len(parts)
    _, rows, width = parts[0].shape
    if width % LANES:
        out = jnp.zeros((n, *parts[0].shape), bf)
        for part, at in zip(parts, places):
            out = place(out, part, at)
        out = jnp.transpose(out, (1, 2, 0, 3)).reshape(3, rows, n * width).astype(f32)
        return [out[i] for i in range(3)]
    return pl.pallas_call(
        functools.partial(finish_kernel, n),
        grid_spec=pltpu.PrefetchScalarGridSpec(
            num_scalar_prefetch=1,
            grid=(1,),
            in_specs=[full(parts[0].shape)] * n,
            out_specs=[full((rows, n * width))] * 3,
        ),
        out_shape=[jax.ShapeDtypeStruct((rows, n * width), f32)] * 3,
        compiler_params=params(),
        cost_estimate=cost(5),
        name="finish",
    )(jnp.stack(places).astype(jnp.int32), *parts)


def hidden_kernel(n, *refs):
    n_ref, g_ref = refs[:2]
    act_ref, dg_ref, du_ref = refs[2 + n :]
    normed, cot = n_ref[...], g_ref[...]
    for i in range(n):
        w_ref = refs[2 + i]
        gate = dot_n(normed, w_ref[0])
        up = dot_n(normed, w_ref[1])
        d_act = dot_n(cot, w_ref[2])
        sigma = jax.nn.sigmoid(gate)
        silu = gate * sigma
        act_ref[i] = (silu * up).astype(bf)
        du_ref[i] = (d_act * silu).astype(bf)
        dg_ref[i] = (d_act * up * (sigma * (1.0 + gate * (1.0 - sigma)))).astype(bf)


def hidden(normed, cot, weights, rows):
    count, dim = normed.shape
    n = len(weights)
    width = weights[0].shape[2]
    tiled = pl.BlockSpec((rows, dim), lambda i: (i, 0))
    out = pl.BlockSpec((n, rows, width), lambda i: (0, i, 0))
    return pl.pallas_call(
        functools.partial(hidden_kernel, n),
        grid=(count // rows,),
        in_specs=[tiled, tiled] + [full(w.shape) for w in weights],
        out_specs=[out] * 3,
        out_shape=[jax.ShapeDtypeStruct((n, count, width), bf)] * 3,
        compiler_params=params(),
        cost_estimate=cost(20),
        name="hidden",
    )(normed, cot, *weights)


def mix_kernel(which, n, *refs):
    lefts, weights, out_ref = refs[: len(which)], refs[len(which) : -1], refs[-1]
    total = 0.0
    for k in range(len(which)):
        for i in range(n):
            total = total + dot_t(lefts[k][i], weights[i][k])
    out_ref[...] = total.astype(bf)


def mix(lefts, weights, which, rows):
    n, count, width = lefts[0].shape
    dim = weights[0].shape[1]
    chosen = pl.BlockSpec((len(which), dim, width), lambda i: (which[0] // len(which), 0, 0))
    return pl.pallas_call(
        functools.partial(mix_kernel, which, n),
        grid=(count // rows,),
        in_specs=[pl.BlockSpec((n, rows, width), lambda i: (0, i, 0))] * len(which)
        + [chosen] * n,
        out_specs=pl.BlockSpec((rows, dim), lambda i: (i, 0)),
        out_shape=jax.ShapeDtypeStruct((count, dim), bf),
        compiler_params=params(),
        cost_estimate=cost(8 * len(which)),
        name="mix",
    )(*lefts, *weights)


def hidden_grads_kernel(n_ref, g_ref, dg_ref, du_ref, act_ref, *outs):
    normed, cot = n_ref[...].T, g_ref[...].T
    for i, out_ref in enumerate(outs):
        out_ref[0] = dot_n(normed, dg_ref[i]).astype(bf)
        out_ref[1] = dot_n(normed, du_ref[i]).astype(bf)
        out_ref[2] = dot_n(cot, act_ref[i]).astype(bf)


def hidden_grads(normed, cot, d_gate, d_up, act, block):
    count, dim = normed.shape
    n, _, width = act.shape
    columns = pl.BlockSpec((count, block), lambda i: (0, i))
    return pl.pallas_call(
        hidden_grads_kernel,
        grid=(dim // block,),
        in_specs=[columns, columns] + [full(act.shape)] * 3,
        out_specs=[pl.BlockSpec((3, block, width), lambda i: (0, i, 0))] * n,
        out_shape=[jax.ShapeDtypeStruct((3, dim, width), bf)] * n,
        compiler_params=params(),
        cost_estimate=cost(25),
        name="hidden_grads",
    )(normed, cot, d_gate, d_up, act)


def on_device(
    tokens,
    segments,
    cotangent,
    attn_gain,
    w_query,
    w_key,
    w_value,
    w_output,
    mlp_gain,
    w_gate,
    w_up,
    w_down,
):
    nb, nu = lax.axis_size("blk"), lax.axis_size("uly")
    b, u = lax.axis_index("blk"), lax.axis_index("uly")
    tok, dim = tokens.shape
    seq = segments.shape[0]
    rows, feats_u = w_query.shape
    group = feats_u * nu // nb
    strided = (feats_u // HD) % nb == 0 and rows % LANES == 0
    count = nb * tok
    tile = 2
    both = ("blk", "uly")
    block = rows if strided else 2 * LANES
    blocks = dim // block
    pieces = nu if strided else 1
    piece = group // nu if strided else -(-group // LANES) * LANES
    feats = pieces * piece
    step = 2 * tok

    seg_mine = pick(jnp.swapaxes(segments.reshape(nb, nu, tok), 0, 1), u).reshape(count)
    index = (
        jnp.arange(nb, dtype=jnp.int32)[:, None] * (nu * tok)
        + u * tok
        + jnp.arange(tok, dtype=jnp.int32)[None, :]
    ).reshape(count)
    first = jnp.sum((segments[None, :] < seg_mine[:, None]).astype(jnp.int32), axis=1)
    lane = jnp.arange(LANES, dtype=jnp.int32)
    freq = theta_base ** (-((lane % (HD // 2)).astype(f32) * 2.0) / HD)
    angles = (index - first).astype(f32)[:, None] * freq[None, :]
    cosine = jnp.cos(angles)
    sine = jnp.sin(angles) * jnp.where(lane % HD < HD // 2, -1.0, 1.0)[None, :]
    seg_col = segments[:, None]
    seg_rows = seg_mine.reshape(nb // tile, 1, tile * tok)
    pos_rows = index.reshape(nb // tile, 1, tile * tok)

    ff_u = w_gate.shape[1]
    ff_piece = ff_u // nb
    tokens_plan = gather_plan(tokens, "blk")

    def prepared():
        (value,) = yield [prepare(w_gate, w_up, w_down, nb)]
        return value

    if strided:
        sent, out_flipped = flip(w_query, w_key, w_value, w_output, attn_gain, mlp_gain, nb)
        x_all, ff_sent, w_qkv = together(
            tokens_plan,
            prepared(),
            chain(swap_plan(sent, "blk"), lambda got: gather_plan(got, "uly")),
        )
    else:
        gains = jnp.stack([attn_gain, mlp_gain]).astype(bf)
        flipped = [jnp.transpose(w.astype(bf)) for w in (w_query, w_key, w_value, w_output)]
        out_flipped = flipped[3]
        sent = gather(jnp.stack(flipped[:3])[None], "uly")
        sent = jnp.transpose(sent, (0, 2, 1, 3)).reshape(nb, group, 3, rows)
        x_all, ff_sent, got = together(tokens_plan, prepared(), swap_plan(sent, "blk"))
        got = jnp.transpose(got, (2, 1, 0, 3)).reshape(3, group, dim)
        got = jnp.pad(got, ((0, 0), (0, piece - group), (0, 0))).reshape(3 * piece, dim)
        all_gains = jnp.transpose(gather(gains[None], "blk"), (1, 0, 2)).reshape(2, dim)
        got = jnp.concatenate([got, jnp.pad(all_gains, ((0, PAD - 2), (0, 0)))])
        w_qkv = jnp.transpose(got.reshape(3 * piece + PAD, blocks, block), (1, 0, 2))[None]
    x_all = x_all.reshape(count, dim)
    gain1, gain2 = [
        w_qkv[0, :, 3 * piece + i, :].reshape(1, dim).astype(f32) for i in range(2)
    ]

    ff_sent = after(ff_sent, x_all)
    ff_got, ff_places = exchange(lambda i: pick(ff_sent, i), "blk")
    w_out = gather(after(out_flipped, x_all)[None], both)
    cot_all = gather(after(cotangent, x_all, w_out), "blk")
    if strided:
        w_out = w_out.reshape(nb, nu, nb, piece, rows)
    else:
        w_out = jnp.transpose(w_out.reshape(nb, nu * feats_u, rows), (1, 0, 2))
        w_out = jnp.pad(
            w_out.reshape(nb, group, dim), ((0, 0), (0, piece - group), (0, 0))
        )
        w_out = jnp.transpose(w_out.reshape(nb, piece, blocks, block), (2, 0, 1, 3))[:, None]

    q, kv, normed = project(x_all, w_qkv, cosine, sine, piece, step)
    (kv_all,) = together(gather_plan(kv.reshape(2, nb, tok, feats), "uly"))
    o, lse = attend(seg_col, seg_rows, pos_rows, q, kv_all, tile)
    *ff_got, o = lax.optimization_barrier((*ff_got, o))
    w_ff, o_all = together(
        gather_near_plan(assemble(ff_got, ff_places), "uly", nb // 4), gather_plan(o, "blk")
    )
    x1, normed2 = output_project(x_all, o_all, w_out, gain2, step)

    act, d_gate, d_up = hidden(normed2, cot_all, w_ff, step)
    d_norm2 = mix([d_gate, d_up], w_ff, (0, 1), step)

    def meanwhile():
        (out,) = yield [mix([after(act, d_norm2)], w_ff, (2,), step)]
        grads = yield hidden_grads(after(normed2, out), cot_all, d_gate, d_up, act, block)
        return out, grads

    d_norm2, (mlp_out, ff_grads) = together(
        scatter_plan(d_norm2.reshape(nb, tok, dim), "blk"), meanwhile()
    )
    x1_own = lax.dynamic_slice_in_dim(x1, b * tok, tok, 0)
    mlp_out = scatter(after(mlp_out, d_norm2), "blk")
    r2_own = rms_scale(x1_own)
    gain2_part = jnp.sum(d_norm2 * x1_own * r2_own, axis=0, keepdims=True)
    z_two = gain2 * d_norm2
    dx1 = (
        cotangent.astype(f32)
        + r2_own * z_two
        - x1_own * r2_own * r2_own * r2_own * jnp.mean(z_two * x1_own, axis=-1, keepdims=True)
    )
    d_attn = dx1.astype(bf)

    d_o = output_back(d_attn, w_out)
    d_columns = jnp.transpose(d_attn.reshape(tok, nb, rows), (1, 0, 2))
    (d_o,) = together(swap_plan(d_o, "blk"))
    (ff_mine,) = together(scatter_near_plan(ff_grads, "uly"))
    d_o = d_o.reshape(count, feats)
    ff_mine = ff_mine.reshape(3, nb, rows, ff_piece)
    ff_got, ff_places = exchange(lambda i: lax.dynamic_index_in_dim(ff_mine, i, 1, False), "blk")
    d_got, d_places = exchange(lambda i: pick(d_columns, i), "blk")
    dq, dkv = attend_back(
        seg_col, seg_rows, pos_rows, cosine, sine, q, d_o, o, lse, kv_all, tile
    )
    *d_got, dkv = lax.optimization_barrier((*d_got, dkv))
    d_columns = jnp.zeros_like(d_columns)
    for got, at in zip(d_got, d_places):
        d_columns = place(d_columns, got, at)
    out_grads = output_grads(o_all, d_columns.reshape(count, rows), pieces)
    if not strided:
        out_grads = out_grads[:, :, :group]
    dkv, out_grads = together(
        scatter_plan(dkv, "uly"), scatter_plan(out_grads.reshape(nu, feats_u, rows), "uly")
    )
    grad_output = jnp.transpose(out_grads)
    dkv = dkv.astype(bf).reshape(2, count, feats)
    *ff_got, dkv = lax.optimization_barrier((*ff_got, dkv))
    ff_grads = finish(ff_got, ff_places)
    dk, d_norm1, gain1_part = project_back(x_all, w_qkv, cosine, sine, dq, dkv, piece, step)
    gain_parts = jnp.pad(jnp.concatenate([gain1_part, gain2_part]), ((0, PAD - 2), (0, 0)))
    grads = projection_grads(
        [dq, dk, dkv[1]], after(normed, d_norm1), gain_parts, pieces, block
    )
    last = scatter_plan(d_norm1.reshape(nb, tok, dim), "blk")
    if strided:
        d_norm1, got = together(
            last,
            chain(
                scatter_plan(grads, "uly"), lambda mine: swap_plan(mine.astype(bf), "blk")
            ),
        )
        gain_sums = jnp.sum(got[:, 3 * piece : 3 * piece + 2].astype(f32), axis=0)
        heads = [got[:, i * piece : (i + 1) * piece].reshape(feats_u, rows) for i in range(3)]
    else:
        wanted = grads[0, :, : 3 * piece].reshape(blocks, 3, piece, block)[:, :, :group]
        wanted = jnp.transpose(wanted, (1, 2, 0, 3)).reshape(3, group, nb, rows)
        d_norm1, got = together(last, swap_plan(jnp.transpose(wanted, (2, 1, 0, 3)), "blk"))
        got = scatter(got.reshape(nu, feats_u, 3, rows), "uly")[0]
        heads = [got[:, i] for i in range(3)]
        gain_sums = lax.dynamic_slice_in_dim(lax.psum(gain_parts[:2], both), b * rows, rows, 1)
    grad_query, grad_key, grad_value = [jnp.transpose(h).astype(f32) for h in heads]
    x_own = tokens.astype(f32)
    r1_own = rms_scale(x_own)
    z_one = gain1 * d_norm1
    grad_tokens = (
        dx1
        + r1_own * z_one
        - x_own * r1_own * r1_own * r1_own * jnp.mean(z_one * x_own, axis=-1, keepdims=True)
    )
    mlp_out, d_norm1 = lax.optimization_barrier((mlp_out, d_norm1))
    output = x1_own + mlp_out.astype(f32)
    return (
        output,
        grad_tokens,
        gain_sums[0],
        grad_query,
        grad_key,
        grad_value,
        grad_output,
        gain_sums[1],
        *ff_grads,
    )


def solution(mesh):
    tokens_split = P(("blk", "uly"), None)
    weights = P("blk", "uly")
    return jax.shard_map(
        on_device,
        mesh=mesh,
        in_specs=(
            tokens_split,
            P(),
            tokens_split,
            P("blk"),
            weights,
            weights,
            weights,
            weights,
            P("blk"),
            weights,
            weights,
            weights,
        ),
        out_specs=(
            tokens_split,
            tokens_split,
            P("blk"),
            weights,
            weights,
            weights,
            weights,
            P("blk"),
            weights,
            weights,
            weights,
        ),
        check_vma=False,
    )
```

time: 1260 us -> 847 us (0.67)
  blocking collectives: 322 us -> 0 us
  Pallas kernels: 91.6 us -> 238 us
  local copies, waits for them, and re-layouts: 200 us -> 55.9 us
  starting transfers between devices: 12.5 us -> 148 us
  waiting for transfers between devices: 462 us -> 331 us
  matrix products: 114 us -> 0 us
  other arithmetic: 32.4 us -> 46.9 us
    ppermute x0 -> x82, waiting for transfers between devices: none -> 331 us  [hop(): return lax.ppermute(value, axis, pairs)]
    reduce_scatter x6 -> x1, waiting for transfers between devices: 301 us -> 0.01 us  [scatter(): return lax.psum_scatter(value, axis, scatter_dimension=0, tiled=True)]
    all_to_all x3 -> x0, blocking collectives: 179 us -> none  [swap(): return lax.all_to_all(value, axis, 0, 0, tiled=True)]
    all_gather x9 -> x2, waiting for transfers between devices: 160 us -> 0.01 us  [gather(): return lax.all_gather(value, axis, axis=0, tiled=True)]
    ppermute x0 -> x82, starting transfers between devices: none -> 148 us  [hop(): return lax.ppermute(value, axis, pairs)]
    pallas_call x0 -> x14, Pallas kernels: none -> 143 us  [the longest x2 22.9 us: mix(): pl.pallas_call(functools.partial(mix_kernel, which, n), grid=(count // ro...]
    psum x1 -> x0, blocking collectives: 124 us -> none  [on_device(): gain_sums = lax.psum(jnp.stack([gain1_part, gain2_part]), both)]
    dot_general x18 -> x0, matrix products: 114 us -> none  [the longest x8 52.8 us: dot_n(): return jnp.dot(left, right, preferred_element_type=f32)]
  transfers between devices with their start and end apart: 17 -> 85, of which waited for: 11 -> 30; matrix products, arithmetic and copies ran while one was open for 21% -> 10% of each run, Pallas kernels for 7% -> 24%
where the time goes in v2:
time: 847 us; the launch traced here: 835 us
  waiting for transfers between devices  331 us (39%)
  Pallas kernels  238 us (28%)
  starting transfers between devices  148 us (17%)
  local copies, waits for them, and re-layouts  55.9 us (7%)
  other arithmetic  46.9 us (6%)
  between operations  15.3 us (2%)
    ppermute x82, waiting for transfers between devices, hop(): return lax.ppermute(value, axis, pairs)  331 us
    ppermute x82, starting transfers between devices, hop(): return lax.ppermute(value, axis, pairs)  148 us
    pallas_call x1, Pallas kernels, attend_back(): pl.pallas_call(functools.partial(attend_back_kernel, tile), grid=(pairs,...  50.6 us
    pallas_call x1, Pallas kernels, attend(): pl.pallas_call(functools.partial(attend_kernel, tile), grid=(pairs, nq),...  43.8 us
    pallas_call x2, Pallas kernels, mix(): pl.pallas_call(functools.partial(mix_kernel, which, n), grid=(count // ro...  22.9 us
    pallas_call x1, Pallas kernels, hidden(): pl.pallas_call(functools.partial(hidden_kernel, n), grid=(count // rows,)...  20.6 us
    pallas_call x1, Pallas kernels, hidden_grads(): pl.pallas_call(hidden_grads_kernel, grid=(dim // block,), in_specs=[colum...  19.3 us
    dynamic_update_slice x41, local copies, waits for them, and re-layouts, place(): return lax.dynamic_update_slice_in_dim(out, piece[None], at, 0)  18 us
  transfers between devices with their start and end apart: 85, of which 30 were waited for; matrix products, arithmetic and copies ran while one was open for 10% of the time, Pallas kernels for 24%

profile of v2, /device:TPU:0, one launch (start us, length us, event | category | flops | bytes accessed | tf_op | source)
XLA Modules:
  0.0 835.0 jit_solution(12837261323304950108)
XLA Ops:
  43.0 13.5 %collective-permute-done.4 = bf16[2,208,256]{2,1,0:T(8,128)(2,1)S(1)} collective-permute-done((bf16[2,208,256]{2,1,0:T(8,128)(2,1)S(1)}, bf16[2,208,256]{2,1,0:T(8,128)(2,1)S(1)}, u32[]{:S(2)}, u32[]{:S(2)}) %collective-permute-start.4) | collective-permute-done | bytes 213024 | tf_op jit(solution)/shard_map/ppermute | solution.py:59
  69.5 9.5 %collective-permute-done.9 = bf16[128,2048]{1,0:T(8,128)(2,1)S(1)} collective-permute-done((bf16[128,2048]{1,0:T(8,128)(2,1)S(1)}, bf16[128,2048]{1,0:T(8,128)(2,1)S(1)}, u32[]{:S(2)}, u32[]{:S(2)}) %collective-permute-start.9) | collective-permute-done | bytes 524320 | tf_op jit(solution)/shard_map/ppermute | solution.py:59
  79.0 10.7 %collective-permute-done.10 = bf16[128,2048]{1,0:T(8,128)(2,1)S(1)} collective-permute-done((bf16[128,2048]{1,0:T(8,128)(2,1)S(1)}, bf16[128,2048]{1,0:T(8,128)(2,1)S(1)}, u32[]{:S(2)}, u32[]{:S(2)}) %collective-permute-start.10) | collective-permute-done | bytes 524320 | tf_op jit(solution)/shard_map/ppermute | solution.py:59
  101.0 9.7 %project.1 = (bf16[1024,256]{1,0:T(8,128)(2,1)}, bf16[2,1024,256]{2,1,0:T(8,128)(2,1)}, bf16[1024,2048]{1,0:T(8,128)(2,1)}) custom-call(bf16[1024,2048]{1,0:T(8,128)(2,1)} %bitcast.23.x_ref, bf16[4,8,208,256]{3,2,1,0:T(8,128)(2,1)} %copy-done.8, f32[1024,128]{1,0:T(8,128)} %get-tuple-element.350.cos_ref, f32[1024,128]{1,0:T(8,128)} %get-tuple-element.349.sin_ref), custom_call_target="tpu_custom_call" | custom-call | flops 2534400000 | tf_op jit(solution)/shard_map/project/pallas_call | solution.py:252
  114.8 25.1 %collective-permute-done.21 = bf16[2,8,128,256]{3,2,1,0:T(8,128)(2,1)} collective-permute-done((bf16[2,8,128,256]{3,2,1,0:T(8,128)(2,1)}, bf16[2,8,128,256]{3,2,1,0:T(8,128)(2,1)}, u32[]{:S(2)}, u32[]{:S(2)}) %collective-permute-start.21) | collective-permute-done | bytes 1048608 | tf_op jit(solution)/shard_map/ppermute | solution.py:59
  172.1 43.8 %attend.1 = (bf16[1024,256]{1,0:T(8,128)(2,1)}, f32[2,4,2,256]{3,2,1,0:T(2,128)}) custom-call(s32[4096,1]{1,0:T(8,128)} %copy.70.segk_ref, s32[4,1,256]{2,1,0:T(1,128)} %bitcast.403, s32[4,1,256]{2,1,0:T(1,128)} %broadcast_add_fusion.posq_ref, bf16[1024,256]{1,0:T(8,128)(2,1)} %get-tuple-element.149.q_ref, bf16[4,2,8,128,256]{4,3,2,1,0:T(8,128)(2,1)} %copy-done.6), custom_call_target="tpu_custom_call" | custom-call | flops 12099999744 | tf_op jit(solution)/shard_map/attend/pallas_call | solution.py:360
  228.8 17.1 %collective-permute-start.24 = (bf16[1024,256]{1,0:T(8,128)(2,1)S(1)}, bf16[1024,256]{1,0:T(8,128)(2,1)S(1)}, u32[]{:S(2)}, u32[]{:S(2)}) collective-permute-start(bf16[1024,256]{1,0:T(8,128)(2,1)S(1)} %copy-done.17), channel_id=1, source_target_pairs={{0,8},{4,12},{8,16},{12,20},{16,24},{20,28},{24,0},{28,4},{1,9},{5... | collective-permute-start | bytes 1572872 | tf_op jit(solution)/shard_map/ppermute | solution.py:59
  248.5 19.0 %collective-permute-done.24 = bf16[1024,256]{1,0:T(8,128)(2,1)S(1)} collective-permute-done((bf16[1024,256]{1,0:T(8,128)(2,1)S(1)}, bf16[1024,256]{1,0:T(8,128)(2,1)S(1)}, u32[]{:S(2)}, u32[]{:S(2)}) %collective-permute-start.24) | collective-permute-done | bytes 524320 | tf_op jit(solution)/shard_map/ppermute | solution.py:59
  267.5 10.2 %collective-permute-done.25 = bf16[1024,256]{1,0:T(8,128)(2,1)S(1)} collective-permute-done((bf16[1024,256]{1,0:T(8,128)(2,1)S(1)}, bf16[1024,256]{1,0:T(8,128)(2,1)S(1)}, u32[]{:S(2)}, u32[]{:S(2)}) %collective-permute-start.25) | collective-permute-done | bytes 524320 | tf_op jit(solution)/shard_map/ppermute | solution.py:59
  282.4 22.5 %collective-permute-done.26 = bf16[1024,256]{1,0:T(8,128)(2,1)S(1)} collective-permute-done((bf16[1024,256]{1,0:T(8,128)(2,1)S(1)}, bf16[1024,256]{1,0:T(8,128)(2,1)S(1)}, u32[]{:S(2)}, u32[]{:S(2)}) %collective-permute-start.26) | collective-permute-done | bytes 524320 | tf_op jit(solution)/shard_map/ppermute | solution.py:59
  306.3 15.4 %collective-permute-done.29 = bf16[1024,256]{1,0:T(8,128)(2,1)S(1)} collective-permute-done((bf16[1024,256]{1,0:T(8,128)(2,1)S(1)}, bf16[1024,256]{1,0:T(8,128)(2,1)S(1)}, u32[]{:S(2)}, u32[]{:S(2)}) %collective-permute-start.29) | collective-permute-done | bytes 524320 | tf_op jit(solution)/shard_map/ppermute | solution.py:59
  321.7 11.2 %collective-permute-done.30 = bf16[1024,256]{1,0:T(8,128)(2,1)S(1)} collective-permute-done((bf16[1024,256]{1,0:T(8,128)(2,1)S(1)}, bf16[1024,256]{1,0:T(8,128)(2,1)S(1)}, u32[]{:S(2)}, u32[]{:S(2)}) %collective-permute-start.30) | collective-permute-done | bytes 524320 | tf_op jit(solution)/shard_map/ppermute | solution.py:59
  332.9 10.1 %collective-permute-done.31 = bf16[1024,256]{1,0:T(8,128)(2,1)S(1)} collective-permute-done((bf16[1024,256]{1,0:T(8,128)(2,1)S(1)}, bf16[1024,256]{1,0:T(8,128)(2,1)S(1)}, u32[]{:S(2)}, u32[]{:S(2)}) %collective-permute-start.31) | collective-permute-done | bytes 524320 | tf_op jit(solution)/shard_map/ppermute | solution.py:59
  353.7 15.9 %output_project.1 = (f32[1024,2048]{1,0:T(8,128)}, bf16[1024,2048]{1,0:T(8,128)(2,1)}) custom-call(bf16[1024,2048]{1,0:T(8,128)(2,1)} %bitcast.23.x_ref, bf16[8,1024,256]{2,1,0:T(8,128)(2,1)} %bitcast_dynamic-update-slice_fusion.7.o_ref, bf16[8,4,8,64,256]{4,3,2,1,0:T(8,128)(2,1)} %bitcast.352, f32[1,2048]{1,0:T(1,128)} %bitcast.386), custom_call_target="tpu_custom_call" | custom-call | flops 4224000000 | tf_op jit(solution)/shard_map/output_project/pallas_call | solution.py:511
  369.6 20.6 %hidden.1 = (bf16[4,1024,256]{2,1,0:T(8,128)(2,1)}, bf16[4,1024,256]{2,1,0:T(8,128)(2,1)}, bf16[4,1024,256]{2,1,0:T(8,128)(2,1)}) custom-call(bf16[1024,2048]{1,0:T(8,128)(2,1)} %get-tuple-element.183.refs_0_.n_ref, bf16[1024,2048]{1,0:T(8,128)(2,1)} %all-gather.4.cloned.1.call-done.refs_1_.g_ref, bf16[3,2048,256]{2,1,0:T(8,128)(2,1)} %assemble.1.refs_2_.refs_1_, ...), custom_call_target="tpu_custom_call" | custom-call | flops 5500000256 | tf_op jit(solution)/shard_map/hidden/pallas_call | solution.py:781
  390.2 14.3 %mix.2 = bf16[1024,2048]{1,0:T(8,128)(2,1)} custom-call(bf16[4,1024,256]{2,1,0:T(8,128)(2,1)} %get-tuple-element.177.refs_0_.dg_ref, bf16[4,1024,256]{2,1,0:T(8,128)(2,1)} %get-tuple-element.178.refs_1_.du_ref, bf16[3,2048,256]{2,1,0:T(8,128)(2,1)} %assemble.1.refs_2_.refs_1_, bf16[3,2048,256]{2,1,0:T(8,128)(2,1)} %copy-done, ...), custom_call_target="tpu_custom_call" | custom-call | flops 4400000000 | tf_op jit(solution)/shard_map/mix/pallas_call | solution.py:806
  411.2 8.6 %mix.3 = bf16[1024,2048]{1,0:T(8,128)(2,1)} custom-call(bf16[4,1024,256]{2,1,0:T(8,128)(2,1)} %get-tuple-element.180.refs_0_.act_ref, bf16[3,2048,256]{2,1,0:T(8,128)(2,1)} %assemble.1.refs_2_.refs_1_, bf16[3,2048,256]{2,1,0:T(8,128)(2,1)} %copy-done, bf16[3,2048,256]{2,1,0:T(8,128)(2,1)} %collective-permute-done.32.refs_4_.refs_3_, ...), custom_call_target="tpu_custom_call" | custom-call | flops 2200000000 | tf_op jit(solution)/shard_map/mix/pallas_call | solution.py:806
  422.1 11.2 %collective-permute-done.39 = bf16[128,2048]{1,0:T(8,128)(2,1)S(1)} collective-permute-done((bf16[128,2048]{1,0:T(8,128)(2,1)S(1)}, bf16[128,2048]{1,0:T(8,128)(2,1)S(1)}, u32[]{:S(2)}, u32[]{:S(2)}) %collective-permute-start.39) | collective-permute-done | bytes 524320 | tf_op jit(solution)/shard_map/ppermute | solution.py:59
  438.9 19.3 %hidden_grads.1 = (bf16[3,2048,256]{2,1,0:T(8,128)(2,1)}, bf16[3,2048,256]{2,1,0:T(8,128)(2,1)}, bf16[3,2048,256]{2,1,0:T(8,128)(2,1)}, bf16[3,2048,256]{2,1,0:T(8,128)(2,1)}) custom-call(bf16[1024,2048]{1,0:T(8,128)(2,1)} %get-tuple-element.183.refs_0_.n_ref, bf16[1024,2048]{1,0:T(8,128)(2,1)} %all-gather.4.cloned.1.call-done.refs_1_.g_ref, ...), custom_call_target="tpu_custom_call" | custom-call | flops 6874999808 | tf_op jit(solution)/shard_map/hidden_grads/pallas_call | solution.py:831
  461.8 12.0 %collective-permute-done.38 = bf16[128,2048]{1,0:T(8,128)(2,1)S(1)} collective-permute-done((bf16[128,2048]{1,0:T(8,128)(2,1)S(1)}, bf16[128,2048]{1,0:T(8,128)(2,1)S(1)}, u32[]{:S(2)}, u32[]{:S(2)}) %collective-permute-start.38) | collective-permute-done | bytes 524320 | tf_op jit(solution)/shard_map/ppermute | solution.py:59
  478.2 8.7 %output_back.1 = bf16[8,128,256]{2,1,0:T(8,128)(2,1)} custom-call(bf16[128,2048]{1,0:T(8,128)(2,1)} %get-tuple-element.280.d_ref, bf16[8,4,8,64,256]{4,3,2,1,0:T(8,128)(2,1)} %bitcast.353), custom_call_target="tpu_custom_call" | custom-call | flops 2200000000 | tf_op jit(solution)/shard_map/output_back/pallas_call | solution.py:543
  520.9 50.6 %attend_back.1 = (bf16[1024,256]{1,0:T(8,128)(2,1)}, bf16[4,2,8,128,256]{4,3,2,1,0:T(8,128)(2,1)}) custom-call(s32[4096,1]{1,0:T(8,128)} %copy.70.segk_ref, s32[4,1,256]{2,1,0:T(1,128)} %bitcast.404, s32[4,1,256]{2,1,0:T(1,128)} %broadcast_add_fusion.posq_ref, f32[1024,128]{1,0:T(8,128)} %get-tuple-element.350.cos_ref, ...), custom_call_target="tpu_custom_call" | custom-call | flops 13749999616 | tf_op jit(solution)/shard_map/attend_back/pallas_call | solution.py:466
  600.4 20.6 %collective-permute-done.67 = bf16[512,256]{0,1:T(8,128)(2,1)S(1)} collective-permute-done((bf16[512,256]{0,1:T(8,128)(2,1)}, bf16[512,256]{0,1:T(8,128)(2,1)S(1)}, u32[]{:S(2)}, u32[]{:S(2)}) %collective-permute-start.67) | collective-permute-done | bytes 262176 | tf_op jit(solution)/shard_map/ppermute | solution.py:59
  629.9 37.2 %collective-permute-done.51.refs_4_ = bf16[3,256,256]{2,1,0:T(8,128)(2,1)S(1)} collective-permute-done((bf16[3,256,256]{2,1,0:T(8,128)(2,1)}, bf16[3,256,256]{2,1,0:T(8,128)(2,1)S(1)}, u32[]{:S(2)}, u32[]{:S(2)}) %collective-permute-start.51) | collective-permute-done | bytes 393248 | tf_op jit(solution)/shard_map/ppermute | solution.py:59
  667.1 12.0 %collective-permute-done.52.refs_5_ = bf16[3,256,256]{2,1,0:T(8,128)(2,1)S(1)} collective-permute-done((bf16[3,256,256]{2,1,0:T(8,128)(2,1)}, bf16[3,256,256]{2,1,0:T(8,128)(2,1)S(1)}, u32[]{:S(2)}, u32[]{:S(2)}) %collective-permute-start.52) | collective-permute-done | bytes 393248 | tf_op jit(solution)/shard_map/ppermute | solution.py:59
  680.1 9.8 %project_back.1 = (bf16[1024,256]{1,0:T(8,128)(2,1)}, bf16[1024,2048]{1,0:T(8,128)(2,1)}, f32[1,2048]{1,0:T(1,128)}) custom-call(bf16[1024,2048]{1,0:T(8,128)(2,1)} %bitcast.23.x_ref, bf16[4,8,208,256]{3,2,1,0:T(8,128)(2,1)} %copy-done.8, f32[1024,128]{1,0:T(8,128)} %get-tuple-element.350.cos_ref, f32[1024,128]{1,0:T(8,128)} %get-tuple-element.349.sin_ref, ...), custom_call_target="tpu_custom_call" | custom-call | flops 2816000000 | tf_op jit(solution)/shard_map/project_back/pallas_call | solution.py:588
  692.1 9.7 %projection_grads.1 = bf16[4,8,208,256]{3,2,1,0:T(8,128)(2,1)} custom-call(bf16[1024,256]{1,0:T(8,128)(2,1)} %get-tuple-element.198.dq_ref.refs_0_, bf16[1024,256]{1,0:T(8,128)(2,1)} %get-tuple-element.221.refs_1_, bf16[1024,256]{1,0:T(8,128)(2,1)} %slice_bitcast_fusion.refs_2_, bf16[1024,2048]{1,0:T(8,128)(2,1)} %get-tuple-element.223.refs_3_, ...), custom_call_target="tpu_custom_call" | custom-call | flops 2062499968 | tf_op jit(solution)/shard_map/projection_grads/pallas_call | solution.py:636
  707.5 12.3 %collective-permute-done.70 = bf16[128,2048]{1,0:T(8,128)(2,1)S(1)} collective-permute-done((bf16[128,2048]{1,0:T(8,128)(2,1)S(1)}, bf16[128,2048]{1,0:T(8,128)(2,1)S(1)}, u32[]{:S(2)}, u32[]{:S(2)}) %collective-permute-start.70) | collective-permute-done | bytes 524320 | tf_op jit(solution)/shard_map/ppermute | solution.py:59
  721.9 25.4 %collective-permute-start.72 = (bf16[128,2048]{1,0:T(8,128)(2,1)S(1)}, bf16[128,2048]{1,0:T(8,128)(2,1)S(1)}, u32[]{:S(2)}, u32[]{:S(2)}) collective-permute-start(bf16[128,2048]{1,0:T(8,128)(2,1)S(1)} %fusion.13), channel_id=1, source_target_pairs={{0,8},{4,12},{8,16},{12,20},{16,24},{20,28},{24,0},{28,4},{1,9},{5... | collective-permute-start | bytes 1572872 | tf_op jit(solution)/shard_map/ppermute | solution.py:59
  747.8 13.0 %collective-permute-done.72 = bf16[128,2048]{1,0:T(8,128)(2,1)S(1)} collective-permute-done((bf16[128,2048]{1,0:T(8,128)(2,1)S(1)}, bf16[128,2048]{1,0:T(8,128)(2,1)S(1)}, u32[]{:S(2)}, u32[]{:S(2)}) %collective-permute-start.72) | collective-permute-done | bytes 524320 | tf_op jit(solution)/shard_map/ppermute | solution.py:59
  766.0 9.0 %collective-permute-done.77 = bf16[4,208,256]{2,1,0:T(8,128)(2,1)} collective-permute-done((bf16[4,208,256]{2,1,0:T(8,128)(2,1)}, bf16[4,208,256]{2,1,0:T(8,128)(2,1)}, u32[]{:S(2)}, u32[]{:S(2)}) %collective-permute-start.77) | collective-permute-done | bytes 426016 | tf_op jit(solution)/shard_map/ppermute | solution.py:59
  797.1 15.7 %collective-permute-done.79 = bf16[2,208,256]{2,1,0:T(8,128)(2,1)S(1)} collective-permute-done((bf16[2,208,256]{2,1,0:T(8,128)(2,1)S(1)}, bf16[2,208,256]{2,1,0:T(8,128)(2,1)S(1)}, u32[]{:S(2)}, u32[]{:S(2)}) %collective-permute-start.79) | collective-permute-done | bytes 213024 | tf_op jit(solution)/shard_map/ppermute | solution.py:59
  (361 shorter events, 276.1 us)
Async XLA Ops:
  7.2 346.5 %all-gather.6.cloned.1.call-start = ((), (), s32[]{:S(2)}) async-start(), calls=%async_computation.3 | async-start | bytes 8650752 | tf_op jit(solution)/shard_map/all_gather | solution.py:198
  12.4 57.1 %collective-permute-start.7 = (bf16[128,2048]{1,0:T(8,128)(2,1)}, bf16[128,2048]{1,0:T(8,128)(2,1)S(1)}, u32[]{:S(2)}, u32[]{:S(2)}) collective-permute-start(bf16[128,2048]{1,0:T(8,128)(2,1)} %param.12), channel_id=1, source_target_pairs={{0,4},{4,0},{8,12},{12,8},{16,20},{20,16},{24,28},{28,24},{1,5},{5... | collective-permute-start | bytes 1572872 | tf_op jit(solution)/shard_map/ppermute | solution.py:59
  93.0 276.6 %all-gather.4.cloned.1.call-start = ((), (), s32[]{:S(2)}) async-start(), calls=%async_computation.1 | async-start | bytes 4718592 | tf_op jit(solution)/shard_map/all_gather | solution.py:198
  144.1 71.9 %collective-permute-start.14 = (bf16[3,256,256]{2,1,0:T(8,128)(2,1)}, bf16[3,256,256]{2,1,0:T(8,128)(2,1)S(1)}, u32[]{:S(2)}, u32[]{:S(2)}) collective-permute-start(bf16[3,256,256]{2,1,0:T(8,128)(2,1)} %get-tuple-element.313), channel_id=1, source_target_pairs={{0,12},{4,8},{8,20},{12,16},{16,28},{20,24},{24,4},{28,0},{1,13},{... | collective-permute-start | bytes 1179656 | tf_op jit(solution)/shard_map/ppermute | solution.py:59
  148.9 675.3 %reduce-scatter.2.cloned.1.call-start = ((), (), s32[]{:S(2)}) async-start(), calls=%async_computation.2 | async-start | bytes 4718592 | tf_op jit(solution)/shard_map/reduce_scatter | solution.py:202
  150.9 65.1 %collective-permute-start.15 = (bf16[3,256,256]{2,1,0:T(8,128)(2,1)}, bf16[3,256,256]{2,1,0:T(8,128)(2,1)S(1)}, u32[]{:S(2)}, u32[]{:S(2)}) collective-permute-start(bf16[3,256,256]{2,1,0:T(8,128)(2,1)} %get-tuple-element.312), channel_id=1, source_target_pairs={{0,16},{4,20},{8,24},{12,28},{16,0},{20,4},{24,8},{28,12},{1,17},{... | collective-permute-start | bytes 1179656 | tf_op jit(solution)/shard_map/ppermute | solution.py:59
  151.0 70.8 %collective-permute-start.16 = (bf16[3,256,256]{2,1,0:T(8,128)(2,1)}, bf16[3,256,256]{2,1,0:T(8,128)(2,1)S(1)}, u32[]{:S(2)}, u32[]{:S(2)}) collective-permute-start(bf16[3,256,256]{2,1,0:T(8,128)(2,1)} %get-tuple-element.311), channel_id=1, source_target_pairs={{0,20},{4,16},{8,28},{12,24},{16,4},{20,0},{24,12},{28,8},{1,21},{... | collective-permute-start | bytes 1179656 | tf_op jit(solution)/shard_map/ppermute | solution.py:59
  161.4 60.4 %collective-permute-start.17 = (bf16[3,256,256]{2,1,0:T(8,128)(2,1)}, bf16[3,256,256]{2,1,0:T(8,128)(2,1)S(1)}, u32[]{:S(2)}, u32[]{:S(2)}) collective-permute-start(bf16[3,256,256]{2,1,0:T(8,128)(2,1)} %get-tuple-element.310), channel_id=1, source_target_pairs={{0,24},{4,28},{8,0},{12,4},{16,8},{20,12},{24,16},{28,20},{1,25},{... | collective-permute-start | bytes 1179656 | tf_op jit(solution)/shard_map/ppermute | solution.py:59
  165.8 56.0 %collective-permute-start.18 = (bf16[3,256,256]{2,1,0:T(8,128)(2,1)S(1)}, bf16[3,256,256]{2,1,0:T(8,128)(2,1)S(1)}, u32[]{:S(2)}, u32[]{:S(2)}) collective-permute-start(bf16[3,256,256]{2,1,0:T(8,128)(2,1)S(1)} %get-tuple-element.309), channel_id=1, source_target_pairs={{0,28},{4,24},{8,4},{12,0},{16,12},{20,8},{24,20},{28,16},{1,29},{... | collective-permute-start | bytes 1179656 | tf_op jit(solution)/shard_map/ppermute | solution.py:59
  227.3 115.8 %collective-permute-start.27 = (bf16[3,2048,256]{2,1,0:T(8,128)(2,1)}, bf16[3,2048,256]{2,1,0:T(8,128)(2,1)S(1)}, u32[]{:S(2)}, u32[]{:S(2)}) collective-permute-start(bf16[3,2048,256]{2,1,0:T(8,128)(2,1)} %assemble.1.refs_2_.refs_1_), channel_id=1, source_target_pairs={{0,2},{1,3},{2,0},{3,1},{4,6},{5,7},{6,4},{7,5},{8,10},{9,11},{10,... | collective-permute-start | bytes 9437192 | tf_op jit(solution)/shard_map/ppermute | solution.py:59
  228.8 38.7 %collective-permute-start.24 = (bf16[1024,256]{1,0:T(8,128)(2,1)S(1)}, bf16[1024,256]{1,0:T(8,128)(2,1)S(1)}, u32[]{:S(2)}, u32[]{:S(2)}) collective-permute-start(bf16[1024,256]{1,0:T(8,128)(2,1)S(1)} %copy-done.17), channel_id=1, source_target_pairs={{0,8},{4,12},{8,16},{12,20},{16,24},{20,28},{24,0},{28,4},{1,9},{5... | collective-permute-start | bytes 1572872 | tf_op jit(solution)/shard_map/ppermute | solution.py:59
  280.4 41.4 %collective-permute-start.29 = (bf16[1024,256]{1,0:T(8,128)(2,1)S(1)}, bf16[1024,256]{1,0:T(8,128)(2,1)S(1)}, u32[]{:S(2)}, u32[]{:S(2)}) collective-permute-start(bf16[1024,256]{1,0:T(8,128)(2,1)S(1)} %collective-permute-done.24), channel_id=1, source_target_pairs={{0,4},{4,0},{8,12},{12,8},{16,20},{20,16},{24,28},{28,24},{1,5},{5... | collective-permute-start | bytes 1572872 | tf_op jit(solution)/shard_map/ppermute | solution.py:59
  282.4 50.6 %collective-permute-start.30 = (bf16[1024,256]{1,0:T(8,128)(2,1)S(1)}, bf16[1024,256]{1,0:T(8,128)(2,1)S(1)}, u32[]{:S(2)}, u32[]{:S(2)}) collective-permute-start(bf16[1024,256]{1,0:T(8,128)(2,1)S(1)} %collective-permute-done.25), channel_id=1, source_target_pairs={{0,4},{4,0},{8,12},{12,8},{16,20},{20,16},{24,28},{28,24},{1,5},{5... | collective-permute-start | bytes 1572872 | tf_op jit(solution)/shard_map/ppermute | solution.py:59
  306.3 47.4 %collective-permute-start.32 = (bf16[3,2048,256]{2,1,0:T(8,128)(2,1)}, bf16[3,2048,256]{2,1,0:T(8,128)(2,1)}, u32[]{:S(2)}, u32[]{:S(2)}) collective-permute-start(bf16[3,2048,256]{2,1,0:T(8,128)(2,1)} %assemble.1.refs_2_.refs_1_), channel_id=1, source_target_pairs={{0,1},{1,0},{2,3},{3,2},{4,5},{5,4},{6,7},{7,6},{8,9},{9,8},{10,11... | collective-permute-start | bytes 9437192 | tf_op jit(solution)/shard_map/ppermute | solution.py:59
  409.2 48.9 %collective-permute-start.36 = (bf16[128,2048]{1,0:T(8,128)(2,1)}, bf16[128,2048]{1,0:T(8,128)(2,1)S(1)}, u32[]{:S(2)}, u32[]{:S(2)}) collective-permute-start(bf16[128,2048]{1,0:T(8,128)(2,1)} %get-tuple-element.294), channel_id=1, source_target_pairs={{0,4},{4,0},{8,12},{12,8},{16,20},{20,16},{24,28},{28,24},{1,5},{5... | collective-permute-start | bytes 1572872 | tf_op jit(solution)/shard_map/ppermute | solution.py:59
  409.5 52.2 %collective-permute-start.35 = (bf16[128,2048]{1,0:T(8,128)(2,1)S(1)}, bf16[128,2048]{1,0:T(8,128)(2,1)S(1)}, u32[]{:S(2)}, u32[]{:S(2)}) collective-permute-start(bf16[128,2048]{1,0:T(8,128)(2,1)S(1)} %get-tuple-element.295), channel_id=1, source_target_pairs={{0,4},{4,0},{8,12},{12,8},{16,20},{20,16},{24,28},{28,24},{1,5},{5... | collective-permute-start | bytes 1572872 | tf_op jit(solution)/shard_map/ppermute | solution.py:59
  459.8 47.7 %collective-permute-start.45 = (bf16[3,2048,256]{2,1,0:T(8,128)(2,1)}, bf16[3,2048,256]{2,1,0:T(8,128)(2,1)}, u32[]{:S(2)}, u32[]{:S(2)}) collective-permute-start(bf16[3,2048,256]{2,1,0:T(8,128)(2,1)} %get-tuple-element.200), channel_id=1, source_target_pairs={{0,1},{1,0},{2,3},{3,2},{4,5},{5,4},{6,7},{7,6},{8,9},{9,8},{10,11... | collective-permute-start | bytes 9437192 | tf_op jit(solution)/shard_map/ppermute | solution.py:59
  459.9 49.8 %collective-permute-start.46 = (bf16[3,2048,256]{2,1,0:T(8,128)(2,1)}, bf16[3,2048,256]{2,1,0:T(8,128)(2,1)}, u32[]{:S(2)}, u32[]{:S(2)}) collective-permute-start(bf16[3,2048,256]{2,1,0:T(8,128)(2,1)} %get-tuple-element.201), channel_id=1, source_target_pairs={{0,1},{1,0},{2,3},{3,2},{4,5},{5,4},{6,7},{7,6},{8,9},{9,8},{10,11... | collective-permute-start | bytes 9437192 | tf_op jit(solution)/shard_map/ppermute | solution.py:59
  507.5 64.1 %collective-permute-start.58 = (bf16[128,256]{1,0:T(8,128)(2,1)S(1)}, bf16[128,256]{1,0:T(8,128)(2,1)S(1)}, u32[]{:S(2)}, u32[]{:S(2)}) collective-permute-start(bf16[128,256]{1,0:T(8,128)(2,1)S(1)} %bitcast.394), channel_id=1, source_target_pairs={{0,16},{4,20},{8,24},{12,28},{16,0},{20,4},{24,8},{28,12},{1,17},{... | collective-permute-start | bytes 196616 | tf_op jit(solution)/shard_map/ppermute | solution.py:59
  509.6 62.0 %collective-permute-start.59 = (bf16[128,256]{1,0:T(8,128)(2,1)S(1)}, bf16[128,256]{1,0:T(8,128)(2,1)S(1)}, u32[]{:S(2)}, u32[]{:S(2)}) collective-permute-start(bf16[128,256]{1,0:T(8,128)(2,1)S(1)} %bitcast.393), channel_id=1, source_target_pairs={{0,20},{4,16},{8,28},{12,24},{16,4},{20,0},{24,12},{28,8},{1,21},{... | collective-permute-start | bytes 196616 | tf_op jit(solution)/shard_map/ppermute | solution.py:59
  515.5 56.1 %collective-permute-start.60 = (bf16[128,256]{1,0:T(8,128)(2,1)S(1)}, bf16[128,256]{1,0:T(8,128)(2,1)S(1)}, u32[]{:S(2)}, u32[]{:S(2)}) collective-permute-start(bf16[128,256]{1,0:T(8,128)(2,1)S(1)} %bitcast.392), channel_id=1, source_target_pairs={{0,24},{4,28},{8,0},{12,4},{16,8},{20,12},{24,16},{28,20},{1,25},{... | collective-permute-start | bytes 196616 | tf_op jit(solution)/shard_map/ppermute | solution.py:59
  517.9 53.8 %collective-permute-start.61 = (bf16[128,256]{1,0:T(8,128)(2,1)S(1)}, bf16[128,256]{1,0:T(8,128)(2,1)S(1)}, u32[]{:S(2)}, u32[]{:S(2)}) collective-permute-start(bf16[128,256]{1,0:T(8,128)(2,1)S(1)} %bitcast.391), channel_id=1, source_target_pairs={{0,28},{4,24},{8,4},{12,0},{16,12},{20,8},{24,20},{28,16},{1,29},{... | collective-permute-start | bytes 196616 | tf_op jit(solution)/shard_map/ppermute | solution.py:59
  519.4 71.0 %collective-permute-start.47 = (bf16[3,2048,256]{2,1,0:T(8,128)(2,1)}, bf16[3,2048,256]{2,1,0:T(8,128)(2,1)}, u32[]{:S(2)}, u32[]{:S(2)}) collective-permute-start(bf16[3,2048,256]{2,1,0:T(8,128)(2,1)} %add_convert_fusion.1), channel_id=1, source_target_pairs={{0,2},{1,3},{2,0},{3,1},{4,6},{5,7},{6,4},{7,5},{8,10},{9,11},{10,... | collective-permute-start | bytes 9437192 | tf_op jit(solution)/shard_map/ppermute | solution.py:59
  621.0 46.1 %collective-permute-start.51 = (bf16[3,256,256]{2,1,0:T(8,128)(2,1)}, bf16[3,256,256]{2,1,0:T(8,128)(2,1)S(1)}, u32[]{:S(2)}, u32[]{:S(2)}) collective-permute-start(bf16[3,256,256]{2,1,0:T(8,128)(2,1)} %get-tuple-element.304), channel_id=1, source_target_pairs={{0,16},{4,20},{8,24},{12,28},{16,0},{20,4},{24,8},{28,12},{1,17},{... | collective-permute-start | bytes 1179656 | tf_op jit(solution)/shard_map/ppermute | solution.py:59
  621.0 58.1 %collective-permute-start.52 = (bf16[3,256,256]{2,1,0:T(8,128)(2,1)}, bf16[3,256,256]{2,1,0:T(8,128)(2,1)S(1)}, u32[]{:S(2)}, u32[]{:S(2)}) collective-permute-start(bf16[3,256,256]{2,1,0:T(8,128)(2,1)} %get-tuple-element.303), channel_id=1, source_target_pairs={{0,20},{4,16},{8,28},{12,24},{16,4},{20,0},{24,12},{28,8},{1,21},{... | collective-permute-start | bytes 1179656 | tf_op jit(solution)/shard_map/ppermute | solution.py:59
  624.8 54.3 %collective-permute-start.53 = (bf16[3,256,256]{2,1,0:T(8,128)(2,1)S(1)}, bf16[3,256,256]{2,1,0:T(8,128)(2,1)S(1)}, u32[]{:S(2)}, u32[]{:S(2)}) collective-permute-start(bf16[3,256,256]{2,1,0:T(8,128)(2,1)S(1)} %get-tuple-element.302), channel_id=1, source_target_pairs={{0,24},{4,28},{8,0},{12,4},{16,8},{20,12},{24,16},{28,20},{1,25},{... | collective-permute-start | bytes 1179656 | tf_op jit(solution)/shard_map/ppermute | solution.py:59
  626.3 52.8 %collective-permute-start.54 = (bf16[3,256,256]{2,1,0:T(8,128)(2,1)S(1)}, bf16[3,256,256]{2,1,0:T(8,128)(2,1)S(1)}, u32[]{:S(2)}, u32[]{:S(2)}) collective-permute-start(bf16[3,256,256]{2,1,0:T(8,128)(2,1)S(1)} %get-tuple-element.301), channel_id=1, source_target_pairs={{0,28},{4,24},{8,4},{12,0},{16,12},{20,8},{24,20},{28,16},{1,29},{... | collective-permute-start | bytes 1179656 | tf_op jit(solution)/shard_map/ppermute | solution.py:59
  707.0 40.8 %collective-permute-start.73 = (bf16[8,208,256]{2,1,0:T(8,128)(2,1)S(1)}, bf16[8,208,256]{2,1,0:T(8,128)(2,1)S(1)}, u32[]{:S(2)}, u32[]{:S(2)}) collective-permute-start(bf16[8,208,256]{2,1,0:T(8,128)(2,1)S(1)} %get-tuple-element.297), channel_id=1, source_target_pairs={{0,1},{1,0},{2,3},{3,2},{4,5},{5,4},{6,7},{7,6},{8,9},{9,8},{10,11... | collective-permute-start | bytes 2555912 | tf_op jit(solution)/shard_map/ppermute | solution.py:59
  707.2 40.6 %collective-permute-start.69 = (bf16[128,2048]{1,0:T(8,128)(2,1)S(1)}, bf16[128,2048]{1,0:T(8,128)(2,1)S(1)}, u32[]{:S(2)}, u32[]{:S(2)}) collective-permute-start(bf16[128,2048]{1,0:T(8,128)(2,1)S(1)} %get-tuple-element.287), channel_id=1, source_target_pairs={{0,4},{4,0},{8,12},{12,8},{16,20},{20,16},{24,28},{28,24},{1,5},{5... | collective-permute-start | bytes 1572872 | tf_op jit(solution)/shard_map/ppermute | solution.py:59
  720.1 40.7 %collective-permute-start.74 = (bf16[8,208,256]{2,1,0:T(8,128)(2,1)S(1)}, bf16[8,208,256]{2,1,0:T(8,128)(2,1)S(1)}, u32[]{:S(2)}, u32[]{:S(2)}) collective-permute-start(bf16[8,208,256]{2,1,0:T(8,128)(2,1)S(1)} %fusion.5), channel_id=1, source_target_pairs={{0,2},{1,3},{2,0},{3,1},{4,6},{5,7},{6,4},{7,5},{8,10},{9,11},{10,... | collective-permute-start | bytes 2555912 | tf_op jit(solution)/shard_map/ppermute | solution.py:59
  721.9 38.9 %collective-permute-start.72 = (bf16[128,2048]{1,0:T(8,128)(2,1)S(1)}, bf16[128,2048]{1,0:T(8,128)(2,1)S(1)}, u32[]{:S(2)}, u32[]{:S(2)}) collective-permute-start(bf16[128,2048]{1,0:T(8,128)(2,1)S(1)} %fusion.13), channel_id=1, source_target_pairs={{0,8},{4,12},{8,16},{12,20},{16,24},{20,28},{24,0},{28,4},{1,9},{5... | collective-permute-start | bytes 1572872 | tf_op jit(solution)/shard_map/ppermute | solution.py:59
  776.8 40.6 %collective-permute-start.75 = (bf16[128,2048]{1,0:T(8,128)(2,1)S(1)}, bf16[128,2048]{1,0:T(8,128)(2,1)S(1)}, u32[]{:S(2)}, u32[]{:S(2)}) collective-permute-start(bf16[128,2048]{1,0:T(8,128)(2,1)S(1)} %get-tuple-element.284), channel_id=1, source_target_pairs={{0,8},{4,12},{8,16},{12,20},{16,24},{20,28},{24,0},{28,4},{1,9},{5... | collective-permute-start | bytes 1572872 | tf_op jit(solution)/shard_map/ppermute | solution.py:59
  (92 other events, 1706.3 us)
Sparse Core Ops, SparseCore 0:
  93.1 123.0 all-gather.5
  218.3 112.1 all-gather.3
  600.3 147.8 reduce-scatter.1

commit v3 on v2

--- a/solution.py
+++ b/solution.py
@@ -73,23 +73,46 @@
     return lax.dynamic_index_in_dim(parts, at, 0, False)
 
 
-def together(*plans):
-    results = [None] * len(plans)
-    sent = {i: None for i in range(len(plans))}
-    while sent:
-        waiting = {}
-        for i, value in sent.items():
-            try:
-                waiting[i] = list(plans[i].send(value))
-            except StopIteration as end:
-                results[i] = end.value
-        flat = [v for values in waiting.values() for v in values]
+class Rounds:
+    def __init__(self):
+        self.live, self.results = {}, {}
+
+    def add(self, **plans):
+        for name, plan in plans.items():
+            self.advance(name, plan, None)
+
+    def advance(self, name, plan, value):
+        try:
+            self.live[name] = (plan, list(plan.send(value)))
+        except StopIteration as end:
+            self.live.pop(name, None)
+            self.results[name] = end.value
+
+    def round(self, *also):
+        waiting = list(self.live.items())
+        flat = [v for _, (_, values) in waiting for v in values] + list(also)
         if flat:
             flat = list(lax.optimization_barrier(tuple(flat)))
-        sent = {}
-        for i, values in waiting.items():
-            sent[i] = [flat.pop(0) for _ in values]
-    return results
+        for name, (plan, values) in waiting:
+            self.advance(name, plan, [flat.pop(0) for _ in values])
+        return flat
+
+    def until(self, *names):
+        while any(name in self.live for name in names):
+            self.round()
+        return [self.results[name] for name in names]
+
+
+def together(*plans):
+    rounds = Rounds()
+    names = [str(i) for i in range(len(plans))]
+    rounds.add(**dict(zip(names, plans)))
+    return rounds.until(*names)
+
+
+def idle(count):
+    for _ in range(count):
+        yield []
 
 
 def chain(first, *rest):
@@ -104,20 +127,22 @@
     ring = size // 2
     out = jnp.zeros((size, *value.shape), value.dtype)
     fresh = {0: value}
-    crossed = {}
-    for s in range(1, ring // 2 + 2):
+    crossing = {0: hop(value, axis, 0, 1)}
+    for s in range(1, ring // 2 + 1):
+        arriving = {-s: hop(fresh[1 - s], axis, 1, 0)}
+        if s <= (ring - 1) // 2:
+            arriving[s] = hop(fresh[s - 1], axis, -1, 0)
+        got = yield [*arriving.values(), *crossing.values()]
+        for at, piece in zip(crossing, got[len(arriving) :]):
+            out = place(out, piece, near(axis, at, 1))
+        fresh = dict(zip(arriving, got))
         for at, piece in fresh.items():
             out = place(out, piece, near(axis, at, 0))
-            crossed[at] = hop(piece, axis, 0, 1)
-        arriving = {}
-        if s <= ring // 2:
-            arriving[-s] = hop(fresh[1 - s], axis, 1, 0)
-        if s <= (ring - 1) // 2:
-            arriving[s] = hop(fresh[s - 1], axis, -1, 0)
-        if arriving:
-            fresh = dict(zip(arriving, (yield list(arriving.values()))))
-    landed = dict(zip(crossed, (yield list(crossed.values()))))
-    for at, piece in landed.items():
+        crossing = {at: hop(piece, axis, 0, 1) for at, piece in fresh.items()}
+        if s == 1:
+            out = place(out, value, near(axis, 0, 0))
+    got = yield list(crossing.values())
+    for at, piece in zip(crossing, got):
         out = place(out, piece, near(axis, at, 1))
     return out
 
@@ -125,26 +150,44 @@
 def scatter_plan(parts, axis):
     ring = lax.axis_size(axis) // 2
     far, back = ring // 2, (ring - 1) // 2
-    order = []
-    for s in range(far, 0, -1):
-        order.append((s, 1))
-        if s <= back:
-            order.append((s, -1))
-    crossing = {
-        s * way: hop(pick(parts, near(axis, s * way, 1)), axis, 0, 1) for s, way in order
-    }
-    crossing[0] = hop(pick(parts, near(axis, 0, 1)), axis, 0, 1)
-    carried = {1: None, -1: None}
-    for s, way in order:
-        wait = [crossing[s * way]] + ([] if carried[way] is None else [carried[way]])
-        total = pick(parts, near(axis, s * way, 0)).astype(f32)
-        for piece in (yield wait):
-            total = total + piece.astype(f32)
-        carried[way] = hop(total.astype(bf), axis, way, 0)
-    total = pick(parts, near(axis, 0, 0)).astype(f32)
-    for piece in (yield [crossing[0]] + [v for v in carried.values() if v is not None]):
-        total = total + piece.astype(f32)
-    return total
+
+    def column(offsets, fast):
+        return jnp.stack([pick(parts, near(axis, s, fast)) for s in offsets])
+
+    steps = [[s] + ([-s] if s <= back else []) for s in range(far, 0, -1)]
+    if ring == 4:
+        steps = [[2, -1], [1]]
+    steps[-1] = steps[-1] + [0]
+    up = down = None
+    for offsets in steps:
+        crossed = hop(column(offsets, 1), axis, 0, 1)
+        got = yield [crossed, *[v for v in (up, down) if v is not None]]
+        crossed, carried = got[0], got[1:]
+        totals = {
+            s: pick(parts, near(axis, s, 0)).astype(f32) + crossed[k].astype(f32)
+            for k, s in enumerate(offsets)
+        }
+        if up is not None:
+            up = carried.pop(0).astype(f32)
+        if down is not None:
+            down = carried.pop(0).astype(f32)
+        ups = [s for s in offsets if s > 0]
+        downs = [s for s in offsets if s < 0]
+        held = down
+        if ups:
+            total = totals[ups[0]] if up is None else totals[ups[0]] + up
+            up = hop(total.astype(bf), axis, 1, 0)
+        if downs:
+            total = totals[downs[0]] if down is None else totals[downs[0]] + down
+            down = hop(total.astype(bf), axis, -1, 0)
+            held = None
+        own = totals.get(0)
+    if held is not None:
+        own = own + held
+        down = None
+    for piece in (yield [v for v in (up, down) if v is not None]):
+        own = own + piece.astype(f32)
+    return own
 
 
 def swap_plan(parts, axis):
@@ -162,36 +205,33 @@
     return out.reshape(parts.shape)
 
 
-def exchange(part, axis):
-    got, places = [], []
-    for slow in range(lax.axis_size(axis) // 2):
-        for fast in range(2):
-            piece = part(near(axis, slow, fast))
-            got.append(hop(piece, axis, slow, fast) if slow or fast else piece)
-            places.append(near(axis, -slow, fast))
-    return got, places
-
-
 def gather_near_plan(value, axis, spare=0):
     ring = lax.axis_size(axis) // 2
     crossed = [hop(value, axis, 0, 1)]
     got = [hop(value, axis, s, 0) for s in range(1, ring)]
-    for _ in range(spare):
-        yield []
+    yield from idle(spare)
     got = yield got
     crossed += [hop(piece, axis, 0, 1) for piece in got]
     crossed = yield crossed
     return [value, *got, *crossed]
 
 
-def scatter_near_plan(parts, axis):
+def scatter_near_plan(parts, axis, spare=0):
     ring = lax.axis_size(axis) // 2
     crossed = yield [hop(part, axis, 0, 1) for part in parts[ring:]]
     sums = [mine.astype(f32) + piece.astype(f32) for mine, piece in zip(parts, crossed)]
-    total = sums[0]
-    for piece in (yield [hop(sums[s].astype(bf), axis, -s, 0) for s in range(1, ring)]):
+    total = sums[0].astype(bf)
+    total, *given = yield [total, *[part.astype(bf) for part in sums[1:]]]
+    got = [hop(part, axis, -s, 0) for s, part in enumerate(given, 1)]
+    yield from idle(spare)
+    total = total.astype(f32)
+    for piece in (yield got):
         total = total + piece.astype(f32)
     return total.astype(bf)
+
+
+def swap(parts, axis):
+    return lax.all_to_all(parts, axis, 0, 0, tiled=True)
 
 
 def gather(value, axis):
@@ -381,6 +421,8 @@
 
 def attend_back_kernel(
     tile,
+    first_ref,
+    clear_ref,
     segk_ref,
     segq_ref,
     posq_ref,
@@ -400,7 +442,8 @@
     nq = segq_ref.shape[0]
     width = nu * tok
     rows = tile * tok
-    chunk = pl.program_id(1)
+    chunk = pl.program_id(0)
+    nb = pl.num_programs(0)
     scale = jnp.asarray(1.0 / math.sqrt(HD), bf)
 
     @pl.when(chunk == 0)
@@ -424,18 +467,20 @@
     k = kv_ref[:, 0, 0].reshape(width, LANES)
     v = kv_ref[:, 1, 0].reshape(width, LANES)
 
-    def step(j, state):
+    def step(masked, j, state):
         dk, dv = state
         at = pl.ds(pl.multiple_of(j * rows, rows), rows)
         q = q_ref[at, :] * scale
         do = do_ref[at, :]
-        ok = allowed_block(segk_ref, segq_ref[j], posq_ref[j], chunk, width)
+        if masked:
+            ok = allowed_block(segk_ref, segq_ref[j], posq_ref[j], chunk, width)
         parts = []
         for h in range(2):
             mine = head_lanes(rows, h)
             q_h = jnp.where(mine, q, jnp.zeros_like(q))
             do_h = jnp.where(mine, do, jnp.zeros_like(do))
-            p = jnp.exp(jnp.where(ok, dot_t(k, q_h) - lse_ref[0, j, h : h + 1], NEG))
+            s = dot_t(k, q_h) - lse_ref[0, j, h : h + 1]
+            p = jnp.exp(jnp.where(ok, s, NEG) if masked else s)
             ds = (p * (dot_t(v, do_h) - delta_ref[j, h : h + 1])).astype(bf)
             dv = dv + dot_n(p.astype(bf), do_h)
             dk = dk + dot_n(ds, q_h)
@@ -444,50 +489,58 @@
         return dk, dv
 
     zero = jnp.zeros((width, LANES), f32)
-    dk, dv = lax.fori_loop(chunk // tile, nq, step, (zero, zero))
+    dk, dv = lax.fori_loop(chunk // tile, nq, functools.partial(step, True), (zero, zero))
     dkv_ref[:, 0, 0] = dk.astype(bf).reshape(nu, tok, LANES)
     dkv_ref[:, 1, 0] = dv.astype(bf).reshape(nu, tok, LANES)
 
-    @pl.when(chunk == pl.num_programs(1) - 1)
+    @pl.when(chunk == nb - 1)
     def _():
         dq = acc_ref[...] * (1.0 / math.sqrt(HD))
         dq_ref[...] = (dq * cos_ref[...] - turned(dq) * sin_ref[...]).astype(bf)
 
 
-def attend_back(segments, seg_q, pos_q, cosine, sine, q, do, o, lse, kv, tile):
-    nu, _, nb, tok, feats = kv.shape
+def attend_back(where, cosine, sine, q, do, o, lse, kv, pair, tile):
+    nu, _, nb, tok, _ = kv.shape
+    first, clear, segments, seg_q, pos_q = where
     rows = tile * tok
     nq = nb // tile
-    pairs = feats // LANES
     whole_rows = full((nq, 1, rows))
     table = full((nb * tok, LANES))
-    q_spec = pl.BlockSpec((nb * tok, LANES), lambda p, c: (0, p))
-    kv_spec = pl.BlockSpec((nu, 2, 1, tok, LANES), lambda p, c: (0, 0, c, 0, p))
+    pair_spec = pl.BlockSpec((nb * tok, LANES), lambda c, *_: (0, pair))
     return pl.pallas_call(
         functools.partial(attend_back_kernel, tile),
-        grid=(pairs, nb),
-        in_specs=[
-            full(segments.shape),
-            whole_rows,
-            whole_rows,
-            table,
-            table,
-            q_spec,
-            q_spec,
-            q_spec,
-            pl.BlockSpec((1, nq, 2, rows), lambda p, c: (p, 0, 0, 0)),
-            kv_spec,
-        ],
-        out_specs=[q_spec, kv_spec],
+        grid_spec=pltpu.PrefetchScalarGridSpec(
+            num_scalar_prefetch=2,
+            grid=(nb,),
+            in_specs=[
+                full(segments.shape),
+                whole_rows,
+                whole_rows,
+                table,
+                table,
+                pair_spec,
+                pair_spec,
+                pair_spec,
+                pl.BlockSpec((1, nq, 2, rows), lambda c, *_: (pair, 0, 0, 0)),
+                pl.BlockSpec((nu, 2, 1, tok, LANES), lambda c, *_: (0, 0, c, 0, pair)),
+            ],
+            out_specs=[
+                table,
+                pl.BlockSpec((nu, 2, 1, tok, LANES), lambda c, *_: (0, 0, c, 0, 0)),
+            ],
+            scratch_shapes=[
+                pltpu.VMEM((nb * tok, LANES), f32),
+                pltpu.VMEM((nq, 8, rows), f32),
+            ],
+        ),
         out_shape=[
-            jax.ShapeDtypeStruct((nb * tok, feats), bf),
-            jax.ShapeDtypeStruct((nu, 2, nb, tok, feats), bf),
-        ],
-        scratch_shapes=[pltpu.VMEM((nb * tok, LANES), f32), pltpu.VMEM((nq, 8, rows), f32)],
-        compiler_params=params(),
-        cost_estimate=cost(50 * nb * tok * nb / 8192),
+            jax.ShapeDtypeStruct((nb * tok, LANES), bf),
+            jax.ShapeDtypeStruct((nu, 2, nb, tok, LANES), bf),
+        ],
+        compiler_params=params(),
+        cost_estimate=cost(25 * nb * tok * nb / 8192),
         name="attend_back",
-    )(segments, seg_q, pos_q, cosine, sine, q, do, o, lse, kv)
+    )(first, clear, segments, seg_q, pos_q, cosine, sine, q, do, o, lse, kv)
 
 
 def output_kernel(x_ref, o_ref, w_ref, gain_ref, x1_ref, normed_ref):
@@ -555,18 +608,21 @@
     )(d_attn, w_out)
 
 
-def project_back_kernel(
-    piece, x_ref, w_ref, cos_ref, sin_ref, dq_ref, dkv_ref, dk_ref, dn_ref, gain_ref
-):
+def project_back_kernel(piece, n, x_ref, w_ref, cos_ref, sin_ref, *refs):
+    dq_refs, dkv_refs, (all_ref, dn_ref, gain_ref) = refs[:n], refs[n : 2 * n], refs[2 * n :]
     blocks, width = w_ref.shape[1], w_ref.shape[3]
-    feats = dq_ref.shape[1]
+    feats = n * LANES
     cosine, sine = wide(cos_ref[...], feats), wide(sin_ref[...], feats)
-    dk = dkv_ref[0].astype(f32)
-    dk = (dk * cosine - turned(dk) * sine).astype(bf)
-    dk_ref[...] = dk
+    dk = jnp.concatenate([ref[0] for ref in dkv_refs], axis=1).astype(f32)
+    parts = (
+        jnp.concatenate([ref[...] for ref in dq_refs], axis=1),
+        (dk * cosine - turned(dk) * sine).astype(bf),
+        jnp.concatenate([ref[1] for ref in dkv_refs], axis=1),
+    )
+    for i in range(3):
+        all_ref[i] = parts[i]
     x = x_ref[...].astype(f32)
     r1 = rms_scale(x)
-    parts = (dq_ref[...], dk, dkv_ref[1])
 
     @pl.when(pl.program_id(0) == 0)
     def _():
@@ -583,40 +639,45 @@
 
 def project_back(x_all, w, cosine, sine, dq, dkv, piece, rows):
     count, dim = x_all.shape
-    feats = dq.shape[1]
-    tiled = lambda n: pl.BlockSpec((rows, n), lambda i: (i, 0))
-    return pl.pallas_call(
-        functools.partial(project_back_kernel, piece),
+    n = len(dq)
+    feats = n * LANES
+    tiled = lambda width: pl.BlockSpec((rows, width), lambda i: (i, 0))
+    return pl.pallas_call(
+        functools.partial(project_back_kernel, piece, n),
         grid=(count // rows,),
         in_specs=[
             tiled(dim),
             full(w.shape),
             tiled(LANES),
             tiled(LANES),
-            tiled(feats),
-            pl.BlockSpec((2, rows, feats), lambda i: (0, i, 0)),
-        ],
-        out_specs=[tiled(feats), tiled(dim), full((1, dim))],
+            *[tiled(LANES)] * n,
+            *[pl.BlockSpec((2, rows, LANES), lambda i: (0, i, 0))] * n,
+        ],
+        out_specs=[
+            pl.BlockSpec((3, rows, feats), lambda i: (0, i, 0)),
+            tiled(dim),
+            full((1, dim)),
+        ],
         out_shape=[
-            jax.ShapeDtypeStruct((count, feats), bf),
+            jax.ShapeDtypeStruct((3, count, feats), bf),
             jax.ShapeDtypeStruct((count, dim), bf),
             jax.ShapeDtypeStruct((1, dim), f32),
         ],
         compiler_params=params(),
         cost_estimate=cost(count * 0.01),
         name="project_back",
-    )(x_all, w, cosine, sine, dq, dkv)
-
-
-def projection_grads_kernel(pieces, n, *refs):
-    lefts, (right_ref, gain_ref, out_ref, turned_ref) = refs[:n], refs[n:]
+    )(x_all, w, cosine, sine, *dq, *dkv)
+
+
+def projection_grads_kernel(left_ref, right_ref, gain_ref, out_ref, turned_ref):
+    n, feats, _ = turned_ref.shape
+    pieces = out_ref.shape[0]
 
     @pl.when(pl.program_id(0) == 0)
     def _():
         for i in range(n):
-            turned_ref[i] = lefts[i][...].T
-
-    feats = turned_ref.shape[1]
+            turned_ref[i] = left_ref[i].T
+
     piece = feats // pieces
     right = right_ref[...]
     width = right.shape[1]
@@ -629,15 +690,14 @@
 
 
 def projection_grads(lefts, right, gain, pieces, width):
-    n = len(lefts)
-    count, feats = lefts[0].shape
+    n, count, feats = lefts.shape
     dim = right.shape[1]
     rows = n * (feats // pieces) + PAD
     return pl.pallas_call(
-        functools.partial(projection_grads_kernel, pieces, n),
+        projection_grads_kernel,
         grid=(dim // width,),
-        in_specs=[full((count, feats))] * n
-        + [
+        in_specs=[
+            full(lefts.shape),
             pl.BlockSpec((count, width), lambda i: (0, i)),
             pl.BlockSpec((PAD, width), lambda i: (0, i)),
         ],
@@ -647,7 +707,7 @@
         compiler_params=params(),
         cost_estimate=cost(2.5 * n),
         name="projection_grads",
-    )(*lefts, right, gain)
+    )(lefts, right, gain)
 
 
 def output_grads_kernel(o_ref, d_ref, out_ref):
@@ -699,61 +759,30 @@
     )(w_gate, w_up, w_down)
 
 
-def assemble_kernel(n, at_ref, *refs):
-    rows = refs[0].shape[1]
+def finish_kernel(in_ref, *outs):
+    n, _, _, width = in_ref.shape
     for k in range(n):
-        at = pl.ds(pl.multiple_of(at_ref[k] * rows, rows), rows)
-        refs[n][:, at, :] = refs[k][...]
-
-
-def assemble(parts, places):
-    n = len(parts)
-    _, rows, width = parts[0].shape
-    return pl.pallas_call(
-        functools.partial(assemble_kernel, n),
-        grid_spec=pltpu.PrefetchScalarGridSpec(
-            num_scalar_prefetch=1,
-            grid=(1,),
-            in_specs=[full(parts[0].shape)] * n,
-            out_specs=full((3, n * rows, width)),
-        ),
-        out_shape=jax.ShapeDtypeStruct((3, n * rows, width), bf),
-        compiler_params=params(),
-        cost_estimate=cost(4),
-        name="assemble",
-    )(jnp.stack(places).astype(jnp.int32), *parts)
-
-
-def finish_kernel(n, at_ref, *refs):
-    width = refs[0].shape[2]
-    for k in range(n):
-        at = pl.ds(pl.multiple_of(at_ref[k] * width, width), width)
         for i in range(3):
-            refs[n + i][:, at] = refs[k][i].astype(f32)
-
-
-def finish(parts, places):
-    n = len(parts)
-    _, rows, width = parts[0].shape
+            outs[i][:, k * width : (k + 1) * width] = in_ref[k, i].astype(f32)
+
+
+def finish(parts):
+    n, _, rows, width = parts.shape
     if width % LANES:
-        out = jnp.zeros((n, *parts[0].shape), bf)
-        for part, at in zip(parts, places):
-            out = place(out, part, at)
-        out = jnp.transpose(out, (1, 2, 0, 3)).reshape(3, rows, n * width).astype(f32)
+        out = jnp.transpose(parts, (1, 2, 0, 3)).reshape(3, rows, n * width).astype(f32)
         return [out[i] for i in range(3)]
     return pl.pallas_call(
-        functools.partial(finish_kernel, n),
-        grid_spec=pltpu.PrefetchScalarGridSpec(
-            num_scalar_prefetch=1,
-            grid=(1,),
-            in_specs=[full(parts[0].shape)] * n,
-            out_specs=[full((rows, n * width))] * 3,
-        ),
+        finish_kernel,
         out_shape=[jax.ShapeDtypeStruct((rows, n * width), f32)] * 3,
         compiler_params=params(),
         cost_estimate=cost(5),
         name="finish",
-    )(jnp.stack(places).astype(jnp.int32), *parts)
+    )(parts)
+
+
+def whole_weight(ref, k):
+    w = ref[:, k]
+    return w.reshape(w.shape[0] * w.shape[1], w.shape[2])
 
 
 def hidden_kernel(n, *refs):
@@ -762,9 +791,9 @@
     normed, cot = n_ref[...], g_ref[...]
     for i in range(n):
         w_ref = refs[2 + i]
-        gate = dot_n(normed, w_ref[0])
-        up = dot_n(normed, w_ref[1])
-        d_act = dot_n(cot, w_ref[2])
+        gate = dot_n(normed, whole_weight(w_ref, 0))
+        up = dot_n(normed, whole_weight(w_ref, 1))
+        d_act = dot_n(cot, whole_weight(w_ref, 2))
         sigma = jax.nn.sigmoid(gate)
         silu = gate * sigma
         act_ref[i] = (silu * up).astype(bf)
@@ -775,7 +804,7 @@
 def hidden(normed, cot, weights, rows):
     count, dim = normed.shape
     n = len(weights)
-    width = weights[0].shape[2]
+    width = weights[0].shape[3]
     tiled = pl.BlockSpec((rows, dim), lambda i: (i, 0))
     out = pl.BlockSpec((n, rows, width), lambda i: (0, i, 0))
     return pl.pallas_call(
@@ -795,14 +824,17 @@
     total = 0.0
     for k in range(len(which)):
         for i in range(n):
-            total = total + dot_t(lefts[k][i], weights[i][k])
+            total = total + dot_t(lefts[k][i], whole_weight(weights[i], k))
     out_ref[...] = total.astype(bf)
 
 
 def mix(lefts, weights, which, rows):
     n, count, width = lefts[0].shape
-    dim = weights[0].shape[1]
-    chosen = pl.BlockSpec((len(which), dim, width), lambda i: (which[0] // len(which), 0, 0))
+    blocks, _, rows_w, _ = weights[0].shape
+    dim = blocks * rows_w
+    chosen = pl.BlockSpec(
+        (blocks, len(which), rows_w, width), lambda i: (0, which[0] // len(which), 0, 0)
+    )
     return pl.pallas_call(
         functools.partial(mix_kernel, which, n),
         grid=(count // rows,),
@@ -819,21 +851,23 @@
 def hidden_grads_kernel(n_ref, g_ref, dg_ref, du_ref, act_ref, *outs):
     normed, cot = n_ref[...].T, g_ref[...].T
     for i, out_ref in enumerate(outs):
-        out_ref[0] = dot_n(normed, dg_ref[i]).astype(bf)
-        out_ref[1] = dot_n(normed, du_ref[i]).astype(bf)
-        out_ref[2] = dot_n(cot, act_ref[i]).astype(bf)
-
-
-def hidden_grads(normed, cot, d_gate, d_up, act, block):
+        for k, grad in enumerate(
+            (dot_n(normed, dg_ref[i]), dot_n(normed, du_ref[i]), dot_n(cot, act_ref[i]))
+        ):
+            out_ref[:, k] = grad.astype(bf).reshape(out_ref.shape[0], *out_ref.shape[2:])
+
+
+def hidden_grads(normed, cot, d_gate, d_up, act, rows):
     count, dim = normed.shape
+    block = max(rows, LANES)
     n, _, width = act.shape
     columns = pl.BlockSpec((count, block), lambda i: (0, i))
     return pl.pallas_call(
         hidden_grads_kernel,
         grid=(dim // block,),
         in_specs=[columns, columns] + [full(act.shape)] * 3,
-        out_specs=[pl.BlockSpec((3, block, width), lambda i: (0, i, 0))] * n,
-        out_shape=[jax.ShapeDtypeStruct((3, dim, width), bf)] * n,
+        out_specs=[pl.BlockSpec((block // rows, 3, rows, width), lambda i: (i, 0, 0, 0))] * n,
+        out_shape=[jax.ShapeDtypeStruct((dim // rows, 3, rows, width), bf)] * n,
         compiler_params=params(),
         cost_estimate=cost(25),
         name="hidden_grads",
@@ -883,24 +917,42 @@
     angles = (index - first).astype(f32)[:, None] * freq[None, :]
     cosine = jnp.cos(angles)
     sine = jnp.sin(angles) * jnp.where(lane % HD < HD // 2, -1.0, 1.0)[None, :]
-    seg_col = segments[:, None]
-    seg_rows = seg_mine.reshape(nb // tile, 1, tile * tok)
-    pos_rows = index.reshape(nb // tile, 1, tile * tok)
+    width = nu * tok
+    rows_q = tile * tok
+    seg_rows = seg_mine.reshape(nb // tile, 1, rows_q)
+    pos_rows = index.reshape(nb // tile, 1, rows_q)
+    seg_k = segments.reshape(nb, width)
+    low_q, high_q = seg_rows[:, 0, :1], seg_rows[:, 0, -1:]
+    first_chunk = jnp.sum((seg_k[None, :, -1] < low_q).astype(jnp.int32), axis=1)
+    clear = (
+        (low_q == high_q)
+        & (seg_k[None, :, 0] == low_q)
+        & (seg_k[None, :, -1] == low_q)
+        & (jnp.arange(1, nb + 1, dtype=jnp.int32)[None, :] * width <= pos_rows[:, 0, :1])
+    )
+    where = (first_chunk, clear.astype(jnp.int32).reshape(-1), segments[:, None], seg_rows, pos_rows)
 
     ff_u = w_gate.shape[1]
     ff_piece = ff_u // nb
     tokens_plan = gather_plan(tokens, "blk")
 
     def prepared():
+        yield []
         (value,) = yield [prepare(w_gate, w_up, w_down, nb)]
         return value
+
+    def swapped(parts, spare=0):
+        got = swap(parts, "blk")
+        yield from idle(spare)
+        (got,) = yield [got]
+        return got
 
     if strided:
         sent, out_flipped = flip(w_query, w_key, w_value, w_output, attn_gain, mlp_gain, nb)
         x_all, ff_sent, w_qkv = together(
             tokens_plan,
             prepared(),
-            chain(swap_plan(sent, "blk"), lambda got: gather_plan(got, "uly")),
+            chain(swapped(sent, 1), lambda got: gather_plan(got, "uly")),
         )
     else:
         gains = jnp.stack([attn_gain, mlp_gain]).astype(bf)
@@ -908,7 +960,7 @@
         out_flipped = flipped[3]
         sent = gather(jnp.stack(flipped[:3])[None], "uly")
         sent = jnp.transpose(sent, (0, 2, 1, 3)).reshape(nb, group, 3, rows)
-        x_all, ff_sent, got = together(tokens_plan, prepared(), swap_plan(sent, "blk"))
+        x_all, ff_sent, got = together(tokens_plan, prepared(), swapped(sent))
         got = jnp.transpose(got, (2, 1, 0, 3)).reshape(3, group, dim)
         got = jnp.pad(got, ((0, 0), (0, piece - group), (0, 0))).reshape(3 * piece, dim)
         all_gains = jnp.transpose(gather(gains[None], "blk"), (1, 0, 2)).reshape(2, dim)
@@ -919,8 +971,7 @@
         w_qkv[0, :, 3 * piece + i, :].reshape(1, dim).astype(f32) for i in range(2)
     ]
 
-    ff_sent = after(ff_sent, x_all)
-    ff_got, ff_places = exchange(lambda i: pick(ff_sent, i), "blk")
+    ff_got = swap(after(ff_sent, x_all), "blk")
     w_out = gather(after(out_flipped, x_all)[None], both)
     cot_all = gather(after(cotangent, x_all, w_out), "blk")
     if strided:
@@ -934,24 +985,36 @@
 
     q, kv, normed = project(x_all, w_qkv, cosine, sine, piece, step)
     (kv_all,) = together(gather_plan(kv.reshape(2, nb, tok, feats), "uly"))
-    o, lse = attend(seg_col, seg_rows, pos_rows, q, kv_all, tile)
-    *ff_got, o = lax.optimization_barrier((*ff_got, o))
-    w_ff, o_all = together(
-        gather_near_plan(assemble(ff_got, ff_places), "uly", nb // 4), gather_plan(o, "blk")
-    )
+    o, lse = attend(*where[2:], q, kv_all, tile)
+    ff_got, o = lax.optimization_barrier((ff_got, o))
+    rounds = Rounds()
+    rounds.add(o=gather_plan(o, "blk"), ff=gather_near_plan(ff_got, "uly", nb // 4))
+    (o_all,) = rounds.until("o")
     x1, normed2 = output_project(x_all, o_all, w_out, gain2, step)
+
+    (w_ff,) = rounds.until("ff")
 
     act, d_gate, d_up = hidden(normed2, cot_all, w_ff, step)
     d_norm2 = mix([d_gate, d_up], w_ff, (0, 1), step)
 
-    def meanwhile():
-        (out,) = yield [mix([after(act, d_norm2)], w_ff, (2,), step)]
-        grads = yield hidden_grads(after(normed2, out), cot_all, d_gate, d_up, act, block)
-        return out, grads
-
-    d_norm2, (mlp_out, ff_grads) = together(
-        scatter_plan(d_norm2.reshape(nb, tok, dim), "blk"), meanwhile()
+    def mlp_plan():
+        (out,) = yield [mix([act], w_ff, (2,), step)]
+        return out
+
+    def hidden_grads_plan():
+        yield []
+        grads = yield hidden_grads(
+            after(normed2, d_norm2), cot_all, d_gate, d_up, act, rows
+        )
+        return (yield from scatter_near_plan(grads, "uly", 2 * nb))
+
+    rounds = Rounds()
+    rounds.add(
+        d_norm2=scatter_plan(d_norm2.reshape(nb, tok, dim), "blk"),
+        mlp=mlp_plan(),
+        ff=hidden_grads_plan(),
     )
+    d_norm2, mlp_out = rounds.until("d_norm2", "mlp")
     x1_own = lax.dynamic_slice_in_dim(x1, b * tok, tok, 0)
     mlp_out = scatter(after(mlp_out, d_norm2), "blk")
     r2_own = rms_scale(x1_own)
@@ -966,51 +1029,50 @@
 
     d_o = output_back(d_attn, w_out)
     d_columns = jnp.transpose(d_attn.reshape(tok, nb, rows), (1, 0, 2))
-    (d_o,) = together(swap_plan(d_o, "blk"))
-    (ff_mine,) = together(scatter_near_plan(ff_grads, "uly"))
-    d_o = d_o.reshape(count, feats)
-    ff_mine = ff_mine.reshape(3, nb, rows, ff_piece)
-    ff_got, ff_places = exchange(lambda i: lax.dynamic_index_in_dim(ff_mine, i, 1, False), "blk")
-    d_got, d_places = exchange(lambda i: pick(d_columns, i), "blk")
-    dq, dkv = attend_back(
-        seg_col, seg_rows, pos_rows, cosine, sine, q, d_o, o, lse, kv_all, tile
-    )
-    *d_got, dkv = lax.optimization_barrier((*d_got, dkv))
-    d_columns = jnp.zeros_like(d_columns)
-    for got, at in zip(d_got, d_places):
-        d_columns = place(d_columns, got, at)
+    rounds.add(d_o=swap_plan(d_o, "blk"))
+    (got,) = rounds.until("d_o")
+    d_o = got.reshape(count, feats)
+    d_columns = swap(after(d_columns, d_o), "blk")
+    pairs = feats // LANES
+    dq = []
+    for pair in range(pairs):
+        dq_pair, dkv = attend_back(where, cosine, sine, q, d_o, o, lse, kv_all, pair, tile)
+        if pair == 0:
+            dkv, d_o, d_columns = lax.optimization_barrier((dkv, d_o, d_columns))
+            (ff_mine,) = rounds.until("ff")
+            ff_mine, d_o, d_columns = lax.optimization_barrier((ff_mine, d_o, d_columns))
+            ff_got = swap(ff_mine, "blk")
+        rounds.add(**{f"dkv{pair}": scatter_plan(dkv, "uly")})
+        dq.append(dq_pair)
+    mlp_out, d_columns = rounds.round(mlp_out, d_columns)
     out_grads = output_grads(o_all, d_columns.reshape(count, rows), pieces)
     if not strided:
         out_grads = out_grads[:, :, :group]
-    dkv, out_grads = together(
-        scatter_plan(dkv, "uly"), scatter_plan(out_grads.reshape(nu, feats_u, rows), "uly")
-    )
-    grad_output = jnp.transpose(out_grads)
-    dkv = dkv.astype(bf).reshape(2, count, feats)
-    *ff_got, dkv = lax.optimization_barrier((*ff_got, dkv))
-    ff_grads = finish(ff_got, ff_places)
-    dk, d_norm1, gain1_part = project_back(x_all, w_qkv, cosine, sine, dq, dkv, piece, step)
+    dkv = rounds.until(*[f"dkv{pair}" for pair in range(pairs)])
+    *dkv, out_grads, ff_got = lax.optimization_barrier((*dkv, out_grads, ff_got))
+    rounds.add(out=scatter_plan(out_grads.reshape(nu, feats_u, rows), "uly"))
+    dkv = [part.astype(bf).reshape(2, count, LANES) for part in dkv]
+    d_qkv, d_norm1, gain1_part = project_back(x_all, w_qkv, cosine, sine, dq, dkv, piece, step)
     gain_parts = jnp.pad(jnp.concatenate([gain1_part, gain2_part]), ((0, PAD - 2), (0, 0)))
-    grads = projection_grads(
-        [dq, dk, dkv[1]], after(normed, d_norm1), gain_parts, pieces, block
-    )
+    grads = projection_grads(d_qkv, after(normed, d_norm1), gain_parts, pieces, block)
     last = scatter_plan(d_norm1.reshape(nb, tok, dim), "blk")
     if strided:
-        d_norm1, got = together(
-            last,
-            chain(
-                scatter_plan(grads, "uly"), lambda mine: swap_plan(mine.astype(bf), "blk")
-            ),
+        rounds.add(
+            last=last,
+            grads=chain(scatter_plan(grads, "uly"), lambda mine: swapped(mine.astype(bf))),
         )
+        d_norm1, got, out_grads = rounds.until("last", "grads", "out")
         gain_sums = jnp.sum(got[:, 3 * piece : 3 * piece + 2].astype(f32), axis=0)
         heads = [got[:, i * piece : (i + 1) * piece].reshape(feats_u, rows) for i in range(3)]
     else:
         wanted = grads[0, :, : 3 * piece].reshape(blocks, 3, piece, block)[:, :, :group]
         wanted = jnp.transpose(wanted, (1, 2, 0, 3)).reshape(3, group, nb, rows)
-        d_norm1, got = together(last, swap_plan(jnp.transpose(wanted, (2, 1, 0, 3)), "blk"))
+        rounds.add(last=last, grads=swapped(jnp.transpose(wanted, (2, 1, 0, 3))))
+        d_norm1, got, out_grads = rounds.until("last", "grads", "out")
         got = scatter(got.reshape(nu, feats_u, 3, rows), "uly")[0]
         heads = [got[:, i] for i in range(3)]
         gain_sums = lax.dynamic_slice_in_dim(lax.psum(gain_parts[:2], both), b * rows, rows, 1)
+    grad_output = jnp.transpose(out_grads)
     grad_query, grad_key, grad_value = [jnp.transpose(h).astype(f32) for h in heads]
     x_own = tokens.astype(f32)
     r1_own = rms_scale(x_own)
@@ -1020,7 +1082,6 @@
         + r1_own * z_one
         - x_own * r1_own * r1_own * r1_own * jnp.mean(z_one * x_own, axis=-1, keepdims=True)
     )
-    mlp_out, d_norm1 = lax.optimization_barrier((mlp_out, d_norm1))
     output = x1_own + mlp_out.astype(f32)
     return (
         output,
@@ -1031,7 +1092,7 @@
         grad_value,
         grad_output,
         gain_sums[1],
-        *ff_grads,
+        *finish(ff_got),
     )
 
 

time: 847 us -> 737 us (0.87)
  starting transfers between devices: 148 us -> 67.8 us
  waiting for transfers between devices: 331 us -> 278 us
  other arithmetic: 46.9 us -> 71.6 us
    ppermute x82 -> x48, starting transfers between devices: 148 us -> 46.4 us  [hop(): return lax.ppermute(value, axis, pairs)]
    ppermute x82 -> x48, waiting for transfers between devices: 331 us -> 265 us  [hop(): return lax.ppermute(value, axis, pairs)]
    all_to_all x0 -> x5, starting transfers between devices: none -> 21.3 us  [swap(): return lax.all_to_all(parts, axis, 0, 0, tiled=True)]
    squeeze x8 -> x1, local copies, waits for them, and re-layouts: 13.3 us -> 0.97 us  [pick(): return lax.dynamic_index_in_dim(parts, at, 0, False)]
    unnamed x92 -> x100, local copies, waits for them, and re-layouts: 8.87 us -> 18.4 us
    another operation x0 -> x8, other arithmetic: none -> 9.02 us  [column(): return jnp.stack([pick(parts, near(axis, s, fast)) for s in offsets])]
    convert_element_type x9 -> x11, other arithmetic: 16.9 us -> 21.5 us  [the longest x6 9.88 us: scatter_plan(): up = hop(total.astype(bf), axis, 1, 0)]
    dynamic_update_slice x41 -> x27, local copies, waits for them, and re-layouts: 18 us -> 17 us  [place(): return lax.dynamic_update_slice_in_dim(out, piece[None], at, 0)]
  transfers between devices with their start and end apart: 85 -> 56, of which waited for: 30 -> 33; matrix products, arithmetic and copies ran while one was open for 10% -> 13% of each run, Pallas kernels for 24% -> 25%
where the time goes in v3:
time: 737 us; the launch traced here: 727 us
  waiting for transfers between devices  278 us (38%)
  Pallas kernels  237 us (32%)
  other arithmetic  71.6 us (10%)
  starting transfers between devices  67.8 us (9%)
  local copies, waits for them, and re-layouts  58.5 us (8%)
  between operations  15.1 us (2%)
    ppermute x48, waiting for transfers between devices, hop(): return lax.ppermute(value, axis, pairs)  265 us
    pallas_call x2, Pallas kernels, attend_back(): pl.pallas_call(functools.partial(attend_back_kernel, tile), grid_spec=plt...  54.1 us
    ppermute x48, starting transfers between devices, hop(): return lax.ppermute(value, axis, pairs)  46.4 us
    pallas_call x1, Pallas kernels, attend(): pl.pallas_call(functools.partial(attend_kernel, tile), grid=(pairs, nq),...  43.8 us
    pallas_call x2, Pallas kernels, mix(): pl.pallas_call(functools.partial(mix_kernel, which, n), grid=(count // ro...  23.1 us
    all_to_all x5, starting transfers between devices, swap(): return lax.all_to_all(parts, axis, 0, 0, tiled=True)  21.3 us
    pallas_call x1, Pallas kernels, hidden(): pl.pallas_call(functools.partial(hidden_kernel, n), grid=(count // rows,)...  20.5 us
    pallas_call x1, Pallas kernels, hidden_grads(): pl.pallas_call(hidden_grads_kernel, grid=(dim // block,), in_specs=[colum...  18.8 us
  transfers between devices with their start and end apart: 56, of which 33 were waited for; matrix products, arithmetic and copies ran while one was open for 13% of the time, Pallas kernels for 25%

profile of v3, /device:TPU:0, one launch (start us, length us, event | category | flops | bytes accessed | tf_op | source)
XLA Modules:
  0.0 727.1 jit_solution(629183662928933166)
XLA Ops:
  28.6 10.0 %collective-permute-done = bf16[128,2048]{1,0:T(8,128)(2,1)S(1)} collective-permute-done((bf16[128,2048]{1,0:T(8,128)(2,1)}, bf16[128,2048]{1,0:T(8,128)(2,1)S(1)}, u32[]{:S(2)}, u32[]{:S(2)}) %collective-permute-start) | collective-permute-done | bytes 524320 | tf_op jit(solution)/shard_map/ppermute | solution.py:59
  47.9 18.3 %collective-permute-done.5 = bf16[128,2048]{1,0:T(8,128)(2,1)S(1)} collective-permute-done((bf16[128,2048]{1,0:T(8,128)(2,1)S(1)}, bf16[128,2048]{1,0:T(8,128)(2,1)S(1)}, u32[]{:S(2)}, u32[]{:S(2)}) %collective-permute-start.5) | collective-permute-done | bytes 524320 | tf_op jit(solution)/shard_map/ppermute | solution.py:59
  72.2 10.4 %collective-permute-done.6 = bf16[128,2048]{1,0:T(8,128)(2,1)S(1)} collective-permute-done((bf16[128,2048]{1,0:T(8,128)(2,1)S(1)}, bf16[128,2048]{1,0:T(8,128)(2,1)S(1)}, u32[]{:S(2)}, u32[]{:S(2)}) %collective-permute-start.6) | collective-permute-done | bytes 524320 | tf_op jit(solution)/shard_map/ppermute | solution.py:59
  103.8 9.5 %project.1 = (bf16[1024,256]{1,0:T(8,128)(2,1)}, bf16[2,1024,256]{2,1,0:T(8,128)(2,1)}, bf16[1024,2048]{1,0:T(8,128)(2,1)}) custom-call(bf16[1024,2048]{1,0:T(8,128)(2,1)} %bitcast.10.x_ref, bf16[4,8,208,256]{3,2,1,0:T(8,128)(2,1)} %copy-done.8, f32[1024,128]{1,0:T(8,128)} %get-tuple-element.260.cos_ref, f32[1024,128]{1,0:T(8,128)} %get-tuple-element.259.sin_ref), custom_call_target="tpu_custom_call" | custom-call | flops 2534400000 | tf_op jit(solution)/shard_map/project/pallas_call | solution.py:292
  116.4 22.8 %collective-permute-done.10 = bf16[2,8,128,256]{3,2,1,0:T(8,128)(2,1)} collective-permute-done((bf16[2,8,128,256]{3,2,1,0:T(8,128)(2,1)}, bf16[2,8,128,256]{3,2,1,0:T(8,128)(2,1)}, u32[]{:S(2)}, u32[]{:S(2)}) %collective-permute-start.10) | collective-permute-done | bytes 1048608 | tf_op jit(solution)/shard_map/ppermute | solution.py:59
  148.7 43.8 %attend.1 = (bf16[1024,256]{1,0:T(8,128)(2,1)}, f32[2,4,2,256]{3,2,1,0:T(2,128)}) custom-call(s32[4096,1]{1,0:T(8,128)} %copy.56.segk_ref, s32[4,1,256]{2,1,0:T(1,128)} %bitcast.212, s32[4,1,256]{2,1,0:T(1,128)} %broadcast_add_fusion.posq_ref, bf16[1024,256]{1,0:T(8,128)(2,1)} %get-tuple-element.126.q_ref, bf16[4,2,8,128,256]{4,3,2,1,0:T(8,128)(2,1)} %copy-done.6), custom_call_target="tpu_custom_call" | custom-call | flops 12099999744 | tf_op jit(solution)/shard_map/attend/pallas_call | solution.py:400
  199.3 9.1 %collective-permute-done.15 = bf16[1024,256]{1,0:T(8,128)(2,1)S(1)} collective-permute-done((bf16[1024,256]{1,0:T(8,128)(2,1)}, bf16[1024,256]{1,0:T(8,128)(2,1)S(1)}, u32[]{:S(2)}, u32[]{:S(2)}) %collective-permute-start.15) | collective-permute-done | bytes 524320 | tf_op jit(solution)/shard_map/ppermute | solution.py:59
  208.4 8.7 %collective-permute-done.14 = bf16[1024,256]{1,0:T(8,128)(2,1)S(1)} collective-permute-done((bf16[1024,256]{1,0:T(8,128)(2,1)}, bf16[1024,256]{1,0:T(8,128)(2,1)S(1)}, u32[]{:S(2)}, u32[]{:S(2)}) %collective-permute-start.14) | collective-permute-done | bytes 524320 | tf_op jit(solution)/shard_map/ppermute | solution.py:59
  217.1 12.0 %collective-permute-done.13 = bf16[1024,256]{1,0:T(8,128)(2,1)S(1)} collective-permute-done((bf16[1024,256]{1,0:T(8,128)(2,1)}, bf16[1024,256]{1,0:T(8,128)(2,1)S(1)}, u32[]{:S(2)}, u32[]{:S(2)}) %collective-permute-start.13) | collective-permute-done | bytes 524320 | tf_op jit(solution)/shard_map/ppermute | solution.py:59
  231.3 18.3 %collective-permute-done.18 = bf16[1024,256]{1,0:T(8,128)(2,1)S(1)} collective-permute-done((bf16[1024,256]{1,0:T(8,128)(2,1)S(1)}, bf16[1024,256]{1,0:T(8,128)(2,1)S(1)}, u32[]{:S(2)}, u32[]{:S(2)}) %collective-permute-start.18) | collective-permute-done | bytes 524320 | tf_op jit(solution)/shard_map/ppermute | solution.py:59
  249.6 9.8 %collective-permute-done.17 = bf16[1024,256]{1,0:T(8,128)(2,1)S(1)} collective-permute-done((bf16[1024,256]{1,0:T(8,128)(2,1)S(1)}, bf16[1024,256]{1,0:T(8,128)(2,1)S(1)}, u32[]{:S(2)}, u32[]{:S(2)}) %collective-permute-start.17) | collective-permute-done | bytes 524320 | tf_op jit(solution)/shard_map/ppermute | solution.py:59
  261.1 17.7 %collective-permute-done.19 = bf16[1024,256]{1,0:T(8,128)(2,1)S(1)} collective-permute-done((bf16[1024,256]{1,0:T(8,128)(2,1)S(1)}, bf16[1024,256]{1,0:T(8,128)(2,1)S(1)}, u32[]{:S(2)}, u32[]{:S(2)}) %collective-permute-start.19) | collective-permute-done | bytes 524320 | tf_op jit(solution)/shard_map/ppermute | solution.py:59
  285.5 15.9 %output_project.1 = (f32[1024,2048]{1,0:T(8,128)}, bf16[1024,2048]{1,0:T(8,128)(2,1)}) custom-call(bf16[1024,2048]{1,0:T(8,128)(2,1)} %bitcast.10.x_ref, bf16[8,1024,256]{2,1,0:T(8,128)(2,1)} %copy-done.1, bf16[8,4,8,64,256]{4,3,2,1,0:T(8,128)(2,1)} %bitcast.176, f32[1,2048]{1,0:T(1,128)} %bitcast.202), custom_call_target="tpu_custom_call" | custom-call | flops 4224000000 | tf_op jit(solution)/shard_map/output_project/pallas_call | solution.py:564
  301.4 6.9 all-gather.4.cloned.1.call-done.refs_1_.g_ref
  308.3 20.5 %hidden.1 = (bf16[4,1024,256]{2,1,0:T(8,128)(2,1)}, bf16[4,1024,256]{2,1,0:T(8,128)(2,1)}, bf16[4,1024,256]{2,1,0:T(8,128)(2,1)}) custom-call(bf16[1024,2048]{1,0:T(8,128)(2,1)} %get-tuple-element.152.refs_0_.n_ref, bf16[1024,2048]{1,0:T(8,128)(2,1)} %all-gather.4.cloned.1.call-done.refs_1_.g_ref, bf16[8,3,256,256]{3,2,1,0:T(8,128)(2,1)} %copy-done, ...), custom_call_target="tpu_custom_call" | custom-call | flops 5500000256 | tf_op jit(solution)/shard_map/hidden/pallas_call | solution.py:810
  328.8 14.4 %mix.2 = bf16[1024,2048]{1,0:T(8,128)(2,1)} custom-call(bf16[4,1024,256]{2,1,0:T(8,128)(2,1)} %get-tuple-element.148.refs_0_.dg_ref, bf16[4,1024,256]{2,1,0:T(8,128)(2,1)} %get-tuple-element.149.refs_1_.du_ref, bf16[8,3,256,256]{3,2,1,0:T(8,128)(2,1)} %copy-done, bf16[8,3,256,256]{3,2,1,0:T(8,128)(2,1)} %collective-permute-done.20.refs_3_.refs_2_, ...), custom_call_target="tpu_custom_call" | custom-call | flops 4400000000 | tf_op jit(solution)/shard_map/mix/pallas_call | solution.py:838
  348.2 8.7 %mix.3 = bf16[1024,2048]{1,0:T(8,128)(2,1)} custom-call(bf16[4,1024,256]{2,1,0:T(8,128)(2,1)} %get-tuple-element.150.refs_0_.act_ref, bf16[8,3,256,256]{3,2,1,0:T(8,128)(2,1)} %copy-done, bf16[8,3,256,256]{3,2,1,0:T(8,128)(2,1)} %collective-permute-done.20.refs_3_.refs_2_, bf16[8,3,256,256]{3,2,1,0:T(8,128)(2,1)} %collective-permute-done.21.refs_4_.refs_3_, ...), custom_call_target="tpu_custom_call" | custom-call | flops 2200000000 | tf_op jit(solution)/shard_map/mix/pallas_call | solution.py:838
  356.8 15.4 %collective-permute-done.24 = bf16[2,128,2048]{2,1,0:T(8,128)(2,1)S(1)} collective-permute-done((bf16[2,128,2048]{2,1,0:T(8,128)(2,1)}, bf16[2,128,2048]{2,1,0:T(8,128)(2,1)S(1)}, u32[]{:S(2)}, u32[]{:S(2)}) %collective-permute-start.24) | collective-permute-done | bytes 1048608 | tf_op jit(solution)/shard_map/ppermute | solution.py:59
  375.9 18.8 %hidden_grads.1 = (bf16[8,3,256,256]{3,2,1,0:T(8,128)(2,1)}, bf16[8,3,256,256]{3,2,1,0:T(8,128)(2,1)}, bf16[8,3,256,256]{3,2,1,0:T(8,128)(2,1)}, bf16[8,3,256,256]{3,2,1,0:T(8,128)(2,1)}) custom-call(bf16[1024,2048]{1,0:T(8,128)(2,1)} %get-tuple-element.152.refs_0_.n_ref, bf16[1024,2048]{1,0:T(8,128)(2,1)} %all-gather.4.cloned.1.call-done.refs_1_.g_ref, ...), custom_call_target="tpu_custom_call" | custom-call | flops 6874999808 | tf_op jit(solution)/shard_map/hidden_grads/pallas_call | solution.py:865
  402.6 13.6 %collective-permute-done.27 = bf16[128,2048]{1,0:T(8,128)(2,1)} collective-permute-done((bf16[128,2048]{1,0:T(8,128)(2,1)}, bf16[128,2048]{1,0:T(8,128)(2,1)}, u32[]{:S(2)}, u32[]{:S(2)}) %collective-permute-start.27) | collective-permute-done | bytes 524320 | tf_op jit(solution)/shard_map/ppermute | solution.py:59
  423.6 8.7 %output_back.1 = bf16[8,128,256]{2,1,0:T(8,128)(2,1)} custom-call(bf16[128,2048]{1,0:T(8,128)(2,1)} %get-tuple-element.223.d_ref, bf16[8,4,8,64,256]{4,3,2,1,0:T(8,128)(2,1)} %bitcast.177), custom_call_target="tpu_custom_call" | custom-call | flops 2200000000 | tf_op jit(solution)/shard_map/output_back/pallas_call | solution.py:596
  453.2 6.8 collective-permute-done.33
  460.9 11.7 %collective-permute-done.32 = bf16[2,128,256]{2,1,0:T(8,128)(2,1)S(1)} collective-permute-done((bf16[2,128,256]{2,1,0:T(8,128)(2,1)}, bf16[2,128,256]{2,1,0:T(8,128)(2,1)S(1)}, u32[]{:S(2)}, u32[]{:S(2)}) %collective-permute-start.32) | collective-permute-done | bytes 131104 | tf_op jit(solution)/shard_map/ppermute | solution.py:59
  481.4 27.1 %attend_back.2 = (bf16[1024,128]{1,0:T(8,128)(2,1)}, bf16[4,2,8,128,128]{4,3,2,1,0:T(8,128)(2,1)}) custom-call(s32[4]{0:T(128)} %convert_reduce_fusion.2.first_ref, s32[32]{0:T(128)} %reshape.326.clear_ref, s32[4096,1]{1,0:T(8,128)} %copy.56.segk_ref, s32[4,1,256]{2,1,0:T(1,128)} %bitcast.213, s32[4,1,256]{2,1,0:T(1,128)} %broadcast_add_fusion.posq_ref, ...), custom_call_target="tpu_custom_call" | custom-call | flops 6874999808 | tf_op jit(solution)/shard_map/attend_back/pallas_call | solution.py:510
  521.7 27.0 %attend_back.3 = (bf16[1024,128]{1,0:T(8,128)(2,1)}, bf16[4,2,8,128,128]{4,3,2,1,0:T(8,128)(2,1)}) custom-call(s32[4]{0:T(128)} %convert_reduce_fusion.2.first_ref, s32[32]{0:T(128)} %reshape.326.clear_ref, s32[4096,1]{1,0:T(8,128)} %copy.56.segk_ref, s32[4,1,256]{2,1,0:T(1,128)} %bitcast.214, s32[4,1,256]{2,1,0:T(1,128)} %broadcast_add_fusion.posq_ref, ...), custom_call_target="tpu_custom_call" | custom-call | flops 6874999808 | tf_op jit(solution)/shard_map/attend_back/pallas_call | solution.py:510
  559.0 7.3 %output_grads.1 = bf16[4,8,64,256]{3,2,1,0:T(8,128)(2,1)} custom-call(bf16[8,1024,256]{2,1,0:T(8,128)(2,1)} %copy-done.1, bf16[1024,256]{1,0:T(8,128)(2,1)} %bitcast.62.d_ref), custom_call_target="tpu_custom_call" | custom-call | flops 1650000000 | tf_op jit(solution)/shard_map/output_grads/pallas_call | solution.py:723
  571.7 10.7 %collective-permute-done.37 = bf16[2,8,128,128]{3,2,1,0:T(8,128)(2,1)S(1)} collective-permute-done((bf16[2,8,128,128]{3,2,1,0:T(8,128)(2,1)S(1)}, bf16[2,8,128,128]{3,2,1,0:T(8,128)(2,1)S(1)}, u32[]{:S(2)}, u32[]{:S(2)}) %collective-permute-start.37) | collective-permute-done | bytes 524320 | tf_op jit(solution)/shard_map/ppermute | solution.py:59
  588.5 11.0 %project_back.1 = (bf16[3,1024,256]{2,1,0:T(8,128)(2,1)}, bf16[1024,2048]{1,0:T(8,128)(2,1)}, f32[1,2048]{1,0:T(1,128)}) custom-call(bf16[1024,2048]{1,0:T(8,128)(2,1)} %bitcast.10.x_ref, bf16[4,8,208,256]{3,2,1,0:T(8,128)(2,1)} %copy-done.8, f32[1024,128]{1,0:T(8,128)} %get-tuple-element.260.cos_ref, f32[1024,128]{1,0:T(8,128)} %get-tuple-element.259.sin_ref, ...), custom_call_target="tpu_custom_call" | custom-call | flops 2816000000 | tf_op jit(solution)/shard_map/project_back/pallas_call | solution.py:645
  600.9 9.7 %projection_grads.1 = bf16[4,8,208,256]{3,2,1,0:T(8,128)(2,1)} custom-call(bf16[3,1024,256]{2,1,0:T(8,128)(2,1)} %get-tuple-element.197.left_ref, bf16[1024,2048]{1,0:T(8,128)(2,1)} %get-tuple-element.199.right_ref, f32[16,2048]{1,0:T(8,128)} %select_maximum_fusion.gain_ref), custom_call_target="tpu_custom_call" | custom-call | flops 2062499968 | tf_op jit(solution)/shard_map/projection_grads/pallas_call | solution.py:696
  626.1 16.0 %collective-permute-done.40 = bf16[2,128,2048]{2,1,0:T(8,128)(2,1)} collective-permute-done((bf16[2,128,2048]{2,1,0:T(8,128)(2,1)}, bf16[2,128,2048]{2,1,0:T(8,128)(2,1)}, u32[]{:S(2)}, u32[]{:S(2)}) %collective-permute-start.40) | collective-permute-done | bytes 1048608 | tf_op jit(solution)/shard_map/ppermute | solution.py:59
  654.5 9.7 %collective-permute-done.43 = bf16[2,128,2048]{2,1,0:T(8,128)(2,1)} collective-permute-done((bf16[2,128,2048]{2,1,0:T(8,128)(2,1)}, bf16[2,128,2048]{2,1,0:T(8,128)(2,1)}, u32[]{:S(2)}, u32[]{:S(2)}) %collective-permute-start.43) | collective-permute-done | bytes 1048608 | tf_op jit(solution)/shard_map/ppermute | solution.py:59
  693.8 13.9 %collective-permute-done.47 = bf16[128,2048]{1,0:T(8,128)(2,1)S(1)} collective-permute-done((bf16[128,2048]{1,0:T(8,128)(2,1)S(1)}, bf16[128,2048]{1,0:T(8,128)(2,1)S(1)}, u32[]{:S(2)}, u32[]{:S(2)}) %collective-permute-start.47) | collective-permute-done | bytes 524320 | tf_op jit(solution)/shard_map/ppermute | solution.py:59
  (304 shorter events, 247.9 us)
Async XLA Ops:
  13.8 24.8 %collective-permute-start = (bf16[128,2048]{1,0:T(8,128)(2,1)}, bf16[128,2048]{1,0:T(8,128)(2,1)S(1)}, u32[]{:S(2)}, u32[]{:S(2)}) collective-permute-start(bf16[128,2048]{1,0:T(8,128)(2,1)} %param.12), channel_id=1, source_target_pairs={{0,8},{4,12},{8,16},{12,20},{16,24},{20,28},{24,0},{28,4},{1,9},{5... | collective-permute-start | bytes 1572872 | tf_op jit(solution)/shard_map/ppermute | solution.py:59
  16.6 50.4 %all-to-all-start = ((bf16[8,208,256]{2,1,0:T(8,128)(2,1)}), bf16[8,208,256]{2,1,0:T(8,128)(2,1)S(1)}, u32[]{:S(2)}, u32[]{:S(2)}) async-start(bf16[8,208,256]{2,1,0:T(8,128)(2,1)} %get-tuple-element.116), calls=%async_computation | async-start | bytes 1703936 | tf_op jit(solution)/shard_map/all_to_all | solution.py:234
  21.7 263.9 %all-gather.6.cloned.1.call-start = ((), (), s32[]{:S(2)}) async-start(), calls=%async_computation.8 | async-start | bytes 8650752 | tf_op jit(solution)/shard_map/all_gather | solution.py:238
  38.6 27.7 %collective-permute-start.4 = (bf16[128,2048]{1,0:T(8,128)(2,1)S(1)}, bf16[128,2048]{1,0:T(8,128)(2,1)S(1)}, u32[]{:S(2)}, u32[]{:S(2)}) collective-permute-start(bf16[128,2048]{1,0:T(8,128)(2,1)S(1)} %collective-permute-done), channel_id=1, source_target_pairs={{0,4},{4,0},{8,12},{12,8},{16,20},{20,16},{24,28},{28,24},{1,5},{5... | collective-permute-start | bytes 1572872 | tf_op jit(solution)/shard_map/ppermute | solution.py:59
  39.1 27.9 %collective-permute-start.3 = (bf16[128,2048]{1,0:T(8,128)(2,1)S(1)}, bf16[128,2048]{1,0:T(8,128)(2,1)S(1)}, u32[]{:S(2)}, u32[]{:S(2)}) collective-permute-start(bf16[128,2048]{1,0:T(8,128)(2,1)S(1)} %collective-permute-done), channel_id=1, source_target_pairs={{0,8},{4,12},{8,16},{12,20},{16,24},{20,28},{24,0},{28,4},{1,9},{5... | collective-permute-start | bytes 1572872 | tf_op jit(solution)/shard_map/ppermute | solution.py:59
  40.6 25.6 %collective-permute-start.5 = (bf16[128,2048]{1,0:T(8,128)(2,1)S(1)}, bf16[128,2048]{1,0:T(8,128)(2,1)S(1)}, u32[]{:S(2)}, u32[]{:S(2)}) collective-permute-start(bf16[128,2048]{1,0:T(8,128)(2,1)S(1)} %collective-permute-done.1), channel_id=1, source_target_pairs={{0,4},{4,0},{8,12},{12,8},{16,20},{20,16},{24,28},{28,24},{1,5},{5... | collective-permute-start | bytes 1572872 | tf_op jit(solution)/shard_map/ppermute | solution.py:59
  92.0 100.9 %all-to-all-start.1 = ((bf16[8,3,256,256]{3,2,1,0:T(8,128)(2,1)}), bf16[8,3,256,256]{3,2,1,0:T(8,128)(2,1)S(1)}, u32[]{:S(2)}, u32[]{:S(2)}) async-start(bf16[8,3,256,256]{3,2,1,0:T(8,128)(2,1)} %prepare.1), calls=%async_computation.1 | async-start | bytes 6291456 | tf_op jit(solution)/shard_map/all_to_all | solution.py:234
  95.7 212.7 %all-gather.4.cloned.1.call-start = ((), (), s32[]{:S(2)}) async-start(), calls=%async_computation.6 | async-start | bytes 4718592 | tf_op jit(solution)/shard_map/all_gather | solution.py:238
  113.7 25.4 %collective-permute-start.10 = (bf16[2,8,128,256]{3,2,1,0:T(8,128)(2,1)}, bf16[2,8,128,256]{3,2,1,0:T(8,128)(2,1)}, u32[]{:S(2)}, u32[]{:S(2)}) collective-permute-start(bf16[2,8,128,256]{3,2,1,0:T(8,128)(2,1)} %bitcast.193), channel_id=1, source_target_pairs={{0,2},{1,3},{2,0},{3,1},{4,6},{5,7},{6,4},{7,5},{8,10},{9,11},{10,... | collective-permute-start | bytes 3145736 | tf_op jit(solution)/shard_map/ppermute | solution.py:59
  141.8 412.4 %reduce-scatter.2.cloned.1.call-start = ((), (), s32[]{:S(2)}) async-start(), calls=%async_computation.7 | async-start | bytes 4718592 | tf_op jit(solution)/shard_map/reduce_scatter | solution.py:242
  193.0 85.8 %collective-permute-start.20 = (bf16[8,3,256,256]{3,2,1,0:T(8,128)(2,1)S(1)}, bf16[8,3,256,256]{3,2,1,0:T(8,128)(2,1)}, u32[]{:S(2)}, u32[]{:S(2)}) collective-permute-start(bf16[8,3,256,256]{3,2,1,0:T(8,128)(2,1)S(1)} %all-to-all-done.1.refs_2_.refs_1_), channel_id=1, source_target_pairs={{0,2},{1,3},{2,0},{3,1},{4,6},{5,7},{6,4},{7,5},{8,10},{9,11},{10,... | collective-permute-start | bytes 9437192 | tf_op jit(solution)/shard_map/ppermute | solution.py:59
  199.3 29.8 %collective-permute-start.13 = (bf16[1024,256]{1,0:T(8,128)(2,1)}, bf16[1024,256]{1,0:T(8,128)(2,1)S(1)}, u32[]{:S(2)}, u32[]{:S(2)}) collective-permute-start(bf16[1024,256]{1,0:T(8,128)(2,1)} %get-tuple-element.131.o_ref), channel_id=1, source_target_pairs={{0,8},{4,12},{8,16},{12,20},{16,24},{20,28},{24,0},{28,4},{1,9},{5... | collective-permute-start | bytes 1572872 | tf_op jit(solution)/shard_map/ppermute | solution.py:59
  230.6 28.8 %collective-permute-start.17 = (bf16[1024,256]{1,0:T(8,128)(2,1)S(1)}, bf16[1024,256]{1,0:T(8,128)(2,1)S(1)}, u32[]{:S(2)}, u32[]{:S(2)}) collective-permute-start(bf16[1024,256]{1,0:T(8,128)(2,1)S(1)} %collective-permute-done.13), channel_id=1, source_target_pairs={{0,4},{4,0},{8,12},{12,8},{16,20},{20,16},{24,28},{28,24},{1,5},{5... | collective-permute-start | bytes 1572872 | tf_op jit(solution)/shard_map/ppermute | solution.py:59
  231.1 28.3 %collective-permute-start.16 = (bf16[1024,256]{1,0:T(8,128)(2,1)S(1)}, bf16[1024,256]{1,0:T(8,128)(2,1)S(1)}, u32[]{:S(2)}, u32[]{:S(2)}) collective-permute-start(bf16[1024,256]{1,0:T(8,128)(2,1)S(1)} %collective-permute-done.13), channel_id=1, source_target_pairs={{0,8},{4,12},{8,16},{12,20},{16,24},{20,28},{24,0},{28,4},{1,9},{5... | collective-permute-start | bytes 1572872 | tf_op jit(solution)/shard_map/ppermute | solution.py:59
  261.1 21.7 %collective-permute-start.21 = (bf16[8,3,256,256]{3,2,1,0:T(8,128)(2,1)S(1)}, bf16[8,3,256,256]{3,2,1,0:T(8,128)(2,1)}, u32[]{:S(2)}, u32[]{:S(2)}) collective-permute-start(bf16[8,3,256,256]{3,2,1,0:T(8,128)(2,1)S(1)} %all-to-all-done.1.refs_2_.refs_1_), channel_id=1, source_target_pairs={{0,1},{1,0},{2,3},{3,2},{4,5},{5,4},{6,7},{7,6},{8,9},{9,8},{10,11... | collective-permute-start | bytes 9437192 | tf_op jit(solution)/shard_map/ppermute | solution.py:59
  346.0 26.3 %collective-permute-start.24 = (bf16[2,128,2048]{2,1,0:T(8,128)(2,1)}, bf16[2,128,2048]{2,1,0:T(8,128)(2,1)S(1)}, u32[]{:S(2)}, u32[]{:S(2)}) collective-permute-start(bf16[2,128,2048]{2,1,0:T(8,128)(2,1)} %pad_maximum_fusion.2), channel_id=1, source_target_pairs={{0,4},{4,0},{8,12},{12,8},{16,20},{20,16},{24,28},{28,24},{1,5},{5... | collective-permute-start | bytes 3145736 | tf_op jit(solution)/shard_map/ppermute | solution.py:59
  347.2 47.5 %collective-permute-start.23 = (bf16[2,128,2048]{2,1,0:T(8,128)(2,1)S(1)}, bf16[2,128,2048]{2,1,0:T(8,128)(2,1)S(1)}, u32[]{:S(2)}, u32[]{:S(2)}) collective-permute-start(bf16[2,128,2048]{2,1,0:T(8,128)(2,1)S(1)} %pad_maximum_fusion.1), channel_id=1, source_target_pairs={{0,4},{4,0},{8,12},{12,8},{16,20},{20,16},{24,28},{28,24},{1,5},{5... | collective-permute-start | bytes 3145736 | tf_op jit(solution)/shard_map/ppermute | solution.py:59
  374.8 22.4 %collective-permute-start.25 = (bf16[128,2048]{1,0:T(8,128)(2,1)S(1)}, bf16[128,2048]{1,0:T(8,128)(2,1)S(1)}, u32[]{:S(2)}, u32[]{:S(2)}) collective-permute-start(bf16[128,2048]{1,0:T(8,128)(2,1)S(1)} %get-tuple-element.229), channel_id=1, source_target_pairs={{0,8},{4,12},{8,16},{12,20},{16,24},{20,28},{24,0},{28,4},{1,9},{5... | collective-permute-start | bytes 1572872 | tf_op jit(solution)/shard_map/ppermute | solution.py:59
  441.0 68.9 %collective-permute-start.35 = (bf16[8,3,256,256]{3,2,1,0:T(8,128)(2,1)}, bf16[8,3,256,256]{3,2,1,0:T(8,128)(2,1)}, u32[]{:S(2)}, u32[]{:S(2)}) collective-permute-start(bf16[8,3,256,256]{3,2,1,0:T(8,128)(2,1)} %add_convert_fusion.1), channel_id=1, source_target_pairs={{0,2},{1,3},{2,0},{3,1},{4,6},{5,7},{6,4},{7,5},{8,10},{9,11},{10,... | collective-permute-start | bytes 9437192 | tf_op jit(solution)/shard_map/ppermute | solution.py:59
  447.7 24.9 %collective-permute-start.32 = (bf16[2,128,256]{2,1,0:T(8,128)(2,1)}, bf16[2,128,256]{2,1,0:T(8,128)(2,1)S(1)}, u32[]{:S(2)}, u32[]{:S(2)}) collective-permute-start(bf16[2,128,256]{2,1,0:T(8,128)(2,1)} %get-tuple-element.258), channel_id=1, source_target_pairs={{0,16},{4,20},{8,24},{12,28},{16,0},{20,4},{24,8},{28,12},{1,17},{... | collective-permute-start | bytes 393224 | tf_op jit(solution)/shard_map/ppermute | solution.py:59
  474.5 34.0 %all-to-all-start.2 = ((bf16[8,128,256]{2,1,0:T(8,128)(2,1)}), bf16[8,128,256]{2,1,0:T(8,128)(2,1)}, u32[]{:S(2)}, u32[]{:S(2)}) async-start(bf16[8,128,256]{2,1,0:T(8,128)(2,1)} %bitcast.190), calls=%async_computation.2 | async-start | bytes 1048576 | tf_op jit(solution)/shard_map/all_to_all | solution.py:234
  514.6 73.9 %all-to-all-start.3 = ((bf16[8,3,256,256]{3,2,1,0:T(8,128)(2,1)}), bf16[8,3,256,256]{3,2,1,0:T(8,128)(2,1)S(1)}, u32[]{:S(2)}, u32[]{:S(2)}) async-start(bf16[8,3,256,256]{3,2,1,0:T(8,128)(2,1)} %add_convert_fusion), calls=%async_computation.4 | async-start | bytes 6291456 | tf_op jit(solution)/shard_map/all_to_all | solution.py:234
  521.7 29.9 %collective-permute-start.34 = (bf16[2,2,8,128,128]{4,3,2,1,0:T(8,128)(2,1)}, bf16[2,2,8,128,128]{4,3,2,1,0:T(8,128)(2,1)}, u32[]{:S(2)}, u32[]{:S(2)}) collective-permute-start(bf16[2,2,8,128,128]{4,3,2,1,0:T(8,128)(2,1)} %pad_maximum_fusion.3), channel_id=1, source_target_pairs={{0,1},{1,0},{2,3},{3,2},{4,5},{5,4},{6,7},{7,6},{8,9},{9,8},{10,11... | collective-permute-start | bytes 3145736 | tf_op jit(solution)/shard_map/ppermute | solution.py:59
  557.9 24.5 %collective-permute-start.37 = (bf16[2,8,128,128]{3,2,1,0:T(8,128)(2,1)S(1)}, bf16[2,8,128,128]{3,2,1,0:T(8,128)(2,1)S(1)}, u32[]{:S(2)}, u32[]{:S(2)}) collective-permute-start(bf16[2,8,128,128]{3,2,1,0:T(8,128)(2,1)S(1)} %fusion.16), channel_id=1, source_target_pairs={{0,2},{1,3},{2,0},{3,1},{4,6},{5,7},{6,4},{7,5},{8,10},{9,11},{10,... | collective-permute-start | bytes 1572872 | tf_op jit(solution)/shard_map/ppermute | solution.py:59
  613.6 28.5 %collective-permute-start.41 = (bf16[2,8,208,256]{3,2,1,0:T(8,128)(2,1)}, bf16[2,8,208,256]{3,2,1,0:T(8,128)(2,1)}, u32[]{:S(2)}, u32[]{:S(2)}) collective-permute-start(bf16[2,8,208,256]{3,2,1,0:T(8,128)(2,1)} %pad_maximum_fusion), channel_id=1, source_target_pairs={{0,1},{1,0},{2,3},{3,2},{4,5},{5,4},{6,7},{7,6},{8,9},{9,8},{10,11... | collective-permute-start | bytes 5111816 | tf_op jit(solution)/shard_map/ppermute | solution.py:59
  615.8 26.3 %collective-permute-start.40 = (bf16[2,128,2048]{2,1,0:T(8,128)(2,1)}, bf16[2,128,2048]{2,1,0:T(8,128)(2,1)}, u32[]{:S(2)}, u32[]{:S(2)}) collective-permute-start(bf16[2,128,2048]{2,1,0:T(8,128)(2,1)} %pad_maximum_fusion.5), channel_id=1, source_target_pairs={{0,4},{4,0},{8,12},{12,8},{16,20},{20,16},{24,28},{28,24},{1,5},{5... | collective-permute-start | bytes 3145736 | tf_op jit(solution)/shard_map/ppermute | solution.py:59
  625.5 38.7 %collective-permute-start.43 = (bf16[2,128,2048]{2,1,0:T(8,128)(2,1)}, bf16[2,128,2048]{2,1,0:T(8,128)(2,1)}, u32[]{:S(2)}, u32[]{:S(2)}) collective-permute-start(bf16[2,128,2048]{2,1,0:T(8,128)(2,1)} %pad_maximum_fusion.6), channel_id=1, source_target_pairs={{0,4},{4,0},{8,12},{12,8},{16,20},{20,16},{24,28},{28,24},{1,5},{5... | collective-permute-start | bytes 3145736 | tf_op jit(solution)/shard_map/ppermute | solution.py:59
  644.4 29.2 %collective-permute-start.46 = (bf16[8,208,256]{2,1,0:T(8,128)(2,1)}, bf16[8,208,256]{2,1,0:T(8,128)(2,1)}, u32[]{:S(2)}, u32[]{:S(2)}) collective-permute-start(bf16[8,208,256]{2,1,0:T(8,128)(2,1)} %fusion.12), channel_id=1, source_target_pairs={{0,2},{1,3},{2,0},{3,1},{4,6},{5,7},{6,4},{7,5},{8,10},{9,11},{10,... | collective-permute-start | bytes 2555912 | tf_op jit(solution)/shard_map/ppermute | solution.py:59
  648.8 21.7 %collective-permute-start.45 = (bf16[128,2048]{1,0:T(8,128)(2,1)}, bf16[128,2048]{1,0:T(8,128)(2,1)}, u32[]{:S(2)}, u32[]{:S(2)}) collective-permute-start(bf16[128,2048]{1,0:T(8,128)(2,1)} %get-tuple-element.226), channel_id=1, source_target_pairs={{0,24},{4,28},{8,0},{12,4},{16,8},{20,12},{24,16},{28,20},{1,25},{... | collective-permute-start | bytes 1572872 | tf_op jit(solution)/shard_map/ppermute | solution.py:59
  651.0 22.5 %collective-permute-start.44 = (bf16[128,2048]{1,0:T(8,128)(2,1)}, bf16[128,2048]{1,0:T(8,128)(2,1)}, u32[]{:S(2)}, u32[]{:S(2)}) collective-permute-start(bf16[128,2048]{1,0:T(8,128)(2,1)} %get-tuple-element.227), channel_id=1, source_target_pairs={{0,8},{4,12},{8,16},{12,20},{16,24},{20,28},{24,0},{28,4},{1,9},{5... | collective-permute-start | bytes 1572872 | tf_op jit(solution)/shard_map/ppermute | solution.py:59
  676.2 35.2 %all-to-all-start.4 = ((bf16[8,208,256]{2,1,0:T(8,128)(2,1)}), bf16[8,208,256]{2,1,0:T(8,128)(2,1)S(1)}, u32[]{:S(2)}, u32[]{:S(2)}) async-start(bf16[8,208,256]{2,1,0:T(8,128)(2,1)} %fusion), calls=%async_computation.5 | async-start | bytes 1703936 | tf_op jit(solution)/shard_map/all_to_all | solution.py:234
  681.5 26.3 %collective-permute-start.47 = (bf16[128,2048]{1,0:T(8,128)(2,1)S(1)}, bf16[128,2048]{1,0:T(8,128)(2,1)S(1)}, u32[]{:S(2)}, u32[]{:S(2)}) collective-permute-start(bf16[128,2048]{1,0:T(8,128)(2,1)S(1)} %fusion.7), channel_id=1, source_target_pairs={{0,8},{4,12},{8,16},{12,20},{16,24},{20,28},{24,0},{28,4},{1,9},{5... | collective-permute-start | bytes 1572872 | tf_op jit(solution)/shard_map/ppermute | solution.py:59
  (72 other events, 1004.0 us)
Sparse Core Ops, SparseCore 0:
  90.3 121.2 all-gather.5
  213.8 94.5 all-gather.3
  420.9 99.9 reduce-scatter.1

commit v4 on v3

--- a/solution.py
+++ b/solution.py
@@ -147,24 +147,43 @@
     return out
 
 
-def scatter_plan(parts, axis):
+def scatter_steps(axis):
     ring = lax.axis_size(axis) // 2
     far, back = ring // 2, (ring - 1) // 2
-
-    def column(offsets, fast):
-        return jnp.stack([pick(parts, near(axis, s, fast)) for s in offsets])
-
     steps = [[s] + ([-s] if s <= back else []) for s in range(far, 0, -1)]
     if ring == 4:
         steps = [[2, -1], [1]]
     steps[-1] = steps[-1] + [0]
+    return steps
+
+
+def scatter_order(axis):
+    steps = sum(scatter_steps(axis), [])
+    return jnp.stack([near(axis, s, fast) for fast in (1, 0) for s in steps]).astype(jnp.int32)
+
+
+def scatter_plan(parts, axis, ordered=False):
+    steps = scatter_steps(axis)
+    places = sum(steps, [])
+
+    def part(s, fast):
+        if ordered:
+            return parts[places.index(s) + (0 if fast else len(places))]
+        return pick(parts, near(axis, s, fast))
+
+    def column(offsets, fast):
+        if ordered:
+            at = places.index(offsets[0])
+            return parts[at : at + len(offsets)]
+        return jnp.stack([part(s, fast) for s in offsets])
+
     up = down = None
     for offsets in steps:
         crossed = hop(column(offsets, 1), axis, 0, 1)
         got = yield [crossed, *[v for v in (up, down) if v is not None]]
         crossed, carried = got[0], got[1:]
         totals = {
-            s: pick(parts, near(axis, s, 0)).astype(f32) + crossed[k].astype(f32)
+            s: part(s, 0).astype(f32) + crossed[k].astype(f32)
             for k, s in enumerate(offsets)
         }
         if up is not None:
@@ -221,8 +240,7 @@
     crossed = yield [hop(part, axis, 0, 1) for part in parts[ring:]]
     sums = [mine.astype(f32) + piece.astype(f32) for mine, piece in zip(parts, crossed)]
     total = sums[0].astype(bf)
-    total, *given = yield [total, *[part.astype(bf) for part in sums[1:]]]
-    got = [hop(part, axis, -s, 0) for s, part in enumerate(given, 1)]
+    got = [hop(sums[s].astype(bf), axis, -s, 0) for s in range(1, ring)]
     yield from idle(spare)
     total = total.astype(f32)
     for piece in (yield got):
@@ -337,45 +355,46 @@
     )(w_query, w_key, w_value, w_output, attn_gain[None], mlp_gain[None])
 
 
-def allowed_block(segk_ref, seg_q, pos_q, chunk, width):
-    seg_k = segk_ref[pl.ds(pl.multiple_of(chunk * width, width), width), :]
-    pos_k = chunk * width + lax.broadcasted_iota(jnp.int32, (width, 1), 0)
-    return (seg_k == seg_q) & (pos_k <= pos_q)
-
-
 def head_lanes(rows, head):
     lane = lax.broadcasted_iota(jnp.int32, (rows, LANES), 1)
     return (lane < HD) if head == 0 else (lane >= HD)
 
 
-def attend_kernel(tile, segk_ref, segq_ref, posq_ref, q_ref, kv_ref, o_ref, lse_ref, vt_ref):
-    nu, _, nb, tok, _ = kv_ref.shape
+def attend_kernel(tile, low_ref, high_ref, q_ref, kv_ref, o_ref, lse_ref, vt_ref):
+    nu, _, nb, tok, feats = kv_ref.shape
     width = nu * tok
     rows = tile * tok
-    j = pl.program_id(1)
+    pairs = feats // LANES
+    heads = range(2 * pairs)
+    lanes = [slice(h // 2 * LANES, (h // 2 + 1) * LANES) for h in heads]
+    j = pl.program_id(0)
 
     @pl.when(j == 0)
     def _():
         for c in range(nb):
-            vt_ref[c] = kv_ref[:, 1, c].reshape(width, LANES).T
-
-    seg_q, pos_q = segq_ref[0], posq_ref[0]
+            vt_ref[c] = kv_ref[:, 1, c].reshape(width, feats).T
+
+    low, high = low_ref[0], high_ref[0]
     q = q_ref[...] * jnp.asarray(1.0 / math.sqrt(HD), bf)
-    q_heads = [jnp.where(head_lanes(rows, h), q, jnp.zeros_like(q)) for h in range(2)]
+    q_heads = [
+        jnp.where(head_lanes(rows, h % 2), q[:, lanes[h]], jnp.zeros((rows, LANES), bf))
+        for h in heads
+    ]
+    place_k = lax.broadcasted_iota(jnp.int32, (width, rows), 0)
 
     def step(chunk, state):
-        k = kv_ref[:, 0, chunk].reshape(width, LANES)
-        v_t = vt_ref[chunk]
-        ok = allowed_block(segk_ref, seg_q, pos_q, chunk, width)
+        k = kv_ref[:, 0, chunk].reshape(width, feats)
+        start = chunk * width
+        ok = (place_k >= low - start) & (place_k <= high - start)
+        scores = [jnp.where(ok, dot_t(k[:, lanes[h]], q_heads[h]), NEG) for h in heads]
         new = []
-        for h in range(2):
+        for h in heads:
             best, total, acc = state[h]
-            s = jnp.where(ok, dot_t(k, q_heads[h]), NEG)
-            best_new = jnp.maximum(best, jnp.max(s, axis=0, keepdims=True))
-            p = jnp.exp(s - best_new)
+            best_new = jnp.maximum(best, jnp.max(scores[h], axis=0, keepdims=True))
+            p = jnp.exp(scores[h] - best_new)
             factor = jnp.exp(best - best_new)
             total = total * factor + jnp.sum(p, axis=0, keepdims=True)
-            acc = acc * factor + dot_n(v_t[h * HD : (h + 1) * HD], p.astype(bf))
+            acc = acc * factor + dot_n(vt_ref[chunk, h * HD : (h + 1) * HD], p.astype(bf))
             new.append((best_new, total, acc))
         return tuple(new)
 
@@ -384,48 +403,38 @@
         jnp.zeros((1, rows), f32),
         jnp.zeros((HD, rows), f32),
     )
-    state = lax.fori_loop(0, (j + 1) * tile, step, (start, start))
-    o_t = jnp.concatenate([acc / total for _, total, acc in state], axis=0)
-    o_ref[...] = o_t.T.astype(bf)
-    lse_ref[0, 0] = jnp.concatenate([best + jnp.log(total) for best, total, _ in state], axis=0)
-
-
-def attend(segments, seg_q, pos_q, q, kv, tile):
+    state = lax.fori_loop(0, (j + 1) * tile, step, (start,) * len(heads))
+    o_ref[...] = jnp.concatenate([acc / total for _, total, acc in state], axis=0).T.astype(bf)
+    lse_ref[0] = jnp.concatenate([best + jnp.log(total) for best, total, _ in state], axis=0)
+
+
+def attend(low, high, q, kv, tile):
     nu, _, nb, tok, feats = kv.shape
     rows = tile * tok
     nq = nb // tile
-    pairs = feats // LANES
-    row_spec = pl.BlockSpec((1, 1, rows), lambda p, j: (j, 0, 0))
-    q_spec = pl.BlockSpec((rows, LANES), lambda p, j: (j, p))
+    heads = feats // HD
+    row_spec = pl.BlockSpec((1, 1, rows), lambda j: (j, 0, 0))
+    q_spec = pl.BlockSpec((rows, feats), lambda j: (j, 0))
     return pl.pallas_call(
         functools.partial(attend_kernel, tile),
-        grid=(pairs, nq),
-        in_specs=[
-            full(segments.shape),
-            row_spec,
-            row_spec,
-            q_spec,
-            pl.BlockSpec((nu, 2, nb, tok, LANES), lambda p, j: (0, 0, 0, 0, p)),
-        ],
-        out_specs=[q_spec, pl.BlockSpec((1, 1, 2, rows), lambda p, j: (p, j, 0, 0))],
+        grid=(nq,),
+        in_specs=[row_spec, row_spec, q_spec, full(kv.shape)],
+        out_specs=[q_spec, pl.BlockSpec((1, heads, rows), lambda j: (j, 0, 0))],
         out_shape=[
             jax.ShapeDtypeStruct((nb * tok, feats), bf),
-            jax.ShapeDtypeStruct((pairs, nq, 2, rows), f32),
-        ],
-        scratch_shapes=[pltpu.VMEM((nb, LANES, nu * tok), bf)],
-        compiler_params=params(),
-        cost_estimate=cost(44 * nb * tok * nb / 8192),
+            jax.ShapeDtypeStruct((nq, heads, rows), f32),
+        ],
+        scratch_shapes=[pltpu.VMEM((nb, feats, nu * tok), bf)],
+        compiler_params=params(),
+        cost_estimate=cost(27 * nb * tok * nb / 8192),
         name="attend",
-    )(segments, seg_q, pos_q, q, kv)
+    )(low, high, q, kv)
 
 
 def attend_back_kernel(
     tile,
-    first_ref,
-    clear_ref,
-    segk_ref,
-    segq_ref,
-    posq_ref,
+    low_ref,
+    high_ref,
     cos_ref,
     sin_ref,
     q_ref,
@@ -437,110 +446,110 @@
     dkv_ref,
     acc_ref,
     delta_ref,
+    sums_ref,
 ):
-    nu, _, _, tok, _ = kv_ref.shape
-    nq = segq_ref.shape[0]
+    nu, _, _, tok, feats = kv_ref.shape
+    nq, heads, rows = lse_ref.shape
     width = nu * tok
-    rows = tile * tok
+    pairs = feats // LANES
     chunk = pl.program_id(0)
-    nb = pl.num_programs(0)
     scale = jnp.asarray(1.0 / math.sqrt(HD), bf)
 
     @pl.when(chunk == 0)
     def _():
         acc_ref[...] = jnp.zeros_like(acc_ref)
-        lane = lax.broadcasted_iota(jnp.int32, (8, LANES), 1)
-        row = lax.broadcasted_iota(jnp.int32, (8, LANES), 0)
+        lane = lax.broadcasted_iota(jnp.int32, (8, feats), 1)
+        row = lax.broadcasted_iota(jnp.int32, (8, feats), 0)
         mine = jnp.where(lane // HD == row, 1.0, 0.0).astype(f32)
         for j in range(nq):
-            part = do_ref[pl.ds(j * rows, rows), :].astype(f32) * o_ref[
-                pl.ds(j * rows, rows), :
-            ].astype(f32)
+            at = pl.ds(j * rows, rows)
             delta_ref[j] = lax.dot_general(
                 mine,
-                part,
+                do_ref[at, :].astype(f32) * o_ref[at, :].astype(f32),
                 (((1,), (1,)), ((), ())),
                 preferred_element_type=f32,
                 precision=lax.Precision.HIGHEST,
             )
 
-    k = kv_ref[:, 0, 0].reshape(width, LANES)
-    v = kv_ref[:, 1, 0].reshape(width, LANES)
-
-    def step(masked, j, state):
-        dk, dv = state
+    k_all = kv_ref[:, 0, 0].reshape(width, feats)
+    v_all = kv_ref[:, 1, 0].reshape(width, feats)
+    lanes = [slice(p * LANES, (p + 1) * LANES) for p in range(pairs)]
+    k = [k_all[:, at] for at in lanes]
+    v = [v_all[:, at] for at in lanes]
+    k_turned = [part.T for part in k]
+    place_k = lax.broadcasted_iota(jnp.int32, (width, rows), 0)
+    start = chunk * width
+    sums_ref[...] = jnp.zeros_like(sums_ref)
+
+    def step(j, _):
         at = pl.ds(pl.multiple_of(j * rows, rows), rows)
         q = q_ref[at, :] * scale
         do = do_ref[at, :]
-        if masked:
-            ok = allowed_block(segk_ref, segq_ref[j], posq_ref[j], chunk, width)
-        parts = []
-        for h in range(2):
-            mine = head_lanes(rows, h)
-            q_h = jnp.where(mine, q, jnp.zeros_like(q))
-            do_h = jnp.where(mine, do, jnp.zeros_like(do))
-            s = dot_t(k, q_h) - lse_ref[0, j, h : h + 1]
-            p = jnp.exp(jnp.where(ok, s, NEG) if masked else s)
-            ds = (p * (dot_t(v, do_h) - delta_ref[j, h : h + 1])).astype(bf)
-            dv = dv + dot_n(p.astype(bf), do_h)
-            dk = dk + dot_n(ds, q_h)
-            parts.append(dot_c(ds, k))
-        acc_ref[at, :] = acc_ref[at, :] + jnp.where(head_lanes(rows, 0), parts[0], parts[1])
-        return dk, dv
-
-    zero = jnp.zeros((width, LANES), f32)
-    dk, dv = lax.fori_loop(chunk // tile, nq, functools.partial(step, True), (zero, zero))
-    dkv_ref[:, 0, 0] = dk.astype(bf).reshape(nu, tok, LANES)
-    dkv_ref[:, 1, 0] = dv.astype(bf).reshape(nu, tok, LANES)
-
-    @pl.when(chunk == nb - 1)
+        ok = (place_k >= low_ref[j] - start) & (place_k <= high_ref[j] - start)
+        q_heads, do_heads = [
+            [
+                jnp.where(head_lanes(rows, h % 2), part[:, lanes[h // 2]], jnp.zeros((rows, LANES), bf))
+                for h in range(2 * pairs)
+            ]
+            for part in (q, do)
+        ]
+        scores = [dot_t(k[h // 2], q_heads[h]) for h in range(2 * pairs)]
+        d_probs = [dot_t(v[h // 2], do_heads[h]) for h in range(2 * pairs)]
+        for pair in range(pairs):
+            dk = dv = 0.0
+            dq = []
+            for i in range(2):
+                h = 2 * pair + i
+                p = jnp.exp(jnp.where(ok, scores[h] - lse_ref[j, h : h + 1], NEG))
+                ds = (p * (d_probs[h] - delta_ref[j, h : h + 1])).astype(bf)
+                dv = dv + dot_n(p.astype(bf), do_heads[h])
+                dk = dk + dot_n(ds, q_heads[h])
+                dq.append(dot_n(k_turned[pair][i * HD : (i + 1) * HD], ds))
+            acc_ref[j, lanes[pair]] = acc_ref[j, lanes[pair]] + jnp.concatenate(dq, axis=0)
+            sums_ref[0, pair] = sums_ref[0, pair] + dk
+            sums_ref[1, pair] = sums_ref[1, pair] + dv
+        return 0
+
+    lax.fori_loop(chunk // tile, nq, step, 0)
+    for i in range(2):
+        for pair in range(pairs):
+            dkv_ref[:, i, 0, :, lanes[pair]] = (
+                sums_ref[i, pair].astype(bf).reshape(nu, tok, LANES)
+            )
+
+    @pl.when(chunk == pl.num_programs(0) - 1)
     def _():
-        dq = acc_ref[...] * (1.0 / math.sqrt(HD))
-        dq_ref[...] = (dq * cos_ref[...] - turned(dq) * sin_ref[...]).astype(bf)
-
-
-def attend_back(where, cosine, sine, q, do, o, lse, kv, pair, tile):
-    nu, _, nb, tok, _ = kv.shape
-    first, clear, segments, seg_q, pos_q = where
+        dq = jnp.concatenate([acc_ref[j].T for j in range(nq)], axis=0) * (1.0 / math.sqrt(HD))
+        cosine, sine = wide(cos_ref[...], feats), wide(sin_ref[...], feats)
+        dq_ref[...] = (dq * cosine - turned(dq) * sine).astype(bf)
+
+
+def attend_back(low, high, cosine, sine, q, do, o, lse, kv, tile):
+    nu, _, nb, tok, feats = kv.shape
     rows = tile * tok
     nq = nb // tile
-    whole_rows = full((nq, 1, rows))
-    table = full((nb * tok, LANES))
-    pair_spec = pl.BlockSpec((nb * tok, LANES), lambda c, *_: (0, pair))
+    kv_spec = pl.BlockSpec((nu, 2, 1, tok, feats), lambda c: (0, 0, c, 0, 0))
     return pl.pallas_call(
         functools.partial(attend_back_kernel, tile),
-        grid_spec=pltpu.PrefetchScalarGridSpec(
-            num_scalar_prefetch=2,
-            grid=(nb,),
-            in_specs=[
-                full(segments.shape),
-                whole_rows,
-                whole_rows,
-                table,
-                table,
-                pair_spec,
-                pair_spec,
-                pair_spec,
-                pl.BlockSpec((1, nq, 2, rows), lambda c, *_: (pair, 0, 0, 0)),
-                pl.BlockSpec((nu, 2, 1, tok, LANES), lambda c, *_: (0, 0, c, 0, pair)),
-            ],
-            out_specs=[
-                table,
-                pl.BlockSpec((nu, 2, 1, tok, LANES), lambda c, *_: (0, 0, c, 0, 0)),
-            ],
-            scratch_shapes=[
-                pltpu.VMEM((nb * tok, LANES), f32),
-                pltpu.VMEM((nq, 8, rows), f32),
-            ],
-        ),
+        grid=(nb,),
+        in_specs=[
+            *[full(part.shape) for part in (low, high, cosine, sine, q, do, o, lse)],
+            kv_spec,
+        ],
+        out_specs=[full(q.shape), kv_spec],
         out_shape=[
-            jax.ShapeDtypeStruct((nb * tok, LANES), bf),
-            jax.ShapeDtypeStruct((nu, 2, nb, tok, LANES), bf),
-        ],
-        compiler_params=params(),
-        cost_estimate=cost(25 * nb * tok * nb / 8192),
+            jax.ShapeDtypeStruct(q.shape, bf),
+            jax.ShapeDtypeStruct(kv.shape, bf),
+        ],
+        scratch_shapes=[
+            pltpu.VMEM((nq, feats, rows), f32),
+            pltpu.VMEM((nq, 8, rows), f32),
+            pltpu.VMEM((2, feats // LANES, nu * tok, LANES), f32),
+        ],
+        compiler_params=params(),
+        cost_estimate=cost(41 * nb * tok * nb / 8192),
         name="attend_back",
-    )(first, clear, segments, seg_q, pos_q, cosine, sine, q, do, o, lse, kv)
+    )(low, high, cosine, sine, q, do, o, lse, kv)
 
 
 def output_kernel(x_ref, o_ref, w_ref, gain_ref, x1_ref, normed_ref):
@@ -608,16 +617,17 @@
     )(d_attn, w_out)
 
 
-def project_back_kernel(piece, n, x_ref, w_ref, cos_ref, sin_ref, *refs):
-    dq_refs, dkv_refs, (all_ref, dn_ref, gain_ref) = refs[:n], refs[n : 2 * n], refs[2 * n :]
+def project_back_kernel(
+    piece, _, x_ref, w_ref, cos_ref, sin_ref, dq_ref, dkv_ref, all_ref, dn_ref, gain_ref
+):
     blocks, width = w_ref.shape[1], w_ref.shape[3]
-    feats = n * LANES
+    feats = dq_ref.shape[1]
     cosine, sine = wide(cos_ref[...], feats), wide(sin_ref[...], feats)
-    dk = jnp.concatenate([ref[0] for ref in dkv_refs], axis=1).astype(f32)
+    dk = dkv_ref[0].astype(f32)
     parts = (
-        jnp.concatenate([ref[...] for ref in dq_refs], axis=1),
+        dq_ref[...],
         (dk * cosine - turned(dk) * sine).astype(bf),
-        jnp.concatenate([ref[1] for ref in dkv_refs], axis=1),
+        dkv_ref[1],
     )
     for i in range(3):
         all_ref[i] = parts[i]
@@ -633,40 +643,44 @@
         total = 0.0
         for part in range(3):
             total = total + dot_n(parts[part], weight_block(w_ref, block, part, piece))
-        dn_ref[:, at] = total.astype(bf)
+        dn_ref[0, :, at] = total.astype(bf)
         gain_ref[:, at] = gain_ref[:, at] + jnp.sum(total * (x[:, at] * r1), axis=0, keepdims=True)
 
 
-def project_back(x_all, w, cosine, sine, dq, dkv, piece, rows):
+def project_back(x_all, w, cosine, sine, dq, dkv, piece, order):
     count, dim = x_all.shape
-    n = len(dq)
-    feats = n * LANES
-    tiled = lambda width: pl.BlockSpec((rows, width), lambda i: (i, 0))
-    return pl.pallas_call(
-        functools.partial(project_back_kernel, piece, n),
-        grid=(count // rows,),
-        in_specs=[
-            tiled(dim),
-            full(w.shape),
-            tiled(LANES),
-            tiled(LANES),
-            *[tiled(LANES)] * n,
-            *[pl.BlockSpec((2, rows, LANES), lambda i: (0, i, 0))] * n,
-        ],
-        out_specs=[
-            pl.BlockSpec((3, rows, feats), lambda i: (0, i, 0)),
-            tiled(dim),
-            full((1, dim)),
-        ],
+    size = order.shape[0]
+    rows = count // size
+    feats = dq.shape[1]
+    tiled = lambda width: pl.BlockSpec((rows, width), lambda i, at: (at[i], 0))
+    return pl.pallas_call(
+        functools.partial(project_back_kernel, piece),
+        grid_spec=pltpu.PrefetchScalarGridSpec(
+            num_scalar_prefetch=1,
+            grid=(size,),
+            in_specs=[
+                tiled(dim),
+                full(w.shape),
+                tiled(LANES),
+                tiled(LANES),
+                tiled(feats),
+                pl.BlockSpec((2, rows, feats), lambda i, at: (0, at[i], 0)),
+            ],
+            out_specs=[
+                pl.BlockSpec((3, rows, feats), lambda i, at: (0, at[i], 0)),
+                pl.BlockSpec((1, rows, dim), lambda i, _: (i, 0, 0)),
+                full((1, dim)),
+            ],
+        ),
         out_shape=[
             jax.ShapeDtypeStruct((3, count, feats), bf),
-            jax.ShapeDtypeStruct((count, dim), bf),
+            jax.ShapeDtypeStruct((size, rows, dim), bf),
             jax.ShapeDtypeStruct((1, dim), f32),
         ],
         compiler_params=params(),
         cost_estimate=cost(count * 0.01),
         name="project_back",
-    )(x_all, w, cosine, sine, *dq, *dkv)
+    )(order, x_all, w, cosine, sine, dq, dkv)
 
 
 def projection_grads_kernel(left_ref, right_ref, gain_ref, out_ref, turned_ref):
@@ -819,33 +833,43 @@
     )(normed, cot, *weights)
 
 
-def mix_kernel(which, n, *refs):
-    lefts, weights, out_ref = refs[: len(which)], refs[len(which) : -1], refs[-1]
+def mix_kernel(which, n, _, *refs):
+    m = len(which)
+    lefts, weights, out_ref = refs[: 2 * m], refs[2 * m : -1], refs[-1]
     total = 0.0
-    for k in range(len(which)):
+    for k in range(m):
         for i in range(n):
-            total = total + dot_t(lefts[k][i], whole_weight(weights[i], k))
-    out_ref[...] = total.astype(bf)
-
-
-def mix(lefts, weights, which, rows):
+            left = jnp.concatenate([lefts[2 * k][i], lefts[2 * k + 1][i]], axis=0)
+            total = total + dot_t(left, whole_weight(weights[i], k))
+    out_ref[...] = total.astype(bf).reshape(out_ref.shape)
+
+
+def mix(lefts, weights, which, order):
     n, count, width = lefts[0].shape
+    size = order.shape[0]
+    rows = count // size
     blocks, _, rows_w, _ = weights[0].shape
     dim = blocks * rows_w
     chosen = pl.BlockSpec(
-        (blocks, len(which), rows_w, width), lambda i: (0, which[0] // len(which), 0, 0)
+        (blocks, len(which), rows_w, width), lambda i, _: (0, which[0] // len(which), 0, 0)
     )
+    pair = [
+        pl.BlockSpec((n, rows, width), lambda i, at: (0, at[2 * i], 0)),
+        pl.BlockSpec((n, rows, width), lambda i, at: (0, at[2 * i + 1], 0)),
+    ]
     return pl.pallas_call(
         functools.partial(mix_kernel, which, n),
-        grid=(count // rows,),
-        in_specs=[pl.BlockSpec((n, rows, width), lambda i: (0, i, 0))] * len(which)
-        + [chosen] * n,
-        out_specs=pl.BlockSpec((rows, dim), lambda i: (i, 0)),
-        out_shape=jax.ShapeDtypeStruct((count, dim), bf),
+        grid_spec=pltpu.PrefetchScalarGridSpec(
+            num_scalar_prefetch=1,
+            grid=(size // 2,),
+            in_specs=pair * len(which) + [chosen] * n,
+            out_specs=pl.BlockSpec((2, rows, dim), lambda i, _: (i, 0, 0)),
+        ),
+        out_shape=jax.ShapeDtypeStruct((size, rows, dim), bf),
         compiler_params=params(),
         cost_estimate=cost(8 * len(which)),
         name="mix",
-    )(*lefts, *weights)
+    )(order, *[left for left in lefts for _ in range(2)], *weights)
 
 
 def hidden_grads_kernel(n_ref, g_ref, dg_ref, du_ref, act_ref, *outs):
@@ -917,20 +941,8 @@
     angles = (index - first).astype(f32)[:, None] * freq[None, :]
     cosine = jnp.cos(angles)
     sine = jnp.sin(angles) * jnp.where(lane % HD < HD // 2, -1.0, 1.0)[None, :]
-    width = nu * tok
-    rows_q = tile * tok
-    seg_rows = seg_mine.reshape(nb // tile, 1, rows_q)
-    pos_rows = index.reshape(nb // tile, 1, rows_q)
-    seg_k = segments.reshape(nb, width)
-    low_q, high_q = seg_rows[:, 0, :1], seg_rows[:, 0, -1:]
-    first_chunk = jnp.sum((seg_k[None, :, -1] < low_q).astype(jnp.int32), axis=1)
-    clear = (
-        (low_q == high_q)
-        & (seg_k[None, :, 0] == low_q)
-        & (seg_k[None, :, -1] == low_q)
-        & (jnp.arange(1, nb + 1, dtype=jnp.int32)[None, :] * width <= pos_rows[:, 0, :1])
-    )
-    where = (first_chunk, clear.astype(jnp.int32).reshape(-1), segments[:, None], seg_rows, pos_rows)
+    low = first.reshape(nb // tile, 1, tile * tok)
+    high = index.reshape(nb // tile, 1, tile * tok)
 
     ff_u = w_gate.shape[1]
     ff_piece = ff_u // nb
@@ -985,7 +997,7 @@
 
     q, kv, normed = project(x_all, w_qkv, cosine, sine, piece, step)
     (kv_all,) = together(gather_plan(kv.reshape(2, nb, tok, feats), "uly"))
-    o, lse = attend(*where[2:], q, kv_all, tile)
+    o, lse = attend(low, high, q, kv_all, tile)
     ff_got, o = lax.optimization_barrier((ff_got, o))
     rounds = Rounds()
     rounds.add(o=gather_plan(o, "blk"), ff=gather_near_plan(ff_got, "uly", nb // 4))
@@ -995,14 +1007,15 @@
     (w_ff,) = rounds.until("ff")
 
     act, d_gate, d_up = hidden(normed2, cot_all, w_ff, step)
-    d_norm2 = mix([d_gate, d_up], w_ff, (0, 1), step)
+    order, plain = scatter_order("blk"), jnp.arange(nb, dtype=jnp.int32)
+    d_norm2 = mix([d_gate, d_up], w_ff, (0, 1), order)
 
     def mlp_plan():
-        (out,) = yield [mix([act], w_ff, (2,), step)]
+        yield []
+        (out,) = yield [mix([act], w_ff, (2,), plain)]
         return out
 
     def hidden_grads_plan():
-        yield []
         grads = yield hidden_grads(
             after(normed2, d_norm2), cot_all, d_gate, d_up, act, rows
         )
@@ -1010,13 +1023,13 @@
 
     rounds = Rounds()
     rounds.add(
-        d_norm2=scatter_plan(d_norm2.reshape(nb, tok, dim), "blk"),
+        d_norm2=scatter_plan(d_norm2, "blk", True),
         mlp=mlp_plan(),
         ff=hidden_grads_plan(),
     )
     d_norm2, mlp_out = rounds.until("d_norm2", "mlp")
     x1_own = lax.dynamic_slice_in_dim(x1, b * tok, tok, 0)
-    mlp_out = scatter(after(mlp_out, d_norm2), "blk")
+    mlp_out = scatter(after(mlp_out, d_norm2).reshape(count, dim), "blk")
     r2_own = rms_scale(x1_own)
     gain2_part = jnp.sum(d_norm2 * x1_own * r2_own, axis=0, keepdims=True)
     z_two = gain2 * d_norm2
@@ -1033,29 +1046,22 @@
     (got,) = rounds.until("d_o")
     d_o = got.reshape(count, feats)
     d_columns = swap(after(d_columns, d_o), "blk")
-    pairs = feats // LANES
-    dq = []
-    for pair in range(pairs):
-        dq_pair, dkv = attend_back(where, cosine, sine, q, d_o, o, lse, kv_all, pair, tile)
-        if pair == 0:
-            dkv, d_o, d_columns = lax.optimization_barrier((dkv, d_o, d_columns))
-            (ff_mine,) = rounds.until("ff")
-            ff_mine, d_o, d_columns = lax.optimization_barrier((ff_mine, d_o, d_columns))
-            ff_got = swap(ff_mine, "blk")
-        rounds.add(**{f"dkv{pair}": scatter_plan(dkv, "uly")})
-        dq.append(dq_pair)
-    mlp_out, d_columns = rounds.round(mlp_out, d_columns)
+    dq, dkv = attend_back(low, high, cosine, sine, q, d_o, o, lse, kv_all, tile)
+    dkv, mlp_out, d_columns = lax.optimization_barrier((dkv, mlp_out, d_columns))
+    rounds.add(dkv=scatter_plan(dkv, "uly"))
+    (ff_mine,) = rounds.until("ff")
+    ff_got = swap(ff_mine, "blk")
     out_grads = output_grads(o_all, d_columns.reshape(count, rows), pieces)
     if not strided:
         out_grads = out_grads[:, :, :group]
-    dkv = rounds.until(*[f"dkv{pair}" for pair in range(pairs)])
-    *dkv, out_grads, ff_got = lax.optimization_barrier((*dkv, out_grads, ff_got))
+    (dkv,) = rounds.until("dkv")
+    dkv, out_grads = lax.optimization_barrier((dkv, out_grads))
     rounds.add(out=scatter_plan(out_grads.reshape(nu, feats_u, rows), "uly"))
-    dkv = [part.astype(bf).reshape(2, count, LANES) for part in dkv]
-    d_qkv, d_norm1, gain1_part = project_back(x_all, w_qkv, cosine, sine, dq, dkv, piece, step)
+    dkv = dkv.astype(bf).reshape(2, count, feats)
+    d_qkv, d_norm1, gain1_part = project_back(x_all, w_qkv, cosine, sine, dq, dkv, piece, order)
     gain_parts = jnp.pad(jnp.concatenate([gain1_part, gain2_part]), ((0, PAD - 2), (0, 0)))
     grads = projection_grads(d_qkv, after(normed, d_norm1), gain_parts, pieces, block)
-    last = scatter_plan(d_norm1.reshape(nb, tok, dim), "blk")
+    last = scatter_plan(d_norm1, "blk", True)
     if strided:
         rounds.add(
             last=last,

time: 737 us -> 710 us (0.963)
  Pallas kernels: 237 us -> 209 us
  other arithmetic: 71.6 us -> 59.7 us
  starting transfers between devices: 67.8 us -> 78.4 us
  waiting for transfers between devices: 278 us -> 287 us
    pallas_call x6 -> x5, Pallas kernels: 132 us -> 104 us  [the longest x1 40.5 us: attend_back(): pl.pallas_call(functools.partial(attend_back_kernel, tile), grid=(nb,), i...]
    all_to_all x5, waiting for transfers between devices: 5.67 us -> 24.7 us  [swap(): return lax.all_to_all(parts, axis, 0, 0, tiled=True)]
    ppermute x48 -> x46, waiting for transfers between devices: 265 us -> 253 us  [hop(): return lax.ppermute(value, axis, pairs)]
    ppermute x48 -> x46, starting transfers between devices: 46.4 us -> 51.8 us  [hop(): return lax.ppermute(value, axis, pairs)]
    unnamed x100 -> x84, local copies, waits for them, and re-layouts: 18.4 us -> 14 us
  transfers between devices with their start and end apart: 56 -> 54, of which waited for: 33 -> 31; matrix products, arithmetic and copies ran while one was open for 13% -> 12% of each run, Pallas kernels for 25% -> 25%
where the time goes in v4:
time: 710 us; the launch traced here: 701 us
  waiting for transfers between devices  287 us (40%)
  Pallas kernels  209 us (29%)
  starting transfers between devices  78.4 us (11%)
  other arithmetic  59.7 us (8%)
  local copies, waits for them, and re-layouts  51.4 us (7%)
  between operations  15 us (2%)
    ppermute x46, waiting for transfers between devices, hop(): return lax.ppermute(value, axis, pairs)  253 us
    ppermute x46, starting transfers between devices, hop(): return lax.ppermute(value, axis, pairs)  51.8 us
    pallas_call x1, Pallas kernels, attend_back(): pl.pallas_call(functools.partial(attend_back_kernel, tile), grid=(nb,), i...  40.5 us
    all_to_all x5, starting transfers between devices, swap(): return lax.all_to_all(parts, axis, 0, 0, tiled=True)  26.5 us
    pallas_call x1, Pallas kernels, attend(): pl.pallas_call(functools.partial(attend_kernel, tile), grid=(nq,), in_spe...  26.4 us
    pallas_call x2, Pallas kernels, mix(): pl.pallas_call(functools.partial(mix_kernel, which, n), grid_spec=pltpu.P...  24.9 us
    all_to_all x5, waiting for transfers between devices, swap(): return lax.all_to_all(parts, axis, 0, 0, tiled=True)  24.7 us
    pallas_call x1, Pallas kernels, hidden(): pl.pallas_call(functools.partial(hidden_kernel, n), grid=(count // rows,)...  20.5 us
  transfers between devices with their start and end apart: 54, of which 31 were waited for; matrix products, arithmetic and copies ran while one was open for 12% of the time, Pallas kernels for 25%

profile of v4, /device:TPU:0, one launch (start us, length us, event | category | flops | bytes accessed | tf_op | source)
XLA Modules:
  0.0 700.6 jit_solution(2106482185383782829)
XLA Ops:
  20.5 6.8 prepare.1
  27.3 8.5 %collective-permute-done.1 = bf16[128,2048]{1,0:T(8,128)(2,1)S(1)} collective-permute-done((bf16[128,2048]{1,0:T(8,128)(2,1)}, bf16[128,2048]{1,0:T(8,128)(2,1)S(1)}, u32[]{:S(2)}, u32[]{:S(2)}) %collective-permute-start.1) | collective-permute-done | bytes 524320 | tf_op jit(solution)/shard_map/ppermute | solution.py:59
  47.3 13.4 %collective-permute-done.3 = bf16[128,2048]{1,0:T(8,128)(2,1)S(1)} collective-permute-done((bf16[128,2048]{1,0:T(8,128)(2,1)S(1)}, bf16[128,2048]{1,0:T(8,128)(2,1)S(1)}, u32[]{:S(2)}, u32[]{:S(2)}) %collective-permute-start.3) | collective-permute-done | bytes 524320 | tf_op jit(solution)/shard_map/ppermute | solution.py:59
  60.7 6.7 collective-permute-done.5
  72.5 10.8 %collective-permute-done.6 = bf16[128,2048]{1,0:T(8,128)(2,1)S(1)} collective-permute-done((bf16[128,2048]{1,0:T(8,128)(2,1)S(1)}, bf16[128,2048]{1,0:T(8,128)(2,1)S(1)}, u32[]{:S(2)}, u32[]{:S(2)}) %collective-permute-start.6) | collective-permute-done | bytes 524320 | tf_op jit(solution)/shard_map/ppermute | solution.py:59
  102.1 9.5 %project.1 = (bf16[1024,256]{1,0:T(8,128)(2,1)}, bf16[2,1024,256]{2,1,0:T(8,128)(2,1)}, bf16[1024,2048]{1,0:T(8,128)(2,1)}) custom-call(bf16[1024,2048]{1,0:T(8,128)(2,1)} %bitcast.10.x_ref, bf16[4,8,208,256]{3,2,1,0:T(8,128)(2,1)} %copy-done.9, f32[1024,128]{1,0:T(8,128)} %get-tuple-element.216.cos_ref, f32[1024,128]{1,0:T(8,128)} %get-tuple-element.215.sin_ref), custom_call_target="tpu_custom_call" | custom-call | flops 2534400000 | tf_op jit(solution)/shard_map/project/pallas_call | solution.py:310
  113.3 24.1 %collective-permute-done.10 = bf16[2,8,128,256]{3,2,1,0:T(8,128)(2,1)} collective-permute-done((bf16[2,8,128,256]{3,2,1,0:T(8,128)(2,1)}, bf16[2,8,128,256]{3,2,1,0:T(8,128)(2,1)}, u32[]{:S(2)}, u32[]{:S(2)}) %collective-permute-start.10) | collective-permute-done | bytes 1048608 | tf_op jit(solution)/shard_map/ppermute | solution.py:59
  144.9 26.4 %attend.1 = (bf16[1024,256]{1,0:T(8,128)(2,1)}, f32[4,4,256]{2,1,0:T(4,128)}) custom-call(s32[4,1,256]{2,1,0:T(1,128)} %bitcast.199, s32[4,1,256]{2,1,0:T(1,128)} %broadcast_add_fusion.high_ref, bf16[1024,256]{1,0:T(8,128)(2,1)} %get-tuple-element.109.q_ref, bf16[4,2,8,128,256]{4,3,2,1,0:T(8,128)(2,1)} %copy-done.7), custom_call_target="tpu_custom_call" | custom-call | flops 7424999936 | tf_op jit(solution)/shard_map/attend/pallas_call | solution.py:418
  171.3 21.1 %all-to-all-done.1.refs_2_.refs_4_ = bf16[8,3,256,256]{3,2,1,0:T(8,128)(2,1)S(1)} async-done(((bf16[8,3,256,256]{3,2,1,0:T(8,128)(2,1)}), bf16[8,3,256,256]{3,2,1,0:T(8,128)(2,1)S(1)}, u32[]{:S(2)}, u32[]{:S(2)}) %all-to-all-start.1) | async-done | bytes 3145760 | tf_op jit(solution)/shard_map/all_to_all | solution.py:252
  200.2 15.8 %collective-permute-done.13 = bf16[1024,256]{1,0:T(8,128)(2,1)S(1)} collective-permute-done((bf16[1024,256]{1,0:T(8,128)(2,1)}, bf16[1024,256]{1,0:T(8,128)(2,1)S(1)}, u32[]{:S(2)}, u32[]{:S(2)}) %collective-permute-start.13) | collective-permute-done | bytes 524320 | tf_op jit(solution)/shard_map/ppermute | solution.py:59
  216.0 6.7 collective-permute-done.14
  225.5 17.0 %collective-permute-done.16 = bf16[1024,256]{1,0:T(8,128)(2,1)S(1)} collective-permute-done((bf16[1024,256]{1,0:T(8,128)(2,1)S(1)}, bf16[1024,256]{1,0:T(8,128)(2,1)S(1)}, u32[]{:S(2)}, u32[]{:S(2)}) %collective-permute-start.16) | collective-permute-done | bytes 524320 | tf_op jit(solution)/shard_map/ppermute | solution.py:59
  244.0 9.6 %collective-permute-done.18 = bf16[1024,256]{1,0:T(8,128)(2,1)S(1)} collective-permute-done((bf16[1024,256]{1,0:T(8,128)(2,1)S(1)}, bf16[1024,256]{1,0:T(8,128)(2,1)S(1)}, u32[]{:S(2)}, u32[]{:S(2)}) %collective-permute-start.18) | collective-permute-done | bytes 524320 | tf_op jit(solution)/shard_map/ppermute | solution.py:59
  254.9 19.0 %collective-permute-done.19 = bf16[1024,256]{1,0:T(8,128)(2,1)S(1)} collective-permute-done((bf16[1024,256]{1,0:T(8,128)(2,1)S(1)}, bf16[1024,256]{1,0:T(8,128)(2,1)S(1)}, u32[]{:S(2)}, u32[]{:S(2)}) %collective-permute-start.19) | collective-permute-done | bytes 524320 | tf_op jit(solution)/shard_map/ppermute | solution.py:59
  280.8 16.0 %output_project.1 = (f32[1024,2048]{1,0:T(8,128)}, bf16[1024,2048]{1,0:T(8,128)(2,1)}) custom-call(bf16[1024,2048]{1,0:T(8,128)(2,1)} %bitcast.10.x_ref, bf16[8,1024,256]{2,1,0:T(8,128)(2,1)} %copy-done.1, bf16[8,4,8,64,256]{4,3,2,1,0:T(8,128)(2,1)} %bitcast.177, f32[1,2048]{1,0:T(1,128)} %bitcast.192), custom_call_target="tpu_custom_call" | custom-call | flops 4224000000 | tf_op jit(solution)/shard_map/output_project/pallas_call | solution.py:573
  301.6 20.5 %hidden.1 = (bf16[4,1024,256]{2,1,0:T(8,128)(2,1)}, bf16[4,1024,256]{2,1,0:T(8,128)(2,1)}, bf16[4,1024,256]{2,1,0:T(8,128)(2,1)}) custom-call(bf16[1024,2048]{1,0:T(8,128)(2,1)} %get-tuple-element.133.refs_0_.n_ref, bf16[1024,2048]{1,0:T(8,128)(2,1)} %all-gather.4.cloned.1.call-done.refs_1_.g_ref, bf16[8,3,256,256]{3,2,1,0:T(8,128)(2,1)} %copy-done, ...), custom_call_target="tpu_custom_call" | custom-call | flops 5500000256 | tf_op jit(solution)/shard_map/hidden/pallas_call | solution.py:824
  322.1 15.3 %mix.2 = bf16[8,128,2048]{2,1,0:T(8,128)(2,1)} custom-call(s32[8]{0:T(128)} %stack.59._, bf16[4,1024,256]{2,1,0:T(8,128)(2,1)} %get-tuple-element.131.refs_0_.refs_1_.dg_ref, bf16[4,1024,256]{2,1,0:T(8,128)(2,1)} %get-tuple-element.131.refs_0_.refs_1_.dg_ref, bf16[4,1024,256]{2,1,0:T(8,128)(2,1)} %get-tuple-element.132.refs_2_.refs_3_.du_ref, ...), custom_call_target="tpu_custom_call" | custom-call | flops 4400000000 | tf_op jit(solution)/shard_map/mix/pallas_call | solution.py:860
  339.8 18.7 %hidden_grads.1 = (bf16[8,3,256,256]{3,2,1,0:T(8,128)(2,1)}, bf16[8,3,256,256]{3,2,1,0:T(8,128)(2,1)}, bf16[8,3,256,256]{3,2,1,0:T(8,128)(2,1)}, bf16[8,3,256,256]{3,2,1,0:T(8,128)(2,1)}) custom-call(bf16[1024,2048]{1,0:T(8,128)(2,1)} %get-tuple-element.133.refs_0_.n_ref, bf16[1024,2048]{1,0:T(8,128)(2,1)} %all-gather.4.cloned.1.call-done.refs_1_.g_ref, ...), custom_call_target="tpu_custom_call" | custom-call | flops 6874999808 | tf_op jit(solution)/shard_map/hidden_grads/pallas_call | solution.py:889
  371.4 9.6 %mix.3 = bf16[8,128,2048]{2,1,0:T(8,128)(2,1)} custom-call(s32[8]{0:T(128)} %iota.43._, bf16[4,1024,256]{2,1,0:T(8,128)(2,1)} %get-tuple-element.134.act_ref.refs_0_.refs_1_, bf16[4,1024,256]{2,1,0:T(8,128)(2,1)} %get-tuple-element.134.act_ref.refs_0_.refs_1_, bf16[8,3,256,256]{3,2,1,0:T(8,128)(2,1)} %copy-done, ...), custom_call_target="tpu_custom_call" | custom-call | flops 2200000000 | tf_op jit(solution)/shard_map/mix/pallas_call | solution.py:860
  381.0 8.8 %collective-permute-done.23 = bf16[2,128,2048]{2,1,0:T(8,128)(2,1)S(1)} collective-permute-done((bf16[2,128,2048]{2,1,0:T(8,128)(2,1)S(1)}, bf16[2,128,2048]{2,1,0:T(8,128)(2,1)S(1)}, u32[]{:S(2)}, u32[]{:S(2)}) %collective-permute-start.23) | collective-permute-done | bytes 1048608 | tf_op jit(solution)/shard_map/ppermute | solution.py:59
  397.2 13.7 %collective-permute-done.29 = bf16[128,2048]{1,0:T(8,128)(2,1)S(1)} collective-permute-done((bf16[128,2048]{1,0:T(8,128)(2,1)S(1)}, bf16[128,2048]{1,0:T(8,128)(2,1)S(1)}, u32[]{:S(2)}, u32[]{:S(2)}) %collective-permute-start.29) | collective-permute-done | bytes 524320 | tf_op jit(solution)/shard_map/ppermute | solution.py:59
  416.6 8.7 %output_back.1 = bf16[8,128,256]{2,1,0:T(8,128)(2,1)} custom-call(bf16[128,2048]{1,0:T(8,128)(2,1)} %get-tuple-element.185.d_ref, bf16[8,4,8,64,256]{4,3,2,1,0:T(8,128)(2,1)} %bitcast.178), custom_call_target="tpu_custom_call" | custom-call | flops 2200000000 | tf_op jit(solution)/shard_map/output_back/pallas_call | solution.py:605
  427.8 6.9 collective-permute-done.30
  448.1 7.7 %collective-permute-done.32 = bf16[2,128,256]{2,1,0:T(8,128)(2,1)S(1)} collective-permute-done((bf16[2,128,256]{2,1,0:T(8,128)(2,1)S(1)}, bf16[2,128,256]{2,1,0:T(8,128)(2,1)S(1)}, u32[]{:S(2)}, u32[]{:S(2)}) %collective-permute-start.32) | collective-permute-done | bytes 131104 | tf_op jit(solution)/shard_map/ppermute | solution.py:59
  457.8 10.0 %all-to-all-start.2 = ((bf16[8,128,256]{2,1,0:T(8,128)(2,1)}), bf16[8,128,256]{2,1,0:T(8,128)(2,1)S(1)}, u32[]{:S(2)}, u32[]{:S(2)}) async-start(bf16[8,128,256]{2,1,0:T(8,128)(2,1)} %bitcast.176), calls=%async_computation.3 | async-start | bytes 1048576 | tf_op jit(solution)/shard_map/all_to_all | solution.py:252
  467.8 40.5 %attend_back.1 = (bf16[1024,256]{1,0:T(8,128)(2,1)}, bf16[4,2,8,128,256]{4,3,2,1,0:T(8,128)(2,1)}) custom-call(s32[4,1,256]{2,1,0:T(1,128)} %bitcast.200, s32[4,1,256]{2,1,0:T(1,128)} %broadcast_add_fusion.high_ref, f32[1024,128]{1,0:T(8,128)} %get-tuple-element.216.cos_ref, f32[1024,128]{1,0:T(8,128)} %get-tuple-element.215.sin_ref, ...), custom_call_target="tpu_custom_call" | custom-call | flops 11274999808 | tf_op jit(solution)/shard_map/attend_back/pallas_call | solution.py:532
  535.3 7.3 %output_grads.1 = bf16[4,8,64,256]{3,2,1,0:T(8,128)(2,1)} custom-call(bf16[8,1024,256]{2,1,0:T(8,128)(2,1)} %copy-done.1, bf16[1024,256]{1,0:T(8,128)(2,1)} %bitcast.188), custom_call_target="tpu_custom_call" | custom-call | flops 1650000000 | tf_op jit(solution)/shard_map/output_grads/pallas_call | solution.py:737
  551.8 12.5 %project_back.1 = (bf16[3,1024,256]{2,1,0:T(8,128)(2,1)}, bf16[8,128,2048]{2,1,0:T(8,128)(2,1)}, f32[1,2048]{1,0:T(1,128)}) custom-call(s32[8]{0:T(128)} %stack.59._, bf16[1024,2048]{1,0:T(8,128)(2,1)} %bitcast.10.x_ref, bf16[4,8,208,256]{3,2,1,0:T(8,128)(2,1)} %copy-done.9, f32[1024,128]{1,0:T(8,128)} %get-tuple-element.216.cos_ref, ...), custom_call_target="tpu_custom_call" | custom-call | flops 2816000000 | tf_op jit(solution)/shard_map/project_back/pallas_call | solution.py:656
  565.7 9.7 %projection_grads.1 = bf16[4,8,208,256]{3,2,1,0:T(8,128)(2,1)} custom-call(bf16[3,1024,256]{2,1,0:T(8,128)(2,1)} %get-tuple-element.160.left_ref, bf16[1024,2048]{1,0:T(8,128)(2,1)} %get-tuple-element.162.right_ref, f32[16,2048]{1,0:T(8,128)} %select_maximum_fusion.gain_ref), custom_call_target="tpu_custom_call" | custom-call | flops 2062499968 | tf_op jit(solution)/shard_map/projection_grads/pallas_call | solution.py:710
  589.1 23.4 %collective-permute-done.37 = bf16[2,128,2048]{2,1,0:T(8,128)(2,1)} collective-permute-done((bf16[2,128,2048]{2,1,0:T(8,128)(2,1)}, bf16[2,128,2048]{2,1,0:T(8,128)(2,1)}, u32[]{:S(2)}, u32[]{:S(2)}) %collective-permute-start.37) | collective-permute-done | bytes 1048608 | tf_op jit(solution)/shard_map/ppermute | solution.py:59
  626.4 8.1 %collective-permute-done.40 = bf16[2,128,2048]{2,1,0:T(8,128)(2,1)} collective-permute-done((bf16[2,128,2048]{2,1,0:T(8,128)(2,1)}, bf16[2,128,2048]{2,1,0:T(8,128)(2,1)}, u32[]{:S(2)}, u32[]{:S(2)}) %collective-permute-start.40) | collective-permute-done | bytes 1048608 | tf_op jit(solution)/shard_map/ppermute | solution.py:59
  665.5 15.8 %collective-permute-done.44 = bf16[128,2048]{1,0:T(8,128)(2,1)S(1)} collective-permute-done((bf16[128,2048]{1,0:T(8,128)(2,1)S(1)}, bf16[128,2048]{1,0:T(8,128)(2,1)S(1)}, u32[]{:S(2)}, u32[]{:S(2)}) %collective-permute-start.44) | collective-permute-done | bytes 524320 | tf_op jit(solution)/shard_map/ppermute | solution.py:59
  (267 shorter events, 237.1 us)
Async XLA Ops:
  10.3 25.5 %collective-permute-start.1 = (bf16[128,2048]{1,0:T(8,128)(2,1)}, bf16[128,2048]{1,0:T(8,128)(2,1)S(1)}, u32[]{:S(2)}, u32[]{:S(2)}) collective-permute-start(bf16[128,2048]{1,0:T(8,128)(2,1)} %param.12), channel_id=1, source_target_pairs={{0,24},{4,28},{8,0},{12,4},{16,8},{20,12},{24,16},{28,20},{1,25},{... | collective-permute-start | bytes 1572872 | tf_op jit(solution)/shard_map/ppermute | solution.py:59
  12.3 23.5 %collective-permute-start.2 = (bf16[128,2048]{1,0:T(8,128)(2,1)}, bf16[128,2048]{1,0:T(8,128)(2,1)S(1)}, u32[]{:S(2)}, u32[]{:S(2)}) collective-permute-start(bf16[128,2048]{1,0:T(8,128)(2,1)} %param.12), channel_id=1, source_target_pairs={{0,4},{4,0},{8,12},{12,8},{16,20},{20,16},{24,28},{28,24},{1,5},{5... | collective-permute-start | bytes 1572872 | tf_op jit(solution)/shard_map/ppermute | solution.py:59
  16.8 50.7 %all-to-all-start = ((bf16[8,208,256]{2,1,0:T(8,128)(2,1)}), bf16[8,208,256]{2,1,0:T(8,128)(2,1)S(1)}, u32[]{:S(2)}, u32[]{:S(2)}) async-start(bf16[8,208,256]{2,1,0:T(8,128)(2,1)} %get-tuple-element.99), calls=%async_computation | async-start | bytes 1703936 | tf_op jit(solution)/shard_map/all_to_all | solution.py:252
  20.3 260.5 %all-gather.6.cloned.1.call-start = ((), (), s32[]{:S(2)}) async-start(), calls=%async_computation.8 | async-start | bytes 8650752 | tf_op jit(solution)/shard_map/all_gather | solution.py:256
  35.8 24.9 %collective-permute-start.3 = (bf16[128,2048]{1,0:T(8,128)(2,1)S(1)}, bf16[128,2048]{1,0:T(8,128)(2,1)S(1)}, u32[]{:S(2)}, u32[]{:S(2)}) collective-permute-start(bf16[128,2048]{1,0:T(8,128)(2,1)S(1)} %collective-permute-done), channel_id=1, source_target_pairs={{0,8},{4,12},{8,16},{12,20},{16,24},{20,28},{24,0},{28,4},{1,9},{5... | collective-permute-start | bytes 1572872 | tf_op jit(solution)/shard_map/ppermute | solution.py:59
  37.6 23.2 %collective-permute-start.4 = (bf16[128,2048]{1,0:T(8,128)(2,1)S(1)}, bf16[128,2048]{1,0:T(8,128)(2,1)S(1)}, u32[]{:S(2)}, u32[]{:S(2)}) collective-permute-start(bf16[128,2048]{1,0:T(8,128)(2,1)S(1)} %collective-permute-done), channel_id=1, source_target_pairs={{0,4},{4,0},{8,12},{12,8},{16,20},{20,16},{24,28},{28,24},{1,5},{5... | collective-permute-start | bytes 1572872 | tf_op jit(solution)/shard_map/ppermute | solution.py:59
  41.3 26.1 %collective-permute-start.5 = (bf16[128,2048]{1,0:T(8,128)(2,1)S(1)}, bf16[128,2048]{1,0:T(8,128)(2,1)}, u32[]{:S(2)}, u32[]{:S(2)}) collective-permute-start(bf16[128,2048]{1,0:T(8,128)(2,1)S(1)} %collective-permute-done.1), channel_id=1, source_target_pairs={{0,4},{4,0},{8,12},{12,8},{16,20},{20,16},{24,28},{28,24},{1,5},{5... | collective-permute-start | bytes 1572872 | tf_op jit(solution)/shard_map/ppermute | solution.py:59
  88.7 103.7 %all-to-all-start.1 = ((bf16[8,3,256,256]{3,2,1,0:T(8,128)(2,1)}), bf16[8,3,256,256]{3,2,1,0:T(8,128)(2,1)S(1)}, u32[]{:S(2)}, u32[]{:S(2)}) async-start(bf16[8,3,256,256]{3,2,1,0:T(8,128)(2,1)} %prepare.1), calls=%async_computation.1 | async-start | bytes 6291456 | tf_op jit(solution)/shard_map/all_to_all | solution.py:252
  92.3 209.3 %all-gather.4.cloned.1.call-start = ((), (), s32[]{:S(2)}) async-start(), calls=%async_computation.6 | async-start | bytes 4718592 | tf_op jit(solution)/shard_map/all_gather | solution.py:256
  111.6 25.9 %collective-permute-start.10 = (bf16[2,8,128,256]{3,2,1,0:T(8,128)(2,1)}, bf16[2,8,128,256]{3,2,1,0:T(8,128)(2,1)}, u32[]{:S(2)}, u32[]{:S(2)}) collective-permute-start(bf16[2,8,128,256]{3,2,1,0:T(8,128)(2,1)} %bitcast.185), channel_id=1, source_target_pairs={{0,2},{1,3},{2,0},{3,1},{4,6},{5,7},{6,4},{7,5},{8,10},{9,11},{10,... | collective-permute-start | bytes 3145736 | tf_op jit(solution)/shard_map/ppermute | solution.py:59
  113.1 24.3 %collective-permute-start.11 = (bf16[2,8,128,256]{3,2,1,0:T(8,128)(2,1)}, bf16[2,8,128,256]{3,2,1,0:T(8,128)(2,1)}, u32[]{:S(2)}, u32[]{:S(2)}) collective-permute-start(bf16[2,8,128,256]{3,2,1,0:T(8,128)(2,1)} %bitcast.186), channel_id=1, source_target_pairs={{0,1},{1,0},{2,3},{3,2},{4,5},{5,4},{6,7},{7,6},{8,9},{9,8},{10,11... | collective-permute-start | bytes 3145736 | tf_op jit(solution)/shard_map/ppermute | solution.py:59
  138.2 374.3 %reduce-scatter.2.cloned.1.call-start = ((), (), s32[]{:S(2)}) async-start(), calls=%async_computation.7 | async-start | bytes 4718592 | tf_op jit(solution)/shard_map/reduce_scatter | solution.py:260
  192.3 81.6 %collective-permute-start.20 = (bf16[8,3,256,256]{3,2,1,0:T(8,128)(2,1)S(1)}, bf16[8,3,256,256]{3,2,1,0:T(8,128)(2,1)}, u32[]{:S(2)}, u32[]{:S(2)}) collective-permute-start(bf16[8,3,256,256]{3,2,1,0:T(8,128)(2,1)S(1)} %all-to-all-done.1.refs_2_.refs_4_), channel_id=1, source_target_pairs={{0,2},{1,3},{2,0},{3,1},{4,6},{5,7},{6,4},{7,5},{8,10},{9,11},{10,... | collective-permute-start | bytes 9437192 | tf_op jit(solution)/shard_map/ppermute | solution.py:59
  196.4 26.3 %collective-permute-start.14 = (bf16[1024,256]{1,0:T(8,128)(2,1)}, bf16[1024,256]{1,0:T(8,128)(2,1)S(1)}, u32[]{:S(2)}, u32[]{:S(2)}) collective-permute-start(bf16[1024,256]{1,0:T(8,128)(2,1)} %get-tuple-element.114.o_ref), channel_id=1, source_target_pairs={{0,24},{4,28},{8,0},{12,4},{16,8},{20,12},{24,16},{28,20},{1,25},{... | collective-permute-start | bytes 1572872 | tf_op jit(solution)/shard_map/ppermute | solution.py:59
  224.9 28.7 %collective-permute-start.18 = (bf16[1024,256]{1,0:T(8,128)(2,1)S(1)}, bf16[1024,256]{1,0:T(8,128)(2,1)S(1)}, u32[]{:S(2)}, u32[]{:S(2)}) collective-permute-start(bf16[1024,256]{1,0:T(8,128)(2,1)S(1)} %collective-permute-done.14), channel_id=1, source_target_pairs={{0,4},{4,0},{8,12},{12,8},{16,20},{20,16},{24,28},{28,24},{1,5},{5... | collective-permute-start | bytes 1572872 | tf_op jit(solution)/shard_map/ppermute | solution.py:59
  254.9 23.8 %collective-permute-start.21 = (bf16[8,3,256,256]{3,2,1,0:T(8,128)(2,1)S(1)}, bf16[8,3,256,256]{3,2,1,0:T(8,128)(2,1)}, u32[]{:S(2)}, u32[]{:S(2)}) collective-permute-start(bf16[8,3,256,256]{3,2,1,0:T(8,128)(2,1)S(1)} %all-to-all-done.1.refs_2_.refs_4_), channel_id=1, source_target_pairs={{0,1},{1,0},{2,3},{3,2},{4,5},{5,4},{6,7},{7,6},{8,9},{9,8},{10,11... | collective-permute-start | bytes 9437192 | tf_op jit(solution)/shard_map/ppermute | solution.py:59
  339.2 25.0 %collective-permute-start.24 = (bf16[2,128,2048]{2,1,0:T(8,128)(2,1)S(1)}, bf16[2,128,2048]{2,1,0:T(8,128)(2,1)S(1)}, u32[]{:S(2)}, u32[]{:S(2)}) collective-permute-start(bf16[2,128,2048]{2,1,0:T(8,128)(2,1)S(1)} %get-tuple-element.196), channel_id=1, source_target_pairs={{0,4},{4,0},{8,12},{12,8},{16,20},{20,16},{24,28},{28,24},{1,5},{5... | collective-permute-start | bytes 3145736 | tf_op jit(solution)/shard_map/ppermute | solution.py:59
  364.2 29.5 %collective-permute-start.27 = (bf16[8,3,256,256]{3,2,1,0:T(8,128)(2,1)}, bf16[8,3,256,256]{3,2,1,0:T(8,128)(2,1)}, u32[]{:S(2)}, u32[]{:S(2)}) collective-permute-start(bf16[8,3,256,256]{3,2,1,0:T(8,128)(2,1)} %get-tuple-element.140), channel_id=1, source_target_pairs={{0,1},{1,0},{2,3},{3,2},{4,5},{5,4},{6,7},{7,6},{8,9},{9,8},{10,11... | collective-permute-start | bytes 9437192 | tf_op jit(solution)/shard_map/ppermute | solution.py:59
  364.2 29.5 %collective-permute-start.28 = (bf16[8,3,256,256]{3,2,1,0:T(8,128)(2,1)}, bf16[8,3,256,256]{3,2,1,0:T(8,128)(2,1)}, u32[]{:S(2)}, u32[]{:S(2)}) collective-permute-start(bf16[8,3,256,256]{3,2,1,0:T(8,128)(2,1)} %get-tuple-element.141), channel_id=1, source_target_pairs={{0,1},{1,0},{2,3},{3,2},{4,5},{5,4},{6,7},{7,6},{8,9},{9,8},{10,11... | collective-permute-start | bytes 9437192 | tf_op jit(solution)/shard_map/ppermute | solution.py:59
  364.7 25.1 %collective-permute-start.23 = (bf16[2,128,2048]{2,1,0:T(8,128)(2,1)S(1)}, bf16[2,128,2048]{2,1,0:T(8,128)(2,1)S(1)}, u32[]{:S(2)}, u32[]{:S(2)}) collective-permute-start(bf16[2,128,2048]{2,1,0:T(8,128)(2,1)S(1)} %get-tuple-element.197), channel_id=1, source_target_pairs={{0,4},{4,0},{8,12},{12,8},{16,20},{20,16},{24,28},{28,24},{1,5},{5... | collective-permute-start | bytes 3145736 | tf_op jit(solution)/shard_map/ppermute | solution.py:59
  367.1 22.7 %collective-permute-start.25 = (bf16[128,2048]{1,0:T(8,128)(2,1)S(1)}, bf16[128,2048]{1,0:T(8,128)(2,1)S(1)}, u32[]{:S(2)}, u32[]{:S(2)}) collective-permute-start(bf16[128,2048]{1,0:T(8,128)(2,1)S(1)} %get-tuple-element.191), channel_id=1, source_target_pairs={{0,8},{4,12},{8,16},{12,20},{16,24},{20,28},{24,0},{28,4},{1,9},{5... | collective-permute-start | bytes 1572872 | tf_op jit(solution)/shard_map/ppermute | solution.py:59
  369.5 24.2 %collective-permute-start.26 = (bf16[128,2048]{1,0:T(8,128)(2,1)S(1)}, bf16[128,2048]{1,0:T(8,128)(2,1)S(1)}, u32[]{:S(2)}, u32[]{:S(2)}) collective-permute-start(bf16[128,2048]{1,0:T(8,128)(2,1)S(1)} %get-tuple-element.190), channel_id=1, source_target_pairs={{0,24},{4,28},{8,0},{12,4},{16,8},{20,12},{24,16},{28,20},{1,25},{... | collective-permute-start | bytes 1572872 | tf_op jit(solution)/shard_map/ppermute | solution.py:59
  445.6 70.0 %collective-permute-start.45 = (bf16[8,3,256,256]{3,2,1,0:T(8,128)(2,1)}, bf16[8,3,256,256]{3,2,1,0:T(8,128)(2,1)}, u32[]{:S(2)}, u32[]{:S(2)}) collective-permute-start(bf16[8,3,256,256]{3,2,1,0:T(8,128)(2,1)} %add_convert_fusion.1), channel_id=1, source_target_pairs={{0,2},{1,3},{2,0},{3,1},{4,6},{5,7},{6,4},{7,5},{8,10},{9,11},{10,... | collective-permute-start | bytes 9437192 | tf_op jit(solution)/shard_map/ppermute | solution.py:59
  457.8 50.4 %all-to-all-start.2 = ((bf16[8,128,256]{2,1,0:T(8,128)(2,1)}), bf16[8,128,256]{2,1,0:T(8,128)(2,1)S(1)}, u32[]{:S(2)}, u32[]{:S(2)}) async-start(bf16[8,128,256]{2,1,0:T(8,128)(2,1)} %bitcast.176), calls=%async_computation.3 | async-start | bytes 1048576 | tf_op jit(solution)/shard_map/all_to_all | solution.py:252
  523.0 25.5 %collective-permute-start.35 = (bf16[2,8,128,256]{3,2,1,0:T(8,128)(2,1)}, bf16[2,8,128,256]{3,2,1,0:T(8,128)(2,1)}, u32[]{:S(2)}, u32[]{:S(2)}) collective-permute-start(bf16[2,8,128,256]{3,2,1,0:T(8,128)(2,1)} %fusion.7), channel_id=1, source_target_pairs={{0,2},{1,3},{2,0},{3,1},{4,6},{5,7},{6,4},{7,5},{8,10},{9,11},{10,... | collective-permute-start | bytes 3145736 | tf_op jit(solution)/shard_map/ppermute | solution.py:59
  530.6 117.4 %all-to-all-start.4 = ((bf16[8,3,256,256]{3,2,1,0:T(8,128)(2,1)}), bf16[8,3,256,256]{3,2,1,0:T(8,128)(2,1)}, u32[]{:S(2)}, u32[]{:S(2)}) async-start(bf16[8,3,256,256]{3,2,1,0:T(8,128)(2,1)} %add_convert_fusion), calls=%async_computation.5 | async-start | bytes 6291456 | tf_op jit(solution)/shard_map/all_to_all | solution.py:252
  578.4 34.1 %collective-permute-start.38 = (bf16[2,8,208,256]{3,2,1,0:T(8,128)(2,1)}, bf16[2,8,208,256]{3,2,1,0:T(8,128)(2,1)}, u32[]{:S(2)}, u32[]{:S(2)}) collective-permute-start(bf16[2,8,208,256]{3,2,1,0:T(8,128)(2,1)} %pad_maximum_fusion.1), channel_id=1, source_target_pairs={{0,1},{1,0},{2,3},{3,2},{4,5},{5,4},{6,7},{7,6},{8,9},{9,8},{10,11... | collective-permute-start | bytes 5111816 | tf_op jit(solution)/shard_map/ppermute | solution.py:59
  579.9 32.6 %collective-permute-start.37 = (bf16[2,128,2048]{2,1,0:T(8,128)(2,1)}, bf16[2,128,2048]{2,1,0:T(8,128)(2,1)}, u32[]{:S(2)}, u32[]{:S(2)}) collective-permute-start(bf16[2,128,2048]{2,1,0:T(8,128)(2,1)} %get-tuple-element.193), channel_id=1, source_target_pairs={{0,4},{4,0},{8,12},{12,8},{16,20},{20,16},{24,28},{28,24},{1,5},{5... | collective-permute-start | bytes 3145736 | tf_op jit(solution)/shard_map/ppermute | solution.py:59
  587.3 47.3 %collective-permute-start.40 = (bf16[2,128,2048]{2,1,0:T(8,128)(2,1)}, bf16[2,128,2048]{2,1,0:T(8,128)(2,1)}, u32[]{:S(2)}, u32[]{:S(2)}) collective-permute-start(bf16[2,128,2048]{2,1,0:T(8,128)(2,1)} %get-tuple-element.192), channel_id=1, source_target_pairs={{0,4},{4,0},{8,12},{12,8},{16,20},{20,16},{24,28},{28,24},{1,5},{5... | collective-permute-start | bytes 3145736 | tf_op jit(solution)/shard_map/ppermute | solution.py:59
  614.8 30.6 %collective-permute-start.43 = (bf16[8,208,256]{2,1,0:T(8,128)(2,1)}, bf16[8,208,256]{2,1,0:T(8,128)(2,1)}, u32[]{:S(2)}, u32[]{:S(2)}) collective-permute-start(bf16[8,208,256]{2,1,0:T(8,128)(2,1)} %fusion.13), channel_id=1, source_target_pairs={{0,2},{1,3},{2,0},{3,1},{4,6},{5,7},{6,4},{7,5},{8,10},{9,11},{10,... | collective-permute-start | bytes 2555912 | tf_op jit(solution)/shard_map/ppermute | solution.py:59
  621.9 23.5 %collective-permute-start.42 = (bf16[128,2048]{1,0:T(8,128)(2,1)}, bf16[128,2048]{1,0:T(8,128)(2,1)}, u32[]{:S(2)}, u32[]{:S(2)}) collective-permute-start(bf16[128,2048]{1,0:T(8,128)(2,1)} %get-tuple-element.188), channel_id=1, source_target_pairs={{0,24},{4,28},{8,0},{12,4},{16,8},{20,12},{24,16},{28,20},{1,25},{... | collective-permute-start | bytes 1572872 | tf_op jit(solution)/shard_map/ppermute | solution.py:59
  648.0 37.0 %all-to-all-start.3 = ((bf16[8,208,256]{2,1,0:T(8,128)(2,1)}), bf16[8,208,256]{2,1,0:T(8,128)(2,1)S(1)}, u32[]{:S(2)}, u32[]{:S(2)}) async-start(bf16[8,208,256]{2,1,0:T(8,128)(2,1)} %fusion), calls=%async_computation.4 | async-start | bytes 1703936 | tf_op jit(solution)/shard_map/all_to_all | solution.py:252
  (62 other events, 886.6 us)
Sparse Core Ops, SparseCore 0:
  88.8 130.1 all-gather.5
  221.1 80.4 all-gather.3
  413.9 98.4 reduce-scatter.1

commit v5 on v4

--- a/solution.py
+++ b/solution.py
@@ -948,10 +948,11 @@
     ff_piece = ff_u // nb
     tokens_plan = gather_plan(tokens, "blk")
 
+    tables = (cosine, sine, low, high)
+
     def prepared():
         yield []
-        (value,) = yield [prepare(w_gate, w_up, w_down, nb)]
-        return value
+        return (yield [prepare(w_gate, w_up, w_down, nb), *tables])
 
     def swapped(parts, spare=0):
         got = swap(parts, "blk")
@@ -961,7 +962,7 @@
 
     if strided:
         sent, out_flipped = flip(w_query, w_key, w_value, w_output, attn_gain, mlp_gain, nb)
-        x_all, ff_sent, w_qkv = together(
+        x_all, (ff_sent, cosine, sine, low, high), w_qkv = together(
             tokens_plan,
             prepared(),
             chain(swapped(sent, 1), lambda got: gather_plan(got, "uly")),
@@ -972,7 +973,7 @@
         out_flipped = flipped[3]
         sent = gather(jnp.stack(flipped[:3])[None], "uly")
         sent = jnp.transpose(sent, (0, 2, 1, 3)).reshape(nb, group, 3, rows)
-        x_all, ff_sent, got = together(tokens_plan, prepared(), swapped(sent))
+        x_all, (ff_sent, cosine, sine, low, high), got = together(tokens_plan, prepared(), swapped(sent))
         got = jnp.transpose(got, (2, 1, 0, 3)).reshape(3, group, dim)
         got = jnp.pad(got, ((0, 0), (0, piece - group), (0, 0))).reshape(3 * piece, dim)
         all_gains = jnp.transpose(gather(gains[None], "blk"), (1, 0, 2)).reshape(2, dim)

time: 710 us -> 710 us (level)
  transfers between devices with their start and end apart: 54 -> 54, of which waited for: 31 -> 32; matrix products, arithmetic and copies ran while one was open for 12% -> 12% of each run, Pallas kernels for 25% -> 25%
where the time goes in v5:
time: 710 us; the launch traced here: 701 us
  waiting for transfers between devices  287 us (40%)
  Pallas kernels  209 us (29%)
  starting transfers between devices  78.8 us (11%)
  other arithmetic  59.7 us (8%)
  local copies, waits for them, and re-layouts  51.4 us (7%)
  between operations  15 us (2%)
    ppermute x46, waiting for transfers between devices, hop(): return lax.ppermute(value, axis, pairs)  248 us
    ppermute x46, starting transfers between devices, hop(): return lax.ppermute(value, axis, pairs)  52.2 us
    pallas_call x1, Pallas kernels, attend_back(): pl.pallas_call(functools.partial(attend_back_kernel, tile), grid=(nb,), i...  40.5 us
    all_to_all x5, waiting for transfers between devices, swap(): return lax.all_to_all(parts, axis, 0, 0, tiled=True)  29.7 us
    all_to_all x5, starting transfers between devices, swap(): return lax.all_to_all(parts, axis, 0, 0, tiled=True)  26.5 us
    pallas_call x1, Pallas kernels, attend(): pl.pallas_call(functools.partial(attend_kernel, tile), grid=(nq,), in_spe...  26.4 us
    pallas_call x2, Pallas kernels, mix(): pl.pallas_call(functools.partial(mix_kernel, which, n), grid_spec=pltpu.P...  24.9 us
    pallas_call x1, Pallas kernels, hidden(): pl.pallas_call(functools.partial(hidden_kernel, n), grid=(count // rows,)...  20.5 us
  transfers between devices with their start and end apart: 54, of which 32 were waited for; matrix products, arithmetic and copies ran while one was open for 12% of the time, Pallas kernels for 25%

profile of v5, /device:TPU:0, one launch (start us, length us, event | category | flops | bytes accessed | tf_op | source)
XLA Modules:
  0.0 700.5 jit_solution(4385416704827822178)
XLA Ops:
  22.3 6.7 prepare.1
  47.3 13.4 %collective-permute-done.3 = bf16[128,2048]{1,0:T(8,128)(2,1)S(1)} collective-permute-done((bf16[128,2048]{1,0:T(8,128)(2,1)S(1)}, bf16[128,2048]{1,0:T(8,128)(2,1)S(1)}, u32[]{:S(2)}, u32[]{:S(2)}) %collective-permute-start.3) | collective-permute-done | bytes 524320 | tf_op jit(solution)/shard_map/ppermute | solution.py:59
  60.7 6.7 collective-permute-done.5
  72.5 10.8 %collective-permute-done.6 = bf16[128,2048]{1,0:T(8,128)(2,1)S(1)} collective-permute-done((bf16[128,2048]{1,0:T(8,128)(2,1)S(1)}, bf16[128,2048]{1,0:T(8,128)(2,1)S(1)}, u32[]{:S(2)}, u32[]{:S(2)}) %collective-permute-start.6) | collective-permute-done | bytes 524320 | tf_op jit(solution)/shard_map/ppermute | solution.py:59
  98.1 9.5 %project.1 = (bf16[1024,256]{1,0:T(8,128)(2,1)}, bf16[2,1024,256]{2,1,0:T(8,128)(2,1)}, bf16[1024,2048]{1,0:T(8,128)(2,1)}) custom-call(bf16[1024,2048]{1,0:T(8,128)(2,1)} %bitcast.16.x_ref, bf16[4,8,208,256]{3,2,1,0:T(8,128)(2,1)} %copy-done.9, f32[1024,128]{1,0:T(8,128)} %get-tuple-element.115.cos_ref, f32[1024,128]{1,0:T(8,128)} %get-tuple-element.116.sin_ref), custom_call_target="tpu_custom_call" | custom-call | flops 2534400000 | tf_op jit(solution)/shard_map/project/pallas_call | solution.py:310
  109.1 24.0 %collective-permute-done.10 = bf16[2,8,128,256]{3,2,1,0:T(8,128)(2,1)} collective-permute-done((bf16[2,8,128,256]{3,2,1,0:T(8,128)(2,1)}, bf16[2,8,128,256]{3,2,1,0:T(8,128)(2,1)}, u32[]{:S(2)}, u32[]{:S(2)}) %collective-permute-start.10) | collective-permute-done | bytes 1048608 | tf_op jit(solution)/shard_map/ppermute | solution.py:59
  139.8 26.4 %attend.1 = (bf16[1024,256]{1,0:T(8,128)(2,1)}, f32[4,4,256]{2,1,0:T(4,128)}) custom-call(s32[4,1,256]{2,1,0:T(1,128)} %bitcast.199, s32[4,1,256]{2,1,0:T(1,128)} %broadcast_add_fusion.high_ref, bf16[1024,256]{1,0:T(8,128)(2,1)} %get-tuple-element.117.q_ref, bf16[4,2,8,128,256]{4,3,2,1,0:T(8,128)(2,1)} %copy-done.7), custom_call_target="tpu_custom_call" | custom-call | flops 7424999936 | tf_op jit(solution)/shard_map/attend/pallas_call | solution.py:418
  166.3 26.0 %all-to-all-done.1.refs_2_.refs_4_ = bf16[8,3,256,256]{3,2,1,0:T(8,128)(2,1)S(1)} async-done(((bf16[8,3,256,256]{3,2,1,0:T(8,128)(2,1)}), bf16[8,3,256,256]{3,2,1,0:T(8,128)(2,1)S(1)}, u32[]{:S(2)}, u32[]{:S(2)}) %all-to-all-start.1) | async-done | bytes 3145760 | tf_op jit(solution)/shard_map/all_to_all | solution.py:252
  200.6 15.4 %collective-permute-done.13 = bf16[1024,256]{1,0:T(8,128)(2,1)S(1)} collective-permute-done((bf16[1024,256]{1,0:T(8,128)(2,1)}, bf16[1024,256]{1,0:T(8,128)(2,1)S(1)}, u32[]{:S(2)}, u32[]{:S(2)}) %collective-permute-start.13) | collective-permute-done | bytes 524320 | tf_op jit(solution)/shard_map/ppermute | solution.py:59
  216.0 6.7 collective-permute-done.14
  225.5 17.0 %collective-permute-done.16 = bf16[1024,256]{1,0:T(8,128)(2,1)S(1)} collective-permute-done((bf16[1024,256]{1,0:T(8,128)(2,1)S(1)}, bf16[1024,256]{1,0:T(8,128)(2,1)S(1)}, u32[]{:S(2)}, u32[]{:S(2)}) %collective-permute-start.16) | collective-permute-done | bytes 524320 | tf_op jit(solution)/shard_map/ppermute | solution.py:59
  244.0 9.6 %collective-permute-done.18 = bf16[1024,256]{1,0:T(8,128)(2,1)S(1)} collective-permute-done((bf16[1024,256]{1,0:T(8,128)(2,1)S(1)}, bf16[1024,256]{1,0:T(8,128)(2,1)S(1)}, u32[]{:S(2)}, u32[]{:S(2)}) %collective-permute-start.18) | collective-permute-done | bytes 524320 | tf_op jit(solution)/shard_map/ppermute | solution.py:59
  254.9 18.9 %collective-permute-done.19 = bf16[1024,256]{1,0:T(8,128)(2,1)S(1)} collective-permute-done((bf16[1024,256]{1,0:T(8,128)(2,1)S(1)}, bf16[1024,256]{1,0:T(8,128)(2,1)S(1)}, u32[]{:S(2)}, u32[]{:S(2)}) %collective-permute-start.19) | collective-permute-done | bytes 524320 | tf_op jit(solution)/shard_map/ppermute | solution.py:59
  280.7 16.0 %output_project.1 = (f32[1024,2048]{1,0:T(8,128)}, bf16[1024,2048]{1,0:T(8,128)(2,1)}) custom-call(bf16[1024,2048]{1,0:T(8,128)(2,1)} %bitcast.16.x_ref, bf16[8,1024,256]{2,1,0:T(8,128)(2,1)} %copy-done.1, bf16[8,4,8,64,256]{4,3,2,1,0:T(8,128)(2,1)} %bitcast.177, f32[1,2048]{1,0:T(1,128)} %bitcast.192), custom_call_target="tpu_custom_call" | custom-call | flops 4224000000 | tf_op jit(solution)/shard_map/output_project/pallas_call | solution.py:573
  301.6 20.5 %hidden.1 = (bf16[4,1024,256]{2,1,0:T(8,128)(2,1)}, bf16[4,1024,256]{2,1,0:T(8,128)(2,1)}, bf16[4,1024,256]{2,1,0:T(8,128)(2,1)}) custom-call(bf16[1024,2048]{1,0:T(8,128)(2,1)} %get-tuple-element.141.refs_0_.n_ref, bf16[1024,2048]{1,0:T(8,128)(2,1)} %all-gather.4.cloned.1.call-done.refs_1_.g_ref, bf16[8,3,256,256]{3,2,1,0:T(8,128)(2,1)} %copy-done, ...), custom_call_target="tpu_custom_call" | custom-call | flops 5500000256 | tf_op jit(solution)/shard_map/hidden/pallas_call | solution.py:824
  322.0 15.3 %mix.2 = bf16[8,128,2048]{2,1,0:T(8,128)(2,1)} custom-call(s32[8]{0:T(128)} %stack.59._, bf16[4,1024,256]{2,1,0:T(8,128)(2,1)} %get-tuple-element.139.refs_0_.refs_1_.dg_ref, bf16[4,1024,256]{2,1,0:T(8,128)(2,1)} %get-tuple-element.139.refs_0_.refs_1_.dg_ref, bf16[4,1024,256]{2,1,0:T(8,128)(2,1)} %get-tuple-element.140.refs_2_.refs_3_.du_ref, ...), custom_call_target="tpu_custom_call" | custom-call | flops 4400000000 | tf_op jit(solution)/shard_map/mix/pallas_call | solution.py:860
  339.7 18.7 %hidden_grads.1 = (bf16[8,3,256,256]{3,2,1,0:T(8,128)(2,1)}, bf16[8,3,256,256]{3,2,1,0:T(8,128)(2,1)}, bf16[8,3,256,256]{3,2,1,0:T(8,128)(2,1)}, bf16[8,3,256,256]{3,2,1,0:T(8,128)(2,1)}) custom-call(bf16[1024,2048]{1,0:T(8,128)(2,1)} %get-tuple-element.141.refs_0_.n_ref, bf16[1024,2048]{1,0:T(8,128)(2,1)} %all-gather.4.cloned.1.call-done.refs_1_.g_ref, ...), custom_call_target="tpu_custom_call" | custom-call | flops 6874999808 | tf_op jit(solution)/shard_map/hidden_grads/pallas_call | solution.py:889
  371.3 9.6 %mix.3 = bf16[8,128,2048]{2,1,0:T(8,128)(2,1)} custom-call(s32[8]{0:T(128)} %iota.43._, bf16[4,1024,256]{2,1,0:T(8,128)(2,1)} %get-tuple-element.142.act_ref.refs_0_.refs_1_, bf16[4,1024,256]{2,1,0:T(8,128)(2,1)} %get-tuple-element.142.act_ref.refs_0_.refs_1_, bf16[8,3,256,256]{3,2,1,0:T(8,128)(2,1)} %copy-done, ...), custom_call_target="tpu_custom_call" | custom-call | flops 2200000000 | tf_op jit(solution)/shard_map/mix/pallas_call | solution.py:860
  380.9 8.9 %collective-permute-done.23 = bf16[2,128,2048]{2,1,0:T(8,128)(2,1)S(1)} collective-permute-done((bf16[2,128,2048]{2,1,0:T(8,128)(2,1)S(1)}, bf16[2,128,2048]{2,1,0:T(8,128)(2,1)S(1)}, u32[]{:S(2)}, u32[]{:S(2)}) %collective-permute-start.23) | collective-permute-done | bytes 1048608 | tf_op jit(solution)/shard_map/ppermute | solution.py:59
  397.1 13.7 %collective-permute-done.29 = bf16[128,2048]{1,0:T(8,128)(2,1)S(1)} collective-permute-done((bf16[128,2048]{1,0:T(8,128)(2,1)S(1)}, bf16[128,2048]{1,0:T(8,128)(2,1)S(1)}, u32[]{:S(2)}, u32[]{:S(2)}) %collective-permute-start.29) | collective-permute-done | bytes 524320 | tf_op jit(solution)/shard_map/ppermute | solution.py:59
  416.4 8.7 %output_back.1 = bf16[8,128,256]{2,1,0:T(8,128)(2,1)} custom-call(bf16[128,2048]{1,0:T(8,128)(2,1)} %get-tuple-element.193.d_ref, bf16[8,4,8,64,256]{4,3,2,1,0:T(8,128)(2,1)} %bitcast.178), custom_call_target="tpu_custom_call" | custom-call | flops 2200000000 | tf_op jit(solution)/shard_map/output_back/pallas_call | solution.py:605
  427.7 6.9 collective-permute-done.30
  448.0 7.7 %collective-permute-done.32 = bf16[2,128,256]{2,1,0:T(8,128)(2,1)S(1)} collective-permute-done((bf16[2,128,256]{2,1,0:T(8,128)(2,1)S(1)}, bf16[2,128,256]{2,1,0:T(8,128)(2,1)S(1)}, u32[]{:S(2)}, u32[]{:S(2)}) %collective-permute-start.32) | collective-permute-done | bytes 131104 | tf_op jit(solution)/shard_map/ppermute | solution.py:59
  457.7 10.0 %all-to-all-start.2 = ((bf16[8,128,256]{2,1,0:T(8,128)(2,1)}), bf16[8,128,256]{2,1,0:T(8,128)(2,1)S(1)}, u32[]{:S(2)}, u32[]{:S(2)}) async-start(bf16[8,128,256]{2,1,0:T(8,128)(2,1)} %bitcast.176), calls=%async_computation.3 | async-start | bytes 1048576 | tf_op jit(solution)/shard_map/all_to_all | solution.py:252
  467.7 40.5 %attend_back.1 = (bf16[1024,256]{1,0:T(8,128)(2,1)}, bf16[4,2,8,128,256]{4,3,2,1,0:T(8,128)(2,1)}) custom-call(s32[4,1,256]{2,1,0:T(1,128)} %bitcast.200, s32[4,1,256]{2,1,0:T(1,128)} %broadcast_add_fusion.high_ref, f32[1024,128]{1,0:T(8,128)} %get-tuple-element.115.cos_ref, f32[1024,128]{1,0:T(8,128)} %get-tuple-element.116.sin_ref, ...), custom_call_target="tpu_custom_call" | custom-call | flops 11274999808 | tf_op jit(solution)/shard_map/attend_back/pallas_call | solution.py:532
  535.2 7.3 %output_grads.1 = bf16[4,8,64,256]{3,2,1,0:T(8,128)(2,1)} custom-call(bf16[8,1024,256]{2,1,0:T(8,128)(2,1)} %copy-done.1, bf16[1024,256]{1,0:T(8,128)(2,1)} %bitcast.188), custom_call_target="tpu_custom_call" | custom-call | flops 1650000000 | tf_op jit(solution)/shard_map/output_grads/pallas_call | solution.py:737
  551.7 12.5 %project_back.1 = (bf16[3,1024,256]{2,1,0:T(8,128)(2,1)}, bf16[8,128,2048]{2,1,0:T(8,128)(2,1)}, f32[1,2048]{1,0:T(1,128)}) custom-call(s32[8]{0:T(128)} %stack.59._, bf16[1024,2048]{1,0:T(8,128)(2,1)} %bitcast.16.x_ref, bf16[4,8,208,256]{3,2,1,0:T(8,128)(2,1)} %copy-done.9, f32[1024,128]{1,0:T(8,128)} %get-tuple-element.115.cos_ref, ...), custom_call_target="tpu_custom_call" | custom-call | flops 2816000000 | tf_op jit(solution)/shard_map/project_back/pallas_call | solution.py:656
  565.6 9.7 %projection_grads.1 = bf16[4,8,208,256]{3,2,1,0:T(8,128)(2,1)} custom-call(bf16[3,1024,256]{2,1,0:T(8,128)(2,1)} %get-tuple-element.168.left_ref, bf16[1024,2048]{1,0:T(8,128)(2,1)} %get-tuple-element.170.right_ref, f32[16,2048]{1,0:T(8,128)} %select_maximum_fusion.gain_ref), custom_call_target="tpu_custom_call" | custom-call | flops 2062499968 | tf_op jit(solution)/shard_map/projection_grads/pallas_call | solution.py:710
  589.0 23.4 %collective-permute-done.37 = bf16[2,128,2048]{2,1,0:T(8,128)(2,1)} collective-permute-done((bf16[2,128,2048]{2,1,0:T(8,128)(2,1)}, bf16[2,128,2048]{2,1,0:T(8,128)(2,1)}, u32[]{:S(2)}, u32[]{:S(2)}) %collective-permute-start.37) | collective-permute-done | bytes 1048608 | tf_op jit(solution)/shard_map/ppermute | solution.py:59
  626.3 8.1 %collective-permute-done.40 = bf16[2,128,2048]{2,1,0:T(8,128)(2,1)} collective-permute-done((bf16[2,128,2048]{2,1,0:T(8,128)(2,1)}, bf16[2,128,2048]{2,1,0:T(8,128)(2,1)}, u32[]{:S(2)}, u32[]{:S(2)}) %collective-permute-start.40) | collective-permute-done | bytes 1048608 | tf_op jit(solution)/shard_map/ppermute | solution.py:59
  634.5 6.3 collective-permute-done.39
  665.4 15.8 %collective-permute-done.44 = bf16[128,2048]{1,0:T(8,128)(2,1)S(1)} collective-permute-done((bf16[128,2048]{1,0:T(8,128)(2,1)S(1)}, bf16[128,2048]{1,0:T(8,128)(2,1)S(1)}, u32[]{:S(2)}, u32[]{:S(2)}) %collective-permute-start.44) | collective-permute-done | bytes 524320 | tf_op jit(solution)/shard_map/ppermute | solution.py:59
  (267 shorter events, 234.9 us)
Async XLA Ops:
  7.2 25.6 %collective-permute-start = (bf16[128,2048]{1,0:T(8,128)(2,1)}, bf16[128,2048]{1,0:T(8,128)(2,1)S(1)}, u32[]{:S(2)}, u32[]{:S(2)}) collective-permute-start(bf16[128,2048]{1,0:T(8,128)(2,1)} %param.12), channel_id=1, source_target_pairs={{0,8},{4,12},{8,16},{12,20},{16,24},{20,28},{24,0},{28,4},{1,9},{5... | collective-permute-start | bytes 1572872 | tf_op jit(solution)/shard_map/ppermute | solution.py:59
  10.3 25.5 %collective-permute-start.1 = (bf16[128,2048]{1,0:T(8,128)(2,1)}, bf16[128,2048]{1,0:T(8,128)(2,1)S(1)}, u32[]{:S(2)}, u32[]{:S(2)}) collective-permute-start(bf16[128,2048]{1,0:T(8,128)(2,1)} %param.12), channel_id=1, source_target_pairs={{0,24},{4,28},{8,0},{12,4},{16,8},{20,12},{24,16},{28,20},{1,25},{... | collective-permute-start | bytes 1572872 | tf_op jit(solution)/shard_map/ppermute | solution.py:59
  12.4 23.5 %collective-permute-start.2 = (bf16[128,2048]{1,0:T(8,128)(2,1)}, bf16[128,2048]{1,0:T(8,128)(2,1)S(1)}, u32[]{:S(2)}, u32[]{:S(2)}) collective-permute-start(bf16[128,2048]{1,0:T(8,128)(2,1)} %param.12), channel_id=1, source_target_pairs={{0,4},{4,0},{8,12},{12,8},{16,20},{20,16},{24,28},{28,24},{1,5},{5... | collective-permute-start | bytes 1572872 | tf_op jit(solution)/shard_map/ppermute | solution.py:59
  16.8 50.7 %all-to-all-start = ((bf16[8,208,256]{2,1,0:T(8,128)(2,1)}), bf16[8,208,256]{2,1,0:T(8,128)(2,1)S(1)}, u32[]{:S(2)}, u32[]{:S(2)}) async-start(bf16[8,208,256]{2,1,0:T(8,128)(2,1)} %get-tuple-element.103), calls=%async_computation | async-start | bytes 1703936 | tf_op jit(solution)/shard_map/all_to_all | solution.py:252
  20.3 260.4 %all-gather.6.cloned.1.call-start = ((), (), s32[]{:S(2)}) async-start(), calls=%async_computation.8 | async-start | bytes 8650752 | tf_op jit(solution)/shard_map/all_gather | solution.py:256
  35.8 24.9 %collective-permute-start.3 = (bf16[128,2048]{1,0:T(8,128)(2,1)S(1)}, bf16[128,2048]{1,0:T(8,128)(2,1)S(1)}, u32[]{:S(2)}, u32[]{:S(2)}) collective-permute-start(bf16[128,2048]{1,0:T(8,128)(2,1)S(1)} %collective-permute-done), channel_id=1, source_target_pairs={{0,8},{4,12},{8,16},{12,20},{16,24},{20,28},{24,0},{28,4},{1,9},{5... | collective-permute-start | bytes 1572872 | tf_op jit(solution)/shard_map/ppermute | solution.py:59
  37.6 23.2 %collective-permute-start.4 = (bf16[128,2048]{1,0:T(8,128)(2,1)S(1)}, bf16[128,2048]{1,0:T(8,128)(2,1)S(1)}, u32[]{:S(2)}, u32[]{:S(2)}) collective-permute-start(bf16[128,2048]{1,0:T(8,128)(2,1)S(1)} %collective-permute-done), channel_id=1, source_target_pairs={{0,4},{4,0},{8,12},{12,8},{16,20},{20,16},{24,28},{28,24},{1,5},{5... | collective-permute-start | bytes 1572872 | tf_op jit(solution)/shard_map/ppermute | solution.py:59
  41.4 26.1 %collective-permute-start.5 = (bf16[128,2048]{1,0:T(8,128)(2,1)S(1)}, bf16[128,2048]{1,0:T(8,128)(2,1)}, u32[]{:S(2)}, u32[]{:S(2)}) collective-permute-start(bf16[128,2048]{1,0:T(8,128)(2,1)S(1)} %collective-permute-done.1), channel_id=1, source_target_pairs={{0,4},{4,0},{8,12},{12,8},{16,20},{20,16},{24,28},{28,24},{1,5},{5... | collective-permute-start | bytes 1572872 | tf_op jit(solution)/shard_map/ppermute | solution.py:59
  88.7 103.6 %all-to-all-start.1 = ((bf16[8,3,256,256]{3,2,1,0:T(8,128)(2,1)}), bf16[8,3,256,256]{3,2,1,0:T(8,128)(2,1)S(1)}, u32[]{:S(2)}, u32[]{:S(2)}) async-start(bf16[8,3,256,256]{3,2,1,0:T(8,128)(2,1)} %prepare.1), calls=%async_computation.1 | async-start | bytes 6291456 | tf_op jit(solution)/shard_map/all_to_all | solution.py:252
  92.3 209.2 %all-gather.4.cloned.1.call-start = ((), (), s32[]{:S(2)}) async-start(), calls=%async_computation.6 | async-start | bytes 4718592 | tf_op jit(solution)/shard_map/all_gather | solution.py:256
  107.6 25.5 %collective-permute-start.10 = (bf16[2,8,128,256]{3,2,1,0:T(8,128)(2,1)}, bf16[2,8,128,256]{3,2,1,0:T(8,128)(2,1)}, u32[]{:S(2)}, u32[]{:S(2)}) collective-permute-start(bf16[2,8,128,256]{3,2,1,0:T(8,128)(2,1)} %bitcast.185), channel_id=1, source_target_pairs={{0,2},{1,3},{2,0},{3,1},{4,6},{5,7},{6,4},{7,5},{8,10},{9,11},{10,... | collective-permute-start | bytes 3145736 | tf_op jit(solution)/shard_map/ppermute | solution.py:59
  109.1 24.0 %collective-permute-start.11 = (bf16[2,8,128,256]{3,2,1,0:T(8,128)(2,1)}, bf16[2,8,128,256]{3,2,1,0:T(8,128)(2,1)}, u32[]{:S(2)}, u32[]{:S(2)}) collective-permute-start(bf16[2,8,128,256]{3,2,1,0:T(8,128)(2,1)} %bitcast.186), channel_id=1, source_target_pairs={{0,1},{1,0},{2,3},{3,2},{4,5},{5,4},{6,7},{7,6},{8,9},{9,8},{10,11... | collective-permute-start | bytes 3145736 | tf_op jit(solution)/shard_map/ppermute | solution.py:59
  133.1 379.2 %reduce-scatter.2.cloned.1.call-start = ((), (), s32[]{:S(2)}) async-start(), calls=%async_computation.7 | async-start | bytes 4718592 | tf_op jit(solution)/shard_map/reduce_scatter | solution.py:260
  192.3 81.6 %collective-permute-start.20 = (bf16[8,3,256,256]{3,2,1,0:T(8,128)(2,1)S(1)}, bf16[8,3,256,256]{3,2,1,0:T(8,128)(2,1)}, u32[]{:S(2)}, u32[]{:S(2)}) collective-permute-start(bf16[8,3,256,256]{3,2,1,0:T(8,128)(2,1)S(1)} %all-to-all-done.1.refs_2_.refs_4_), channel_id=1, source_target_pairs={{0,2},{1,3},{2,0},{3,1},{4,6},{5,7},{6,4},{7,5},{8,10},{9,11},{10,... | collective-permute-start | bytes 9437192 | tf_op jit(solution)/shard_map/ppermute | solution.py:59
  196.8 25.9 %collective-permute-start.14 = (bf16[1024,256]{1,0:T(8,128)(2,1)}, bf16[1024,256]{1,0:T(8,128)(2,1)S(1)}, u32[]{:S(2)}, u32[]{:S(2)}) collective-permute-start(bf16[1024,256]{1,0:T(8,128)(2,1)} %get-tuple-element.122.o_ref), channel_id=1, source_target_pairs={{0,24},{4,28},{8,0},{12,4},{16,8},{20,12},{24,16},{28,20},{1,25},{... | collective-permute-start | bytes 1572872 | tf_op jit(solution)/shard_map/ppermute | solution.py:59
  224.9 28.7 %collective-permute-start.18 = (bf16[1024,256]{1,0:T(8,128)(2,1)S(1)}, bf16[1024,256]{1,0:T(8,128)(2,1)S(1)}, u32[]{:S(2)}, u32[]{:S(2)}) collective-permute-start(bf16[1024,256]{1,0:T(8,128)(2,1)S(1)} %collective-permute-done.14), channel_id=1, source_target_pairs={{0,4},{4,0},{8,12},{12,8},{16,20},{20,16},{24,28},{28,24},{1,5},{5... | collective-permute-start | bytes 1572872 | tf_op jit(solution)/shard_map/ppermute | solution.py:59
  254.9 23.8 %collective-permute-start.21 = (bf16[8,3,256,256]{3,2,1,0:T(8,128)(2,1)S(1)}, bf16[8,3,256,256]{3,2,1,0:T(8,128)(2,1)}, u32[]{:S(2)}, u32[]{:S(2)}) collective-permute-start(bf16[8,3,256,256]{3,2,1,0:T(8,128)(2,1)S(1)} %all-to-all-done.1.refs_2_.refs_4_), channel_id=1, source_target_pairs={{0,1},{1,0},{2,3},{3,2},{4,5},{5,4},{6,7},{7,6},{8,9},{9,8},{10,11... | collective-permute-start | bytes 9437192 | tf_op jit(solution)/shard_map/ppermute | solution.py:59
  339.1 25.0 %collective-permute-start.24 = (bf16[2,128,2048]{2,1,0:T(8,128)(2,1)S(1)}, bf16[2,128,2048]{2,1,0:T(8,128)(2,1)S(1)}, u32[]{:S(2)}, u32[]{:S(2)}) collective-permute-start(bf16[2,128,2048]{2,1,0:T(8,128)(2,1)S(1)} %get-tuple-element.204), channel_id=1, source_target_pairs={{0,4},{4,0},{8,12},{12,8},{16,20},{20,16},{24,28},{28,24},{1,5},{5... | collective-permute-start | bytes 3145736 | tf_op jit(solution)/shard_map/ppermute | solution.py:59
  364.2 29.4 %collective-permute-start.27 = (bf16[8,3,256,256]{3,2,1,0:T(8,128)(2,1)}, bf16[8,3,256,256]{3,2,1,0:T(8,128)(2,1)}, u32[]{:S(2)}, u32[]{:S(2)}) collective-permute-start(bf16[8,3,256,256]{3,2,1,0:T(8,128)(2,1)} %get-tuple-element.148), channel_id=1, source_target_pairs={{0,1},{1,0},{2,3},{3,2},{4,5},{5,4},{6,7},{7,6},{8,9},{9,8},{10,11... | collective-permute-start | bytes 9437192 | tf_op jit(solution)/shard_map/ppermute | solution.py:59
  364.2 29.4 %collective-permute-start.28 = (bf16[8,3,256,256]{3,2,1,0:T(8,128)(2,1)}, bf16[8,3,256,256]{3,2,1,0:T(8,128)(2,1)}, u32[]{:S(2)}, u32[]{:S(2)}) collective-permute-start(bf16[8,3,256,256]{3,2,1,0:T(8,128)(2,1)} %get-tuple-element.149), channel_id=1, source_target_pairs={{0,1},{1,0},{2,3},{3,2},{4,5},{5,4},{6,7},{7,6},{8,9},{9,8},{10,11... | collective-permute-start | bytes 9437192 | tf_op jit(solution)/shard_map/ppermute | solution.py:59
  364.7 25.1 %collective-permute-start.23 = (bf16[2,128,2048]{2,1,0:T(8,128)(2,1)S(1)}, bf16[2,128,2048]{2,1,0:T(8,128)(2,1)S(1)}, u32[]{:S(2)}, u32[]{:S(2)}) collective-permute-start(bf16[2,128,2048]{2,1,0:T(8,128)(2,1)S(1)} %get-tuple-element.205), channel_id=1, source_target_pairs={{0,4},{4,0},{8,12},{12,8},{16,20},{20,16},{24,28},{28,24},{1,5},{5... | collective-permute-start | bytes 3145736 | tf_op jit(solution)/shard_map/ppermute | solution.py:59
  369.5 24.1 %collective-permute-start.26 = (bf16[128,2048]{1,0:T(8,128)(2,1)S(1)}, bf16[128,2048]{1,0:T(8,128)(2,1)S(1)}, u32[]{:S(2)}, u32[]{:S(2)}) collective-permute-start(bf16[128,2048]{1,0:T(8,128)(2,1)S(1)} %get-tuple-element.198), channel_id=1, source_target_pairs={{0,24},{4,28},{8,0},{12,4},{16,8},{20,12},{24,16},{28,20},{1,25},{... | collective-permute-start | bytes 1572872 | tf_op jit(solution)/shard_map/ppermute | solution.py:59
  445.5 70.0 %collective-permute-start.45 = (bf16[8,3,256,256]{3,2,1,0:T(8,128)(2,1)}, bf16[8,3,256,256]{3,2,1,0:T(8,128)(2,1)}, u32[]{:S(2)}, u32[]{:S(2)}) collective-permute-start(bf16[8,3,256,256]{3,2,1,0:T(8,128)(2,1)} %add_convert_fusion.1), channel_id=1, source_target_pairs={{0,2},{1,3},{2,0},{3,1},{4,6},{5,7},{6,4},{7,5},{8,10},{9,11},{10,... | collective-permute-start | bytes 9437192 | tf_op jit(solution)/shard_map/ppermute | solution.py:59
  457.7 50.4 %all-to-all-start.2 = ((bf16[8,128,256]{2,1,0:T(8,128)(2,1)}), bf16[8,128,256]{2,1,0:T(8,128)(2,1)S(1)}, u32[]{:S(2)}, u32[]{:S(2)}) async-start(bf16[8,128,256]{2,1,0:T(8,128)(2,1)} %bitcast.176), calls=%async_computation.3 | async-start | bytes 1048576 | tf_op jit(solution)/shard_map/all_to_all | solution.py:252
  522.9 25.5 %collective-permute-start.35 = (bf16[2,8,128,256]{3,2,1,0:T(8,128)(2,1)}, bf16[2,8,128,256]{3,2,1,0:T(8,128)(2,1)}, u32[]{:S(2)}, u32[]{:S(2)}) collective-permute-start(bf16[2,8,128,256]{3,2,1,0:T(8,128)(2,1)} %fusion.7), channel_id=1, source_target_pairs={{0,2},{1,3},{2,0},{3,1},{4,6},{5,7},{6,4},{7,5},{8,10},{9,11},{10,... | collective-permute-start | bytes 3145736 | tf_op jit(solution)/shard_map/ppermute | solution.py:59
  530.5 117.4 %all-to-all-start.4 = ((bf16[8,3,256,256]{3,2,1,0:T(8,128)(2,1)}), bf16[8,3,256,256]{3,2,1,0:T(8,128)(2,1)}, u32[]{:S(2)}, u32[]{:S(2)}) async-start(bf16[8,3,256,256]{3,2,1,0:T(8,128)(2,1)} %add_convert_fusion), calls=%async_computation.5 | async-start | bytes 6291456 | tf_op jit(solution)/shard_map/all_to_all | solution.py:252
  578.3 34.0 %collective-permute-start.38 = (bf16[2,8,208,256]{3,2,1,0:T(8,128)(2,1)}, bf16[2,8,208,256]{3,2,1,0:T(8,128)(2,1)}, u32[]{:S(2)}, u32[]{:S(2)}) collective-permute-start(bf16[2,8,208,256]{3,2,1,0:T(8,128)(2,1)} %pad_maximum_fusion.1), channel_id=1, source_target_pairs={{0,1},{1,0},{2,3},{3,2},{4,5},{5,4},{6,7},{7,6},{8,9},{9,8},{10,11... | collective-permute-start | bytes 5111816 | tf_op jit(solution)/shard_map/ppermute | solution.py:59
  579.8 32.6 %collective-permute-start.37 = (bf16[2,128,2048]{2,1,0:T(8,128)(2,1)}, bf16[2,128,2048]{2,1,0:T(8,128)(2,1)}, u32[]{:S(2)}, u32[]{:S(2)}) collective-permute-start(bf16[2,128,2048]{2,1,0:T(8,128)(2,1)} %get-tuple-element.201), channel_id=1, source_target_pairs={{0,4},{4,0},{8,12},{12,8},{16,20},{20,16},{24,28},{28,24},{1,5},{5... | collective-permute-start | bytes 3145736 | tf_op jit(solution)/shard_map/ppermute | solution.py:59
  587.2 47.3 %collective-permute-start.40 = (bf16[2,128,2048]{2,1,0:T(8,128)(2,1)}, bf16[2,128,2048]{2,1,0:T(8,128)(2,1)}, u32[]{:S(2)}, u32[]{:S(2)}) collective-permute-start(bf16[2,128,2048]{2,1,0:T(8,128)(2,1)} %get-tuple-element.200), channel_id=1, source_target_pairs={{0,4},{4,0},{8,12},{12,8},{16,20},{20,16},{24,28},{28,24},{1,5},{5... | collective-permute-start | bytes 3145736 | tf_op jit(solution)/shard_map/ppermute | solution.py:59
  614.7 30.6 %collective-permute-start.43 = (bf16[8,208,256]{2,1,0:T(8,128)(2,1)}, bf16[8,208,256]{2,1,0:T(8,128)(2,1)}, u32[]{:S(2)}, u32[]{:S(2)}) collective-permute-start(bf16[8,208,256]{2,1,0:T(8,128)(2,1)} %fusion.13), channel_id=1, source_target_pairs={{0,2},{1,3},{2,0},{3,1},{4,6},{5,7},{6,4},{7,5},{8,10},{9,11},{10,... | collective-permute-start | bytes 2555912 | tf_op jit(solution)/shard_map/ppermute | solution.py:59
  621.8 23.5 %collective-permute-start.42 = (bf16[128,2048]{1,0:T(8,128)(2,1)}, bf16[128,2048]{1,0:T(8,128)(2,1)}, u32[]{:S(2)}, u32[]{:S(2)}) collective-permute-start(bf16[128,2048]{1,0:T(8,128)(2,1)} %get-tuple-element.196), channel_id=1, source_target_pairs={{0,24},{4,28},{8,0},{12,4},{16,8},{20,12},{24,16},{28,20},{1,25},{... | collective-permute-start | bytes 1572872 | tf_op jit(solution)/shard_map/ppermute | solution.py:59
  647.9 37.0 %all-to-all-start.3 = ((bf16[8,208,256]{2,1,0:T(8,128)(2,1)}), bf16[8,208,256]{2,1,0:T(8,128)(2,1)S(1)}, u32[]{:S(2)}, u32[]{:S(2)}) async-start(bf16[8,208,256]{2,1,0:T(8,128)(2,1)} %fusion), calls=%async_computation.4 | async-start | bytes 1703936 | tf_op jit(solution)/shard_map/all_to_all | solution.py:252
  (62 other events, 877.6 us)
Sparse Core Ops, SparseCore 0:
  88.8 130.1 all-gather.5
  221.1 80.4 all-gather.3
  413.8 98.5 reduce-scatter.1

commit v6 on v4

--- a/solution.py
+++ b/solution.py
@@ -433,6 +433,7 @@
 
 def attend_back_kernel(
     tile,
+    spots_ref,
     low_ref,
     high_ref,
     cos_ref,
@@ -513,9 +514,10 @@
     lax.fori_loop(chunk // tile, nq, step, 0)
     for i in range(2):
         for pair in range(pairs):
-            dkv_ref[:, i, 0, :, lanes[pair]] = (
-                sums_ref[i, pair].astype(bf).reshape(nu, tok, LANES)
-            )
+            for u in range(nu):
+                dkv_ref[spots_ref[u], i, 0, :, lanes[pair]] = (
+                    sums_ref[i, pair, u * tok : (u + 1) * tok].astype(bf)
+                )
 
     @pl.when(chunk == pl.num_programs(0) - 1)
     def _():
@@ -524,32 +526,35 @@
         dq_ref[...] = (dq * cosine - turned(dq) * sine).astype(bf)
 
 
-def attend_back(low, high, cosine, sine, q, do, o, lse, kv, tile):
+def attend_back(spots, low, high, cosine, sine, q, do, o, lse, kv, tile):
     nu, _, nb, tok, feats = kv.shape
     rows = tile * tok
     nq = nb // tile
-    kv_spec = pl.BlockSpec((nu, 2, 1, tok, feats), lambda c: (0, 0, c, 0, 0))
+    kv_spec = pl.BlockSpec((nu, 2, 1, tok, feats), lambda c, _: (0, 0, c, 0, 0))
     return pl.pallas_call(
         functools.partial(attend_back_kernel, tile),
-        grid=(nb,),
-        in_specs=[
-            *[full(part.shape) for part in (low, high, cosine, sine, q, do, o, lse)],
-            kv_spec,
-        ],
-        out_specs=[full(q.shape), kv_spec],
+        grid_spec=pltpu.PrefetchScalarGridSpec(
+            num_scalar_prefetch=1,
+            grid=(nb,),
+            in_specs=[
+                *[full(part.shape) for part in (low, high, cosine, sine, q, do, o, lse)],
+                kv_spec,
+            ],
+            out_specs=[full(q.shape), kv_spec],
+            scratch_shapes=[
+                pltpu.VMEM((nq, feats, rows), f32),
+                pltpu.VMEM((nq, 8, rows), f32),
+                pltpu.VMEM((2, feats // LANES, nu * tok, LANES), f32),
+            ],
+        ),
         out_shape=[
             jax.ShapeDtypeStruct(q.shape, bf),
             jax.ShapeDtypeStruct(kv.shape, bf),
         ],
-        scratch_shapes=[
-            pltpu.VMEM((nq, feats, rows), f32),
-            pltpu.VMEM((nq, 8, rows), f32),
-            pltpu.VMEM((2, feats // LANES, nu * tok, LANES), f32),
-        ],
         compiler_params=params(),
         cost_estimate=cost(41 * nb * tok * nb / 8192),
         name="attend_back",
-    )(low, high, cosine, sine, q, do, o, lse, kv)
+    )(spots, low, high, cosine, sine, q, do, o, lse, kv)
 
 
 def output_kernel(x_ref, o_ref, w_ref, gain_ref, x1_ref, normed_ref):
@@ -617,41 +622,27 @@
     )(d_attn, w_out)
 
 
-def project_back_kernel(
-    piece, _, x_ref, w_ref, cos_ref, sin_ref, dq_ref, dkv_ref, all_ref, dn_ref, gain_ref
-):
+def turned_back(value, cos_ref, sin_ref):
+    feats = value.shape[1]
+    value = value.astype(f32)
+    return (value * wide(cos_ref[...], feats) - turned(value) * wide(sin_ref[...], feats)).astype(bf)
+
+
+def project_back_kernel(piece, _, w_ref, cos_ref, sin_ref, dq_ref, dkv_ref, dn_ref):
     blocks, width = w_ref.shape[1], w_ref.shape[3]
-    feats = dq_ref.shape[1]
-    cosine, sine = wide(cos_ref[...], feats), wide(sin_ref[...], feats)
-    dk = dkv_ref[0].astype(f32)
-    parts = (
-        dq_ref[...],
-        (dk * cosine - turned(dk) * sine).astype(bf),
-        dkv_ref[1],
-    )
-    for i in range(3):
-        all_ref[i] = parts[i]
-    x = x_ref[...].astype(f32)
-    r1 = rms_scale(x)
-
-    @pl.when(pl.program_id(0) == 0)
-    def _():
-        gain_ref[...] = jnp.zeros_like(gain_ref)
-
+    parts = (dq_ref[...], turned_back(dkv_ref[0], cos_ref, sin_ref), dkv_ref[1])
     for block in range(blocks):
-        at = slice(block * width, (block + 1) * width)
         total = 0.0
         for part in range(3):
             total = total + dot_n(parts[part], weight_block(w_ref, block, part, piece))
-        dn_ref[0, :, at] = total.astype(bf)
-        gain_ref[:, at] = gain_ref[:, at] + jnp.sum(total * (x[:, at] * r1), axis=0, keepdims=True)
-
-
-def project_back(x_all, w, cosine, sine, dq, dkv, piece, order):
-    count, dim = x_all.shape
+        dn_ref[0, :, block * width : (block + 1) * width] = total.astype(bf)
+
+
+def project_back(w, cosine, sine, dq, dkv, piece, order):
     size = order.shape[0]
+    count, feats = dq.shape
     rows = count // size
-    feats = dq.shape[1]
+    dim = w.shape[1] * w.shape[3]
     tiled = lambda width: pl.BlockSpec((rows, width), lambda i, at: (at[i], 0))
     return pl.pallas_call(
         functools.partial(project_back_kernel, piece),
@@ -659,69 +650,74 @@
             num_scalar_prefetch=1,
             grid=(size,),
             in_specs=[
-                tiled(dim),
                 full(w.shape),
                 tiled(LANES),
                 tiled(LANES),
                 tiled(feats),
                 pl.BlockSpec((2, rows, feats), lambda i, at: (0, at[i], 0)),
             ],
-            out_specs=[
-                pl.BlockSpec((3, rows, feats), lambda i, at: (0, at[i], 0)),
-                pl.BlockSpec((1, rows, dim), lambda i, _: (i, 0, 0)),
-                full((1, dim)),
-            ],
+            out_specs=pl.BlockSpec((1, rows, dim), lambda i, _: (i, 0, 0)),
         ),
-        out_shape=[
-            jax.ShapeDtypeStruct((3, count, feats), bf),
-            jax.ShapeDtypeStruct((size, rows, dim), bf),
-            jax.ShapeDtypeStruct((1, dim), f32),
-        ],
+        out_shape=jax.ShapeDtypeStruct((size, rows, dim), bf),
         compiler_params=params(),
         cost_estimate=cost(count * 0.01),
         name="project_back",
-    )(order, x_all, w, cosine, sine, dq, dkv)
-
-
-def projection_grads_kernel(left_ref, right_ref, gain_ref, out_ref, turned_ref):
+    )(order, w, cosine, sine, dq, dkv)
+
+
+def projection_grads_kernel(
+    piece, spots_ref, dq_ref, dkv_ref, cos_ref, sin_ref, w_ref, right_ref, gain_ref, out_ref, turned_ref
+):
     n, feats, _ = turned_ref.shape
     pieces = out_ref.shape[0]
 
     @pl.when(pl.program_id(0) == 0)
     def _():
-        for i in range(n):
-            turned_ref[i] = left_ref[i].T
-
-    piece = feats // pieces
+        turned_ref[0] = dq_ref[...].T
+        turned_ref[1] = turned_back(dkv_ref[0], cos_ref, sin_ref).T
+        turned_ref[2] = dkv_ref[1].T
+
     right = right_ref[...]
-    width = right.shape[1]
+    total = 0.0
     for i in range(n):
-        grad = dot_n(turned_ref[i], right).astype(bf)
-        out_ref[:, 0, i * piece : (i + 1) * piece, :] = grad.reshape(pieces, piece, width)
-    gain = gain_ref[...].astype(bf)
+        grad = dot_n(turned_ref[i], right)
+        total = total + jnp.sum(
+            grad * weight_block(w_ref, 0, i, piece).astype(f32), axis=0, keepdims=True
+        )
+        grad = grad.astype(bf)
+        for u in range(pieces):
+            out_ref[spots_ref[u], 0, i * piece : (i + 1) * piece, :] = (
+                grad[u * piece : (u + 1) * piece]
+            )
+    gain = w_ref[0, 0, 3 * piece : 3 * piece + PAD, :][0:1].astype(f32)
+    row = lax.broadcasted_iota(jnp.int32, (PAD, right.shape[1]), 0)
+    gains = jnp.where(row == 0, total / gain, gain_ref[...]).astype(bf)
     for u in range(pieces):
-        out_ref[u, 0, n * piece :, :] = gain
-
-
-def projection_grads(lefts, right, gain, pieces, width):
-    n, count, feats = lefts.shape
-    dim = right.shape[1]
-    rows = n * (feats // pieces) + PAD
-    return pl.pallas_call(
-        projection_grads_kernel,
-        grid=(dim // width,),
-        in_specs=[
-            full(lefts.shape),
-            pl.BlockSpec((count, width), lambda i: (0, i)),
-            pl.BlockSpec((PAD, width), lambda i: (0, i)),
-        ],
-        out_specs=pl.BlockSpec((pieces, 1, rows, width), lambda i: (0, i, 0, 0)),
-        out_shape=jax.ShapeDtypeStruct((pieces, dim // width, rows, width), bf),
-        scratch_shapes=[pltpu.VMEM((n, feats, count), bf)],
-        compiler_params=params(),
-        cost_estimate=cost(2.5 * n),
+        out_ref[u, 0, n * piece :, :] = gains
+
+
+def projection_grads(spots, dq, dkv, cosine, sine, w, right, gain, piece):
+    count, feats = dq.shape
+    pieces, blocks, rows, width = w.shape
+    return pl.pallas_call(
+        functools.partial(projection_grads_kernel, piece),
+        grid_spec=pltpu.PrefetchScalarGridSpec(
+            num_scalar_prefetch=1,
+            grid=(blocks,),
+            in_specs=[
+                *[full(part.shape) for part in (dq, dkv, cosine, sine)],
+                pl.BlockSpec((pieces, 1, rows, width), lambda i, _: (0, i, 0, 0)),
+                pl.BlockSpec((count, width), lambda i, _: (0, i)),
+                pl.BlockSpec((1, width), lambda i, _: (0, i)),
+            ],
+            out_specs=pl.BlockSpec((pieces, 1, rows, width), lambda i, _: (0, i, 0, 0)),
+            scratch_shapes=[pltpu.VMEM((3, feats, count), bf)],
+        ),
+        out_shape=jax.ShapeDtypeStruct(w.shape, bf),
+        compiler_params=params(),
+        cost_estimate=cost(8),
         name="projection_grads",
-    )(lefts, right, gain)
+    )(spots, dq, dkv, cosine, sine, w, right, gain)
 
 
 def output_grads_kernel(o_ref, d_ref, out_ref):
@@ -1008,6 +1004,8 @@
 
     act, d_gate, d_up = hidden(normed2, cot_all, w_ff, step)
     order, plain = scatter_order("blk"), jnp.arange(nb, dtype=jnp.int32)
+    uly_order, each = scatter_order("uly"), jnp.arange(nu, dtype=jnp.int32)
+    spots = jnp.sum(jnp.where(uly_order[:, None] == each[None, :], each[:, None], 0), axis=0)
     d_norm2 = mix([d_gate, d_up], w_ff, (0, 1), order)
 
     def mlp_plan():
@@ -1046,9 +1044,9 @@
     (got,) = rounds.until("d_o")
     d_o = got.reshape(count, feats)
     d_columns = swap(after(d_columns, d_o), "blk")
-    dq, dkv = attend_back(low, high, cosine, sine, q, d_o, o, lse, kv_all, tile)
+    dq, dkv = attend_back(spots, low, high, cosine, sine, q, d_o, o, lse, kv_all, tile)
     dkv, mlp_out, d_columns = lax.optimization_barrier((dkv, mlp_out, d_columns))
-    rounds.add(dkv=scatter_plan(dkv, "uly"))
+    rounds.add(dkv=scatter_plan(dkv, "uly", True))
     (ff_mine,) = rounds.until("ff")
     ff_got = swap(ff_mine, "blk")
     out_grads = output_grads(o_all, d_columns.reshape(count, rows), pieces)
@@ -1058,14 +1056,16 @@
     dkv, out_grads = lax.optimization_barrier((dkv, out_grads))
     rounds.add(out=scatter_plan(out_grads.reshape(nu, feats_u, rows), "uly"))
     dkv = dkv.astype(bf).reshape(2, count, feats)
-    d_qkv, d_norm1, gain1_part = project_back(x_all, w_qkv, cosine, sine, dq, dkv, piece, order)
-    gain_parts = jnp.pad(jnp.concatenate([gain1_part, gain2_part]), ((0, PAD - 2), (0, 0)))
-    grads = projection_grads(d_qkv, after(normed, d_norm1), gain_parts, pieces, block)
+    grads = projection_grads(
+        spots if strided else jnp.zeros((1,), jnp.int32),
+        *(dq, dkv, cosine, sine, w_qkv, normed, gain2_part, piece),
+    )
+    d_norm1 = project_back(w_qkv, cosine, sine, after(dq, grads), dkv, piece, order)
     last = scatter_plan(d_norm1, "blk", True)
     if strided:
         rounds.add(
             last=last,
-            grads=chain(scatter_plan(grads, "uly"), lambda mine: swapped(mine.astype(bf))),
+            grads=chain(scatter_plan(grads, "uly", True), lambda mine: swapped(mine.astype(bf))),
         )
         d_norm1, got, out_grads = rounds.until("last", "grads", "out")
         gain_sums = jnp.sum(got[:, 3 * piece : 3 * piece + 2].astype(f32), axis=0)
@@ -1077,7 +1077,9 @@
         d_norm1, got, out_grads = rounds.until("last", "grads", "out")
         got = scatter(got.reshape(nu, feats_u, 3, rows), "uly")[0]
         heads = [got[:, i] for i in range(3)]
-        gain_sums = lax.dynamic_slice_in_dim(lax.psum(gain_parts[:2], both), b * rows, rows, 1)
+        gain_parts = jnp.transpose(grads[0, :, 3 * piece : 3 * piece + 2], (1, 0, 2)).astype(f32)
+        gain_sums = lax.psum(gain_parts.reshape(2, dim), both)
+        gain_sums = lax.dynamic_slice_in_dim(gain_sums, b * rows, rows, 1)
     grad_output = jnp.transpose(out_grads)
     grad_query, grad_key, grad_value = [jnp.transpose(h).astype(f32) for h in heads]
     x_own = tokens.astype(f32)

time: 710 us -> 711 us (level)
    slice x2 -> x4, local copies, waits for them, and re-layouts: 3.23 us -> 10.9 us  [column(): return parts[at:at + len(offsets)]]
  transfers between devices with their start and end apart: 54 -> 54, of which waited for: 31 -> 29; matrix products, arithmetic and copies ran while one was open for 12% -> 13% of each run, Pallas kernels for 25% -> 25%
where the time goes in v6:
time: 711 us; the launch traced here: 701 us
  waiting for transfers between devices  284 us (40%)
  Pallas kernels  210 us (30%)
  starting transfers between devices  79.4 us (11%)
  local copies, waits for them, and re-layouts  56.9 us (8%)
  other arithmetic  55.5 us (8%)
  between operations  15 us (2%)
    ppermute x46, waiting for transfers between devices, hop(): return lax.ppermute(value, axis, pairs)  252 us
    ppermute x46, starting transfers between devices, hop(): return lax.ppermute(value, axis, pairs)  53.3 us
    pallas_call x1, Pallas kernels, attend_back(): pl.pallas_call(functools.partial(attend_back_kernel, tile), grid_spec=plt...  41.1 us
    pallas_call x1, Pallas kernels, attend(): pl.pallas_call(functools.partial(attend_kernel, tile), grid=(nq,), in_spe...  26.4 us
    all_to_all x5, starting transfers between devices, swap(): return lax.all_to_all(parts, axis, 0, 0, tiled=True)  25.9 us
    pallas_call x2, Pallas kernels, mix(): pl.pallas_call(functools.partial(mix_kernel, which, n), grid_spec=pltpu.P...  24.9 us
    all_to_all x5, waiting for transfers between devices, swap(): return lax.all_to_all(parts, axis, 0, 0, tiled=True)  23.6 us
    pallas_call x1, Pallas kernels, hidden(): pl.pallas_call(functools.partial(hidden_kernel, n), grid=(count // rows,)...  20.5 us
  transfers between devices with their start and end apart: 54, of which 29 were waited for; matrix products, arithmetic and copies ran while one was open for 13% of the time, Pallas kernels for 25%

profile of v6, /device:TPU:0, one launch (start us, length us, event | category | flops | bytes accessed | tf_op | source)
XLA Modules:
  0.0 700.7 jit_solution(10797240217921215162)
XLA Ops:
  20.5 6.8 prepare.1
  27.3 8.5 %collective-permute-done.1 = bf16[128,2048]{1,0:T(8,128)(2,1)S(1)} collective-permute-done((bf16[128,2048]{1,0:T(8,128)(2,1)}, bf16[128,2048]{1,0:T(8,128)(2,1)S(1)}, u32[]{:S(2)}, u32[]{:S(2)}) %collective-permute-start.1) | collective-permute-done | bytes 524320 | tf_op jit(solution)/shard_map/ppermute | solution.py:59
  47.2 13.5 %collective-permute-done.3 = bf16[128,2048]{1,0:T(8,128)(2,1)S(1)} collective-permute-done((bf16[128,2048]{1,0:T(8,128)(2,1)S(1)}, bf16[128,2048]{1,0:T(8,128)(2,1)S(1)}, u32[]{:S(2)}, u32[]{:S(2)}) %collective-permute-start.3) | collective-permute-done | bytes 524320 | tf_op jit(solution)/shard_map/ppermute | solution.py:59
  60.7 6.7 collective-permute-done.5
  72.5 10.8 %collective-permute-done.6 = bf16[128,2048]{1,0:T(8,128)(2,1)S(1)} collective-permute-done((bf16[128,2048]{1,0:T(8,128)(2,1)S(1)}, bf16[128,2048]{1,0:T(8,128)(2,1)S(1)}, u32[]{:S(2)}, u32[]{:S(2)}) %collective-permute-start.6) | collective-permute-done | bytes 524320 | tf_op jit(solution)/shard_map/ppermute | solution.py:59
  102.2 9.5 %project.1 = (bf16[1024,256]{1,0:T(8,128)(2,1)}, bf16[2,1024,256]{2,1,0:T(8,128)(2,1)}, bf16[1024,2048]{1,0:T(8,128)(2,1)}) custom-call(bf16[1024,2048]{1,0:T(8,128)(2,1)} %bitcast.10.x_ref, bf16[4,8,208,256]{3,2,1,0:T(8,128)(2,1)} %copy-done.2, f32[1024,128]{1,0:T(8,128)} %get-tuple-element.206.cos_ref, f32[1024,128]{1,0:T(8,128)} %get-tuple-element.205.sin_ref), custom_call_target="tpu_custom_call" | custom-call | flops 2534400000 | tf_op jit(solution)/shard_map/project/pallas_call | solution.py:310
  113.4 24.1 %collective-permute-done.10 = bf16[2,8,128,256]{3,2,1,0:T(8,128)(2,1)} collective-permute-done((bf16[2,8,128,256]{3,2,1,0:T(8,128)(2,1)}, bf16[2,8,128,256]{3,2,1,0:T(8,128)(2,1)}, u32[]{:S(2)}, u32[]{:S(2)}) %collective-permute-start.10) | collective-permute-done | bytes 1048608 | tf_op jit(solution)/shard_map/ppermute | solution.py:59
  145.0 26.4 %attend.1 = (bf16[1024,256]{1,0:T(8,128)(2,1)}, f32[4,4,256]{2,1,0:T(4,128)}) custom-call(s32[4,1,256]{2,1,0:T(1,128)} %bitcast.203, s32[4,1,256]{2,1,0:T(1,128)} %broadcast_add_fusion.high_ref, bf16[1024,256]{1,0:T(8,128)(2,1)} %get-tuple-element.106.q_ref, bf16[4,2,8,128,256]{4,3,2,1,0:T(8,128)(2,1)} %copy-done.7), custom_call_target="tpu_custom_call" | custom-call | flops 7424999936 | tf_op jit(solution)/shard_map/attend/pallas_call | solution.py:418
  171.4 19.9 %all-to-all-done.1.refs_2_.refs_4_ = bf16[8,3,256,256]{3,2,1,0:T(8,128)(2,1)S(1)} async-done(((bf16[8,3,256,256]{3,2,1,0:T(8,128)(2,1)}), bf16[8,3,256,256]{3,2,1,0:T(8,128)(2,1)S(1)}, u32[]{:S(2)}, u32[]{:S(2)}) %all-to-all-start.1) | async-done | bytes 3145760 | tf_op jit(solution)/shard_map/all_to_all | solution.py:252
  200.3 15.8 %collective-permute-done.13 = bf16[1024,256]{1,0:T(8,128)(2,1)S(1)} collective-permute-done((bf16[1024,256]{1,0:T(8,128)(2,1)}, bf16[1024,256]{1,0:T(8,128)(2,1)S(1)}, u32[]{:S(2)}, u32[]{:S(2)}) %collective-permute-start.13) | collective-permute-done | bytes 524320 | tf_op jit(solution)/shard_map/ppermute | solution.py:59
  225.5 16.8 %collective-permute-done.16 = bf16[1024,256]{1,0:T(8,128)(2,1)S(1)} collective-permute-done((bf16[1024,256]{1,0:T(8,128)(2,1)S(1)}, bf16[1024,256]{1,0:T(8,128)(2,1)S(1)}, u32[]{:S(2)}, u32[]{:S(2)}) %collective-permute-start.16) | collective-permute-done | bytes 524320 | tf_op jit(solution)/shard_map/ppermute | solution.py:59
  244.0 9.6 %collective-permute-done.18 = bf16[1024,256]{1,0:T(8,128)(2,1)S(1)} collective-permute-done((bf16[1024,256]{1,0:T(8,128)(2,1)S(1)}, bf16[1024,256]{1,0:T(8,128)(2,1)S(1)}, u32[]{:S(2)}, u32[]{:S(2)}) %collective-permute-start.18) | collective-permute-done | bytes 524320 | tf_op jit(solution)/shard_map/ppermute | solution.py:59
  254.9 18.9 %collective-permute-done.19 = bf16[1024,256]{1,0:T(8,128)(2,1)S(1)} collective-permute-done((bf16[1024,256]{1,0:T(8,128)(2,1)S(1)}, bf16[1024,256]{1,0:T(8,128)(2,1)S(1)}, u32[]{:S(2)}, u32[]{:S(2)}) %collective-permute-start.19) | collective-permute-done | bytes 524320 | tf_op jit(solution)/shard_map/ppermute | solution.py:59
  280.8 16.0 %output_project.1 = (f32[1024,2048]{1,0:T(8,128)}, bf16[1024,2048]{1,0:T(8,128)(2,1)}) custom-call(bf16[1024,2048]{1,0:T(8,128)(2,1)} %bitcast.10.x_ref, bf16[8,1024,256]{2,1,0:T(8,128)(2,1)} %copy-done.1, bf16[8,4,8,64,256]{4,3,2,1,0:T(8,128)(2,1)} %bitcast.181, f32[1,2048]{1,0:T(1,128)} %bitcast.196), custom_call_target="tpu_custom_call" | custom-call | flops 4224000000 | tf_op jit(solution)/shard_map/output_project/pallas_call | solution.py:578
  301.5 20.5 %hidden.1 = (bf16[4,1024,256]{2,1,0:T(8,128)(2,1)}, bf16[4,1024,256]{2,1,0:T(8,128)(2,1)}, bf16[4,1024,256]{2,1,0:T(8,128)(2,1)}) custom-call(bf16[1024,2048]{1,0:T(8,128)(2,1)} %get-tuple-element.130.refs_0_.n_ref, bf16[1024,2048]{1,0:T(8,128)(2,1)} %all-gather.4.cloned.1.call-done.refs_1_.g_ref, bf16[8,3,256,256]{3,2,1,0:T(8,128)(2,1)} %copy-done, ...), custom_call_target="tpu_custom_call" | custom-call | flops 5500000256 | tf_op jit(solution)/shard_map/hidden/pallas_call | solution.py:820
  322.0 15.3 %mix.2 = bf16[8,128,2048]{2,1,0:T(8,128)(2,1)} custom-call(s32[8]{0:T(128)} %stack.69._, bf16[4,1024,256]{2,1,0:T(8,128)(2,1)} %get-tuple-element.128.refs_0_.refs_1_.dg_ref, bf16[4,1024,256]{2,1,0:T(8,128)(2,1)} %get-tuple-element.128.refs_0_.refs_1_.dg_ref, bf16[4,1024,256]{2,1,0:T(8,128)(2,1)} %get-tuple-element.129.refs_2_.refs_3_.du_ref, ...), custom_call_target="tpu_custom_call" | custom-call | flops 4400000000 | tf_op jit(solution)/shard_map/mix/pallas_call | solution.py:856
  339.7 18.7 %hidden_grads.1 = (bf16[8,3,256,256]{3,2,1,0:T(8,128)(2,1)}, bf16[8,3,256,256]{3,2,1,0:T(8,128)(2,1)}, bf16[8,3,256,256]{3,2,1,0:T(8,128)(2,1)}, bf16[8,3,256,256]{3,2,1,0:T(8,128)(2,1)}) custom-call(bf16[1024,2048]{1,0:T(8,128)(2,1)} %get-tuple-element.130.refs_0_.n_ref, bf16[1024,2048]{1,0:T(8,128)(2,1)} %all-gather.4.cloned.1.call-done.refs_1_.g_ref, ...), custom_call_target="tpu_custom_call" | custom-call | flops 6874999808 | tf_op jit(solution)/shard_map/hidden_grads/pallas_call | solution.py:885
  371.0 9.6 %mix.3 = bf16[8,128,2048]{2,1,0:T(8,128)(2,1)} custom-call(s32[8]{0:T(128)} %iota.50._, bf16[4,1024,256]{2,1,0:T(8,128)(2,1)} %get-tuple-element.131.act_ref.refs_0_.refs_1_, bf16[4,1024,256]{2,1,0:T(8,128)(2,1)} %get-tuple-element.131.act_ref.refs_0_.refs_1_, bf16[8,3,256,256]{3,2,1,0:T(8,128)(2,1)} %copy-done, ...), custom_call_target="tpu_custom_call" | custom-call | flops 2200000000 | tf_op jit(solution)/shard_map/mix/pallas_call | solution.py:856
  380.6 9.2 %collective-permute-done.23 = bf16[2,128,2048]{2,1,0:T(8,128)(2,1)S(1)} collective-permute-done((bf16[2,128,2048]{2,1,0:T(8,128)(2,1)S(1)}, bf16[2,128,2048]{2,1,0:T(8,128)(2,1)S(1)}, u32[]{:S(2)}, u32[]{:S(2)}) %collective-permute-start.23) | collective-permute-done | bytes 1048608 | tf_op jit(solution)/shard_map/ppermute | solution.py:59
  396.8 13.7 %collective-permute-done.29 = bf16[128,2048]{1,0:T(8,128)(2,1)S(1)} collective-permute-done((bf16[128,2048]{1,0:T(8,128)(2,1)S(1)}, bf16[128,2048]{1,0:T(8,128)(2,1)S(1)}, u32[]{:S(2)}, u32[]{:S(2)}) %collective-permute-start.29) | collective-permute-done | bytes 524320 | tf_op jit(solution)/shard_map/ppermute | solution.py:59
  416.7 8.7 %output_back.1 = bf16[8,128,256]{2,1,0:T(8,128)(2,1)} custom-call(bf16[128,2048]{1,0:T(8,128)(2,1)} %get-tuple-element.179.d_ref, bf16[8,4,8,64,256]{4,3,2,1,0:T(8,128)(2,1)} %bitcast.182), custom_call_target="tpu_custom_call" | custom-call | flops 2200000000 | tf_op jit(solution)/shard_map/output_back/pallas_call | solution.py:610
  449.0 7.2 %collective-permute-done.32 = bf16[2,128,256]{2,1,0:T(8,128)(2,1)S(1)} collective-permute-done((bf16[2,128,256]{2,1,0:T(8,128)(2,1)S(1)}, bf16[2,128,256]{2,1,0:T(8,128)(2,1)S(1)}, u32[]{:S(2)}, u32[]{:S(2)}) %collective-permute-start.32) | collective-permute-done | bytes 131104 | tf_op jit(solution)/shard_map/ppermute | solution.py:59
  458.2 10.1 %all-to-all-start.2 = ((bf16[8,128,256]{2,1,0:T(8,128)(2,1)}), bf16[8,128,256]{2,1,0:T(8,128)(2,1)}, u32[]{:S(2)}, u32[]{:S(2)}) async-start(bf16[8,128,256]{2,1,0:T(8,128)(2,1)} %bitcast.180), calls=%async_computation.3 | async-start | bytes 1048576 | tf_op jit(solution)/shard_map/all_to_all | solution.py:252
  468.3 41.1 %attend_back.1 = (bf16[1024,256]{1,0:T(8,128)(2,1)}, bf16[4,2,8,128,256]{4,3,2,1,0:T(8,128)(2,1)}) custom-call(s32[4]{0:T(128)} %select_reduce_fusion.spots_ref, s32[4,1,256]{2,1,0:T(1,128)} %bitcast.204, s32[4,1,256]{2,1,0:T(1,128)} %broadcast_add_fusion.high_ref, f32[1024,128]{1,0:T(8,128)} %get-tuple-element.206.cos_ref, ...), custom_call_target="tpu_custom_call" | custom-call | flops 11274999808 | tf_op jit(solution)/shard_map/attend_back/pallas_call | solution.py:534
  530.7 7.3 %output_grads.1 = bf16[4,8,64,256]{3,2,1,0:T(8,128)(2,1)} custom-call(bf16[8,1024,256]{2,1,0:T(8,128)(2,1)} %copy-done.1, bf16[1024,256]{1,0:T(8,128)(2,1)} %bitcast.71.d_ref), custom_call_target="tpu_custom_call" | custom-call | flops 1650000000 | tf_op jit(solution)/shard_map/output_grads/pallas_call | solution.py:733
  538.0 16.8 %collective-permute-done.35 = bf16[2,8,128,256]{3,2,1,0:T(8,128)(2,1)S(1)} collective-permute-done((bf16[2,8,128,256]{3,2,1,0:T(8,128)(2,1)S(1)}, bf16[2,8,128,256]{3,2,1,0:T(8,128)(2,1)S(1)}, u32[]{:S(2)}, u32[]{:S(2)}) %collective-permute-start.35) | collective-permute-done | bytes 1048608 | tf_op jit(solution)/shard_map/ppermute | solution.py:59
  557.8 11.6 %projection_grads.1 = bf16[4,8,208,256]{3,2,1,0:T(8,128)(2,1)} custom-call(s32[4]{0:T(128)} %select_reduce_fusion.spots_ref, bf16[1024,256]{1,0:T(8,128)(2,1)} %get-tuple-element.156.dq_ref, bf16[2,1024,256]{2,1,0:T(8,128)(2,1)} %bitcast.185, f32[1024,128]{1,0:T(8,128)} %get-tuple-element.206.cos_ref, f32[1024,128]{1,0:T(8,128)} %get-tuple-element.205.sin_ref, ...), custom_call_target="tpu_custom_call" | custom-call | flops 2200000000 | tf_op jit(solution)/shard_map/projection_grads/pallas_call | solution.py:702
  572.1 10.6 %project_back.1 = bf16[8,128,2048]{2,1,0:T(8,128)(2,1)} custom-call(s32[8]{0:T(128)} %stack.69._, bf16[4,8,208,256]{3,2,1,0:T(8,128)(2,1)} %copy-done.2, f32[1024,128]{1,0:T(8,128)} %get-tuple-element.206.cos_ref, f32[1024,128]{1,0:T(8,128)} %get-tuple-element.205.sin_ref, bf16[1024,256]{1,0:T(8,128)(2,1)} %get-tuple-element.156.dq_ref, ...), custom_call_target="tpu_custom_call" | custom-call | flops 2816000000 | tf_op jit(solution)/shard_map/project_back/pallas_call | solution.py:647
  596.6 15.6 %collective-permute-done.37 = bf16[2,128,2048]{2,1,0:T(8,128)(2,1)} collective-permute-done((bf16[2,128,2048]{2,1,0:T(8,128)(2,1)}, bf16[2,128,2048]{2,1,0:T(8,128)(2,1)}, u32[]{:S(2)}, u32[]{:S(2)}) %collective-permute-start.37) | collective-permute-done | bytes 1048608 | tf_op jit(solution)/shard_map/ppermute | solution.py:59
  626.2 8.2 %collective-permute-done.40 = bf16[2,128,2048]{2,1,0:T(8,128)(2,1)} collective-permute-done((bf16[2,128,2048]{2,1,0:T(8,128)(2,1)}, bf16[2,128,2048]{2,1,0:T(8,128)(2,1)}, u32[]{:S(2)}, u32[]{:S(2)}) %collective-permute-start.40) | collective-permute-done | bytes 1048608 | tf_op jit(solution)/shard_map/ppermute | solution.py:59
  634.4 6.7 collective-permute-done.39
  665.0 16.4 %collective-permute-done.44 = bf16[128,2048]{1,0:T(8,128)(2,1)S(1)} collective-permute-done((bf16[128,2048]{1,0:T(8,128)(2,1)S(1)}, bf16[128,2048]{1,0:T(8,128)(2,1)S(1)}, u32[]{:S(2)}, u32[]{:S(2)}) %collective-permute-start.44) | collective-permute-done | bytes 524320 | tf_op jit(solution)/shard_map/ppermute | solution.py:59
  (260 shorter events, 235.0 us)
Async XLA Ops:
  10.3 25.5 %collective-permute-start.1 = (bf16[128,2048]{1,0:T(8,128)(2,1)}, bf16[128,2048]{1,0:T(8,128)(2,1)S(1)}, u32[]{:S(2)}, u32[]{:S(2)}) collective-permute-start(bf16[128,2048]{1,0:T(8,128)(2,1)} %param.12), channel_id=1, source_target_pairs={{0,24},{4,28},{8,0},{12,4},{16,8},{20,12},{24,16},{28,20},{1,25},{... | collective-permute-start | bytes 1572872 | tf_op jit(solution)/shard_map/ppermute | solution.py:59
  12.3 23.5 %collective-permute-start.2 = (bf16[128,2048]{1,0:T(8,128)(2,1)}, bf16[128,2048]{1,0:T(8,128)(2,1)S(1)}, u32[]{:S(2)}, u32[]{:S(2)}) collective-permute-start(bf16[128,2048]{1,0:T(8,128)(2,1)} %param.12), channel_id=1, source_target_pairs={{0,4},{4,0},{8,12},{12,8},{16,20},{20,16},{24,28},{28,24},{1,5},{5... | collective-permute-start | bytes 1572872 | tf_op jit(solution)/shard_map/ppermute | solution.py:59
  16.8 50.7 %all-to-all-start = ((bf16[8,208,256]{2,1,0:T(8,128)(2,1)}), bf16[8,208,256]{2,1,0:T(8,128)(2,1)S(1)}, u32[]{:S(2)}, u32[]{:S(2)}) async-start(bf16[8,208,256]{2,1,0:T(8,128)(2,1)} %get-tuple-element.96), calls=%async_computation | async-start | bytes 1703936 | tf_op jit(solution)/shard_map/all_to_all | solution.py:252
  20.3 260.5 %all-gather.6.cloned.1.call-start = ((), (), s32[]{:S(2)}) async-start(), calls=%async_computation.8 | async-start | bytes 8650752 | tf_op jit(solution)/shard_map/all_gather | solution.py:256
  35.8 24.9 %collective-permute-start.3 = (bf16[128,2048]{1,0:T(8,128)(2,1)S(1)}, bf16[128,2048]{1,0:T(8,128)(2,1)S(1)}, u32[]{:S(2)}, u32[]{:S(2)}) collective-permute-start(bf16[128,2048]{1,0:T(8,128)(2,1)S(1)} %collective-permute-done), channel_id=1, source_target_pairs={{0,8},{4,12},{8,16},{12,20},{16,24},{20,28},{24,0},{28,4},{1,9},{5... | collective-permute-start | bytes 1572872 | tf_op jit(solution)/shard_map/ppermute | solution.py:59
  37.6 23.2 %collective-permute-start.4 = (bf16[128,2048]{1,0:T(8,128)(2,1)S(1)}, bf16[128,2048]{1,0:T(8,128)(2,1)S(1)}, u32[]{:S(2)}, u32[]{:S(2)}) collective-permute-start(bf16[128,2048]{1,0:T(8,128)(2,1)S(1)} %collective-permute-done), channel_id=1, source_target_pairs={{0,4},{4,0},{8,12},{12,8},{16,20},{20,16},{24,28},{28,24},{1,5},{5... | collective-permute-start | bytes 1572872 | tf_op jit(solution)/shard_map/ppermute | solution.py:59
  41.3 26.1 %collective-permute-start.5 = (bf16[128,2048]{1,0:T(8,128)(2,1)S(1)}, bf16[128,2048]{1,0:T(8,128)(2,1)}, u32[]{:S(2)}, u32[]{:S(2)}) collective-permute-start(bf16[128,2048]{1,0:T(8,128)(2,1)S(1)} %collective-permute-done.1), channel_id=1, source_target_pairs={{0,4},{4,0},{8,12},{12,8},{16,20},{20,16},{24,28},{28,24},{1,5},{5... | collective-permute-start | bytes 1572872 | tf_op jit(solution)/shard_map/ppermute | solution.py:59
  88.7 102.7 %all-to-all-start.1 = ((bf16[8,3,256,256]{3,2,1,0:T(8,128)(2,1)}), bf16[8,3,256,256]{3,2,1,0:T(8,128)(2,1)S(1)}, u32[]{:S(2)}, u32[]{:S(2)}) async-start(bf16[8,3,256,256]{3,2,1,0:T(8,128)(2,1)} %prepare.1), calls=%async_computation.1 | async-start | bytes 6291456 | tf_op jit(solution)/shard_map/all_to_all | solution.py:252
  92.3 209.2 %all-gather.4.cloned.1.call-start = ((), (), s32[]{:S(2)}) async-start(), calls=%async_computation.6 | async-start | bytes 4718592 | tf_op jit(solution)/shard_map/all_gather | solution.py:256
  111.7 25.9 %collective-permute-start.10 = (bf16[2,8,128,256]{3,2,1,0:T(8,128)(2,1)}, bf16[2,8,128,256]{3,2,1,0:T(8,128)(2,1)}, u32[]{:S(2)}, u32[]{:S(2)}) collective-permute-start(bf16[2,8,128,256]{3,2,1,0:T(8,128)(2,1)} %bitcast.190), channel_id=1, source_target_pairs={{0,2},{1,3},{2,0},{3,1},{4,6},{5,7},{6,4},{7,5},{8,10},{9,11},{10,... | collective-permute-start | bytes 3145736 | tf_op jit(solution)/shard_map/ppermute | solution.py:59
  113.2 24.3 %collective-permute-start.11 = (bf16[2,8,128,256]{3,2,1,0:T(8,128)(2,1)}, bf16[2,8,128,256]{3,2,1,0:T(8,128)(2,1)}, u32[]{:S(2)}, u32[]{:S(2)}) collective-permute-start(bf16[2,8,128,256]{3,2,1,0:T(8,128)(2,1)} %bitcast.191), channel_id=1, source_target_pairs={{0,1},{1,0},{2,3},{3,2},{4,5},{5,4},{6,7},{7,6},{8,9},{9,8},{10,11... | collective-permute-start | bytes 3145736 | tf_op jit(solution)/shard_map/ppermute | solution.py:59
  138.3 375.1 %reduce-scatter.2.cloned.1.call-start = ((), (), s32[]{:S(2)}) async-start(), calls=%async_computation.7 | async-start | bytes 4718592 | tf_op jit(solution)/shard_map/reduce_scatter | solution.py:260
  191.4 82.5 %collective-permute-start.20 = (bf16[8,3,256,256]{3,2,1,0:T(8,128)(2,1)S(1)}, bf16[8,3,256,256]{3,2,1,0:T(8,128)(2,1)}, u32[]{:S(2)}, u32[]{:S(2)}) collective-permute-start(bf16[8,3,256,256]{3,2,1,0:T(8,128)(2,1)S(1)} %all-to-all-done.1.refs_2_.refs_4_), channel_id=1, source_target_pairs={{0,2},{1,3},{2,0},{3,1},{4,6},{5,7},{6,4},{7,5},{8,10},{9,11},{10,... | collective-permute-start | bytes 9437192 | tf_op jit(solution)/shard_map/ppermute | solution.py:59
  196.5 26.2 %collective-permute-start.14 = (bf16[1024,256]{1,0:T(8,128)(2,1)}, bf16[1024,256]{1,0:T(8,128)(2,1)S(1)}, u32[]{:S(2)}, u32[]{:S(2)}) collective-permute-start(bf16[1024,256]{1,0:T(8,128)(2,1)} %get-tuple-element.111.o_ref), channel_id=1, source_target_pairs={{0,24},{4,28},{8,0},{12,4},{16,8},{20,12},{24,16},{28,20},{1,25},{... | collective-permute-start | bytes 1572872 | tf_op jit(solution)/shard_map/ppermute | solution.py:59
  224.9 28.7 %collective-permute-start.18 = (bf16[1024,256]{1,0:T(8,128)(2,1)S(1)}, bf16[1024,256]{1,0:T(8,128)(2,1)S(1)}, u32[]{:S(2)}, u32[]{:S(2)}) collective-permute-start(bf16[1024,256]{1,0:T(8,128)(2,1)S(1)} %collective-permute-done.14), channel_id=1, source_target_pairs={{0,4},{4,0},{8,12},{12,8},{16,20},{20,16},{24,28},{28,24},{1,5},{5... | collective-permute-start | bytes 1572872 | tf_op jit(solution)/shard_map/ppermute | solution.py:59
  254.9 23.8 %collective-permute-start.21 = (bf16[8,3,256,256]{3,2,1,0:T(8,128)(2,1)S(1)}, bf16[8,3,256,256]{3,2,1,0:T(8,128)(2,1)}, u32[]{:S(2)}, u32[]{:S(2)}) collective-permute-start(bf16[8,3,256,256]{3,2,1,0:T(8,128)(2,1)S(1)} %all-to-all-done.1.refs_2_.refs_4_), channel_id=1, source_target_pairs={{0,1},{1,0},{2,3},{3,2},{4,5},{5,4},{6,7},{7,6},{8,9},{9,8},{10,11... | collective-permute-start | bytes 9437192 | tf_op jit(solution)/shard_map/ppermute | solution.py:59
  339.1 25.2 %collective-permute-start.24 = (bf16[2,128,2048]{2,1,0:T(8,128)(2,1)S(1)}, bf16[2,128,2048]{2,1,0:T(8,128)(2,1)S(1)}, u32[]{:S(2)}, u32[]{:S(2)}) collective-permute-start(bf16[2,128,2048]{2,1,0:T(8,128)(2,1)S(1)} %get-tuple-element.188), channel_id=1, source_target_pairs={{0,4},{4,0},{8,12},{12,8},{16,20},{20,16},{24,28},{28,24},{1,5},{5... | collective-permute-start | bytes 3145736 | tf_op jit(solution)/shard_map/ppermute | solution.py:59
  364.3 29.0 %collective-permute-start.27 = (bf16[8,3,256,256]{3,2,1,0:T(8,128)(2,1)}, bf16[8,3,256,256]{3,2,1,0:T(8,128)(2,1)}, u32[]{:S(2)}, u32[]{:S(2)}) collective-permute-start(bf16[8,3,256,256]{3,2,1,0:T(8,128)(2,1)} %get-tuple-element.137), channel_id=1, source_target_pairs={{0,1},{1,0},{2,3},{3,2},{4,5},{5,4},{6,7},{7,6},{8,9},{9,8},{10,11... | collective-permute-start | bytes 9437192 | tf_op jit(solution)/shard_map/ppermute | solution.py:59
  364.3 29.0 %collective-permute-start.28 = (bf16[8,3,256,256]{3,2,1,0:T(8,128)(2,1)}, bf16[8,3,256,256]{3,2,1,0:T(8,128)(2,1)}, u32[]{:S(2)}, u32[]{:S(2)}) collective-permute-start(bf16[8,3,256,256]{3,2,1,0:T(8,128)(2,1)} %get-tuple-element.138), channel_id=1, source_target_pairs={{0,1},{1,0},{2,3},{3,2},{4,5},{5,4},{6,7},{7,6},{8,9},{9,8},{10,11... | collective-permute-start | bytes 9437192 | tf_op jit(solution)/shard_map/ppermute | solution.py:59
  364.8 25.1 %collective-permute-start.23 = (bf16[2,128,2048]{2,1,0:T(8,128)(2,1)S(1)}, bf16[2,128,2048]{2,1,0:T(8,128)(2,1)S(1)}, u32[]{:S(2)}, u32[]{:S(2)}) collective-permute-start(bf16[2,128,2048]{2,1,0:T(8,128)(2,1)S(1)} %get-tuple-element.189), channel_id=1, source_target_pairs={{0,4},{4,0},{8,12},{12,8},{16,20},{20,16},{24,28},{28,24},{1,5},{5... | collective-permute-start | bytes 3145736 | tf_op jit(solution)/shard_map/ppermute | solution.py:59
  366.6 23.2 %collective-permute-start.25 = (bf16[128,2048]{1,0:T(8,128)(2,1)S(1)}, bf16[128,2048]{1,0:T(8,128)(2,1)S(1)}, u32[]{:S(2)}, u32[]{:S(2)}) collective-permute-start(bf16[128,2048]{1,0:T(8,128)(2,1)S(1)} %get-tuple-element.185), channel_id=1, source_target_pairs={{0,8},{4,12},{8,16},{12,20},{16,24},{20,28},{24,0},{28,4},{1,9},{5... | collective-permute-start | bytes 1572872 | tf_op jit(solution)/shard_map/ppermute | solution.py:59
  369.4 23.8 %collective-permute-start.26 = (bf16[128,2048]{1,0:T(8,128)(2,1)S(1)}, bf16[128,2048]{1,0:T(8,128)(2,1)S(1)}, u32[]{:S(2)}, u32[]{:S(2)}) collective-permute-start(bf16[128,2048]{1,0:T(8,128)(2,1)S(1)} %get-tuple-element.184), channel_id=1, source_target_pairs={{0,24},{4,28},{8,0},{12,4},{16,8},{20,12},{24,16},{28,20},{1,25},{... | collective-permute-start | bytes 1572872 | tf_op jit(solution)/shard_map/ppermute | solution.py:59
  445.8 70.6 %collective-permute-start.45 = (bf16[8,3,256,256]{3,2,1,0:T(8,128)(2,1)}, bf16[8,3,256,256]{3,2,1,0:T(8,128)(2,1)}, u32[]{:S(2)}, u32[]{:S(2)}) collective-permute-start(bf16[8,3,256,256]{3,2,1,0:T(8,128)(2,1)} %add_convert_fusion.1), channel_id=1, source_target_pairs={{0,2},{1,3},{2,0},{3,1},{4,6},{5,7},{6,4},{7,5},{8,10},{9,11},{10,... | collective-permute-start | bytes 9437192 | tf_op jit(solution)/shard_map/ppermute | solution.py:59
  458.2 51.2 %all-to-all-start.2 = ((bf16[8,128,256]{2,1,0:T(8,128)(2,1)}), bf16[8,128,256]{2,1,0:T(8,128)(2,1)}, u32[]{:S(2)}, u32[]{:S(2)}) async-start(bf16[8,128,256]{2,1,0:T(8,128)(2,1)} %bitcast.180), calls=%async_computation.3 | async-start | bytes 1048576 | tf_op jit(solution)/shard_map/all_to_all | solution.py:252
  522.6 125.6 %all-to-all-start.4 = ((bf16[8,3,256,256]{3,2,1,0:T(8,128)(2,1)}), bf16[8,3,256,256]{3,2,1,0:T(8,128)(2,1)}, u32[]{:S(2)}, u32[]{:S(2)}) async-start(bf16[8,3,256,256]{3,2,1,0:T(8,128)(2,1)} %add_convert_fusion), calls=%async_computation.5 | async-start | bytes 6291456 | tf_op jit(solution)/shard_map/all_to_all | solution.py:252
  529.2 25.6 %collective-permute-start.35 = (bf16[2,8,128,256]{3,2,1,0:T(8,128)(2,1)S(1)}, bf16[2,8,128,256]{3,2,1,0:T(8,128)(2,1)S(1)}, u32[]{:S(2)}, u32[]{:S(2)}) collective-permute-start(bf16[2,8,128,256]{3,2,1,0:T(8,128)(2,1)S(1)} %fusion.7), channel_id=1, source_target_pairs={{0,2},{1,3},{2,0},{3,1},{4,6},{5,7},{6,4},{7,5},{8,10},{9,11},{10,... | collective-permute-start | bytes 3145736 | tf_op jit(solution)/shard_map/ppermute | solution.py:59
  572.1 40.1 %collective-permute-start.38 = (bf16[2,8,208,256]{3,2,1,0:T(8,128)(2,1)}, bf16[2,8,208,256]{3,2,1,0:T(8,128)(2,1)}, u32[]{:S(2)}, u32[]{:S(2)}) collective-permute-start(bf16[2,8,208,256]{3,2,1,0:T(8,128)(2,1)} %slice.172), channel_id=1, source_target_pairs={{0,1},{1,0},{2,3},{3,2},{4,5},{5,4},{6,7},{7,6},{8,9},{9,8},{10,11... | collective-permute-start | bytes 5111816 | tf_op jit(solution)/shard_map/ppermute | solution.py:59
  586.0 26.3 %collective-permute-start.37 = (bf16[2,128,2048]{2,1,0:T(8,128)(2,1)}, bf16[2,128,2048]{2,1,0:T(8,128)(2,1)}, u32[]{:S(2)}, u32[]{:S(2)}) collective-permute-start(bf16[2,128,2048]{2,1,0:T(8,128)(2,1)} %get-tuple-element.187), channel_id=1, source_target_pairs={{0,4},{4,0},{8,12},{12,8},{16,20},{20,16},{24,28},{28,24},{1,5},{5... | collective-permute-start | bytes 3145736 | tf_op jit(solution)/shard_map/ppermute | solution.py:59
  594.8 39.6 %collective-permute-start.40 = (bf16[2,128,2048]{2,1,0:T(8,128)(2,1)}, bf16[2,128,2048]{2,1,0:T(8,128)(2,1)}, u32[]{:S(2)}, u32[]{:S(2)}) collective-permute-start(bf16[2,128,2048]{2,1,0:T(8,128)(2,1)} %get-tuple-element.186), channel_id=1, source_target_pairs={{0,4},{4,0},{8,12},{12,8},{16,20},{20,16},{24,28},{28,24},{1,5},{5... | collective-permute-start | bytes 3145736 | tf_op jit(solution)/shard_map/ppermute | solution.py:59
  614.6 31.0 %collective-permute-start.43 = (bf16[8,208,256]{2,1,0:T(8,128)(2,1)}, bf16[8,208,256]{2,1,0:T(8,128)(2,1)}, u32[]{:S(2)}, u32[]{:S(2)}) collective-permute-start(bf16[8,208,256]{2,1,0:T(8,128)(2,1)} %fusion.13), channel_id=1, source_target_pairs={{0,2},{1,3},{2,0},{3,1},{4,6},{5,7},{6,4},{7,5},{8,10},{9,11},{10,... | collective-permute-start | bytes 2555912 | tf_op jit(solution)/shard_map/ppermute | solution.py:59
  621.1 24.5 %collective-permute-start.42 = (bf16[128,2048]{1,0:T(8,128)(2,1)}, bf16[128,2048]{1,0:T(8,128)(2,1)}, u32[]{:S(2)}, u32[]{:S(2)}) collective-permute-start(bf16[128,2048]{1,0:T(8,128)(2,1)} %get-tuple-element.182), channel_id=1, source_target_pairs={{0,24},{4,28},{8,0},{12,4},{16,8},{20,12},{24,16},{28,20},{1,25},{... | collective-permute-start | bytes 1572872 | tf_op jit(solution)/shard_map/ppermute | solution.py:59
  648.2 36.8 %all-to-all-start.3 = ((bf16[8,208,256]{2,1,0:T(8,128)(2,1)}), bf16[8,208,256]{2,1,0:T(8,128)(2,1)S(1)}, u32[]{:S(2)}, u32[]{:S(2)}) async-start(bf16[8,208,256]{2,1,0:T(8,128)(2,1)} %fusion), calls=%async_computation.4 | async-start | bytes 1703936 | tf_op jit(solution)/shard_map/all_to_all | solution.py:252
  (59 other events, 877.4 us)
Sparse Core Ops, SparseCore 0:
  88.8 130.2 all-gather.5
  221.2 80.2 all-gather.3
  414.1 99.2 reduce-scatter.1
